TPU v7x, 512 devices: a whole 4x4x16 slice. The times are simulated.
512 devices in a mesh: gx: 64 (over z, x_lo, core), gy: 8 (over x_hi, y).
Axes of the slice: x: 4 (x_hi: 2, x_lo: 2; x = x_hi * 2 + x_lo), y: 4, z: 16, core: 2. Of those that a mesh axis runs over, the one named last changes fastest.
Arguments:
- source: float32 [128, 128, 128], P('gx', 'gy'), may hold values from -8 to 8
- absorb: float32 [128, 128, 128], P('gx', 'gy'), may hold values from 0.001 to 0.01
- beta: float32 [128, 128, 128], P('gx', 'gy'), may hold values from 0.25 to 4.5
Outputs:
- solution_field: float32 [128, 128, 128], P('gx', 'gy')
All inputs are finite; a program needn't handle non-finite values.
Results may differ from a plain program's by a relative error of at most 0.00004.
Values sent between devices are 32-bit elements; how exact they have to be, the bound alone decides.
No kernel may reach another device: no remote copies, remote signals or barrier semaphores. Data moves between devices by JAX's collectives and lax.ppermute only.
A program may use at most 64 MiB of HBM per device.

v0:
```python
import jax
import jax.numpy as jnp
from jax import lax
from jax.sharding import PartitionSpec as P

LEVELS = 4
SWEEPS = 4
BOTTOM = 8


def extended(shard, sides, width):
    for axis, dim in sides:
        devices, length = (lax.axis_size(axis), shard.shape[dim])
        up = [(i, (i + 1) % devices) for i in range(devices - 1)]
        down = [(j, i) for i, j in up]
        last = lax.slice_in_dim(shard, length - width, length, axis=dim)
        initial = lax.slice_in_dim(shard, 0, width, axis=dim)
        before = lax.ppermute(last, axis, up)
        after = lax.ppermute(initial, axis, down)
        shard = jnp.concatenate([before, shard, after], axis=dim)
    return shard


def shifted(value, axis, steps):
    count = lax.axis_size(axis)
    initial, last = (max(0, -steps), min(count, count - steps))
    return lax.ppermute(value, axis, [(source, source + steps) for source in range(initial, last)])


def chebyshev_table(count):
    centre = 1.125
    half_width = 0.875
    ratio = centre / half_width
    factor = 1.0 / ratio
    table = [(0.0, 1.0 / centre)]
    for order in range(1, count):
        fresh_factor = 1.0 / (2.0 * ratio - factor)
        table.append((fresh_factor * factor, 2.0 * fresh_factor / half_width))
        factor = fresh_factor
    return table


def extend(field, stride):
    sides = extended(field, (("gy", 1),), 1)
    below = shifted(field[-1:], "gx", stride)
    above = shifted(field[:1], "gx", -stride)
    below = jnp.pad(below, ((0, 0), (1, 1), (0, 0)))
    above = jnp.pad(above, ((0, 0), (1, 1), (0, 0)))
    joined = jnp.concatenate([below, sides, above], 0)
    return jnp.pad(joined, ((0, 0), (0, 0), (1, 1)))


def neighbours(padded):
    return [
        padded[:-2, 1:-1, 1:-1],
        padded[2:, 1:-1, 1:-1],
        padded[1:-1, :-2, 1:-1],
        padded[1:-1, 2:, 1:-1],
        padded[1:-1, 1:-1, :-2],
        padded[1:-1, 1:-1, 2:],
    ]


def prepare(absorb, beta, half, stride):
    weights = [half * (beta + other) for other in neighbours(extend(beta, stride))]
    diagonal = absorb
    for weight in weights:
        diagonal = diagonal + weight
    return (weights, diagonal, 1.0 / diagonal)


def operate(field, parts, stride):
    weights, diagonal, inverse = parts
    result = diagonal * field
    for weight, other in zip(weights, neighbours(extend(field, stride))):
        result = result - weight * other
    return result


def smooth(guess, source, parts, count, fresh, stride):
    inverse = parts[2]
    current = guess
    previous = guess
    for order, (carry, push) in enumerate(chebyshev_table(count)):
        if order == 0 and fresh:
            residual = source
        else:
            residual = source - operate(current, parts, stride)
        update = current + carry * (current - previous) + push * (inverse * residual)
        previous = current
        current = update
    return current


def restrict(residual, absorb, beta, stride, position):
    planes, rows, depth = residual.shape
    stacked = jnp.stack([residual, absorb, beta], 0)
    partner = shifted(stacked, "gx", -stride)
    joined = jnp.concatenate([stacked, partner], 1)
    coarse = joined.reshape(3, planes, 2, rows // 2, 2, depth // 2, 2).sum((2, 4, 6)) * 0.125
    holder = position % (2 * stride) == 0
    return (
        jnp.where(holder, coarse[0], 0.0),
        jnp.where(holder, coarse[1], 1.0),
        jnp.where(holder, coarse[2], 1.0),
    )


def prolong(correction, planes, stride, position):
    offsets = jnp.arange(planes, dtype=jnp.int32)
    received = shifted(correction, "gx", stride)
    upper = position // stride % 2
    chosen = jnp.where(upper == 1, received, correction)
    picked = jnp.take(chosen, (planes * upper + offsets) // 2, axis=0)
    return jnp.repeat(jnp.repeat(picked, 2, 1), 2, 2)


def descend(source, absorb, beta, level, position):
    stride = 2**level
    half = 0.5 * 0.25**level
    zeros = jnp.zeros_like(source)
    parts = prepare(absorb, beta, half, stride)
    if level == LEVELS - 1:
        return smooth(zeros, source, parts, BOTTOM, True, stride)
    planes = source.shape[0]
    current = smooth(zeros, source, parts, SWEEPS, True, stride)
    residual = source - operate(current, parts, stride)
    coarse_source, coarse_absorb, coarse_beta = restrict(residual, absorb, beta, stride, position)
    correction = descend(coarse_source, coarse_absorb, coarse_beta, level + 1, position)
    current = current + prolong(correction, planes, stride, position)
    return smooth(current, source, parts, SWEEPS, False, stride)


def body(source, absorb, beta):
    position = lax.axis_index("gx")
    return descend(source, absorb, beta, 0, position)


def solution(mesh):
    placed = (P("gx", "gy", None), P("gx", "gy", None), P("gx", "gy", None))
    return jax.shard_map(
        body, mesh=mesh, in_specs=placed, out_specs=P("gx", "gy", None), check_vma=False
    )
```

profile of v0, /device:TPU:280, one launch (start us, length us, event | category | flops | bytes accessed | tf_op | source)
XLA Modules:
  0.0 729.1 jit_solution(15159091541868610396)
XLA Ops:
  2.6 5.8 collective-permute-start.3
  15.7 7.1 collective-permute-done.2
  26.5 5.8 collective-permute-start.7
  38.2 5.1 collective-permute-done.6
  46.3 5.8 collective-permute-start.11
  54.0 7.5 %collective-permute-start.9 = (f32[2,1,128]{2,1,0:T(1,128)S(1)}, f32[2,1,128]{2,1,0:T(1,128)S(1)}, u32[]{:S(2)}, u32[]{:S(2)}) collective-permute-start(f32[2,1,128]{2,1,0:T(1,128)S(1)} %get-tuple-element.54), channel_id=1, source_target_pairs={{0,1},{1,2},{2,3},{3,4},{4,5},{5,6},{6,7},{8,9},{9,10},{10,11},{11... | collective-permute-start | bytes 3080 | tf_op jit(solution)/shard_map/ppermute | solution.py:18
  65.7 5.8 collective-permute-start.15
  71.5 7.8 %collective-permute-start.13 = (f32[2,1,128]{2,1,0:T(1,128)S(1)}, f32[2,1,128]{2,1,0:T(1,128)S(1)}, u32[]{:S(2)}, u32[]{:S(2)}) collective-permute-start(f32[2,1,128]{2,1,0:T(1,128)S(1)} %get-tuple-element.50), channel_id=1, source_target_pairs={{0,1},{1,2},{2,3},{3,4},{4,5},{5,6},{6,7},{8,9},{9,10},{10,11},{11... | collective-permute-start | bytes 3080 | tf_op jit(solution)/shard_map/ppermute | solution.py:18
  81.3 7.1 collective-permute-done.14
  91.4 5.8 collective-permute-start.19
  103.0 5.1 collective-permute-done.18
  114.3 7.7 %reshape.258 = f32[3,2,2,8,2,64,2]{6,5,4,3,2,1,0:T(8,128)} reshape(f32[3,4,16,128]{3,2,1,0:T(8,128)S(1)} %pad_maximum_fusion) | data formatting | bytes 196608 | tf_op jit(solution)/shard_map/reshape | solution.py:100
  127.3 6.0 collective-permute-start.24
  146.4 6.0 collective-permute-start.28
  165.6 6.0 collective-permute-start.32
  184.7 6.0 collective-permute-start.36
  203.9 6.0 collective-permute-start.40
  230.6 5.1 collective-permute-start.45
  241.7 5.1 collective-permute-done.44
  248.9 5.1 collective-permute-start.49
  260.0 5.1 collective-permute-done.48
  267.1 5.1 collective-permute-start.53
  278.2 5.1 collective-permute-done.52
  285.4 5.1 collective-permute-start.57
  296.5 5.1 collective-permute-done.56
  303.6 5.1 collective-permute-start.61
  314.7 5.1 collective-permute-done.60
  327.9 6.0 collective-permute-start.66
  339.9 5.1 collective-permute-done.65
  347.1 6.0 collective-permute-start.70
  359.0 5.1 collective-permute-done.69
  366.2 6.0 collective-permute-start.74
  378.2 5.1 collective-permute-done.73
  385.3 6.0 collective-permute-start.78
  397.3 5.1 collective-permute-done.77
  404.5 6.0 collective-permute-start.82
  416.4 5.1 collective-permute-done.81
  423.6 6.0 collective-permute-start.86
  435.6 5.1 collective-permute-done.85
  442.8 6.0 collective-permute-start.90
  454.7 5.1 collective-permute-done.89
  461.9 6.0 collective-permute-start.94
  473.9 5.1 collective-permute-done.93
  488.6 5.1 collective-permute-start.99
  507.0 5.1 collective-permute-start.103
  525.3 5.1 collective-permute-start.107
  536.3 5.1 collective-permute-done.106
  543.5 5.1 collective-permute-start.111
  561.8 5.7 collective-permute-done.112
  570.2 6.0 collective-permute-start.116
  582.2 5.1 collective-permute-done.115
  589.4 6.0 collective-permute-start.120
  601.3 5.1 collective-permute-done.119
  608.5 6.0 collective-permute-start.124
  627.7 6.0 collective-permute-start.128
  646.9 5.1 collective-permute-done.129
  654.8 5.8 collective-permute-start.133
  666.5 5.1 collective-permute-done.132
  673.7 5.8 collective-permute-start.137
  685.4 5.1 collective-permute-done.136
  692.6 5.8 collective-permute-start.141
  704.3 5.1 collective-permute-done.140
  711.5 5.8 collective-permute-start.145
  723.2 5.1 collective-permute-done.144
  (496 shorter events, 365.5 us)
Async XLA Ops:
  0.7 14.9 %collective-permute-start = (f32[1,16,128]{2,1,0:T(8,128)S(1)}, f32[1,16,128]{2,1,0:T(8,128)S(1)}, u32[]{:S(2)}, u32[]{:S(2)}) collective-permute-start(f32[1,16,128]{2,1,0:T(8,128)S(1)} %get-tuple-element.63), channel_id=1, source_target_pairs={{0,8},{8,16},{16,24},{24,32},{32,40},{40,48},{48,56},{56,64},{64,7... | collective-permute-start | bytes 24584 | tf_op jit(solution)/shard_map/ppermute | solution.py:27
  2.6 13.0 %collective-permute-start.3 = (f32[1,16,128]{2,1,0:T(8,128)S(1)}, f32[1,16,128]{2,1,0:T(8,128)S(1)}, u32[]{:S(2)}, u32[]{:S(2)}) collective-permute-start(f32[1,16,128]{2,1,0:T(8,128)S(1)} %get-tuple-element.62), channel_id=1, source_target_pairs={{8,0},{16,8},{24,16},{32,24},{40,32},{48,40},{56,48},{64,56},{72,6... | collective-permute-start | bytes 24584 | tf_op jit(solution)/shard_map/ppermute | solution.py:27
  24.6 13.6 %collective-permute-start.4 = (f32[1,16,128]{2,1,0:T(8,128)S(1)}, f32[1,16,128]{2,1,0:T(8,128)S(1)}, u32[]{:S(2)}, u32[]{:S(2)}) collective-permute-start(f32[1,16,128]{2,1,0:T(8,128)S(1)} %get-tuple-element.60), channel_id=1, source_target_pairs={{0,8},{8,16},{16,24},{24,32},{32,40},{40,48},{48,56},{56,64},{64,7... | collective-permute-start | bytes 24584 | tf_op jit(solution)/shard_map/ppermute | solution.py:27
  26.5 11.7 %collective-permute-start.7 = (f32[1,16,128]{2,1,0:T(8,128)S(1)}, f32[1,16,128]{2,1,0:T(8,128)S(1)}, u32[]{:S(2)}, u32[]{:S(2)}) collective-permute-start(f32[1,16,128]{2,1,0:T(8,128)S(1)} %get-tuple-element.61), channel_id=1, source_target_pairs={{8,0},{16,8},{24,16},{32,24},{40,32},{48,40},{56,48},{64,56},{72,6... | collective-permute-start | bytes 24584 | tf_op jit(solution)/shard_map/ppermute | solution.py:27
  44.3 17.2 %collective-permute-start.8 = (f32[1,16,128]{2,1,0:T(8,128)S(1)}, f32[1,16,128]{2,1,0:T(8,128)S(1)}, u32[]{:S(2)}, u32[]{:S(2)}) collective-permute-start(f32[1,16,128]{2,1,0:T(8,128)S(1)} %get-tuple-element.56), channel_id=1, source_target_pairs={{0,8},{8,16},{16,24},{24,32},{32,40},{40,48},{48,56},{56,64},{64,7... | collective-permute-start | bytes 24584 | tf_op jit(solution)/shard_map/ppermute | solution.py:27
  46.3 15.3 %collective-permute-start.11 = (f32[1,16,128]{2,1,0:T(8,128)S(1)}, f32[1,16,128]{2,1,0:T(8,128)S(1)}, u32[]{:S(2)}, u32[]{:S(2)}) collective-permute-start(f32[1,16,128]{2,1,0:T(8,128)S(1)} %get-tuple-element.57), channel_id=1, source_target_pairs={{8,0},{16,8},{24,16},{32,24},{40,32},{48,40},{56,48},{64,56},{72,6... | collective-permute-start | bytes 24584 | tf_op jit(solution)/shard_map/ppermute | solution.py:27
  63.8 17.4 %collective-permute-start.12 = (f32[1,16,128]{2,1,0:T(8,128)S(1)}, f32[1,16,128]{2,1,0:T(8,128)S(1)}, u32[]{:S(2)}, u32[]{:S(2)}) collective-permute-start(f32[1,16,128]{2,1,0:T(8,128)S(1)} %get-tuple-element.52), channel_id=1, source_target_pairs={{0,8},{8,16},{16,24},{24,32},{32,40},{40,48},{48,56},{56,64},{64,7... | collective-permute-start | bytes 24584 | tf_op jit(solution)/shard_map/ppermute | solution.py:27
  65.7 15.5 %collective-permute-start.15 = (f32[1,16,128]{2,1,0:T(8,128)S(1)}, f32[1,16,128]{2,1,0:T(8,128)S(1)}, u32[]{:S(2)}, u32[]{:S(2)}) collective-permute-start(f32[1,16,128]{2,1,0:T(8,128)S(1)} %get-tuple-element.53), channel_id=1, source_target_pairs={{8,0},{16,8},{24,16},{32,24},{40,32},{48,40},{56,48},{64,56},{72,6... | collective-permute-start | bytes 24584 | tf_op jit(solution)/shard_map/ppermute | solution.py:27
  89.4 13.6 %collective-permute-start.16 = (f32[1,16,128]{2,1,0:T(8,128)S(1)}, f32[1,16,128]{2,1,0:T(8,128)S(1)}, u32[]{:S(2)}, u32[]{:S(2)}) collective-permute-start(f32[1,16,128]{2,1,0:T(8,128)S(1)} %get-tuple-element.48), channel_id=1, source_target_pairs={{0,8},{8,16},{16,24},{24,32},{32,40},{40,48},{48,56},{56,64},{64,7... | collective-permute-start | bytes 24584 | tf_op jit(solution)/shard_map/ppermute | solution.py:27
  91.4 11.7 %collective-permute-start.19 = (f32[1,16,128]{2,1,0:T(8,128)S(1)}, f32[1,16,128]{2,1,0:T(8,128)S(1)}, u32[]{:S(2)}, u32[]{:S(2)}) collective-permute-start(f32[1,16,128]{2,1,0:T(8,128)S(1)} %get-tuple-element.49), channel_id=1, source_target_pairs={{8,0},{16,8},{24,16},{32,24},{40,32},{48,40},{56,48},{64,56},{72,6... | collective-permute-start | bytes 24584 | tf_op jit(solution)/shard_map/ppermute | solution.py:27
  125.3 13.9 %collective-permute-start.21 = (f32[1,8,64]{2,1,0:T(8,128)S(1)}, f32[1,8,64]{2,1,0:T(8,128)S(1)}, u32[]{:S(2)}, u32[]{:S(2)}) collective-permute-start(f32[1,8,64]{2,1,0:T(8,128)S(1)} %get-tuple-element.101), channel_id=1, source_target_pairs={{0,16},{8,24},{16,32},{24,40},{32,48},{40,56},{48,64},{56,72},{64,... | collective-permute-start | bytes 6152 | tf_op jit(solution)/shard_map/ppermute | solution.py:27
  127.3 12.0 %collective-permute-start.24 = (f32[1,8,64]{2,1,0:T(8,128)S(1)}, f32[1,8,64]{2,1,0:T(8,128)S(1)}, u32[]{:S(2)}, u32[]{:S(2)}) collective-permute-start(f32[1,8,64]{2,1,0:T(8,128)S(1)} %get-tuple-element.100), channel_id=1, source_target_pairs={{16,0},{24,8},{32,16},{40,24},{48,32},{56,40},{64,48},{72,56},{80,... | collective-permute-start | bytes 6152 | tf_op jit(solution)/shard_map/ppermute | solution.py:27
  144.5 13.8 %collective-permute-start.25 = (f32[1,8,64]{2,1,0:T(8,128)S(1)}, f32[1,8,64]{2,1,0:T(8,128)S(1)}, u32[]{:S(2)}, u32[]{:S(2)}) collective-permute-start(f32[1,8,64]{2,1,0:T(8,128)S(1)} %get-tuple-element.98), channel_id=1, source_target_pairs={{0,16},{8,24},{16,32},{24,40},{32,48},{40,56},{48,64},{56,72},{64,... | collective-permute-start | bytes 6152 | tf_op jit(solution)/shard_map/ppermute | solution.py:27
  146.4 11.9 %collective-permute-start.28 = (f32[1,8,64]{2,1,0:T(8,128)S(1)}, f32[1,8,64]{2,1,0:T(8,128)S(1)}, u32[]{:S(2)}, u32[]{:S(2)}) collective-permute-start(f32[1,8,64]{2,1,0:T(8,128)S(1)} %get-tuple-element.99), channel_id=1, source_target_pairs={{16,0},{24,8},{32,16},{40,24},{48,32},{56,40},{64,48},{72,56},{80,... | collective-permute-start | bytes 6152 | tf_op jit(solution)/shard_map/ppermute | solution.py:27
  163.7 13.8 %collective-permute-start.29 = (f32[1,8,64]{2,1,0:T(8,128)S(1)}, f32[1,8,64]{2,1,0:T(8,128)S(1)}, u32[]{:S(2)}, u32[]{:S(2)}) collective-permute-start(f32[1,8,64]{2,1,0:T(8,128)S(1)} %get-tuple-element.94), channel_id=1, source_target_pairs={{0,16},{8,24},{16,32},{24,40},{32,48},{40,56},{48,64},{56,72},{64,... | collective-permute-start | bytes 6152 | tf_op jit(solution)/shard_map/ppermute | solution.py:27
  165.6 11.9 %collective-permute-start.32 = (f32[1,8,64]{2,1,0:T(8,128)S(1)}, f32[1,8,64]{2,1,0:T(8,128)S(1)}, u32[]{:S(2)}, u32[]{:S(2)}) collective-permute-start(f32[1,8,64]{2,1,0:T(8,128)S(1)} %get-tuple-element.95), channel_id=1, source_target_pairs={{16,0},{24,8},{32,16},{40,24},{48,32},{56,40},{64,48},{72,56},{80,... | collective-permute-start | bytes 6152 | tf_op jit(solution)/shard_map/ppermute | solution.py:27
  182.8 13.8 %collective-permute-start.33 = (f32[1,8,64]{2,1,0:T(8,128)S(1)}, f32[1,8,64]{2,1,0:T(8,128)S(1)}, u32[]{:S(2)}, u32[]{:S(2)}) collective-permute-start(f32[1,8,64]{2,1,0:T(8,128)S(1)} %get-tuple-element.90), channel_id=1, source_target_pairs={{0,16},{8,24},{16,32},{24,40},{32,48},{40,56},{48,64},{56,72},{64,... | collective-permute-start | bytes 6152 | tf_op jit(solution)/shard_map/ppermute | solution.py:27
  184.7 11.9 %collective-permute-start.36 = (f32[1,8,64]{2,1,0:T(8,128)S(1)}, f32[1,8,64]{2,1,0:T(8,128)S(1)}, u32[]{:S(2)}, u32[]{:S(2)}) collective-permute-start(f32[1,8,64]{2,1,0:T(8,128)S(1)} %get-tuple-element.91), channel_id=1, source_target_pairs={{16,0},{24,8},{32,16},{40,24},{48,32},{56,40},{64,48},{72,56},{80,... | collective-permute-start | bytes 6152 | tf_op jit(solution)/shard_map/ppermute | solution.py:27
  202.0 13.9 %collective-permute-start.37 = (f32[1,8,64]{2,1,0:T(8,128)S(1)}, f32[1,8,64]{2,1,0:T(8,128)S(1)}, u32[]{:S(2)}, u32[]{:S(2)}) collective-permute-start(f32[1,8,64]{2,1,0:T(8,128)S(1)} %get-tuple-element.86), channel_id=1, source_target_pairs={{0,16},{8,24},{16,32},{24,40},{32,48},{40,56},{48,64},{56,72},{64,... | collective-permute-start | bytes 6152 | tf_op jit(solution)/shard_map/ppermute | solution.py:27
  203.9 11.9 %collective-permute-start.40 = (f32[1,8,64]{2,1,0:T(8,128)S(1)}, f32[1,8,64]{2,1,0:T(8,128)S(1)}, u32[]{:S(2)}, u32[]{:S(2)}) collective-permute-start(f32[1,8,64]{2,1,0:T(8,128)S(1)} %get-tuple-element.87), channel_id=1, source_target_pairs={{16,0},{24,8},{32,16},{40,24},{48,32},{56,40},{64,48},{72,56},{80,... | collective-permute-start | bytes 6152 | tf_op jit(solution)/shard_map/ppermute | solution.py:27
  228.7 12.9 %collective-permute-start.42 = (f32[1,4,32]{2,1,0:T(4,128)S(1)}, f32[1,4,32]{2,1,0:T(4,128)S(1)}, u32[]{:S(2)}, u32[]{:S(2)}) collective-permute-start(f32[1,4,32]{2,1,0:T(4,128)S(1)} %get-tuple-element.137), channel_id=1, source_target_pairs={{0,32},{8,40},{16,48},{24,56},{32,64},{40,72},{48,80},{56,88},{64,... | collective-permute-start | bytes 1544 | tf_op jit(solution)/shard_map/ppermute | solution.py:27
  247.0 12.9 %collective-permute-start.46 = (f32[1,4,32]{2,1,0:T(4,128)S(1)}, f32[1,4,32]{2,1,0:T(4,128)S(1)}, u32[]{:S(2)}, u32[]{:S(2)}) collective-permute-start(f32[1,4,32]{2,1,0:T(4,128)S(1)} %get-tuple-element.134), channel_id=1, source_target_pairs={{0,32},{8,40},{16,48},{24,56},{32,64},{40,72},{48,80},{56,88},{64,... | collective-permute-start | bytes 1544 | tf_op jit(solution)/shard_map/ppermute | solution.py:27
  265.2 12.9 %collective-permute-start.50 = (f32[1,4,32]{2,1,0:T(4,128)S(1)}, f32[1,4,32]{2,1,0:T(4,128)S(1)}, u32[]{:S(2)}, u32[]{:S(2)}) collective-permute-start(f32[1,4,32]{2,1,0:T(4,128)S(1)} %get-tuple-element.130), channel_id=1, source_target_pairs={{0,32},{8,40},{16,48},{24,56},{32,64},{40,72},{48,80},{56,88},{64,... | collective-permute-start | bytes 1544 | tf_op jit(solution)/shard_map/ppermute | solution.py:27
  267.1 11.0 %collective-permute-start.53 = (f32[1,4,32]{2,1,0:T(4,128)S(1)}, f32[1,4,32]{2,1,0:T(4,128)S(1)}, u32[]{:S(2)}, u32[]{:S(2)}) collective-permute-start(f32[1,4,32]{2,1,0:T(4,128)S(1)} %get-tuple-element.131), channel_id=1, source_target_pairs={{32,0},{40,8},{48,16},{56,24},{64,32},{72,40},{80,48},{88,56},{96,... | collective-permute-start | bytes 1544 | tf_op jit(solution)/shard_map/ppermute | solution.py:27
  283.5 12.9 %collective-permute-start.54 = (f32[1,4,32]{2,1,0:T(4,128)S(1)}, f32[1,4,32]{2,1,0:T(4,128)S(1)}, u32[]{:S(2)}, u32[]{:S(2)}) collective-permute-start(f32[1,4,32]{2,1,0:T(4,128)S(1)} %get-tuple-element.126), channel_id=1, source_target_pairs={{0,32},{8,40},{16,48},{24,56},{32,64},{40,72},{48,80},{56,88},{64,... | collective-permute-start | bytes 1544 | tf_op jit(solution)/shard_map/ppermute | solution.py:27
  301.7 12.9 %collective-permute-start.58 = (f32[1,4,32]{2,1,0:T(4,128)S(1)}, f32[1,4,32]{2,1,0:T(4,128)S(1)}, u32[]{:S(2)}, u32[]{:S(2)}) collective-permute-start(f32[1,4,32]{2,1,0:T(4,128)S(1)} %get-tuple-element.122), channel_id=1, source_target_pairs={{0,32},{8,40},{16,48},{24,56},{32,64},{40,72},{48,80},{56,88},{64,... | collective-permute-start | bytes 1544 | tf_op jit(solution)/shard_map/ppermute | solution.py:27
  303.6 11.0 %collective-permute-start.61 = (f32[1,4,32]{2,1,0:T(4,128)S(1)}, f32[1,4,32]{2,1,0:T(4,128)S(1)}, u32[]{:S(2)}, u32[]{:S(2)}) collective-permute-start(f32[1,4,32]{2,1,0:T(4,128)S(1)} %get-tuple-element.123), channel_id=1, source_target_pairs={{32,0},{40,8},{48,16},{56,24},{64,32},{72,40},{80,48},{88,56},{96,... | collective-permute-start | bytes 1544 | tf_op jit(solution)/shard_map/ppermute | solution.py:27
  326.0 13.8 %collective-permute-start.63 = (f32[1,2,16]{2,1,0:T(2,128)S(1)}, f32[1,2,16]{2,1,0:T(2,128)S(1)}, u32[]{:S(2)}, u32[]{:S(2)}) collective-permute-start(f32[1,2,16]{2,1,0:T(2,128)S(1)} %get-tuple-element.169), channel_id=1, source_target_pairs={{0,64},{8,72},{16,80},{24,88},{32,96},{40,104},{48,112},{56,120},{... | collective-permute-start | bytes 392 | tf_op jit(solution)/shard_map/ppermute | solution.py:27
  327.9 11.9 %collective-permute-start.66 = (f32[1,2,16]{2,1,0:T(2,128)S(1)}, f32[1,2,16]{2,1,0:T(2,128)S(1)}, u32[]{:S(2)}, u32[]{:S(2)}) collective-permute-start(f32[1,2,16]{2,1,0:T(2,128)S(1)} %get-tuple-element.168), channel_id=1, source_target_pairs={{64,0},{72,8},{80,16},{88,24},{96,32},{104,40},{112,48},{120,56},{... | collective-permute-start | bytes 392 | tf_op jit(solution)/shard_map/ppermute | solution.py:27
  345.1 13.8 %collective-permute-start.67 = (f32[1,2,16]{2,1,0:T(2,128)S(1)}, f32[1,2,16]{2,1,0:T(2,128)S(1)}, u32[]{:S(2)}, u32[]{:S(2)}) collective-permute-start(f32[1,2,16]{2,1,0:T(2,128)S(1)} %get-tuple-element.166), channel_id=1, source_target_pairs={{0,64},{8,72},{16,80},{24,88},{32,96},{40,104},{48,112},{56,120},{... | collective-permute-start | bytes 392 | tf_op jit(solution)/shard_map/ppermute | solution.py:27
  347.1 11.9 %collective-permute-start.70 = (f32[1,2,16]{2,1,0:T(2,128)S(1)}, f32[1,2,16]{2,1,0:T(2,128)S(1)}, u32[]{:S(2)}, u32[]{:S(2)}) collective-permute-start(f32[1,2,16]{2,1,0:T(2,128)S(1)} %get-tuple-element.167), channel_id=1, source_target_pairs={{64,0},{72,8},{80,16},{88,24},{96,32},{104,40},{112,48},{120,56},{... | collective-permute-start | bytes 392 | tf_op jit(solution)/shard_map/ppermute | solution.py:27
  364.3 13.8 %collective-permute-start.71 = (f32[1,2,16]{2,1,0:T(2,128)S(1)}, f32[1,2,16]{2,1,0:T(2,128)S(1)}, u32[]{:S(2)}, u32[]{:S(2)}) collective-permute-start(f32[1,2,16]{2,1,0:T(2,128)S(1)} %get-tuple-element.162), channel_id=1, source_target_pairs={{0,64},{8,72},{16,80},{24,88},{32,96},{40,104},{48,112},{56,120},{... | collective-permute-start | bytes 392 | tf_op jit(solution)/shard_map/ppermute | solution.py:27
  366.2 11.9 %collective-permute-start.74 = (f32[1,2,16]{2,1,0:T(2,128)S(1)}, f32[1,2,16]{2,1,0:T(2,128)S(1)}, u32[]{:S(2)}, u32[]{:S(2)}) collective-permute-start(f32[1,2,16]{2,1,0:T(2,128)S(1)} %get-tuple-element.163), channel_id=1, source_target_pairs={{64,0},{72,8},{80,16},{88,24},{96,32},{104,40},{112,48},{120,56},{... | collective-permute-start | bytes 392 | tf_op jit(solution)/shard_map/ppermute | solution.py:27
  383.4 13.8 %collective-permute-start.75 = (f32[1,2,16]{2,1,0:T(2,128)S(1)}, f32[1,2,16]{2,1,0:T(2,128)S(1)}, u32[]{:S(2)}, u32[]{:S(2)}) collective-permute-start(f32[1,2,16]{2,1,0:T(2,128)S(1)} %get-tuple-element.158), channel_id=1, source_target_pairs={{0,64},{8,72},{16,80},{24,88},{32,96},{40,104},{48,112},{56,120},{... | collective-permute-start | bytes 392 | tf_op jit(solution)/shard_map/ppermute | solution.py:27
  385.3 11.9 %collective-permute-start.78 = (f32[1,2,16]{2,1,0:T(2,128)S(1)}, f32[1,2,16]{2,1,0:T(2,128)S(1)}, u32[]{:S(2)}, u32[]{:S(2)}) collective-permute-start(f32[1,2,16]{2,1,0:T(2,128)S(1)} %get-tuple-element.159), channel_id=1, source_target_pairs={{64,0},{72,8},{80,16},{88,24},{96,32},{104,40},{112,48},{120,56},{... | collective-permute-start | bytes 392 | tf_op jit(solution)/shard_map/ppermute | solution.py:27
  402.6 13.8 %collective-permute-start.79 = (f32[1,2,16]{2,1,0:T(2,128)S(1)}, f32[1,2,16]{2,1,0:T(2,128)S(1)}, u32[]{:S(2)}, u32[]{:S(2)}) collective-permute-start(f32[1,2,16]{2,1,0:T(2,128)S(1)} %get-tuple-element.154), channel_id=1, source_target_pairs={{0,64},{8,72},{16,80},{24,88},{32,96},{40,104},{48,112},{56,120},{... | collective-permute-start | bytes 392 | tf_op jit(solution)/shard_map/ppermute | solution.py:27
  404.5 11.9 %collective-permute-start.82 = (f32[1,2,16]{2,1,0:T(2,128)S(1)}, f32[1,2,16]{2,1,0:T(2,128)S(1)}, u32[]{:S(2)}, u32[]{:S(2)}) collective-permute-start(f32[1,2,16]{2,1,0:T(2,128)S(1)} %get-tuple-element.155), channel_id=1, source_target_pairs={{64,0},{72,8},{80,16},{88,24},{96,32},{104,40},{112,48},{120,56},{... | collective-permute-start | bytes 392 | tf_op jit(solution)/shard_map/ppermute | solution.py:27
  421.7 13.8 %collective-permute-start.83 = (f32[1,2,16]{2,1,0:T(2,128)S(1)}, f32[1,2,16]{2,1,0:T(2,128)S(1)}, u32[]{:S(2)}, u32[]{:S(2)}) collective-permute-start(f32[1,2,16]{2,1,0:T(2,128)S(1)} %get-tuple-element.150), channel_id=1, source_target_pairs={{0,64},{8,72},{16,80},{24,88},{32,96},{40,104},{48,112},{56,120},{... | collective-permute-start | bytes 392 | tf_op jit(solution)/shard_map/ppermute | solution.py:27
  423.6 11.9 %collective-permute-start.86 = (f32[1,2,16]{2,1,0:T(2,128)S(1)}, f32[1,2,16]{2,1,0:T(2,128)S(1)}, u32[]{:S(2)}, u32[]{:S(2)}) collective-permute-start(f32[1,2,16]{2,1,0:T(2,128)S(1)} %get-tuple-element.151), channel_id=1, source_target_pairs={{64,0},{72,8},{80,16},{88,24},{96,32},{104,40},{112,48},{120,56},{... | collective-permute-start | bytes 392 | tf_op jit(solution)/shard_map/ppermute | solution.py:27
  440.9 13.8 %collective-permute-start.87 = (f32[1,2,16]{2,1,0:T(2,128)S(1)}, f32[1,2,16]{2,1,0:T(2,128)S(1)}, u32[]{:S(2)}, u32[]{:S(2)}) collective-permute-start(f32[1,2,16]{2,1,0:T(2,128)S(1)} %get-tuple-element.146), channel_id=1, source_target_pairs={{0,64},{8,72},{16,80},{24,88},{32,96},{40,104},{48,112},{56,120},{... | collective-permute-start | bytes 392 | tf_op jit(solution)/shard_map/ppermute | solution.py:27
  442.8 11.9 %collective-permute-start.90 = (f32[1,2,16]{2,1,0:T(2,128)S(1)}, f32[1,2,16]{2,1,0:T(2,128)S(1)}, u32[]{:S(2)}, u32[]{:S(2)}) collective-permute-start(f32[1,2,16]{2,1,0:T(2,128)S(1)} %get-tuple-element.147), channel_id=1, source_target_pairs={{64,0},{72,8},{80,16},{88,24},{96,32},{104,40},{112,48},{120,56},{... | collective-permute-start | bytes 392 | tf_op jit(solution)/shard_map/ppermute | solution.py:27
  460.0 13.8 %collective-permute-start.91 = (f32[1,2,16]{2,1,0:T(2,128)S(1)}, f32[1,2,16]{2,1,0:T(2,128)S(1)}, u32[]{:S(2)}, u32[]{:S(2)}) collective-permute-start(f32[1,2,16]{2,1,0:T(2,128)S(1)} %get-tuple-element.142), channel_id=1, source_target_pairs={{0,64},{8,72},{16,80},{24,88},{32,96},{40,104},{48,112},{56,120},{... | collective-permute-start | bytes 392 | tf_op jit(solution)/shard_map/ppermute | solution.py:27
  461.9 11.9 %collective-permute-start.94 = (f32[1,2,16]{2,1,0:T(2,128)S(1)}, f32[1,2,16]{2,1,0:T(2,128)S(1)}, u32[]{:S(2)}, u32[]{:S(2)}) collective-permute-start(f32[1,2,16]{2,1,0:T(2,128)S(1)} %get-tuple-element.143), channel_id=1, source_target_pairs={{64,0},{72,8},{80,16},{88,24},{96,32},{104,40},{112,48},{120,56},{... | collective-permute-start | bytes 392 | tf_op jit(solution)/shard_map/ppermute | solution.py:27
  486.7 13.1 %collective-permute-start.96 = (f32[1,4,32]{2,1,0:T(4,128)S(1)}, f32[1,4,32]{2,1,0:T(4,128)S(1)}, u32[]{:S(2)}, u32[]{:S(2)}) collective-permute-start(f32[1,4,32]{2,1,0:T(4,128)S(1)} %get-tuple-element.118), channel_id=1, source_target_pairs={{0,32},{8,40},{16,48},{24,56},{32,64},{40,72},{48,80},{56,88},{64,... | collective-permute-start | bytes 1544 | tf_op jit(solution)/shard_map/ppermute | solution.py:27
  488.6 11.2 %collective-permute-start.99 = (f32[1,4,32]{2,1,0:T(4,128)S(1)}, f32[1,4,32]{2,1,0:T(4,128)S(1)}, u32[]{:S(2)}, u32[]{:S(2)}) collective-permute-start(f32[1,4,32]{2,1,0:T(4,128)S(1)} %get-tuple-element.119), channel_id=1, source_target_pairs={{32,0},{40,8},{48,16},{56,24},{64,32},{72,40},{80,48},{88,56},{96,... | collective-permute-start | bytes 1544 | tf_op jit(solution)/shard_map/ppermute | solution.py:27
  505.1 12.9 %collective-permute-start.100 = (f32[1,4,32]{2,1,0:T(4,128)S(1)}, f32[1,4,32]{2,1,0:T(4,128)S(1)}, u32[]{:S(2)}, u32[]{:S(2)}) collective-permute-start(f32[1,4,32]{2,1,0:T(4,128)S(1)} %get-tuple-element.114), channel_id=1, source_target_pairs={{0,32},{8,40},{16,48},{24,56},{32,64},{40,72},{48,80},{56,88},{64,... | collective-permute-start | bytes 1544 | tf_op jit(solution)/shard_map/ppermute | solution.py:27
  523.4 12.9 %collective-permute-start.104 = (f32[1,4,32]{2,1,0:T(4,128)S(1)}, f32[1,4,32]{2,1,0:T(4,128)S(1)}, u32[]{:S(2)}, u32[]{:S(2)}) collective-permute-start(f32[1,4,32]{2,1,0:T(4,128)S(1)} %get-tuple-element.110), channel_id=1, source_target_pairs={{0,32},{8,40},{16,48},{24,56},{32,64},{40,72},{48,80},{56,88},{64,... | collective-permute-start | bytes 1544 | tf_op jit(solution)/shard_map/ppermute | solution.py:27
  541.6 12.9 %collective-permute-start.108 = (f32[1,4,32]{2,1,0:T(4,128)S(1)}, f32[1,4,32]{2,1,0:T(4,128)S(1)}, u32[]{:S(2)}, u32[]{:S(2)}) collective-permute-start(f32[1,4,32]{2,1,0:T(4,128)S(1)} %get-tuple-element.106), channel_id=1, source_target_pairs={{0,32},{8,40},{16,48},{24,56},{32,64},{40,72},{48,80},{56,88},{64,... | collective-permute-start | bytes 1544 | tf_op jit(solution)/shard_map/ppermute | solution.py:27
  568.3 13.8 %collective-permute-start.113 = (f32[1,8,64]{2,1,0:T(8,128)S(1)}, f32[1,8,64]{2,1,0:T(8,128)S(1)}, u32[]{:S(2)}, u32[]{:S(2)}) collective-permute-start(f32[1,8,64]{2,1,0:T(8,128)S(1)} %get-tuple-element.82), channel_id=1, source_target_pairs={{0,16},{8,24},{16,32},{24,40},{32,48},{40,56},{48,64},{56,72},{64,... | collective-permute-start | bytes 6152 | tf_op jit(solution)/shard_map/ppermute | solution.py:27
  570.2 11.9 %collective-permute-start.116 = (f32[1,8,64]{2,1,0:T(8,128)S(1)}, f32[1,8,64]{2,1,0:T(8,128)S(1)}, u32[]{:S(2)}, u32[]{:S(2)}) collective-permute-start(f32[1,8,64]{2,1,0:T(8,128)S(1)} %get-tuple-element.83), channel_id=1, source_target_pairs={{16,0},{24,8},{32,16},{40,24},{48,32},{56,40},{64,48},{72,56},{80,... | collective-permute-start | bytes 6152 | tf_op jit(solution)/shard_map/ppermute | solution.py:27
  587.4 13.8 %collective-permute-start.117 = (f32[1,8,64]{2,1,0:T(8,128)S(1)}, f32[1,8,64]{2,1,0:T(8,128)S(1)}, u32[]{:S(2)}, u32[]{:S(2)}) collective-permute-start(f32[1,8,64]{2,1,0:T(8,128)S(1)} %get-tuple-element.78), channel_id=1, source_target_pairs={{0,16},{8,24},{16,32},{24,40},{32,48},{40,56},{48,64},{56,72},{64,... | collective-permute-start | bytes 6152 | tf_op jit(solution)/shard_map/ppermute | solution.py:27
  589.4 11.9 %collective-permute-start.120 = (f32[1,8,64]{2,1,0:T(8,128)S(1)}, f32[1,8,64]{2,1,0:T(8,128)S(1)}, u32[]{:S(2)}, u32[]{:S(2)}) collective-permute-start(f32[1,8,64]{2,1,0:T(8,128)S(1)} %get-tuple-element.79), channel_id=1, source_target_pairs={{16,0},{24,8},{32,16},{40,24},{48,32},{56,40},{64,48},{72,56},{80,... | collective-permute-start | bytes 6152 | tf_op jit(solution)/shard_map/ppermute | solution.py:27
  606.6 13.8 %collective-permute-start.121 = (f32[1,8,64]{2,1,0:T(8,128)S(1)}, f32[1,8,64]{2,1,0:T(8,128)S(1)}, u32[]{:S(2)}, u32[]{:S(2)}) collective-permute-start(f32[1,8,64]{2,1,0:T(8,128)S(1)} %get-tuple-element.74), channel_id=1, source_target_pairs={{0,16},{8,24},{16,32},{24,40},{32,48},{40,56},{48,64},{56,72},{64,... | collective-permute-start | bytes 6152 | tf_op jit(solution)/shard_map/ppermute | solution.py:27
  608.5 11.9 %collective-permute-start.124 = (f32[1,8,64]{2,1,0:T(8,128)S(1)}, f32[1,8,64]{2,1,0:T(8,128)S(1)}, u32[]{:S(2)}, u32[]{:S(2)}) collective-permute-start(f32[1,8,64]{2,1,0:T(8,128)S(1)} %get-tuple-element.75), channel_id=1, source_target_pairs={{16,0},{24,8},{32,16},{40,24},{48,32},{56,40},{64,48},{72,56},{80,... | collective-permute-start | bytes 6152 | tf_op jit(solution)/shard_map/ppermute | solution.py:27
  625.8 13.8 %collective-permute-start.125 = (f32[1,8,64]{2,1,0:T(8,128)S(1)}, f32[1,8,64]{2,1,0:T(8,128)S(1)}, u32[]{:S(2)}, u32[]{:S(2)}) collective-permute-start(f32[1,8,64]{2,1,0:T(8,128)S(1)} %get-tuple-element.70), channel_id=1, source_target_pairs={{0,16},{8,24},{16,32},{24,40},{32,48},{40,56},{48,64},{56,72},{64,... | collective-permute-start | bytes 6152 | tf_op jit(solution)/shard_map/ppermute | solution.py:27
  627.7 11.9 %collective-permute-start.128 = (f32[1,8,64]{2,1,0:T(8,128)S(1)}, f32[1,8,64]{2,1,0:T(8,128)S(1)}, u32[]{:S(2)}, u32[]{:S(2)}) collective-permute-start(f32[1,8,64]{2,1,0:T(8,128)S(1)} %get-tuple-element.71), channel_id=1, source_target_pairs={{16,0},{24,8},{32,16},{40,24},{48,32},{56,40},{64,48},{72,56},{80,... | collective-permute-start | bytes 6152 | tf_op jit(solution)/shard_map/ppermute | solution.py:27
  652.9 13.6 %collective-permute-start.130 = (f32[1,16,128]{2,1,0:T(8,128)S(1)}, f32[1,16,128]{2,1,0:T(8,128)S(1)}, u32[]{:S(2)}, u32[]{:S(2)}) collective-permute-start(f32[1,16,128]{2,1,0:T(8,128)S(1)} %get-tuple-element.44), channel_id=1, source_target_pairs={{0,8},{8,16},{16,24},{24,32},{32,40},{40,48},{48,56},{56,64},{64,7... | collective-permute-start | bytes 24584 | tf_op jit(solution)/shard_map/ppermute | solution.py:27
  654.8 11.7 %collective-permute-start.133 = (f32[1,16,128]{2,1,0:T(8,128)S(1)}, f32[1,16,128]{2,1,0:T(8,128)S(1)}, u32[]{:S(2)}, u32[]{:S(2)}) collective-permute-start(f32[1,16,128]{2,1,0:T(8,128)S(1)} %get-tuple-element.45), channel_id=1, source_target_pairs={{8,0},{16,8},{24,16},{32,24},{40,32},{48,40},{56,48},{64,56},{72,6... | collective-permute-start | bytes 24584 | tf_op jit(solution)/shard_map/ppermute | solution.py:27
  671.8 13.6 %collective-permute-start.134 = (f32[1,16,128]{2,1,0:T(8,128)S(1)}, f32[1,16,128]{2,1,0:T(8,128)S(1)}, u32[]{:S(2)}, u32[]{:S(2)}) collective-permute-start(f32[1,16,128]{2,1,0:T(8,128)S(1)} %get-tuple-element.40), channel_id=1, source_target_pairs={{0,8},{8,16},{16,24},{24,32},{32,40},{40,48},{48,56},{56,64},{64,7... | collective-permute-start | bytes 24584 | tf_op jit(solution)/shard_map/ppermute | solution.py:27
  673.7 11.7 %collective-permute-start.137 = (f32[1,16,128]{2,1,0:T(8,128)S(1)}, f32[1,16,128]{2,1,0:T(8,128)S(1)}, u32[]{:S(2)}, u32[]{:S(2)}) collective-permute-start(f32[1,16,128]{2,1,0:T(8,128)S(1)} %get-tuple-element.41), channel_id=1, source_target_pairs={{8,0},{16,8},{24,16},{32,24},{40,32},{48,40},{56,48},{64,56},{72,6... | collective-permute-start | bytes 24584 | tf_op jit(solution)/shard_map/ppermute | solution.py:27
  690.7 13.6 %collective-permute-start.138 = (f32[1,16,128]{2,1,0:T(8,128)S(1)}, f32[1,16,128]{2,1,0:T(8,128)S(1)}, u32[]{:S(2)}, u32[]{:S(2)}) collective-permute-start(f32[1,16,128]{2,1,0:T(8,128)S(1)} %get-tuple-element.36), channel_id=1, source_target_pairs={{0,8},{8,16},{16,24},{24,32},{32,40},{40,48},{48,56},{56,64},{64,7... | collective-permute-start | bytes 24584 | tf_op jit(solution)/shard_map/ppermute | solution.py:27
  692.6 11.7 %collective-permute-start.141 = (f32[1,16,128]{2,1,0:T(8,128)S(1)}, f32[1,16,128]{2,1,0:T(8,128)S(1)}, u32[]{:S(2)}, u32[]{:S(2)}) collective-permute-start(f32[1,16,128]{2,1,0:T(8,128)S(1)} %get-tuple-element.37), channel_id=1, source_target_pairs={{8,0},{16,8},{24,16},{32,24},{40,32},{48,40},{56,48},{64,56},{72,6... | collective-permute-start | bytes 24584 | tf_op jit(solution)/shard_map/ppermute | solution.py:27
  709.6 13.6 %collective-permute-start.142 = (f32[1,16,128]{2,1,0:T(8,128)S(1)}, f32[1,16,128]{2,1,0:T(8,128)S(1)}, u32[]{:S(2)}, u32[]{:S(2)}) collective-permute-start(f32[1,16,128]{2,1,0:T(8,128)S(1)} %get-tuple-element.32), channel_id=1, source_target_pairs={{0,8},{8,16},{16,24},{24,32},{32,40},{40,48},{48,56},{56,64},{64,7... | collective-permute-start | bytes 24584 | tf_op jit(solution)/shard_map/ppermute | solution.py:27
  711.5 11.7 %collective-permute-start.145 = (f32[1,16,128]{2,1,0:T(8,128)S(1)}, f32[1,16,128]{2,1,0:T(8,128)S(1)}, u32[]{:S(2)}, u32[]{:S(2)}) collective-permute-start(f32[1,16,128]{2,1,0:T(8,128)S(1)} %get-tuple-element.33), channel_id=1, source_target_pairs={{8,0},{16,8},{24,16},{32,24},{40,32},{48,40},{56,48},{64,56},{72,6... | collective-permute-start | bytes 24584 | tf_op jit(solution)/shard_map/ppermute | solution.py:27
  (85 other events, 2274.5 us)
where the time goes:
time: 736 us; the launch traced here: 729 us
  starting transfers between devices  492 us (67%)
  waiting for transfers between devices  203 us (28%)
  other arithmetic  17 us (2%)
  local copies, waits for them, and re-layouts  14.1 us (2%)
    ppermute x76, starting transfers between devices, shifted(): lax.ppermute(value, axis, [(source, source + steps) for source in range(i...  279 us
    ppermute x35, waiting for transfers between devices, extended(): after = lax.ppermute(initial, axis, down)  177 us
    ppermute x35, starting transfers between devices, extended(): after = lax.ppermute(initial, axis, down)  131 us
    ppermute x35, starting transfers between devices, extended(): before = lax.ppermute(last, axis, up)  81.5 us
    ppermute x76, waiting for transfers between devices, shifted(): lax.ppermute(value, axis, [(source, source + steps) for source in range(i...  24.8 us
  transfers between devices with their start and end apart: 146, of which 41 were waited for; matrix products, arithmetic and copies ran while one was open for 0% of the time, Pallas kernels for 0%

commit v1 on v0

v1 whole, which is shorter than its diff:
```python
import jax
import jax.numpy as jnp
from jax import lax
from jax.experimental import pallas as pl
from jax.experimental.pallas import tpu as pltpu
from jax.sharding import PartitionSpec as P

SWEEPS = 4
BOTTOM = 8
LANES = 128
VMEM = 24 * 1024 * 1024

LAYER = 4
PACK = (1, 2, 4, 8)


def face(level):
    return 0.5 * 0.25**level


def chebyshev_table(count):
    centre = 1.125
    half_width = 0.875
    ratio = centre / half_width
    factor = 1.0 / ratio
    table = [(0.0, 1.0 / centre)]
    for order in range(1, count):
        fresh_factor = 1.0 / (2.0 * ratio - factor)
        table.append((fresh_factor * factor, 2.0 * fresh_factor / half_width))
        factor = fresh_factor
    return table


def position():
    return lax.axis_index("gx")


def column_position():
    return lax.axis_index("gy")


def lanes_of(rows):
    return lax.broadcasted_iota(jnp.int32, (rows, LANES), 1)


def rows_of(rows):
    return lax.broadcasted_iota(jnp.int32, (rows, LANES), 0)


def along(value, steps):
    return pltpu.roll(value, (-steps) % LANES, 1)


def across(value, steps):
    rows = value.shape[0]
    return pltpu.roll(value, (-steps) % rows, 0)


class Packed:
    def __init__(self, rows, pack, period, whole):
        lane = lanes_of(rows)
        row = rows_of(rows) % period
        self.pack = pack
        self.inner = lane % pack
        self.third_last = lane >= LANES - pack
        self.third_first = lane < pack
        self.whole = whole
        self.second_last = (row == period - 1) & (self.inner == pack - 1)
        self.second_first = (row == 0) & (self.inner == 0)

    def second_up(self, value):
        if self.pack == 1:
            return across(value, 1)
        return jnp.where(
            self.inner < self.pack - 1, along(value, 1), across(along(value, 1 - self.pack), 1)
        )

    def second_down(self, value):
        if self.pack == 1:
            return across(value, -1)
        return jnp.where(
            self.inner > 0, along(value, -1), across(along(value, self.pack - 1), -1)
        )

    def faces(self, beta, half):
        up = self.second_up(beta)
        if self.whole:
            up = jnp.where(self.second_last, 0.0, up)
        second = half * (beta + up)
        down = self.second_down(beta)
        if self.whole:
            down = jnp.where(self.second_first, 0.0, down)
        share = half * (beta + down) + second
        if self.whole:
            second = jnp.where(self.second_last, 0.0, second)
        third_up = jnp.where(self.third_last, 0.0, along(beta, self.pack))
        third = half * (beta + third_up)
        third_down = jnp.where(self.third_first, 0.0, along(beta, -self.pack))
        share = share + half * (beta + third_down) + third
        return second, jnp.where(self.third_last, 0.0, third), share

    def coupled(self, value, second, third):
        total = second * self.second_up(value) + self.second_down(second * value)
        total = total + third * along(value, self.pack)
        return total + along(third * value, -self.pack)


def pair_sum(value, width):
    low = (lanes_of(value.shape[0]) & width) == 0
    return value + jnp.where(low, along(value, width), along(value, -width))


def residual(shape, source, diag, first, second, third, field, plane, low, high):
    here = field[plane]
    total = source - diag[plane] * here
    if plane + 1 < high:
        total = total + first[plane] * field[plane + 1]
    if plane > low:
        total = total + first[plane - 1] * field[plane - 1]
    return total + shape.coupled(here, second[plane], third[plane])


def sweep(shape, orders, source, parts, buffers, ranges, low, high):
    diag, inverse, first, second, third = parts
    current, previous = buffers
    for (order, (carry, push)), (start, stop) in zip(orders, ranges):
        for plane in range(start, stop):
            rest = residual(
                shape, source(plane), diag, first, second, third, current, plane, low, high
            )
            here = current[plane]
            fresh = here + push * (inverse[plane] * rest)
            if order > 0:
                fresh = fresh + carry * (here - previous[plane])
            previous[plane] = fresh
        current, previous = previous, current
    return current, previous


DEPTH0 = 18
ROWS0 = 32


def gather_level0(region, own, below, above, left, right):
    for part, piece in enumerate((below, own, above)):
        for member in range(LAYER):
            at = part * LAYER + member
            region[at, :, :, 8:24, :] = piece[member]
            region[at, :, :, 0:8, :] = left[part, member]
            region[at, :, :, 24:32, :] = right[part, member]


def level0_parts(shape, beta, absorb, parts, start, stop):
    diag, inverse, first, second, third = parts
    half = face(0)
    before = beta(start - 1)
    here = beta(start)
    lower = half * (before + here)
    first[start - 1] = lower
    for plane in range(start, stop):
        after = beta(plane + 1)
        upper = half * (here + after)
        first[plane] = upper
        second[plane], third[plane], share = shape.faces(here, half)
        total = absorb(plane) + lower + upper + share
        diag[plane] = total
        inverse[plane] = jnp.where(here > 0.0, 1.0 / total, 0.0)
        here, lower = after, upper


def coarse_rows(ref, value, start, count):
    ref[...] = pair_sum(value, 1)
    take = lambda offset: ref[pl.ds(start + offset, count, stride=4), :]
    even = lanes_of(count) % 2 == 0
    return 0.125 * jnp.where(even, take(0) + take(1), take(2) + take(3))


def pre0_kernel(
    own, below, above, left, right, field_out, pay_out,
    region, diag, inverse, first, second, third, one, two, tmp, tile,
):
    gather_level0(region, own, below, above, left, right)
    member = position() % LAYER
    source = lambda plane: region[member + plane // 2, 0, plane % 2]
    absorb = lambda plane: region[member + plane // 2, 1, plane % 2]
    beta = lambda plane: region[member + plane // 2, 2, plane % 2]
    shape = Packed(ROWS0, 1, ROWS0, False)
    parts = (diag, inverse, first, second, third)
    level0_parts(shape, beta, absorb, parts, 1, 17)
    table = chebyshev_table(SWEEPS)
    for plane in range(1, 17):
        one[plane] = table[0][1] * (inverse[plane] * source(plane))
        two[plane] = jnp.zeros((ROWS0, LANES), jnp.float32)
    ranges = [(1 + order, 17 - order) for order in range(1, SWEEPS)]
    current, _ = sweep(
        shape, list(enumerate(table))[1:], source, parts, (one, two), ranges, -1, 99
    )
    for plane in range(4, 14):
        field_out[plane - 4] = current[plane]
    rest = [
        residual(shape, source(plane), diag, first, second, third, current, plane, -1, 99)
        for plane in (8, 9)
    ]
    tile[0:4, :] = coarse_rows(tmp, rest[0] + rest[1], 8, 4)
    betas = [coarse_rows(tmp, beta(plane) + beta(plane + 1), 0, 8) for plane in (6, 8, 10)]
    wide = coarse_rows(tmp, absorb(8) + absorb(9), 0, 8)
    coarse = Packed(8, 2, 8, False)
    half = face(1)
    _, _, share = coarse.faces(betas[1], half)
    total = wide + half * (betas[1] + betas[0]) + half * (betas[1] + betas[2]) + share
    tmp[0:8, :] = betas[1]
    tmp[8:16, :] = total
    tmp[16:24, :] = wide
    tile[4:8, :] = tmp[2:6, :]
    tile[8:12, :] = tmp[10:14, :]
    tile[12:16, :] = tmp[18:22, :]
    whole = tile[...]
    for slot in range(32):
        pay_out[slot] = whole


def post0_kernel(
    own, below, above, left, right, field, coarse_own, coarse_below, coarse_above, out,
    region, diag, inverse, first, second, third, one, two, tmp, wide,
):
    gather_level0(region, own, below, above, left, right)
    member = position() % LAYER
    source = lambda plane: region[member + plane // 2, 0, plane % 2]
    absorb = lambda plane: region[member + plane // 2, 1, plane % 2]
    beta = lambda plane: region[member + plane // 2, 2, plane % 2]
    shape = Packed(ROWS0, 1, ROWS0, False)
    parts = (diag, inverse, first, second, third)
    level0_parts(shape, beta, absorb, parts, 5, 13)
    zero = jnp.zeros((8, LANES), jnp.float32)
    for plane in range(8):
        wide[plane, 0:8, :] = zero
        wide[plane, 40:48, :] = zero
        if plane < 2:
            wide[plane, 8:40, :] = coarse_below[plane]
        elif plane < 6:
            wide[plane, 8:40, :] = coarse_own[plane - 2]
        else:
            wide[plane, 8:40, :] = coarse_above[plane - 6]
    row = column_position() * 4 + 6
    even = lanes_of(8) % 2 == 0
    for pair in range(5):
        value = wide[member + pair, pl.ds(row, 8), :]
        first_rows = jnp.where(even, value, along(value, -1))
        last_rows = jnp.where(even, along(value, 1), value)
        for offset in range(4):
            tmp[pl.ds(offset, 8, stride=4), :] = first_rows if offset < 2 else last_rows
        for plane in (2 * pair + 4, 2 * pair + 5):
            one[plane] = field[plane - 4] + tmp[...]
    table = chebyshev_table(SWEEPS)
    ranges = [(5 + order, 13 - order) for order in range(SWEEPS)]
    current, _ = sweep(
        shape, list(enumerate(table)), source, parts, (one, two), ranges, -1, 99
    )
    for plane in (8, 9):
        out[plane - 8] = current[plane][8:24, :]


DEPTH1 = 12
ROWS1 = 32


def gather_level1(region, own, below, above):
    for part, piece in enumerate((below, own, above)):
        for member in range(LAYER):
            for block in range(8):
                for kind in range(3):
                    region[kind, part * LAYER + member, 4 * block : 4 * block + 4, :] = piece[
                        member * 8 + block, 4 * kind : 4 * kind + 4, :
                    ]


def level1_parts(shape, region, inverse, first, second, third):
    half = face(1)
    for plane in range(DEPTH1):
        beta = region[1, plane]
        if plane + 1 < DEPTH1:
            first[plane] = half * (beta + region[1, plane + 1])
        if 0 < plane < DEPTH1 - 1:
            second[plane], third[plane], _ = shape.faces(beta, half)
        inverse[plane] = jnp.where(beta > 0.0, 1.0 / region[2, plane], 0.0)


def coarser_rows(ref, value):
    ref[...] = pair_sum(pair_sum(value, 1), 2)
    inner = lanes_of(8) % 4
    total = ref[pl.ds(0, 8, stride=4), :]
    for offset in range(1, 4):
        total = jnp.where(inner == offset, ref[pl.ds(offset, 8, stride=4), :], total)
    return 0.125 * total


def pre1_kernel(
    own, below, above, field_out, pay_out,
    region, inverse, first, second, third, one, two, tmp, tile,
):
    gather_level1(region, own, below, above)
    shape = Packed(ROWS1, 2, ROWS1, True)
    level1_parts(shape, region, inverse, first, second, third)
    diag = region.at[2]
    source = lambda plane: region[0, plane]
    parts = (diag, inverse, first, second, third)
    table = chebyshev_table(SWEEPS)
    for plane in range(DEPTH1):
        one[plane] = table[0][1] * (inverse[plane] * source(plane))
        two[plane] = jnp.zeros((ROWS1, LANES), jnp.float32)
    ranges = [(order, DEPTH1 - order) for order in range(1, SWEEPS)]
    current, _ = sweep(
        shape, list(enumerate(table))[1:], source, parts, (one, two), ranges, -1, 99
    )
    for plane in range(4, 8):
        field_out[plane - 4] = current[plane]
    for pair in range(2):
        planes = (4 + 2 * pair, 5 + 2 * pair)
        rest = [
            residual(shape, source(plane), diag, first, second, third, current, plane, -1, 99)
            for plane in planes
        ]
        tile[8 * pair : 8 * pair + 8, :] = coarser_rows(tmp, rest[0] + rest[1])
        tile[16 + 8 * pair : 24 + 8 * pair, :] = coarser_rows(
            tmp, region[1, planes[0]] + region[1, planes[1]]
        )
        for block in range(8):
            two[0, 4 * block : 4 * block + 4, :] = (
                own[2 * pair * 8 + block, 12:16, :] + own[(2 * pair + 1) * 8 + block, 12:16, :]
            )
        tile[32 + 8 * pair : 40 + 8 * pair, :] = coarser_rows(tmp, two[0])
    whole = tile[...]
    for slot in range(16):
        pay_out[slot] = whole


DEPTH2 = 32
ROWS2 = 8


def level2_parts(shape, beta, absorb, parts):
    diag, inverse, first, second, third = parts
    half = face(2)
    lower = half * beta(0)
    for plane in range(DEPTH2):
        here = beta(plane)
        upper = half * (here + beta(plane + 1)) if plane + 1 < DEPTH2 else half * here
        first[plane] = upper
        second[plane], third[plane], share = shape.faces(here, half)
        total = absorb(plane) + lower + upper + share
        diag[plane] = total
        inverse[plane] = 1.0 / total
        lower = upper


def bottom_rows(ref, planes):
    for pair in range(16):
        ref[8 * pair : 8 * pair + 8, :] = pair_sum(
            pair_sum(planes(2 * pair) + planes(2 * pair + 1), 1), 4
        )
    inner = lanes_of(32) % 8
    total = None
    for offset in range(4):
        value = ref[pl.ds(offset, 32, stride=4), :]
        moved = along(value, 1 if offset % 2 == 0 else -1)
        same = 2 * offset + offset % 2
        value = jnp.where(inner == same, value, moved)
        total = value if total is None else jnp.where(inner // 2 == offset, value, total)
    return 0.125 * total


def bottom_solve(source, absorb, beta):
    shape = Packed(32, 8, 2, True)
    half = face(3)
    plane = rows_of(32) // 2
    last, initial = plane == 15, plane == 0
    up = jnp.where(last, 0.0, across(beta, 2))
    down = jnp.where(initial, 0.0, across(beta, -2))
    second, third, share = shape.faces(beta, half)
    upper = half * (beta + up)
    diag = absorb + half * (beta + down) + upper + share
    first = jnp.where(last, 0.0, upper)
    inverse = 1.0 / diag
    table = chebyshev_table(BOTTOM)
    current = table[0][1] * (inverse * source)
    previous = jnp.zeros_like(current)
    for carry, push in table[1:]:
        rest = source - diag * current + first * across(current, 2) + across(first * current, -2)
        rest = rest + shape.coupled(current, second, third)
        fresh = current + carry * (current - previous) + push * (inverse * rest)
        current, previous = fresh, current
    return current


def bottom_prolong(ref, value):
    inner = lanes_of(32) % 8
    part = inner % 4
    back1, back2 = along(value, -1), along(value, -2)
    fore1, fore2 = along(value, 1), along(value, 2)
    low = jnp.where(part == 0, value, jnp.where(part == 3, back2, back1))
    high = jnp.where(part == 3, value, jnp.where(part == 0, fore2, fore1))
    left = inner < 4
    for offset in range(4):
        base = low if offset % 2 == 0 else high
        if offset < 2:
            moved = jnp.where(left, base, along(base, -4))
        else:
            moved = jnp.where(left, along(base, 4), base)
        ref[pl.ds(offset, 32, stride=4), :] = moved


def solve_kernel(
    packed, own, below, above, field_own, field_below, field_above,
    out, out_first, out_last,
    diag2, inverse2, first2, second2, third2, one2, two2, tall,
    region, inverse, first, second, third, one, two, tmp,
):
    shape = Packed(ROWS2, 4, ROWS2, True)

    def kind(number):
        return lambda plane: packed[
            plane // 2, 16 * number + 8 * (plane % 2) : 16 * number + 8 * (plane % 2) + 8, :
        ]

    source2, beta2, absorb2 = kind(0), kind(1), kind(2)
    parts2 = (diag2, inverse2, first2, second2, third2)
    level2_parts(shape, beta2, absorb2, parts2)
    table = chebyshev_table(SWEEPS)
    zero = jnp.zeros((ROWS2, LANES), jnp.float32)
    for plane in range(DEPTH2):
        one2[plane + 2] = table[0][1] * (inverse2[plane] * source2(plane))
        two2[plane + 2] = zero
    inside = (one2.at[pl.ds(2, DEPTH2)], two2.at[pl.ds(2, DEPTH2)])
    everywhere = [(0, DEPTH2)] * SWEEPS
    current, previous = sweep(
        shape, list(enumerate(table))[1:], source2, parts2, inside, everywhere, 0, DEPTH2
    )
    source3 = bottom_rows(
        tall,
        lambda plane: residual(
            shape, source2(plane), diag2, first2, second2, third2, current, plane, 0, DEPTH2
        ),
    )
    absorb3 = bottom_rows(tall, absorb2)
    beta3 = bottom_rows(tall, beta2)
    bottom_prolong(tall, bottom_solve(source3, absorb3, beta3))
    for plane in range(DEPTH2):
        pair = plane // 2
        current[plane] = current[plane] + tall[8 * pair : 8 * pair + 8, :]
    current, previous = sweep(
        shape, list(enumerate(table)), source2, parts2, (current, previous), everywhere, 0, DEPTH2
    )
    whole = two2
    for plane in (0, 1, DEPTH2 + 2, DEPTH2 + 3):
        whole[plane] = zero

    gather_level1(region, own, below, above)
    shape = Packed(ROWS1, 2, ROWS1, True)
    level1_parts(shape, region, inverse, first, second, third)
    layer = position() // LAYER
    inner = lanes_of(8) % 4
    for pair in range(6):
        value = whole[2 * layer + pair]
        moved = {steps: along(value, steps) for steps in range(-3, 4)}
        for offset in range(4):
            picked = moved[offset]
            for lane in range(1, 4):
                picked = jnp.where(inner == lane, moved[offset - lane], picked)
            tmp[pl.ds(offset, 8, stride=4), :] = picked
        for plane in (2 * pair, 2 * pair + 1):
            if plane < 4:
                old = field_below[plane]
            elif plane < 8:
                old = field_own[plane - 4]
            else:
                old = field_above[plane - 8]
            one[plane] = old + tmp[...]
    parts = (region.at[2], inverse, first, second, third)
    ranges = [(order, DEPTH1 - order) for order in range(1, SWEEPS + 1)]
    current, _ = sweep(
        shape, list(enumerate(table)), lambda plane: region[0, plane], parts, (one, two), ranges,
        -1, 99,
    )
    for plane in range(4):
        value = current[plane + 4]
        out[plane] = value
        if plane < 2:
            out_first[plane] = value
        else:
            out_last[plane - 2] = value


def f32(*shape):
    return jax.ShapeDtypeStruct(shape, jnp.float32)


def buffer(*shape):
    return pltpu.VMEM(shape, jnp.float32)


def call(kernel, out, scratch, name, *operands):
    return pl.pallas_call(
        kernel,
        out_shape=out,
        scratch_shapes=scratch,
        name=name,
        compiler_params=pltpu.CompilerParams(vmem_limit_bytes=VMEM),
    )(*operands)


def pre0(*pieces):
    plane = buffer(DEPTH0, ROWS0, LANES)
    scratch = [buffer(12, 3, 2, ROWS0, LANES)] + [plane] * 7 + [buffer(32, LANES), buffer(16, LANES)]
    return call(pre0_kernel, (f32(10, ROWS0, LANES), f32(32, 16, LANES)), scratch, "pre0", *pieces)


def pre1(*pieces):
    plane = buffer(DEPTH1, ROWS1, LANES)
    scratch = [buffer(3, DEPTH1, ROWS1, LANES)] + [plane] * 6 + [buffer(32, LANES), buffer(48, LANES)]
    return call(pre1_kernel, (f32(4, ROWS1, LANES), f32(16, 48, LANES)), scratch, "pre1", *pieces)


def solve(*pieces):
    small = buffer(DEPTH2, ROWS2, LANES)
    padded = buffer(DEPTH2 + 4, ROWS2, LANES)
    plane = buffer(DEPTH1, ROWS1, LANES)
    scratch = [small] * 5 + [padded] * 2 + [buffer(128, LANES)]
    scratch += [buffer(3, DEPTH1, ROWS1, LANES)] + [plane] * 6 + [buffer(32, LANES)]
    out = (f32(4, ROWS1, LANES), f32(2, ROWS1, LANES), f32(2, ROWS1, LANES))
    return call(solve_kernel, out, scratch, "solve", *pieces)


def post0(*pieces):
    plane = buffer(DEPTH0, ROWS0, LANES)
    scratch = [buffer(12, 3, 2, ROWS0, LANES)] + [plane] * 7
    scratch += [buffer(32, LANES), buffer(8, 48, LANES)]
    return call(post0_kernel, f32(2, 16, LANES), scratch, "post0", *pieces)


def shifted(value, axis, steps):
    count = lax.axis_size(axis)
    pairs = [(i, i + steps) for i in range(count) if 0 <= i + steps < count]
    return lax.ppermute(value, axis, pairs)


def body(source, absorb, beta):
    members = lax.axis_size("gx")
    across_y = lax.axis_size("gy")
    layers = members // LAYER
    near = [[LAYER * z + c for c in range(LAYER)] for z in range(layers)]
    layer = [
        [(LAYER * z + c) * across_y + y for c in range(LAYER) for y in range(across_y)]
        for z in range(layers)
    ]
    column = [[LAYER * z + c for z in range(layers)] for c in range(LAYER)]

    local = jnp.stack([source, absorb, beta])
    own = lax.all_gather(local, "gx", axis_index_groups=near)
    below = shifted(own, "gx", LAYER)
    above = shifted(own, "gx", -LAYER)
    left = shifted(jnp.stack([x[..., 8:, :] for x in (below, own, above)]), "gy", 1)
    right = shifted(jnp.stack([x[..., :8, :] for x in (below, own, above)]), "gy", -1)
    pieces0 = (own, below, above, left, right)
    field0, pay = pre0(*pieces0)

    own1 = lax.all_to_all(pay, ("gx", "gy"), 0, 0, axis_index_groups=layer)
    below1 = shifted(own1, "gx", LAYER)
    above1 = shifted(own1, "gx", -LAYER)
    pieces1 = (own1, below1, above1)
    field1, pay = pre1(*pieces1)

    field_below = shifted(field1, "gx", LAYER)
    field_above = shifted(field1, "gx", -LAYER)
    packed = lax.all_to_all(pay, "gx", 0, 0, axis_index_groups=column)
    coarse, coarse_first, coarse_last = solve(
        packed, *pieces1, field1, field_below, field_above
    )

    coarse_below = shifted(coarse_last, "gx", LAYER)
    coarse_above = shifted(coarse_first, "gx", -LAYER)
    return post0(*pieces0, field0, coarse, coarse_below, coarse_above)


def solution(mesh):
    placed = (P("gx", "gy", None), P("gx", "gy", None), P("gx", "gy", None))
    return jax.shard_map(
        body, mesh=mesh, in_specs=placed, out_specs=P("gx", "gy", None), check_vma=False
    )
```

time: 736 us -> 124 us (0.17)
  the two profiles are of different devices: /device:TPU:280 before, /device:TPU:16 now
where the time goes in v1:
time: 124 us; the launch traced here: 123 us
  starting transfers between devices  45.1 us (36%)
  waiting for transfers between devices  43.4 us (35%)
  blocking collectives  20.8 us (17%)
  Pallas kernels  13 us (10%)
    ppermute x10, waiting for transfers between devices, shifted(): return lax.ppermute(value, axis, pairs)  38.1 us
    ppermute x10, starting transfers between devices, shifted(): return lax.ppermute(value, axis, pairs)  27 us
    all_to_all x1, starting transfers between devices, body(): packed = lax.all_to_all(pay, 'gx', 0, 0, axis_index_groups=column)  18.2 us
    all_to_all x1, blocking collectives, body(): own1 = lax.all_to_all(pay, ('gx', 'gy'), 0, 0, axis_index_groups=layer)  15.2 us
    pallas_call x4, Pallas kernels, call(): pl.pallas_call(kernel, out_shape=out, scratch_shapes=scratch, name=name,...  13 us
    all_gather x1, blocking collectives, body(): own = lax.all_gather(local, 'gx', axis_index_groups=near)  5.59 us
    all_to_all x1, waiting for transfers between devices, body(): packed = lax.all_to_all(pay, 'gx', 0, 0, axis_index_groups=column)  5.35 us
  transfers between devices with their start and end apart: 11, of which 10 were waited for; matrix products, arithmetic and copies ran while one was open for 0% of the time, Pallas kernels for 0%

profile of v1, /device:TPU:16, one launch (start us, length us, event | category | flops | bytes accessed | tf_op | source)
XLA Modules:
  0.0 123.4 jit_solution(9454405360033244051)
XLA Ops:
  0.0 0.8 pad_maximum_fusion.2
  0.8 5.6 %all-gather = f32[12,2,16,128]{3,2,1,0:T(8,128)S(1)} all-gather(f32[3,2,16,128]{3,2,1,0:T(8,128)S(1)} %pad_maximum_fusion.2), channel_id=2, replica_groups={{0,8,16,24},{32,40,48,56},{64,72,80,88},{96,104,112,120},{128,136,144,1..., dimensions={0}, use_global_device_ids=true | all-gather | bytes 245760 | tf_op jit(solution)/shard_map/all_gather | solution.py:558
  6.3 1.3 %collective-permute-start.1 = (f32[4,3,2,16,128]{4,3,2,1,0:T(8,128)S(1)}, f32[4,3,2,16,128]{4,3,2,1,0:T(8,128)S(1)}, u32[]{:S(2)}, u32[]{:S(2)}) collective-permute-start(f32[4,3,2,16,128]{4,3,2,1,0:T(8,128)S(1)} %bitcast.16), channel_id=1, source_target_pairs={{32,0},{40,8},{48,16},{56,24},{64,32},{72,40},{80,48},{88,56},{96,... | collective-permute-start | bytes 589832 | tf_op jit(solution)/shard_map/ppermute | solution.py:543
  7.6 4.6 %collective-permute-start = (f32[4,3,2,16,128]{4,3,2,1,0:T(8,128)S(1)}, f32[4,3,2,16,128]{4,3,2,1,0:T(8,128)S(1)}, u32[]{:S(2)}, u32[]{:S(2)}) collective-permute-start(f32[4,3,2,16,128]{4,3,2,1,0:T(8,128)S(1)} %bitcast.17), channel_id=1, source_target_pairs={{0,32},{8,40},{16,48},{24,56},{32,64},{40,72},{48,80},{56,88},{64,... | collective-permute-start | bytes 589832 | tf_op jit(solution)/shard_map/ppermute | solution.py:543
  12.2 3.3 %collective-permute-done.1.above = f32[4,3,2,16,128]{4,3,2,1,0:T(8,128)S(1)} collective-permute-done((f32[4,3,2,16,128]{4,3,2,1,0:T(8,128)S(1)}, f32[4,3,2,16,128]{4,3,2,1,0:T(8,128)S(1)}, u32[]{:S(2)}, u32[]{:S(2)}) %collective-permute-start.1) | collective-permute-done | bytes 196640 | tf_op jit(solution)/shard_map/ppermute | solution.py:543
  15.6 1.2 collective-permute-done.below
  16.8 3.2 %collective-permute-start.2 = (f32[3,4,3,2,8,128]{5,4,3,2,1,0:T(8,128)S(1)}, f32[3,4,3,2,8,128]{5,4,3,2,1,0:T(8,128)S(1)}, u32[]{:S(2)}, u32[]{:S(2)}) collective-permute-start(f32[3,4,3,2,8,128]{5,4,3,2,1,0:T(8,128)S(1)} %pad_maximum_fusion), channel_id=1, source_target_pairs={{0,1},{1,2},{2,3},{3,4},{4,5},{5,6},{6,7},{8,9},{9,10},{10,11},{11... | collective-permute-start | bytes 884744 | tf_op jit(solution)/shard_map/ppermute | solution.py:543
  20.0 2.7 %collective-permute-start.3 = (f32[3,4,3,2,8,128]{5,4,3,2,1,0:T(8,128)S(1)}, f32[3,4,3,2,8,128]{5,4,3,2,1,0:T(8,128)S(1)}, u32[]{:S(2)}, u32[]{:S(2)}) collective-permute-start(f32[3,4,3,2,8,128]{5,4,3,2,1,0:T(8,128)S(1)} %pad_maximum_fusion.1), channel_id=1, source_target_pairs={{1,0},{2,1},{3,2},{4,3},{5,4},{6,5},{7,6},{9,8},{10,9},{11,10},{12... | collective-permute-start | bytes 884744 | tf_op jit(solution)/shard_map/ppermute | solution.py:543
  22.7 4.4 %collective-permute-done.2.left = f32[3,4,3,2,8,128]{5,4,3,2,1,0:T(8,128)S(1)} collective-permute-done((f32[3,4,3,2,8,128]{5,4,3,2,1,0:T(8,128)S(1)}, f32[3,4,3,2,8,128]{5,4,3,2,1,0:T(8,128)S(1)}, u32[]{:S(2)}, u32[]{:S(2)}) %collective-permute-start.2) | collective-permute-done | bytes 294944 | tf_op jit(solution)/shard_map/ppermute | solution.py:543
  27.0 3.9 %collective-permute-done.3.right = f32[3,4,3,2,8,128]{5,4,3,2,1,0:T(8,128)S(1)} collective-permute-done((f32[3,4,3,2,8,128]{5,4,3,2,1,0:T(8,128)S(1)}, f32[3,4,3,2,8,128]{5,4,3,2,1,0:T(8,128)S(1)}, u32[]{:S(2)}, u32[]{:S(2)}) %collective-permute-start.3) | collective-permute-done | bytes 294944 | tf_op jit(solution)/shard_map/ppermute | solution.py:543
  30.9 1.1 pre0.1
  32.0 15.2 %all_to_all.10.own = f32[32,16,128]{2,1,0:T(8,128)S(1)} all-to-all(f32[32,16,128]{2,1,0:T(8,128)S(1)} %get-tuple-element.13), channel_id=1, replica_groups={{0,1,2,3,4,5,6,7,8,9,10,11,12,13,14,15,16,17,18,19,20,21,22,23,24,25,26..., dimensions={0} | all-to-all | bytes 524288 | tf_op jit(solution)/shard_map/all_to_all | solution.py:566
  47.3 1.3 %collective-permute-start.5 = (f32[32,16,128]{2,1,0:T(8,128)S(1)}, f32[32,16,128]{2,1,0:T(8,128)S(1)}, u32[]{:S(2)}, u32[]{:S(2)}) collective-permute-start(f32[32,16,128]{2,1,0:T(8,128)S(1)} %all_to_all.10.own), channel_id=1, source_target_pairs={{32,0},{40,8},{48,16},{56,24},{64,32},{72,40},{80,48},{88,56},{96,... | collective-permute-start | bytes 786440 | tf_op jit(solution)/shard_map/ppermute | solution.py:543
  48.6 5.0 %collective-permute-start.4 = (f32[32,16,128]{2,1,0:T(8,128)S(1)}, f32[32,16,128]{2,1,0:T(8,128)S(1)}, u32[]{:S(2)}, u32[]{:S(2)}) collective-permute-start(f32[32,16,128]{2,1,0:T(8,128)S(1)} %all_to_all.10.own), channel_id=1, source_target_pairs={{0,32},{8,40},{16,48},{24,56},{32,64},{40,72},{48,80},{56,88},{64,... | collective-permute-start | bytes 786440 | tf_op jit(solution)/shard_map/ppermute | solution.py:543
  53.6 5.2 %collective-permute-done.5.above = f32[32,16,128]{2,1,0:T(8,128)S(1)} collective-permute-done((f32[32,16,128]{2,1,0:T(8,128)S(1)}, f32[32,16,128]{2,1,0:T(8,128)S(1)}, u32[]{:S(2)}, u32[]{:S(2)}) %collective-permute-start.5) | collective-permute-done | bytes 262176 | tf_op jit(solution)/shard_map/ppermute | solution.py:543
  58.8 1.2 collective-permute-done.4.below
  59.9 2.1 %pre1.1 = (f32[4,32,128]{2,1,0:T(8,128)S(1)}, f32[16,48,128]{2,1,0:T(8,128)}) custom-call(f32[32,16,128]{2,1,0:T(8,128)S(1)} %all_to_all.10.own, f32[32,16,128]{2,1,0:T(8,128)S(1)} %collective-permute-done.4.below, f32[32,16,128]{2,1,0:T(8,128)S(1)} %collective-permute-done.5.above), custom_call_target="tpu_custom_call" | custom-call | tf_op jit(solution)/shard_map/pre1/pallas_call | solution.py:502
  62.0 18.2 %all-to-all-start.1 = ((f32[16,48,128]{2,1,0:T(8,128)}), f32[16,48,128]{2,1,0:T(8,128)S(1)}, u32[]{:S(2)}, u32[]{:S(2)}) async-start(f32[16,48,128]{2,1,0:T(8,128)} %get-tuple-element.14), calls=%async_computation.1 | async-start | bytes 786432 | tf_op jit(solution)/shard_map/all_to_all | solution.py:574
  80.2 1.3 %collective-permute-start.7 = (f32[4,32,128]{2,1,0:T(8,128)S(1)}, f32[4,32,128]{2,1,0:T(8,128)S(1)}, u32[]{:S(2)}, u32[]{:S(2)}) collective-permute-start(f32[4,32,128]{2,1,0:T(8,128)S(1)} %get-tuple-element.15.field_own), channel_id=1, source_target_pairs={{32,0},{40,8},{48,16},{56,24},{64,32},{72,40},{80,48},{88,56},{96,... | collective-permute-start | bytes 196616 | tf_op jit(solution)/shard_map/ppermute | solution.py:543
  81.5 4.5 %collective-permute-start.6 = (f32[4,32,128]{2,1,0:T(8,128)S(1)}, f32[4,32,128]{2,1,0:T(8,128)S(1)}, u32[]{:S(2)}, u32[]{:S(2)}) collective-permute-start(f32[4,32,128]{2,1,0:T(8,128)S(1)} %get-tuple-element.15.field_own), channel_id=1, source_target_pairs={{0,32},{8,40},{16,48},{24,56},{32,64},{40,72},{48,80},{56,88},{64,... | collective-permute-start | bytes 196616 | tf_op jit(solution)/shard_map/ppermute | solution.py:543
  86.0 14.5 %collective-permute-done.7.field_above = f32[4,32,128]{2,1,0:T(8,128)S(1)} collective-permute-done((f32[4,32,128]{2,1,0:T(8,128)S(1)}, f32[4,32,128]{2,1,0:T(8,128)S(1)}, u32[]{:S(2)}, u32[]{:S(2)}) %collective-permute-start.7) | collective-permute-done | bytes 65568 | tf_op jit(solution)/shard_map/ppermute | solution.py:543
  100.5 0.0 collective-permute-done.6.field_below
  100.5 5.4 %all-to-all-done.1.packed = f32[16,48,128]{2,1,0:T(8,128)S(1)} async-done(((f32[16,48,128]{2,1,0:T(8,128)}), f32[16,48,128]{2,1,0:T(8,128)S(1)}, u32[]{:S(2)}, u32[]{:S(2)}) %all-to-all-start.1) | async-done | bytes 393248 | tf_op jit(solution)/shard_map/all_to_all | solution.py:574
  105.9 8.7 %solve.1 = (f32[4,32,128]{2,1,0:T(8,128)S(1)}, f32[2,32,128]{2,1,0:T(8,128)S(1)}, f32[2,32,128]{2,1,0:T(8,128)S(1)}) custom-call(f32[16,48,128]{2,1,0:T(8,128)S(1)} %all-to-all-done.1.packed, f32[32,16,128]{2,1,0:T(8,128)S(1)} %all_to_all.10.own, f32[32,16,128]{2,1,0:T(8,128)S(1)} %collective-permute-done.4.below, ...), custom_call_target="tpu_custom_call" | custom-call | tf_op jit(solution)/shard_map/solve/pallas_call | solution.py:502
  114.6 1.8 %collective-permute-start.8 = (f32[2,32,128]{2,1,0:T(8,128)S(1)}, f32[2,32,128]{2,1,0:T(8,128)S(1)}, u32[]{:S(2)}, u32[]{:S(2)}) collective-permute-start(f32[2,32,128]{2,1,0:T(8,128)S(1)} %get-tuple-element.17), channel_id=1, source_target_pairs={{0,32},{8,40},{16,48},{24,56},{32,64},{40,72},{48,80},{56,88},{64,... | collective-permute-start | bytes 98312 | tf_op jit(solution)/shard_map/ppermute | solution.py:543
  116.4 1.3 %collective-permute-start.9 = (f32[2,32,128]{2,1,0:T(8,128)S(1)}, f32[2,32,128]{2,1,0:T(8,128)S(1)}, u32[]{:S(2)}, u32[]{:S(2)}) collective-permute-start(f32[2,32,128]{2,1,0:T(8,128)S(1)} %get-tuple-element.18), channel_id=1, source_target_pairs={{32,0},{40,8},{48,16},{56,24},{64,32},{72,40},{80,48},{88,56},{96,... | collective-permute-start | bytes 98312 | tf_op jit(solution)/shard_map/ppermute | solution.py:543
  117.7 0.3 collective-permute-done.8.coarse_below
  118.0 4.2 %collective-permute-done.9.coarse_above = f32[2,32,128]{2,1,0:T(8,128)S(1)} collective-permute-done((f32[2,32,128]{2,1,0:T(8,128)S(1)}, f32[2,32,128]{2,1,0:T(8,128)S(1)}, u32[]{:S(2)}, u32[]{:S(2)}) %collective-permute-start.9) | collective-permute-done | bytes 32800 | tf_op jit(solution)/shard_map/ppermute | solution.py:543
  122.2 1.2 post0.1
  (5 shorter events, 0.1 us)
Async XLA Ops:
  6.3 9.2 %collective-permute-start.1 = (f32[4,3,2,16,128]{4,3,2,1,0:T(8,128)S(1)}, f32[4,3,2,16,128]{4,3,2,1,0:T(8,128)S(1)}, u32[]{:S(2)}, u32[]{:S(2)}) collective-permute-start(f32[4,3,2,16,128]{4,3,2,1,0:T(8,128)S(1)} %bitcast.16), channel_id=1, source_target_pairs={{32,0},{40,8},{48,16},{56,24},{64,32},{72,40},{80,48},{88,56},{96,... | collective-permute-start | bytes 589832 | tf_op jit(solution)/shard_map/ppermute | solution.py:543
  7.6 9.1 %collective-permute-start = (f32[4,3,2,16,128]{4,3,2,1,0:T(8,128)S(1)}, f32[4,3,2,16,128]{4,3,2,1,0:T(8,128)S(1)}, u32[]{:S(2)}, u32[]{:S(2)}) collective-permute-start(f32[4,3,2,16,128]{4,3,2,1,0:T(8,128)S(1)} %bitcast.17), channel_id=1, source_target_pairs={{0,32},{8,40},{16,48},{24,56},{32,64},{40,72},{48,80},{56,88},{64,... | collective-permute-start | bytes 589832 | tf_op jit(solution)/shard_map/ppermute | solution.py:543
  16.8 10.2 %collective-permute-start.2 = (f32[3,4,3,2,8,128]{5,4,3,2,1,0:T(8,128)S(1)}, f32[3,4,3,2,8,128]{5,4,3,2,1,0:T(8,128)S(1)}, u32[]{:S(2)}, u32[]{:S(2)}) collective-permute-start(f32[3,4,3,2,8,128]{5,4,3,2,1,0:T(8,128)S(1)} %pad_maximum_fusion), channel_id=1, source_target_pairs={{0,1},{1,2},{2,3},{3,4},{4,5},{5,6},{6,7},{8,9},{9,10},{10,11},{11... | collective-permute-start | bytes 884744 | tf_op jit(solution)/shard_map/ppermute | solution.py:543
  20.0 10.9 %collective-permute-start.3 = (f32[3,4,3,2,8,128]{5,4,3,2,1,0:T(8,128)S(1)}, f32[3,4,3,2,8,128]{5,4,3,2,1,0:T(8,128)S(1)}, u32[]{:S(2)}, u32[]{:S(2)}) collective-permute-start(f32[3,4,3,2,8,128]{5,4,3,2,1,0:T(8,128)S(1)} %pad_maximum_fusion.1), channel_id=1, source_target_pairs={{1,0},{2,1},{3,2},{4,3},{5,4},{6,5},{7,6},{9,8},{10,9},{11,10},{12... | collective-permute-start | bytes 884744 | tf_op jit(solution)/shard_map/ppermute | solution.py:543
  47.3 11.5 %collective-permute-start.5 = (f32[32,16,128]{2,1,0:T(8,128)S(1)}, f32[32,16,128]{2,1,0:T(8,128)S(1)}, u32[]{:S(2)}, u32[]{:S(2)}) collective-permute-start(f32[32,16,128]{2,1,0:T(8,128)S(1)} %all_to_all.10.own), channel_id=1, source_target_pairs={{32,0},{40,8},{48,16},{56,24},{64,32},{72,40},{80,48},{88,56},{96,... | collective-permute-start | bytes 786440 | tf_op jit(solution)/shard_map/ppermute | solution.py:543
  48.6 11.4 %collective-permute-start.4 = (f32[32,16,128]{2,1,0:T(8,128)S(1)}, f32[32,16,128]{2,1,0:T(8,128)S(1)}, u32[]{:S(2)}, u32[]{:S(2)}) collective-permute-start(f32[32,16,128]{2,1,0:T(8,128)S(1)} %all_to_all.10.own), channel_id=1, source_target_pairs={{0,32},{8,40},{16,48},{24,56},{32,64},{40,72},{48,80},{56,88},{64,... | collective-permute-start | bytes 786440 | tf_op jit(solution)/shard_map/ppermute | solution.py:543
  62.0 43.9 %all-to-all-start.1 = ((f32[16,48,128]{2,1,0:T(8,128)}), f32[16,48,128]{2,1,0:T(8,128)S(1)}, u32[]{:S(2)}, u32[]{:S(2)}) async-start(f32[16,48,128]{2,1,0:T(8,128)} %get-tuple-element.14), calls=%async_computation.1 | async-start | bytes 786432 | tf_op jit(solution)/shard_map/all_to_all | solution.py:574
  80.2 20.3 %collective-permute-start.7 = (f32[4,32,128]{2,1,0:T(8,128)S(1)}, f32[4,32,128]{2,1,0:T(8,128)S(1)}, u32[]{:S(2)}, u32[]{:S(2)}) collective-permute-start(f32[4,32,128]{2,1,0:T(8,128)S(1)} %get-tuple-element.15.field_own), channel_id=1, source_target_pairs={{32,0},{40,8},{48,16},{56,24},{64,32},{72,40},{80,48},{88,56},{96,... | collective-permute-start | bytes 196616 | tf_op jit(solution)/shard_map/ppermute | solution.py:543
  81.5 19.0 %collective-permute-start.6 = (f32[4,32,128]{2,1,0:T(8,128)S(1)}, f32[4,32,128]{2,1,0:T(8,128)S(1)}, u32[]{:S(2)}, u32[]{:S(2)}) collective-permute-start(f32[4,32,128]{2,1,0:T(8,128)S(1)} %get-tuple-element.15.field_own), channel_id=1, source_target_pairs={{0,32},{8,40},{16,48},{24,56},{32,64},{40,72},{48,80},{56,88},{64,... | collective-permute-start | bytes 196616 | tf_op jit(solution)/shard_map/ppermute | solution.py:543
  114.6 3.4 %collective-permute-start.8 = (f32[2,32,128]{2,1,0:T(8,128)S(1)}, f32[2,32,128]{2,1,0:T(8,128)S(1)}, u32[]{:S(2)}, u32[]{:S(2)}) collective-permute-start(f32[2,32,128]{2,1,0:T(8,128)S(1)} %get-tuple-element.17), channel_id=1, source_target_pairs={{0,32},{8,40},{16,48},{24,56},{32,64},{40,72},{48,80},{56,88},{64,... | collective-permute-start | bytes 98312 | tf_op jit(solution)/shard_map/ppermute | solution.py:543
  116.4 5.8 %collective-permute-start.9 = (f32[2,32,128]{2,1,0:T(8,128)S(1)}, f32[2,32,128]{2,1,0:T(8,128)S(1)}, u32[]{:S(2)}, u32[]{:S(2)}) collective-permute-start(f32[2,32,128]{2,1,0:T(8,128)S(1)} %get-tuple-element.18), channel_id=1, source_target_pairs={{32,0},{40,8},{48,16},{56,24},{64,32},{72,40},{80,48},{88,56},{96,... | collective-permute-start | bytes 98312 | tf_op jit(solution)/shard_map/ppermute | solution.py:543

commit v2 on v1

v2 whole, which is shorter than its diff:
```python
import jax
import jax.numpy as jnp
from jax import lax
from jax.experimental import pallas as pl
from jax.experimental.pallas import tpu as pltpu
from jax.sharding import PartitionSpec as P

SWEEPS = 4
BOTTOM = 8
LANES = 128
VMEM = 24 * 1024 * 1024

LAYER = 4
PACK = (1, 2, 4, 8)


def face(level):
    return 0.5 * 0.25**level


def chebyshev_table(count):
    centre = 1.125
    half_width = 0.875
    ratio = centre / half_width
    factor = 1.0 / ratio
    table = [(0.0, 1.0 / centre)]
    for order in range(1, count):
        fresh_factor = 1.0 / (2.0 * ratio - factor)
        table.append((fresh_factor * factor, 2.0 * fresh_factor / half_width))
        factor = fresh_factor
    return table


def position():
    return lax.axis_index("gx")


def column_position():
    return lax.axis_index("gy")


def lanes_of(rows):
    return lax.broadcasted_iota(jnp.int32, (rows, LANES), 1)


def rows_of(rows):
    return lax.broadcasted_iota(jnp.int32, (rows, LANES), 0)


def along(value, steps):
    return pltpu.roll(value, (-steps) % LANES, 1)


def across(value, steps):
    rows = value.shape[0]
    return pltpu.roll(value, (-steps) % rows, 0)


class Packed:
    def __init__(self, rows, pack, period, whole):
        lane = lanes_of(rows)
        row = rows_of(rows) % period
        self.pack = pack
        self.inner = lane % pack
        self.third_last = lane >= LANES - pack
        self.third_first = lane < pack
        self.whole = whole
        self.second_last = (row == period - 1) & (self.inner == pack - 1)
        self.second_first = (row == 0) & (self.inner == 0)

    def second_up(self, value):
        if self.pack == 1:
            return across(value, 1)
        return jnp.where(
            self.inner < self.pack - 1, along(value, 1), across(along(value, 1 - self.pack), 1)
        )

    def second_down(self, value):
        if self.pack == 1:
            return across(value, -1)
        return jnp.where(
            self.inner > 0, along(value, -1), across(along(value, self.pack - 1), -1)
        )

    def faces(self, beta, half):
        up = self.second_up(beta)
        if self.whole:
            up = jnp.where(self.second_last, 0.0, up)
        second = half * (beta + up)
        down = self.second_down(beta)
        if self.whole:
            down = jnp.where(self.second_first, 0.0, down)
        share = half * (beta + down) + second
        if self.whole:
            second = jnp.where(self.second_last, 0.0, second)
        third_up = jnp.where(self.third_last, 0.0, along(beta, self.pack))
        third = half * (beta + third_up)
        third_down = jnp.where(self.third_first, 0.0, along(beta, -self.pack))
        share = share + half * (beta + third_down) + third
        return second, jnp.where(self.third_last, 0.0, third), share

    def coupled(self, value, second, third):
        total = second * self.second_up(value) + self.second_down(second * value)
        total = total + third * along(value, self.pack)
        return total + along(third * value, -self.pack)


def pair_sum(value, width):
    low = (lanes_of(value.shape[0]) & width) == 0
    return value + jnp.where(low, along(value, width), along(value, -width))


def residual(shape, source, diag, first, second, third, field, plane, low, high):
    here = field[plane]
    total = source - diag[plane] * here
    if plane + 1 < high:
        total = total + first[plane] * field[plane + 1]
    if plane > low:
        total = total + first[plane - 1] * field[plane - 1]
    return total + shape.coupled(here, second[plane], third[plane])


def sweep(shape, orders, source, parts, buffers, ranges, low, high):
    diag, inverse, first, second, third = parts
    current, previous = buffers
    for (order, (carry, push)), (start, stop) in zip(orders, ranges):
        for plane in range(start, stop):
            rest = residual(
                shape, source(plane), diag, first, second, third, current, plane, low, high
            )
            here = current[plane]
            fresh = here + push * (inverse[plane] * rest)
            if order > 0:
                fresh = fresh + carry * (here - previous[plane])
            previous[plane] = fresh
        current, previous = previous, current
    return current, previous


ROWS0 = 32


def gather_level0(region, own, below, above, left, right):
    for part, piece in enumerate((below, own, above)):
        for member in range(LAYER):
            at = part * LAYER + member
            region[at, :, :, 8:24, :] = piece[member]
            region[at, :, :, 0:8, :] = left[part, member]
            region[at, :, :, 24:32, :] = right[part, member]


def level0_parts(shape, beta, absorb, parts, start, stop):
    diag, inverse, first, second, third = parts
    half = face(0)
    before = beta(start - 1)
    here = beta(start)
    lower = half * (before + here)
    first[start - 1] = lower
    for plane in range(start, stop):
        after = beta(plane + 1)
        upper = half * (here + after)
        first[plane] = upper
        second[plane], third[plane], share = shape.faces(here, half)
        total = absorb(plane) + lower + upper + share
        diag[plane] = total
        inverse[plane] = jnp.where(here > 0.0, 1.0 / total, 0.0)
        here, lower = after, upper


def coarse_rows(ref, value):
    ref[...] = pair_sum(value, 1)
    take = lambda offset: ref[pl.ds(offset, 8, stride=4), :]
    even = lanes_of(8) % 2 == 0
    return 0.125 * jnp.where(even, take(0) + take(1), take(2) + take(3))


def pre0_kernel(
    own, below, above, left, right, field_out, tile_out, absorb_out,
    region, diag, inverse, first, second, third, one, two, tmp,
):
    gather_level0(region, own, below, above, left, right)
    source = lambda plane: region[plane // 2, 0, plane % 2]
    absorb = lambda plane: region[plane // 2, 1, plane % 2]
    beta = lambda plane: region[plane // 2, 2, plane % 2]
    shape = Packed(ROWS0, 1, ROWS0, False)
    parts = (diag, inverse, first, second, third)
    level0_parts(shape, beta, absorb, parts, 1, 23)
    table = chebyshev_table(SWEEPS)
    for plane in range(1, 23):
        one[plane] = table[0][1] * (inverse[plane] * source(plane))
        two[plane] = jnp.zeros((ROWS0, LANES), jnp.float32)
    ranges = [(1 + order, 23 - order) for order in range(1, SWEEPS)]
    current, _ = sweep(
        shape, list(enumerate(table))[1:], source, parts, (one, two), ranges, -1, 99
    )
    base = 2 * (position() % LAYER) + 4
    for plane in range(10):
        field_out[plane] = current[base + plane]
    coarse = Packed(8, 2, 8, False)
    half = face(1)
    betas = [coarse_rows(tmp.at[0], beta(p) + beta(p + 1)) for p in range(4, 20, 2)]
    for pair in range(6):
        plane = 6 + 2 * pair
        rest = [
            residual(shape, source(p), diag, first, second, third, current, p, -1, 99)
            for p in (plane, plane + 1)
        ]
        tile_out[pair, 0] = coarse_rows(tmp.at[1 + pair % 3], rest[0] + rest[1])
        here = betas[pair + 1]
        tile_out[pair, 1] = here
        wide = coarse_rows(tmp.at[1 + (pair + 1) % 3], absorb(plane) + absorb(plane + 1))
        _, _, share = coarse.faces(here, half)
        tile_out[pair, 2] = wide + half * (here + betas[pair]) + half * (here + betas[pair + 2]) + share
        if 0 < pair < 5:
            absorb_out[pair - 1] = wide


DEPTH1 = 22
ROWS1 = 16


def gather_level1(region, middle, left, right):
    row = rows_of(8)
    for plane in range(DEPTH1):
        for kind in range(3):
            moved = across(middle[plane, kind], 4)
            region[kind, plane, 0:8, :] = jnp.where(row < 6, left[plane, kind], moved)
            region[kind, plane, 8:16, :] = jnp.where(row < 2, moved, right[plane, kind])


def level1_parts(shape, region, inverse, first, second, third):
    half = face(1)
    for plane in range(DEPTH1):
        beta = region[1, plane]
        if plane + 1 < DEPTH1:
            first[plane] = half * (beta + region[1, plane + 1])
        if 0 < plane < DEPTH1 - 1:
            second[plane], third[plane], _ = shape.faces(beta, half)
        inverse[plane] = jnp.where(beta > 0.0, 1.0 / region[2, plane], 0.0)


def coarser_row(ref, value, start):
    ref[0 : value.shape[0], :] = pair_sum(pair_sum(value, 1), 2)
    inner = lanes_of(1) % 4
    total = ref[start : start + 1, :]
    for offset in range(1, 4):
        total = jnp.where(inner == offset, ref[start + offset : start + offset + 1, :], total)
    return 0.125 * total


def pre1_kernel(
    middle, left, right, absorb, pay_out, field, region, inverse, first, second, third,
    two, tmp, tile,
):
    gather_level1(region, middle, left, right)
    shape = Packed(ROWS1, 2, ROWS1, False)
    level1_parts(shape, region, inverse, first, second, third)
    diag = region.at[2]
    source = lambda plane: region[0, plane]
    parts = (diag, inverse, first, second, third)
    table = chebyshev_table(SWEEPS)
    for plane in range(DEPTH1):
        two[plane] = table[0][1] * (inverse[plane] * source(plane))
        field[plane] = jnp.zeros((ROWS1, LANES), jnp.float32)
    ranges = [(order, DEPTH1 - order) for order in range(1, SWEEPS)]
    current, _ = sweep(
        shape, list(enumerate(table))[1:], source, parts, (two, field), ranges, -1, 99
    )
    for pair in range(2):
        plane = 9 + 2 * pair
        rest = [
            residual(shape, source(p), diag, first, second, third, current, p, -1, 99)
            for p in (plane, plane + 1)
        ]
        tile[pair : pair + 1, :] = coarser_row(tmp.at[pair], rest[0] + rest[1], 6)
        tile[2 + pair : 3 + pair, :] = coarser_row(
            tmp.at[2 + pair], region[1, plane] + region[1, plane + 1], 6
        )
        tile[4 + pair : 5 + pair, :] = coarser_row(
            tmp.at[4 + pair], absorb[2 * pair] + absorb[2 * pair + 1], 2
        )
    tile[6:8, :] = jnp.zeros((2, LANES), jnp.float32)
    whole = tile[...]
    for slot in range(16):
        pay_out[slot] = whole


DEPTH2 = 32
ROWS2 = 8


def level2_parts(shape, beta, absorb, parts):
    diag, inverse, first, second, third = parts
    half = face(2)
    lower = half * beta(0)
    for plane in range(DEPTH2):
        here = beta(plane)
        upper = half * (here + beta(plane + 1)) if plane + 1 < DEPTH2 else half * here
        first[plane] = upper
        second[plane], third[plane], share = shape.faces(here, half)
        total = absorb(plane) + lower + upper + share
        diag[plane] = total
        inverse[plane] = 1.0 / total
        lower = upper


def bottom_rows(ref, planes):
    for pair in range(16):
        ref[8 * pair : 8 * pair + 8, :] = pair_sum(
            pair_sum(planes(2 * pair) + planes(2 * pair + 1), 1), 4
        )
    inner = lanes_of(32) % 8
    total = None
    for offset in range(4):
        value = ref[pl.ds(offset, 32, stride=4), :]
        moved = along(value, 1 if offset % 2 == 0 else -1)
        same = 2 * offset + offset % 2
        value = jnp.where(inner == same, value, moved)
        total = value if total is None else jnp.where(inner // 2 == offset, value, total)
    return 0.125 * total


def bottom_solve(source, absorb, beta):
    shape = Packed(32, 8, 2, True)
    half = face(3)
    plane = rows_of(32) // 2
    last, initial = plane == 15, plane == 0
    up = jnp.where(last, 0.0, across(beta, 2))
    down = jnp.where(initial, 0.0, across(beta, -2))
    second, third, share = shape.faces(beta, half)
    upper = half * (beta + up)
    diag = absorb + half * (beta + down) + upper + share
    first = jnp.where(last, 0.0, upper)
    inverse = 1.0 / diag
    table = chebyshev_table(BOTTOM)
    current = table[0][1] * (inverse * source)
    previous = jnp.zeros_like(current)
    for carry, push in table[1:]:
        rest = source - diag * current + first * across(current, 2) + across(first * current, -2)
        rest = rest + shape.coupled(current, second, third)
        fresh = current + carry * (current - previous) + push * (inverse * rest)
        current, previous = fresh, current
    return current


def bottom_prolong(ref, value):
    inner = lanes_of(32) % 8
    part = inner % 4
    back1, back2 = along(value, -1), along(value, -2)
    fore1, fore2 = along(value, 1), along(value, 2)
    low = jnp.where(part == 0, value, jnp.where(part == 3, back2, back1))
    high = jnp.where(part == 3, value, jnp.where(part == 0, fore2, fore1))
    left = inner < 4
    for offset in range(4):
        base = low if offset % 2 == 0 else high
        if offset < 2:
            moved = jnp.where(left, base, along(base, -4))
        else:
            moved = jnp.where(left, along(base, 4), base)
        ref[pl.ds(offset, 32, stride=4), :] = moved


def solve23(packed, rows2, parts2, one2, two2, tall):
    shape = Packed(ROWS2, 4, ROWS2, True)
    for number in range(3):
        for plane in range(DEPTH2):
            at = 8 * (plane // 2) + 2 * number + plane % 2
            rows2[number, plane] = packed[pl.ds(at, 8, stride=128), :]

    source2 = lambda plane: rows2[0, plane]
    beta2 = lambda plane: rows2[1, plane]
    absorb2 = lambda plane: rows2[2, plane]
    diag2, inverse2, first2, second2, third2 = parts2
    level2_parts(shape, beta2, absorb2, parts2)
    table = chebyshev_table(SWEEPS)
    for plane in range(DEPTH2):
        one2[plane] = table[0][1] * (inverse2[plane] * source2(plane))
        two2[plane] = jnp.zeros((ROWS2, LANES), jnp.float32)
    everywhere = [(0, DEPTH2)] * SWEEPS
    current, previous = sweep(
        shape, list(enumerate(table))[1:], source2, parts2, (one2, two2), everywhere, 0, DEPTH2
    )
    source3 = bottom_rows(
        tall.at[0],
        lambda plane: residual(
            shape, source2(plane), diag2, first2, second2, third2, current, plane, 0, DEPTH2
        ),
    )
    absorb3 = bottom_rows(tall.at[1], absorb2)
    beta3 = bottom_rows(tall.at[2], beta2)
    bottom_prolong(tall.at[0], bottom_solve(source3, absorb3, beta3))
    for plane in range(DEPTH2):
        pair = plane // 2
        current[plane] = current[plane] + tall[0, 8 * pair : 8 * pair + 8, :]
    current, previous = sweep(
        shape, list(enumerate(table)), source2, parts2, (current, previous), everywhere, 0, DEPTH2
    )
    return current


def post1(middle, left, right, field, whole, region, parts, one, two, wide, tmp):
    inverse, first, second, third = parts
    gather_level1(region, middle, left, right)
    shape = Packed(ROWS1, 2, ROWS1, False)
    level1_parts(shape, region, inverse, first, second, third)
    layer = position() // LAYER
    row = column_position() + 6
    zero = jnp.zeros((8, LANES), jnp.float32)
    for plane in range(DEPTH2 + 6):
        wide[plane, 0:8, :] = zero
        wide[plane, 16:24, :] = zero
        inside = 3 <= plane < DEPTH2 + 3
        wide[plane, 8:16, :] = whole[plane - 3] if inside else zero
    inner = lanes_of(8) % 4
    for pair in range(8):
        value = wide[2 * layer + pair, pl.ds(row, 8), :]
        moved = {steps: along(value, steps) for steps in range(-3, 4)}
        part = tmp.at[pair]
        for offset in range(4):
            picked = moved[offset]
            for lane in range(1, 4):
                picked = jnp.where(inner == lane, moved[offset - lane], picked)
            part[pl.ds(offset, 8, stride=4), :] = picked
        for plane in (2 * pair + 3, 2 * pair + 4):
            one[plane] = field[plane] + part[2:18, :]
    table = chebyshev_table(SWEEPS)
    ranges = [(3 + order, 19 - order) for order in range(1, SWEEPS + 1)]
    current, _ = sweep(
        shape, list(enumerate(table)), lambda plane: region[0, plane],
        (region.at[2], inverse, first, second, third), (one, two), ranges, -1, 99,
    )
    return current


def post0(pieces, field, coarse, out, region, parts, one, two, tmp):
    gather_level0(region, *pieces)
    member = position() % LAYER
    source = lambda plane: region[member + plane // 2, 0, plane % 2]
    absorb = lambda plane: region[member + plane // 2, 1, plane % 2]
    beta = lambda plane: region[member + plane // 2, 2, plane % 2]
    shape = Packed(ROWS0, 1, ROWS0, False)
    level0_parts(shape, beta, absorb, parts, 5, 13)
    even = lanes_of(8) % 2 == 0
    for pair in range(5):
        value = coarse[7 + member + pair, 4:12, :]
        upper_rows = jnp.where(even, value, along(value, -1))
        lower_rows = jnp.where(even, along(value, 1), value)
        part = tmp.at[pair]
        for offset in range(4):
            part[pl.ds(offset, 8, stride=4), :] = upper_rows if offset < 2 else lower_rows
        for plane in (2 * pair + 4, 2 * pair + 5):
            one[plane] = field[plane - 4] + part[...]
    table = chebyshev_table(SWEEPS)
    ranges = [(5 + order, 13 - order) for order in range(SWEEPS)]
    current, _ = sweep(
        shape, list(enumerate(table)), source, parts, (one, two), ranges, -1, 99
    )
    for plane in (8, 9):
        out[plane - 8] = current[plane][8:24, :]


def finish_kernel(
    packed, middle, left1, right1, field1, own, below, above, left, right, field0, out,
    rows2, diag2, inverse2, first2, second2, third2, one2, two2, tall,
    region1, inverse1, first1, second1, third1, one1, two1, wide1, tmp1,
    region0, diag0, inverse0, first0, second0, third0, one0, two0, tmp0,
):
    parts2 = (diag2, inverse2, first2, second2, third2)
    whole = solve23(packed, rows2, parts2, one2, two2, tall)
    parts1 = (inverse1, first1, second1, third1)
    coarse = post1(
        middle, left1, right1, field1, whole, region1, parts1, one1, two1, wide1, tmp1
    )
    parts0 = (diag0, inverse0, first0, second0, third0)
    post0(
        (own, below, above, left, right), field0, coarse, out, region0, parts0, one0, two0, tmp0
    )


def f32(*shape):
    return jax.ShapeDtypeStruct(shape, jnp.float32)


def buffer(*shape):
    return pltpu.VMEM(shape, jnp.float32)


def call(kernel, out, scratch, name, *operands):
    return pl.pallas_call(
        kernel,
        out_shape=out,
        scratch_shapes=scratch,
        name=name,
        compiler_params=pltpu.CompilerParams(vmem_limit_bytes=VMEM),
    )(*operands)


def pre0(*pieces):
    plane = buffer(24, ROWS0, LANES)
    scratch = [buffer(12, 3, 2, ROWS0, LANES)] + [plane] * 7 + [buffer(4, ROWS0, LANES)]
    out = (f32(10, ROWS0, LANES), f32(6, 3, 8, LANES), f32(4, 8, LANES))
    return call(pre0_kernel, out, scratch, "pre0", *pieces)


def pre1(*pieces):
    plane = buffer(DEPTH1, ROWS1, LANES)
    scratch = [buffer(3, DEPTH1, ROWS1, LANES)] + [plane] * 5
    scratch += [buffer(6, ROWS1, LANES), buffer(8, LANES)]
    out = (f32(16, 8, LANES), f32(DEPTH1, ROWS1, LANES))
    return call(pre1_kernel, out, scratch, "pre1", *pieces)


def finish(*pieces):
    plane2 = buffer(DEPTH2, ROWS2, LANES)
    plane1 = buffer(DEPTH1, ROWS1, LANES)
    plane0 = buffer(18, ROWS0, LANES)
    scratch = [buffer(3, DEPTH2, ROWS2, LANES)] + [plane2] * 7 + [buffer(3, 128, LANES)]
    scratch += [buffer(3, DEPTH1, ROWS1, LANES)] + [plane1] * 6
    scratch += [buffer(DEPTH2 + 6, 24, LANES), buffer(8, 32, LANES)]
    scratch += [buffer(12, 3, 2, ROWS0, LANES)] + [plane0] * 7 + [buffer(5, ROWS0, LANES)]
    return call(finish_kernel, f32(2, 16, LANES), scratch, "finish", *pieces)


def shifted(value, axis, steps):
    count = lax.axis_size(axis)
    pairs = [(i, i + steps) for i in range(count) if 0 <= i + steps < count]
    return lax.ppermute(value, axis, pairs)


def body(source, absorb, beta):
    members = lax.axis_size("gx")
    across_y = lax.axis_size("gy")
    layers = members // LAYER
    near = [[LAYER * z + c for c in range(LAYER)] for z in range(layers)]
    column = [[LAYER * z + c for z in range(layers)] for c in range(LAYER)]

    local = jnp.stack([source, absorb, beta])
    own = lax.all_gather(local, "gx", axis_index_groups=near)
    below = shifted(own, "gx", LAYER)
    above = shifted(own, "gx", -LAYER)
    left = shifted(jnp.stack([x[..., 8:, :] for x in (below, own, above)]), "gy", 1)
    right = shifted(jnp.stack([x[..., :8, :] for x in (below, own, above)]), "gy", -1)
    pieces0 = (own, below, above, left, right)
    field0, tile, absorb1 = pre0(*pieces0)

    layer_tiles = [
        shifted(tile, "gx", 2 * LAYER)[0:5],
        shifted(tile, "gx", LAYER)[1:5],
        tile[1:5],
        shifted(tile, "gx", -LAYER)[1:5],
        shifted(tile, "gx", -2 * LAYER)[1:6],
    ]
    middle = jnp.concatenate(layer_tiles)
    pieces1 = (middle, shifted(middle, "gy", 1), shifted(middle, "gy", -1))
    pay, field1 = pre1(*pieces1, absorb1)

    rows = lax.all_to_all(pay, "gx", 0, 0, axis_index_groups=column)
    rows = jnp.broadcast_to(rows, (across_y,) + rows.shape)
    packed = lax.all_to_all(rows, "gy", 0, 0).reshape(-1, LANES)
    return finish(packed, *pieces1, field1, *pieces0, field0)


def solution(mesh):
    placed = (P("gx", "gy", None), P("gx", "gy", None), P("gx", "gy", None))
    return jax.shard_map(
        body, mesh=mesh, in_specs=placed, out_specs=P("gx", "gy", None), check_vma=False
    )
```

time: 124 us -> 126 us (1.016)
  the two profiles are of different devices: /device:TPU:16 before, /device:TPU:2 now
where the time goes in v2:
time: 126 us; the launch traced here: 125 us
  blocking collectives  65.7 us (52%)
  starting transfers between devices  25.9 us (21%)
  waiting for transfers between devices  19.6 us (16%)
  Pallas kernels  12.8 us (10%)
    all_to_all x1, blocking collectives, body(): rows = lax.all_to_all(pay, 'gx', 0, 0, axis_index_groups=column)  30.8 us
    ppermute x10, starting transfers between devices, shifted(): return lax.ppermute(value, axis, pairs)  25.9 us
    all_to_all x1, blocking collectives, body(): packed = lax.all_to_all(rows, 'gy', 0, 0).reshape(-1, LANES)  25.1 us
    ppermute x10, waiting for transfers between devices, shifted(): return lax.ppermute(value, axis, pairs)  19.6 us
    pallas_call x3, Pallas kernels, call(): pl.pallas_call(kernel, out_shape=out, scratch_shapes=scratch, name=name,...  12.8 us
    all_gather x1, blocking collectives, body(): own = lax.all_gather(local, 'gx', axis_index_groups=near)  9.79 us
  transfers between devices with their start and end apart: 10, of which 8 were waited for; matrix products, arithmetic and copies ran while one was open for 0% of the time, Pallas kernels for 0%

profile of v2, /device:TPU:2, one launch (start us, length us, event | category | flops | bytes accessed | tf_op | source)
XLA Modules:
  0.0 125.0 jit_solution(4596845843874775565)
XLA Ops:
  0.0 0.8 pad_maximum_fusion.2
  0.8 9.8 %all-gather = f32[12,2,16,128]{3,2,1,0:T(8,128)S(1)} all-gather(f32[3,2,16,128]{3,2,1,0:T(8,128)S(1)} %pad_maximum_fusion.2), channel_id=2, replica_groups={{0,8,16,24},{32,40,48,56},{64,72,80,88},{96,104,112,120},{128,136,144,1..., dimensions={0}, use_global_device_ids=true | all-gather | bytes 245760 | tf_op jit(solution)/shard_map/all_gather | solution.py:538
  10.5 1.3 %collective-permute-start.1 = (f32[4,3,2,16,128]{4,3,2,1,0:T(8,128)S(1)}, f32[4,3,2,16,128]{4,3,2,1,0:T(8,128)S(1)}, u32[]{:S(2)}, u32[]{:S(2)}) collective-permute-start(f32[4,3,2,16,128]{4,3,2,1,0:T(8,128)S(1)} %bitcast.17), channel_id=1, source_target_pairs={{32,0},{40,8},{48,16},{56,24},{64,32},{72,40},{80,48},{88,56},{96,... | collective-permute-start | bytes 589832 | tf_op jit(solution)/shard_map/ppermute | solution.py:527
  11.8 4.6 %collective-permute-start = (f32[4,3,2,16,128]{4,3,2,1,0:T(8,128)S(1)}, f32[4,3,2,16,128]{4,3,2,1,0:T(8,128)S(1)}, u32[]{:S(2)}, u32[]{:S(2)}) collective-permute-start(f32[4,3,2,16,128]{4,3,2,1,0:T(8,128)S(1)} %bitcast.18), channel_id=1, source_target_pairs={{0,32},{8,40},{16,48},{24,56},{32,64},{40,72},{48,80},{56,88},{64,... | collective-permute-start | bytes 589832 | tf_op jit(solution)/shard_map/ppermute | solution.py:527
  16.4 3.2 %collective-permute-done.1.above = f32[4,3,2,16,128]{4,3,2,1,0:T(8,128)S(1)} collective-permute-done((f32[4,3,2,16,128]{4,3,2,1,0:T(8,128)S(1)}, f32[4,3,2,16,128]{4,3,2,1,0:T(8,128)S(1)}, u32[]{:S(2)}, u32[]{:S(2)}) %collective-permute-start.1) | collective-permute-done | bytes 196640 | tf_op jit(solution)/shard_map/ppermute | solution.py:527
  19.6 1.2 collective-permute-done.below
  20.8 1.3 %collective-permute-start.2 = (f32[3,4,3,2,8,128]{5,4,3,2,1,0:T(8,128)S(1)}, f32[3,4,3,2,8,128]{5,4,3,2,1,0:T(8,128)S(1)}, u32[]{:S(2)}, u32[]{:S(2)}) collective-permute-start(f32[3,4,3,2,8,128]{5,4,3,2,1,0:T(8,128)S(1)} %pad_maximum_fusion), channel_id=1, source_target_pairs={{0,1},{1,2},{2,3},{3,4},{4,5},{5,6},{6,7},{8,9},{9,10},{10,11},{11... | collective-permute-start | bytes 884744 | tf_op jit(solution)/shard_map/ppermute | solution.py:527
  22.2 1.3 %collective-permute-start.3 = (f32[3,4,3,2,8,128]{5,4,3,2,1,0:T(8,128)S(1)}, f32[3,4,3,2,8,128]{5,4,3,2,1,0:T(8,128)S(1)}, u32[]{:S(2)}, u32[]{:S(2)}) collective-permute-start(f32[3,4,3,2,8,128]{5,4,3,2,1,0:T(8,128)S(1)} %pad_maximum_fusion.1), channel_id=1, source_target_pairs={{1,0},{2,1},{3,2},{4,3},{5,4},{6,5},{7,6},{9,8},{10,9},{11,10},{12... | collective-permute-start | bytes 884744 | tf_op jit(solution)/shard_map/ppermute | solution.py:527
  23.5 4.6 %collective-permute-done.2.left = f32[3,4,3,2,8,128]{5,4,3,2,1,0:T(8,128)S(1)} collective-permute-done((f32[3,4,3,2,8,128]{5,4,3,2,1,0:T(8,128)S(1)}, f32[3,4,3,2,8,128]{5,4,3,2,1,0:T(8,128)S(1)}, u32[]{:S(2)}, u32[]{:S(2)}) %collective-permute-start.2) | collective-permute-done | bytes 294944 | tf_op jit(solution)/shard_map/ppermute | solution.py:527
  28.0 4.2 %collective-permute-done.3.right = f32[3,4,3,2,8,128]{5,4,3,2,1,0:T(8,128)S(1)} collective-permute-done((f32[3,4,3,2,8,128]{5,4,3,2,1,0:T(8,128)S(1)}, f32[3,4,3,2,8,128]{5,4,3,2,1,0:T(8,128)S(1)}, u32[]{:S(2)}, u32[]{:S(2)}) %collective-permute-start.3) | collective-permute-done | bytes 294944 | tf_op jit(solution)/shard_map/ppermute | solution.py:527
  32.2 1.9 %pre0.1 = (f32[10,32,128]{2,1,0:T(8,128)S(1)}, f32[6,3,8,128]{3,2,1,0:T(8,128)S(1)}, f32[4,8,128]{2,1,0:T(8,128)S(1)}) custom-call(f32[4,3,2,16,128]{4,3,2,1,0:T(8,128)S(1)} %bitcast.20, f32[4,3,2,16,128]{4,3,2,1,0:T(8,128)S(1)} %collective-permute-done.below, f32[4,3,2,16,128]{4,3,2,1,0:T(8,128)S(1)} %collective-permute-done.1.above, ...), custom_call_target="tpu_custom_call" | custom-call | tf_op jit(solution)/shard_map/pre0/pallas_call | solution.py:489
  34.1 4.4 %collective-permute-start.4 = (f32[6,3,8,128]{3,2,1,0:T(8,128)S(1)}, f32[6,3,8,128]{3,2,1,0:T(8,128)S(1)}, u32[]{:S(2)}, u32[]{:S(2)}) collective-permute-start(f32[6,3,8,128]{3,2,1,0:T(8,128)S(1)} %get-tuple-element.10), channel_id=1, source_target_pairs={{0,64},{8,72},{16,80},{24,88},{32,96},{40,104},{48,112},{56,120},{... | collective-permute-start | bytes 221192 | tf_op jit(solution)/shard_map/ppermute | solution.py:527
  38.6 1.3 %collective-permute-start.7 = (f32[6,3,8,128]{3,2,1,0:T(8,128)S(1)}, f32[6,3,8,128]{3,2,1,0:T(8,128)S(1)}, u32[]{:S(2)}, u32[]{:S(2)}) collective-permute-start(f32[6,3,8,128]{3,2,1,0:T(8,128)S(1)} %get-tuple-element.10), channel_id=1, source_target_pairs={{64,0},{72,8},{80,16},{88,24},{96,32},{104,40},{112,48},{120,56},{... | collective-permute-start | bytes 221192 | tf_op jit(solution)/shard_map/ppermute | solution.py:527
  39.9 1.3 %collective-permute-start.6 = (f32[6,3,8,128]{3,2,1,0:T(8,128)S(1)}, f32[6,3,8,128]{3,2,1,0:T(8,128)S(1)}, u32[]{:S(2)}, u32[]{:S(2)}) collective-permute-start(f32[6,3,8,128]{3,2,1,0:T(8,128)S(1)} %get-tuple-element.10), channel_id=1, source_target_pairs={{32,0},{40,8},{48,16},{56,24},{64,32},{72,40},{80,48},{88,56},{96,... | collective-permute-start | bytes 221192 | tf_op jit(solution)/shard_map/ppermute | solution.py:527
  41.2 4.5 %collective-permute-start.5 = (f32[6,3,8,128]{3,2,1,0:T(8,128)S(1)}, f32[6,3,8,128]{3,2,1,0:T(8,128)S(1)}, u32[]{:S(2)}, u32[]{:S(2)}) collective-permute-start(f32[6,3,8,128]{3,2,1,0:T(8,128)S(1)} %get-tuple-element.10), channel_id=1, source_target_pairs={{0,32},{8,40},{16,48},{24,56},{32,64},{40,72},{48,80},{56,88},{64,... | collective-permute-start | bytes 221192 | tf_op jit(solution)/shard_map/ppermute | solution.py:527
  45.7 0.0 collective-permute-done.4
  45.8 1.9 %collective-permute-done.5 = f32[6,3,8,128]{3,2,1,0:T(8,128)S(1)} collective-permute-done((f32[6,3,8,128]{3,2,1,0:T(8,128)S(1)}, f32[6,3,8,128]{3,2,1,0:T(8,128)S(1)}, u32[]{:S(2)}, u32[]{:S(2)}) %collective-permute-start.5) | collective-permute-done | bytes 73760 | tf_op jit(solution)/shard_map/ppermute | solution.py:527
  47.7 0.0 collective-permute-done.6
  47.7 0.7 collective-permute-done.7
  48.5 1.3 %collective-permute-start.9 = (f32[22,3,8,128]{3,2,1,0:T(8,128)S(1)}, f32[22,3,8,128]{3,2,1,0:T(8,128)S(1)}, u32[]{:S(2)}, u32[]{:S(2)}) collective-permute-start(f32[22,3,8,128]{3,2,1,0:T(8,128)S(1)} %slice_dynamic-update-slice_fusion.middle), channel_id=1, source_target_pairs={{1,0},{2,1},{3,2},{4,3},{5,4},{6,5},{7,6},{9,8},{10,9},{11,10},{12... | collective-permute-start | bytes 811016 | tf_op jit(solution)/shard_map/ppermute | solution.py:527
  49.7 4.6 %collective-permute-start.8 = (f32[22,3,8,128]{3,2,1,0:T(8,128)S(1)}, f32[22,3,8,128]{3,2,1,0:T(8,128)S(1)}, u32[]{:S(2)}, u32[]{:S(2)}) collective-permute-start(f32[22,3,8,128]{3,2,1,0:T(8,128)S(1)} %slice_dynamic-update-slice_fusion.middle), channel_id=1, source_target_pairs={{0,1},{1,2},{2,3},{3,4},{4,5},{5,6},{6,7},{8,9},{9,10},{10,11},{11... | collective-permute-start | bytes 811016 | tf_op jit(solution)/shard_map/ppermute | solution.py:527
  54.3 2.5 %collective-permute-done.9.right.right1 = f32[22,3,8,128]{3,2,1,0:T(8,128)S(1)} collective-permute-done((f32[22,3,8,128]{3,2,1,0:T(8,128)S(1)}, f32[22,3,8,128]{3,2,1,0:T(8,128)S(1)}, u32[]{:S(2)}, u32[]{:S(2)}) %collective-permute-start.9) | collective-permute-done | bytes 270368 | tf_op jit(solution)/shard_map/ppermute | solution.py:527
  56.8 1.5 %collective-permute-done.8.left.left1 = f32[22,3,8,128]{3,2,1,0:T(8,128)S(1)} collective-permute-done((f32[22,3,8,128]{3,2,1,0:T(8,128)S(1)}, f32[22,3,8,128]{3,2,1,0:T(8,128)S(1)}, u32[]{:S(2)}, u32[]{:S(2)}) %collective-permute-start.8) | collective-permute-done | bytes 270368 | tf_op jit(solution)/shard_map/ppermute | solution.py:527
  58.3 1.2 pre1.1
  59.4 30.8 %all_to_all.10 = f32[16,8,128]{2,1,0:T(8,128)S(1)} all-to-all(f32[16,8,128]{2,1,0:T(8,128)S(1)} %get-tuple-element.12), channel_id=1, replica_groups={{0,32,64,96,128,160,192,224,256,288,320,352,384,416,448,480},{8,40,72,1..., dimensions={0} | all-to-all | bytes 131072 | tf_op jit(solution)/shard_map/all_to_all | solution.py:557
  90.3 25.1 %all_to_all.11 = f32[8,16,8,128]{3,2,1,0:T(8,128)S(1)} all-to-all(f32[8,16,8,128]{3,2,1,0:T(8,128)S(1)} %broadcast_in_dim.3), channel_id=1, replica_groups=mesh['gx'=64,'gy'=8] {'gy'}, dimensions={0} | all-to-all | bytes 1048576 | tf_op jit(solution)/shard_map/all_to_all | solution.py:559
  115.4 9.7 %finish.1 = f32[2,16,128]{2,1,0:T(8,128)} custom-call(f32[1024,128]{1,0:T(8,128)S(1)} %bitcast.22, f32[22,3,8,128]{3,2,1,0:T(8,128)S(1)} %slice_dynamic-update-slice_fusion.middle, f32[22,3,8,128]{3,2,1,0:T(8,128)S(1)} %collective-permute-done.8.left.left1, f32[22,3,8,128]{3,2,1,0:T(8,128)S(1)} %collective-permute-done.9.right.right1, ...), custom_call_target="tpu_custom_call" | custom-call | tf_op jit(solution)/shard_map/finish/pallas_call | solution.py:489
  (11 shorter events, 0.1 us)
Async XLA Ops:
  10.5 9.0 %collective-permute-start.1 = (f32[4,3,2,16,128]{4,3,2,1,0:T(8,128)S(1)}, f32[4,3,2,16,128]{4,3,2,1,0:T(8,128)S(1)}, u32[]{:S(2)}, u32[]{:S(2)}) collective-permute-start(f32[4,3,2,16,128]{4,3,2,1,0:T(8,128)S(1)} %bitcast.17), channel_id=1, source_target_pairs={{32,0},{40,8},{48,16},{56,24},{64,32},{72,40},{80,48},{88,56},{96,... | collective-permute-start | bytes 589832 | tf_op jit(solution)/shard_map/ppermute | solution.py:527
  11.8 8.9 %collective-permute-start = (f32[4,3,2,16,128]{4,3,2,1,0:T(8,128)S(1)}, f32[4,3,2,16,128]{4,3,2,1,0:T(8,128)S(1)}, u32[]{:S(2)}, u32[]{:S(2)}) collective-permute-start(f32[4,3,2,16,128]{4,3,2,1,0:T(8,128)S(1)} %bitcast.18), channel_id=1, source_target_pairs={{0,32},{8,40},{16,48},{24,56},{32,64},{40,72},{48,80},{56,88},{64,... | collective-permute-start | bytes 589832 | tf_op jit(solution)/shard_map/ppermute | solution.py:527
  20.8 7.2 %collective-permute-start.2 = (f32[3,4,3,2,8,128]{5,4,3,2,1,0:T(8,128)S(1)}, f32[3,4,3,2,8,128]{5,4,3,2,1,0:T(8,128)S(1)}, u32[]{:S(2)}, u32[]{:S(2)}) collective-permute-start(f32[3,4,3,2,8,128]{5,4,3,2,1,0:T(8,128)S(1)} %pad_maximum_fusion), channel_id=1, source_target_pairs={{0,1},{1,2},{2,3},{3,4},{4,5},{5,6},{6,7},{8,9},{9,10},{10,11},{11... | collective-permute-start | bytes 884744 | tf_op jit(solution)/shard_map/ppermute | solution.py:527
  22.2 10.0 %collective-permute-start.3 = (f32[3,4,3,2,8,128]{5,4,3,2,1,0:T(8,128)S(1)}, f32[3,4,3,2,8,128]{5,4,3,2,1,0:T(8,128)S(1)}, u32[]{:S(2)}, u32[]{:S(2)}) collective-permute-start(f32[3,4,3,2,8,128]{5,4,3,2,1,0:T(8,128)S(1)} %pad_maximum_fusion.1), channel_id=1, source_target_pairs={{1,0},{2,1},{3,2},{4,3},{5,4},{6,5},{7,6},{9,8},{10,9},{11,10},{12... | collective-permute-start | bytes 884744 | tf_op jit(solution)/shard_map/ppermute | solution.py:527
  34.1 11.6 %collective-permute-start.4 = (f32[6,3,8,128]{3,2,1,0:T(8,128)S(1)}, f32[6,3,8,128]{3,2,1,0:T(8,128)S(1)}, u32[]{:S(2)}, u32[]{:S(2)}) collective-permute-start(f32[6,3,8,128]{3,2,1,0:T(8,128)S(1)} %get-tuple-element.10), channel_id=1, source_target_pairs={{0,64},{8,72},{16,80},{24,88},{32,96},{40,104},{48,112},{56,120},{... | collective-permute-start | bytes 221192 | tf_op jit(solution)/shard_map/ppermute | solution.py:527
  38.6 9.9 %collective-permute-start.7 = (f32[6,3,8,128]{3,2,1,0:T(8,128)S(1)}, f32[6,3,8,128]{3,2,1,0:T(8,128)S(1)}, u32[]{:S(2)}, u32[]{:S(2)}) collective-permute-start(f32[6,3,8,128]{3,2,1,0:T(8,128)S(1)} %get-tuple-element.10), channel_id=1, source_target_pairs={{64,0},{72,8},{80,16},{88,24},{96,32},{104,40},{112,48},{120,56},{... | collective-permute-start | bytes 221192 | tf_op jit(solution)/shard_map/ppermute | solution.py:527
  39.9 7.8 %collective-permute-start.6 = (f32[6,3,8,128]{3,2,1,0:T(8,128)S(1)}, f32[6,3,8,128]{3,2,1,0:T(8,128)S(1)}, u32[]{:S(2)}, u32[]{:S(2)}) collective-permute-start(f32[6,3,8,128]{3,2,1,0:T(8,128)S(1)} %get-tuple-element.10), channel_id=1, source_target_pairs={{32,0},{40,8},{48,16},{56,24},{64,32},{72,40},{80,48},{88,56},{96,... | collective-permute-start | bytes 221192 | tf_op jit(solution)/shard_map/ppermute | solution.py:527
  41.2 6.5 %collective-permute-start.5 = (f32[6,3,8,128]{3,2,1,0:T(8,128)S(1)}, f32[6,3,8,128]{3,2,1,0:T(8,128)S(1)}, u32[]{:S(2)}, u32[]{:S(2)}) collective-permute-start(f32[6,3,8,128]{3,2,1,0:T(8,128)S(1)} %get-tuple-element.10), channel_id=1, source_target_pairs={{0,32},{8,40},{16,48},{24,56},{32,64},{40,72},{48,80},{56,88},{64,... | collective-permute-start | bytes 221192 | tf_op jit(solution)/shard_map/ppermute | solution.py:527
  48.5 8.3 %collective-permute-start.9 = (f32[22,3,8,128]{3,2,1,0:T(8,128)S(1)}, f32[22,3,8,128]{3,2,1,0:T(8,128)S(1)}, u32[]{:S(2)}, u32[]{:S(2)}) collective-permute-start(f32[22,3,8,128]{3,2,1,0:T(8,128)S(1)} %slice_dynamic-update-slice_fusion.middle), channel_id=1, source_target_pairs={{1,0},{2,1},{3,2},{4,3},{5,4},{6,5},{7,6},{9,8},{10,9},{11,10},{12... | collective-permute-start | bytes 811016 | tf_op jit(solution)/shard_map/ppermute | solution.py:527
  49.7 8.5 %collective-permute-start.8 = (f32[22,3,8,128]{3,2,1,0:T(8,128)S(1)}, f32[22,3,8,128]{3,2,1,0:T(8,128)S(1)}, u32[]{:S(2)}, u32[]{:S(2)}) collective-permute-start(f32[22,3,8,128]{3,2,1,0:T(8,128)S(1)} %slice_dynamic-update-slice_fusion.middle), channel_id=1, source_target_pairs={{0,1},{1,2},{2,3},{3,4},{4,5},{5,6},{6,7},{8,9},{9,10},{10,11},{11... | collective-permute-start | bytes 811016 | tf_op jit(solution)/shard_map/ppermute | solution.py:527

commit v3 on v2

--- a/solution.py
+++ b/solution.py
@@ -140,13 +140,13 @@
 ROWS0 = 32
 
 
-def gather_level0(region, own, below, above, left, right):
-    for part, piece in enumerate((below, own, above)):
+def gather_level0(region, own, outer, sides):
+    for part, piece in enumerate((outer.at[0], own, outer.at[1])):
         for member in range(LAYER):
             at = part * LAYER + member
             region[at, :, :, 8:24, :] = piece[member]
-            region[at, :, :, 0:8, :] = left[part, member]
-            region[at, :, :, 24:32, :] = right[part, member]
+            region[at, :, :, 0:8, :] = sides[0, part, member]
+            region[at, :, :, 24:32, :] = sides[1, part, member]
 
 
 def level0_parts(shape, beta, absorb, parts, start, stop):
@@ -175,10 +175,10 @@
 
 
 def pre0_kernel(
-    own, below, above, left, right, field_out, tile_out, absorb_out,
+    own, outer, sides, field_out, tile_out, absorb_out,
     region, diag, inverse, first, second, third, one, two, tmp,
 ):
-    gather_level0(region, own, below, above, left, right)
+    gather_level0(region, own, outer, sides)
     source = lambda plane: region[plane // 2, 0, plane % 2]
     absorb = lambda plane: region[plane // 2, 1, plane % 2]
     beta = lambda plane: region[plane // 2, 2, plane % 2]
@@ -219,13 +219,13 @@
 ROWS1 = 16
 
 
-def gather_level1(region, middle, left, right):
+def gather_level1(region, middle, sides):
     row = rows_of(8)
     for plane in range(DEPTH1):
         for kind in range(3):
             moved = across(middle[plane, kind], 4)
-            region[kind, plane, 0:8, :] = jnp.where(row < 6, left[plane, kind], moved)
-            region[kind, plane, 8:16, :] = jnp.where(row < 2, moved, right[plane, kind])
+            region[kind, plane, 0:8, :] = jnp.where(row < 6, sides[0, plane, kind], moved)
+            region[kind, plane, 8:16, :] = jnp.where(row < 2, moved, sides[1, plane, kind])
 
 
 def level1_parts(shape, region, inverse, first, second, third):
@@ -249,10 +249,10 @@
 
 
 def pre1_kernel(
-    middle, left, right, absorb, pay_out, field, region, inverse, first, second, third,
+    middle, sides, absorb, pay_out, field, region, inverse, first, second, third,
     two, tmp, tile,
 ):
-    gather_level1(region, middle, left, right)
+    gather_level1(region, middle, sides)
     shape = Packed(ROWS1, 2, ROWS1, False)
     level1_parts(shape, region, inverse, first, second, third)
     diag = region.at[2]
@@ -398,9 +398,9 @@
     return current
 
 
-def post1(middle, left, right, field, whole, region, parts, one, two, wide, tmp):
+def post1(middle, sides, field, whole, region, parts, one, two, wide, tmp):
     inverse, first, second, third = parts
-    gather_level1(region, middle, left, right)
+    gather_level1(region, middle, sides)
     shape = Packed(ROWS1, 2, ROWS1, False)
     level1_parts(shape, region, inverse, first, second, third)
     layer = position() // LAYER
@@ -460,7 +460,7 @@
 
 
 def finish_kernel(
-    packed, middle, left1, right1, field1, own, below, above, left, right, field0, out,
+    packed, middle, sides1, field1, own, outer, sides0, field0, out,
     rows2, diag2, inverse2, first2, second2, third2, one2, two2, tall,
     region1, inverse1, first1, second1, third1, one1, two1, wide1, tmp1,
     region0, diag0, inverse0, first0, second0, third0, one0, two0, tmp0,
@@ -469,11 +469,11 @@
     whole = solve23(packed, rows2, parts2, one2, two2, tall)
     parts1 = (inverse1, first1, second1, third1)
     coarse = post1(
-        middle, left1, right1, field1, whole, region1, parts1, one1, two1, wide1, tmp1
+        middle, sides1, field1, whole, region1, parts1, one1, two1, wide1, tmp1
     )
     parts0 = (diag0, inverse0, first0, second0, third0)
     post0(
-        (own, below, above, left, right), field0, coarse, out, region0, parts0, one0, two0, tmp0
+        (own, outer, sides0), field0, coarse, out, region0, parts0, one0, two0, tmp0
     )
 
 
@@ -521,10 +521,21 @@
     return call(finish_kernel, f32(2, 16, LANES), scratch, "finish", *pieces)
 
 
-def shifted(value, axis, steps):
-    count = lax.axis_size(axis)
-    pairs = [(i, i + steps) for i in range(count) if 0 <= i + steps < count]
-    return lax.ppermute(value, axis, pairs)
+def layers_apart(value, steps):
+    count = lax.axis_size("gx")
+    ways = [(i, i + (LAYER * steps if i % 2 == 0 else -LAYER * steps)) for i in range(count)]
+    return lax.ppermute(value, "gx", [(i, j) for i, j in ways if 0 <= j < count])
+
+
+def columns_apart(value):
+    count, wide = lax.axis_size("gx"), lax.axis_size("gy")
+    ways = [
+        (i * wide + j, i * wide + j + (1 if i % 2 == 0 else -1))
+        for i in range(count)
+        for j in range(wide)
+        if 0 <= j + (1 if i % 2 == 0 else -1) < wide
+    ]
+    return lax.ppermute(value, ("gx", "gy"), ways)
 
 
 def body(source, absorb, beta):
@@ -532,26 +543,26 @@
     across_y = lax.axis_size("gy")
     layers = members // LAYER
     near = [[LAYER * z + c for c in range(LAYER)] for z in range(layers)]
+    chips = [[2 * chip, 2 * chip + 1] for chip in range(members // 2)]
     column = [[LAYER * z + c for z in range(layers)] for c in range(LAYER)]
+    first_core = lax.axis_index("gx") % 2 == 0
+
+    def both(value):
+        return lax.all_gather(value, "gx", axis_index_groups=chips)
 
     local = jnp.stack([source, absorb, beta])
     own = lax.all_gather(local, "gx", axis_index_groups=near)
-    below = shifted(own, "gx", LAYER)
-    above = shifted(own, "gx", -LAYER)
-    left = shifted(jnp.stack([x[..., 8:, :] for x in (below, own, above)]), "gy", 1)
-    right = shifted(jnp.stack([x[..., :8, :] for x in (below, own, above)]), "gy", -1)
-    pieces0 = (own, below, above, left, right)
+    outer = both(layers_apart(own, 1))
+    edges = [jnp.where(first_core, x[..., 8:, :], x[..., :8, :]) for x in (outer[0], own, outer[1])]
+    sides0 = both(columns_apart(jnp.stack(edges)))
+    pieces0 = (own, outer, sides0)
     field0, tile, absorb1 = pre0(*pieces0)
 
-    layer_tiles = [
-        shifted(tile, "gx", 2 * LAYER)[0:5],
-        shifted(tile, "gx", LAYER)[1:5],
-        tile[1:5],
-        shifted(tile, "gx", -LAYER)[1:5],
-        shifted(tile, "gx", -2 * LAYER)[1:6],
-    ]
-    middle = jnp.concatenate(layer_tiles)
-    pieces1 = (middle, shifted(middle, "gy", 1), shifted(middle, "gy", -1))
+    tiles = both(jnp.stack([layers_apart(tile, 1), layers_apart(tile, 2)]))
+    middle = jnp.concatenate(
+        [tiles[0, 1, 0:5], tiles[0, 0, 1:5], tile[1:5], tiles[1, 0, 1:5], tiles[1, 1, 1:6]]
+    )
+    pieces1 = (middle, both(columns_apart(middle)))
     pay, field1 = pre1(*pieces1, absorb1)
 
     rows = lax.all_to_all(pay, "gx", 0, 0, axis_index_groups=column)

time: 126 us -> 112 us (0.89)
  the two profiles are of different devices: /device:TPU:2 before, /device:TPU:1 now
where the time goes in v3:
time: 112 us; the launch traced here: 111 us
  blocking collectives  68.2 us (61%)
  waiting for transfers between devices  22.4 us (20%)
  Pallas kernels  12.8 us (11%)
  starting transfers between devices  6.45 us (6%)
    all_to_all x1, blocking collectives, body(): rows = lax.all_to_all(pay, 'gx', 0, 0, axis_index_groups=column)  25.6 us
    all_to_all x1, blocking collectives, body(): packed = lax.all_to_all(rows, 'gy', 0, 0).reshape(-1, LANES)  21.1 us
    ppermute x2, waiting for transfers between devices, columns_apart(): return lax.ppermute(value, ('gx', 'gy'), ways)  12.8 us
    pallas_call x3, Pallas kernels, call(): pl.pallas_call(kernel, out_shape=out, scratch_shapes=scratch, name=name,...  12.8 us
    all_gather x1, blocking collectives, body(): own = lax.all_gather(local, 'gx', axis_index_groups=near)  12.3 us
    ppermute x3, waiting for transfers between devices, layers_apart(): lax.ppermute(value, 'gx', [(i, j) for i, j in ways if 0 <= j < count])  9.63 us
    all_gather x4, blocking collectives, both(): return lax.all_gather(value, 'gx', axis_index_groups=chips)  9.18 us
    ppermute x3, starting transfers between devices, layers_apart(): lax.ppermute(value, 'gx', [(i, j) for i, j in ways if 0 <= j < count])  3.86 us
  transfers between devices with their start and end apart: 5, of which 5 were waited for; matrix products, arithmetic and copies ran while one was open for 0% of the time, Pallas kernels for 0%

profile of v3, /device:TPU:1, one launch (start us, length us, event | category | flops | bytes accessed | tf_op | source)
XLA Modules:
  0.0 110.9 jit_solution(5816704303021223050)
XLA Ops:
  0.0 0.8 pad_maximum_fusion.2
  0.8 12.3 %all-gather = f32[12,2,16,128]{3,2,1,0:T(8,128)S(1)} all-gather(f32[3,2,16,128]{3,2,1,0:T(8,128)S(1)} %pad_maximum_fusion.2), channel_id=2, replica_groups={{0,8,16,24},{32,40,48,56},{64,72,80,88},{96,104,112,120},{128,136,144,1..., dimensions={0}, use_global_device_ids=true | all-gather | bytes 245760 | tf_op jit(solution)/shard_map/all_gather | solution.py:554
  13.1 1.3 %collective-permute-start = (f32[4,3,2,16,128]{4,3,2,1,0:T(8,128)S(1)}, f32[4,3,2,16,128]{4,3,2,1,0:T(8,128)S(1)}, u32[]{:S(2)}, u32[]{:S(2)}) collective-permute-start(f32[4,3,2,16,128]{4,3,2,1,0:T(8,128)S(1)} %bitcast.39), channel_id=1, source_target_pairs={{0,32},{16,48},{32,64},{40,8},{48,80},{56,24},{64,96},{72,40},{80,... | collective-permute-start | bytes 589832 | tf_op jit(solution)/shard_map/ppermute | solution.py:527
  14.4 5.1 %collective-permute-done = f32[4,3,2,16,128]{4,3,2,1,0:T(8,128)S(1)} collective-permute-done((f32[4,3,2,16,128]{4,3,2,1,0:T(8,128)S(1)}, f32[4,3,2,16,128]{4,3,2,1,0:T(8,128)S(1)}, u32[]{:S(2)}, u32[]{:S(2)}) %collective-permute-start) | collective-permute-done | bytes 196640 | tf_op jit(solution)/shard_map/ppermute | solution.py:527
  19.5 2.1 %all-gather.1 = f32[8,3,2,16,128]{4,3,2,1,0:T(8,128)S(1)} all-gather(f32[4,3,2,16,128]{4,3,2,1,0:T(8,128)S(1)} %collective-permute-done), channel_id=3, replica_groups={{0,8},{16,24},{32,40},{48,56},{64,72},{80,88},{96,104},{112,120},{128,1..., dimensions={0}, use_global_device_ids=true | all-gather | bytes 589824 | tf_op jit(solution)/shard_map/all_gather | solution.py:551
  21.6 1.3 %collective-permute-start.1 = (f32[3,4,3,2,8,128]{5,4,3,2,1,0:T(8,128)S(1)}, f32[3,4,3,2,8,128]{5,4,3,2,1,0:T(8,128)S(1)}, u32[]{:S(2)}, u32[]{:S(2)}) collective-permute-start(f32[3,4,3,2,8,128]{5,4,3,2,1,0:T(8,128)S(1)} %pad_maximum_fusion), channel_id=1, source_target_pairs={{0,1},{1,2},{2,3},{3,4},{4,5},{5,6},{6,7},{9,8},{10,9},{11,10},{12... | collective-permute-start | bytes 884744 | tf_op jit(solution)/shard_map/ppermute | solution.py:538
  22.9 6.2 %collective-permute-done.1 = f32[3,4,3,2,8,128]{5,4,3,2,1,0:T(8,128)S(1)} collective-permute-done((f32[3,4,3,2,8,128]{5,4,3,2,1,0:T(8,128)S(1)}, f32[3,4,3,2,8,128]{5,4,3,2,1,0:T(8,128)S(1)}, u32[]{:S(2)}, u32[]{:S(2)}) %collective-permute-start.1) | collective-permute-done | bytes 294944 | tf_op jit(solution)/shard_map/ppermute | solution.py:538
  29.1 2.2 %all-gather.2 = f32[6,4,3,2,8,128]{5,4,3,2,1,0:T(8,128)S(1)} all-gather(f32[3,4,3,2,8,128]{5,4,3,2,1,0:T(8,128)S(1)} %collective-permute-done.1), channel_id=4, replica_groups={{0,8},{16,24},{32,40},{48,56},{64,72},{80,88},{96,104},{112,120},{128,1..., dimensions={0}, use_global_device_ids=true | all-gather | bytes 884736 | tf_op jit(solution)/shard_map/all_gather | solution.py:551
  31.3 2.0 %pre0.1 = (f32[10,32,128]{2,1,0:T(8,128)S(1)}, f32[6,3,8,128]{3,2,1,0:T(8,128)S(1)}, f32[4,8,128]{2,1,0:T(8,128)S(1)}) custom-call(f32[4,3,2,16,128]{4,3,2,1,0:T(8,128)S(1)} %bitcast.41, f32[2,4,3,2,16,128]{5,4,3,2,1,0:T(8,128)S(1)} %bitcast.33, f32[2,3,4,3,2,8,128]{6,5,4,3,2,1,0:T(8,128)S(1)} %bitcast.35), custom_call_target="tpu_custom_call" | custom-call | tf_op jit(solution)/shard_map/pre0/pallas_call | solution.py:489
  33.2 1.3 %collective-permute-start.3 = (f32[6,3,8,128]{3,2,1,0:T(8,128)S(1)}, f32[6,3,8,128]{3,2,1,0:T(8,128)S(1)}, u32[]{:S(2)}, u32[]{:S(2)}) collective-permute-start(f32[6,3,8,128]{3,2,1,0:T(8,128)S(1)} %get-tuple-element.10), channel_id=1, source_target_pairs={{0,64},{16,80},{32,96},{48,112},{64,128},{72,8},{80,144},{88,24},{... | collective-permute-start | bytes 221192 | tf_op jit(solution)/shard_map/ppermute | solution.py:527
  34.5 1.3 %collective-permute-start.2 = (f32[6,3,8,128]{3,2,1,0:T(8,128)S(1)}, f32[6,3,8,128]{3,2,1,0:T(8,128)S(1)}, u32[]{:S(2)}, u32[]{:S(2)}) collective-permute-start(f32[6,3,8,128]{3,2,1,0:T(8,128)S(1)} %get-tuple-element.10), channel_id=1, source_target_pairs={{0,32},{16,48},{32,64},{40,8},{48,80},{56,24},{64,96},{72,40},{80,... | collective-permute-start | bytes 221192 | tf_op jit(solution)/shard_map/ppermute | solution.py:527
  35.8 4.1 %collective-permute-done.3 = f32[6,3,8,128]{3,2,1,0:T(8,128)S(1)} collective-permute-done((f32[6,3,8,128]{3,2,1,0:T(8,128)S(1)}, f32[6,3,8,128]{3,2,1,0:T(8,128)S(1)}, u32[]{:S(2)}, u32[]{:S(2)}) %collective-permute-start.3) | collective-permute-done | bytes 73760 | tf_op jit(solution)/shard_map/ppermute | solution.py:527
  39.9 0.5 collective-permute-done.2
  40.4 2.3 %all-gather.3 = f32[4,6,3,8,128]{4,3,2,1,0:T(8,128)S(1)} all-gather(f32[2,6,3,8,128]{4,3,2,1,0:T(8,128)S(1)} %pad_maximum_fusion.1), channel_id=5, replica_groups={{0,8},{16,24},{32,40},{48,56},{64,72},{80,88},{96,104},{112,120},{128,1..., dimensions={0}, use_global_device_ids=true | all-gather | bytes 442368 | tf_op jit(solution)/shard_map/all_gather | solution.py:551
  42.8 1.3 %collective-permute-start.4 = (f32[22,3,8,128]{3,2,1,0:T(8,128)S(1)}, f32[22,3,8,128]{3,2,1,0:T(8,128)S(1)}, u32[]{:S(2)}, u32[]{:S(2)}) collective-permute-start(f32[22,3,8,128]{3,2,1,0:T(8,128)S(1)} %fusion.3.middle), channel_id=1, source_target_pairs={{0,1},{1,2},{2,3},{3,4},{4,5},{5,6},{6,7},{9,8},{10,9},{11,10},{12... | collective-permute-start | bytes 811016 | tf_op jit(solution)/shard_map/ppermute | solution.py:538
  44.1 6.7 %collective-permute-done.4 = f32[22,3,8,128]{3,2,1,0:T(8,128)S(1)} collective-permute-done((f32[22,3,8,128]{3,2,1,0:T(8,128)S(1)}, f32[22,3,8,128]{3,2,1,0:T(8,128)S(1)}, u32[]{:S(2)}, u32[]{:S(2)}) %collective-permute-start.4) | collective-permute-done | bytes 270368 | tf_op jit(solution)/shard_map/ppermute | solution.py:538
  50.7 2.6 %all-gather.4 = f32[44,3,8,128]{3,2,1,0:T(8,128)S(1)} all-gather(f32[22,3,8,128]{3,2,1,0:T(8,128)S(1)} %collective-permute-done.4), channel_id=6, replica_groups={{0,8},{16,24},{32,40},{48,56},{64,72},{80,88},{96,104},{112,120},{128,1..., dimensions={0}, use_global_device_ids=true | all-gather | bytes 811008 | tf_op jit(solution)/shard_map/all_gather | solution.py:551
  53.3 1.2 %pre1.1 = (f32[16,8,128]{2,1,0:T(8,128)S(1)}, f32[22,16,128]{2,1,0:T(8,128)S(1)}) custom-call(f32[22,3,8,128]{3,2,1,0:T(8,128)S(1)} %fusion.3.middle, f32[2,22,3,8,128]{4,3,2,1,0:T(8,128)S(1)} %bitcast.37, f32[4,8,128]{2,1,0:T(8,128)S(1)} %get-tuple-element.11.absorb), custom_call_target="tpu_custom_call" | custom-call | tf_op jit(solution)/shard_map/pre1/pallas_call | solution.py:489
  54.5 25.6 %all_to_all.10 = f32[16,8,128]{2,1,0:T(8,128)S(1)} all-to-all(f32[16,8,128]{2,1,0:T(8,128)S(1)} %get-tuple-element.12), channel_id=1, replica_groups={{0,32,64,96,128,160,192,224,256,288,320,352,384,416,448,480},{8,40,72,1..., dimensions={0} | all-to-all | bytes 131072 | tf_op jit(solution)/shard_map/all_to_all | solution.py:568
  80.1 21.1 %all_to_all.11 = f32[8,16,8,128]{3,2,1,0:T(8,128)S(1)} all-to-all(f32[8,16,8,128]{3,2,1,0:T(8,128)S(1)} %broadcast_in_dim.3), channel_id=1, replica_groups=mesh['gx'=64,'gy'=8] {'gy'}, dimensions={0} | all-to-all | bytes 1048576 | tf_op jit(solution)/shard_map/all_to_all | solution.py:570
  101.2 9.7 %finish.1 = f32[2,16,128]{2,1,0:T(8,128)} custom-call(f32[1024,128]{1,0:T(8,128)S(1)} %bitcast.43, f32[22,3,8,128]{3,2,1,0:T(8,128)S(1)} %fusion.3.middle, f32[2,22,3,8,128]{4,3,2,1,0:T(8,128)S(1)} %bitcast.38, f32[22,16,128]{2,1,0:T(8,128)S(1)} %get-tuple-element.13.field1, f32[4,3,2,16,128]{4,3,2,1,0:T(8,128)S(1)} %bitcast.42, ...), custom_call_target="tpu_custom_call" | custom-call | tf_op jit(solution)/shard_map/finish/pallas_call | solution.py:489
  (10 shorter events, 0.1 us)
Async XLA Ops:
  13.1 6.4 %collective-permute-start = (f32[4,3,2,16,128]{4,3,2,1,0:T(8,128)S(1)}, f32[4,3,2,16,128]{4,3,2,1,0:T(8,128)S(1)}, u32[]{:S(2)}, u32[]{:S(2)}) collective-permute-start(f32[4,3,2,16,128]{4,3,2,1,0:T(8,128)S(1)} %bitcast.39), channel_id=1, source_target_pairs={{0,32},{16,48},{32,64},{40,8},{48,80},{56,24},{64,96},{72,40},{80,... | collective-permute-start | bytes 589832 | tf_op jit(solution)/shard_map/ppermute | solution.py:527
  21.6 7.5 %collective-permute-start.1 = (f32[3,4,3,2,8,128]{5,4,3,2,1,0:T(8,128)S(1)}, f32[3,4,3,2,8,128]{5,4,3,2,1,0:T(8,128)S(1)}, u32[]{:S(2)}, u32[]{:S(2)}) collective-permute-start(f32[3,4,3,2,8,128]{5,4,3,2,1,0:T(8,128)S(1)} %pad_maximum_fusion), channel_id=1, source_target_pairs={{0,1},{1,2},{2,3},{3,4},{4,5},{5,6},{6,7},{9,8},{10,9},{11,10},{12... | collective-permute-start | bytes 884744 | tf_op jit(solution)/shard_map/ppermute | solution.py:538
  33.2 6.7 %collective-permute-start.3 = (f32[6,3,8,128]{3,2,1,0:T(8,128)S(1)}, f32[6,3,8,128]{3,2,1,0:T(8,128)S(1)}, u32[]{:S(2)}, u32[]{:S(2)}) collective-permute-start(f32[6,3,8,128]{3,2,1,0:T(8,128)S(1)} %get-tuple-element.10), channel_id=1, source_target_pairs={{0,64},{16,80},{32,96},{48,112},{64,128},{72,8},{80,144},{88,24},{... | collective-permute-start | bytes 221192 | tf_op jit(solution)/shard_map/ppermute | solution.py:527
  34.5 5.8 %collective-permute-start.2 = (f32[6,3,8,128]{3,2,1,0:T(8,128)S(1)}, f32[6,3,8,128]{3,2,1,0:T(8,128)S(1)}, u32[]{:S(2)}, u32[]{:S(2)}) collective-permute-start(f32[6,3,8,128]{3,2,1,0:T(8,128)S(1)} %get-tuple-element.10), channel_id=1, source_target_pairs={{0,32},{16,48},{32,64},{40,8},{48,80},{56,24},{64,96},{72,40},{80,... | collective-permute-start | bytes 221192 | tf_op jit(solution)/shard_map/ppermute | solution.py:527
  42.8 8.0 %collective-permute-start.4 = (f32[22,3,8,128]{3,2,1,0:T(8,128)S(1)}, f32[22,3,8,128]{3,2,1,0:T(8,128)S(1)}, u32[]{:S(2)}, u32[]{:S(2)}) collective-permute-start(f32[22,3,8,128]{3,2,1,0:T(8,128)S(1)} %fusion.3.middle), channel_id=1, source_target_pairs={{0,1},{1,2},{2,3},{3,4},{4,5},{5,6},{6,7},{9,8},{10,9},{11,10},{12... | collective-permute-start | bytes 811016 | tf_op jit(solution)/shard_map/ppermute | solution.py:538

commit v4 on v3

--- a/solution.py
+++ b/solution.py
@@ -140,15 +140,6 @@
 ROWS0 = 32
 
 
-def gather_level0(region, own, outer, sides):
-    for part, piece in enumerate((outer.at[0], own, outer.at[1])):
-        for member in range(LAYER):
-            at = part * LAYER + member
-            region[at, :, :, 8:24, :] = piece[member]
-            region[at, :, :, 0:8, :] = sides[0, part, member]
-            region[at, :, :, 24:32, :] = sides[1, part, member]
-
-
 def level0_parts(shape, beta, absorb, parts, start, stop):
     diag, inverse, first, second, third = parts
     half = face(0)
@@ -174,14 +165,21 @@
     return 0.125 * jnp.where(even, take(0) + take(1), take(2) + take(3))
 
 
+KEPT0 = 10
+
+
 def pre0_kernel(
-    own, outer, sides, field_out, tile_out, absorb_out,
-    region, diag, inverse, first, second, third, one, two, tmp,
+    own, outer, kept_out, tile_out, absorb_out,
+    diag, inverse, first, second, third, one, two, tmp,
 ):
-    gather_level0(region, own, outer, sides)
-    source = lambda plane: region[plane // 2, 0, plane % 2]
-    absorb = lambda plane: region[plane // 2, 1, plane % 2]
-    beta = lambda plane: region[plane // 2, 2, plane % 2]
+    def piece(plane, kind):
+        part, member = plane // 8, plane % 8 // 2
+        block = own.at[member] if part == 1 else outer.at[part // 2, member]
+        return block[kind, plane % 2]
+
+    source = lambda plane: piece(plane, 0)
+    absorb = lambda plane: piece(plane, 1)
+    beta = lambda plane: piece(plane, 2)
     shape = Packed(ROWS0, 1, ROWS0, False)
     parts = (diag, inverse, first, second, third)
     level0_parts(shape, beta, absorb, parts, 1, 23)
@@ -190,12 +188,15 @@
         one[plane] = table[0][1] * (inverse[plane] * source(plane))
         two[plane] = jnp.zeros((ROWS0, LANES), jnp.float32)
     ranges = [(1 + order, 23 - order) for order in range(1, SWEEPS)]
-    current, _ = sweep(
+    current, previous = sweep(
         shape, list(enumerate(table))[1:], source, parts, (one, two), ranges, -1, 99
     )
+    for plane in range(4, 20):
+        previous[plane] = source(plane)
     base = 2 * (position() % LAYER) + 4
-    for plane in range(10):
-        field_out[plane] = current[base + plane]
+    for plane in range(KEPT0):
+        for number, kept in enumerate((current, previous) + parts):
+            kept_out[number, plane] = kept[base + plane]
     coarse = Packed(8, 2, 8, False)
     half = face(1)
     betas = [coarse_rows(tmp.at[0], beta(p) + beta(p + 1)) for p in range(4, 20, 2)]
@@ -219,13 +220,23 @@
 ROWS1 = 16
 
 
-def gather_level1(region, middle, sides):
-    row = rows_of(8)
+def gather_level1(region, own, outer):
+    zero = jnp.zeros((4, LANES), jnp.float32)
     for plane in range(DEPTH1):
         for kind in range(3):
-            moved = across(middle[plane, kind], 4)
-            region[kind, plane, 0:8, :] = jnp.where(row < 6, sides[0, plane, kind], moved)
-            region[kind, plane, 8:16, :] = jnp.where(row < 2, moved, sides[1, plane, kind])
+            if 5 <= plane < 17:
+                part, index = divmod(plane - 5, 4)
+                if part == 1:
+                    region[kind, plane] = own[index + 1, kind]
+                else:
+                    at = 6 * index + 2 * kind
+                    region[kind, plane, 0:8, :] = outer[part // 2, at]
+                    region[kind, plane, 8:16, :] = outer[part // 2, at + 1]
+            else:
+                part, index = (0, plane) if plane < 5 else (1, plane - 16)
+                region[kind, plane, 0:4, :] = zero
+                region[kind, plane, 4:12, :] = outer[part, 24 + 3 * index + kind]
+                region[kind, plane, 12:16, :] = zero
 
 
 def level1_parts(shape, region, inverse, first, second, third):
@@ -249,10 +260,10 @@
 
 
 def pre1_kernel(
-    middle, sides, absorb, pay_out, field, region, inverse, first, second, third,
+    own, outer, absorb, pay_out, field, region, inverse, first, second, third,
     two, tmp, tile,
 ):
-    gather_level1(region, middle, sides)
+    gather_level1(region, own, outer)
     shape = Packed(ROWS1, 2, ROWS1, False)
     level1_parts(shape, region, inverse, first, second, third)
     diag = region.at[2]
@@ -280,12 +291,13 @@
             tmp.at[4 + pair], absorb[2 * pair] + absorb[2 * pair + 1], 2
         )
     tile[6:8, :] = jnp.zeros((2, LANES), jnp.float32)
-    whole = tile[...]
+    part = tile[pl.ds(2 * (position() % LAYER), 2), :]
     for slot in range(16):
-        pay_out[slot] = whole
+        pay_out[slot] = part
 
 
 DEPTH2 = 32
+KIND_AT = (0, 2, 1)
 ROWS2 = 8
 
 
@@ -364,8 +376,8 @@
     shape = Packed(ROWS2, 4, ROWS2, True)
     for number in range(3):
         for plane in range(DEPTH2):
-            at = 8 * (plane // 2) + 2 * number + plane % 2
-            rows2[number, plane] = packed[pl.ds(at, 8, stride=128), :]
+            at = 256 * KIND_AT[number] + plane
+            rows2[number, plane] = packed[pl.ds(at, 8, stride=32), :]
 
     source2 = lambda plane: rows2[0, plane]
     beta2 = lambda plane: rows2[1, plane]
@@ -398,11 +410,9 @@
     return current
 
 
-def post1(middle, sides, field, whole, region, parts, one, two, wide, tmp):
+def post1(field, whole, region, parts, one, two, wide, tmp):
     inverse, first, second, third = parts
-    gather_level1(region, middle, sides)
     shape = Packed(ROWS1, 2, ROWS1, False)
-    level1_parts(shape, region, inverse, first, second, third)
     layer = position() // LAYER
     row = column_position() + 6
     zero = jnp.zeros((8, LANES), jnp.float32)
@@ -432,14 +442,11 @@
     return current
 
 
-def post0(pieces, field, coarse, out, region, parts, one, two, tmp):
-    gather_level0(region, *pieces)
+def post0(kept, coarse, out, one, two, tmp):
+    field, source = kept.at[0], kept.at[1]
+    parts = tuple(kept.at[number] for number in range(2, 7))
     member = position() % LAYER
-    source = lambda plane: region[member + plane // 2, 0, plane % 2]
-    absorb = lambda plane: region[member + plane // 2, 1, plane % 2]
-    beta = lambda plane: region[member + plane // 2, 2, plane % 2]
     shape = Packed(ROWS0, 1, ROWS0, False)
-    level0_parts(shape, beta, absorb, parts, 5, 13)
     even = lanes_of(8) % 2 == 0
     for pair in range(5):
         value = coarse[7 + member + pair, 4:12, :]
@@ -448,33 +455,28 @@
         part = tmp.at[pair]
         for offset in range(4):
             part[pl.ds(offset, 8, stride=4), :] = upper_rows if offset < 2 else lower_rows
-        for plane in (2 * pair + 4, 2 * pair + 5):
-            one[plane] = field[plane - 4] + part[...]
+        for plane in (2 * pair, 2 * pair + 1):
+            one[plane] = field[plane] + part[...]
     table = chebyshev_table(SWEEPS)
-    ranges = [(5 + order, 13 - order) for order in range(SWEEPS)]
+    ranges = [(1 + order, KEPT0 - 1 - order) for order in range(SWEEPS)]
     current, _ = sweep(
-        shape, list(enumerate(table)), source, parts, (one, two), ranges, -1, 99
-    )
-    for plane in (8, 9):
-        out[plane - 8] = current[plane][8:24, :]
+        shape, list(enumerate(table)), lambda plane: source[plane], parts, (one, two), ranges,
+        -1, 99,
+    )
+    for plane in (4, 5):
+        out[plane - 4] = current[plane][8:24, :]
 
 
 def finish_kernel(
-    packed, middle, sides1, field1, own, outer, sides0, field0, out,
+    packed, field1, region1, inverse1, first1, second1, third1, kept0, out,
     rows2, diag2, inverse2, first2, second2, third2, one2, two2, tall,
-    region1, inverse1, first1, second1, third1, one1, two1, wide1, tmp1,
-    region0, diag0, inverse0, first0, second0, third0, one0, two0, tmp0,
+    one1, two1, wide1, tmp1, one0, two0, tmp0,
 ):
     parts2 = (diag2, inverse2, first2, second2, third2)
     whole = solve23(packed, rows2, parts2, one2, two2, tall)
     parts1 = (inverse1, first1, second1, third1)
-    coarse = post1(
-        middle, sides1, field1, whole, region1, parts1, one1, two1, wide1, tmp1
-    )
-    parts0 = (diag0, inverse0, first0, second0, third0)
-    post0(
-        (own, outer, sides0), field0, coarse, out, region0, parts0, one0, two0, tmp0
-    )
+    coarse = post1(field1, whole, region1, parts1, one1, two1, wide1, tmp1)
+    post0(kept0, coarse, out, one0, two0, tmp0)
 
 
 def f32(*shape):
@@ -497,27 +499,25 @@
 
 def pre0(*pieces):
     plane = buffer(24, ROWS0, LANES)
-    scratch = [buffer(12, 3, 2, ROWS0, LANES)] + [plane] * 7 + [buffer(4, ROWS0, LANES)]
-    out = (f32(10, ROWS0, LANES), f32(6, 3, 8, LANES), f32(4, 8, LANES))
+    scratch = [plane] * 7 + [buffer(4, ROWS0, LANES)]
+    out = (f32(7, KEPT0, ROWS0, LANES), f32(6, 3, 8, LANES), f32(4, 8, LANES))
     return call(pre0_kernel, out, scratch, "pre0", *pieces)
 
 
 def pre1(*pieces):
-    plane = buffer(DEPTH1, ROWS1, LANES)
-    scratch = [buffer(3, DEPTH1, ROWS1, LANES)] + [plane] * 5
-    scratch += [buffer(6, ROWS1, LANES), buffer(8, LANES)]
-    out = (f32(16, 8, LANES), f32(DEPTH1, ROWS1, LANES))
+    plane = f32(DEPTH1, ROWS1, LANES)
+    scratch = [buffer(DEPTH1, ROWS1, LANES), buffer(6, ROWS1, LANES), buffer(8, LANES)]
+    out = (f32(16, 2, LANES), plane, f32(3, DEPTH1, ROWS1, LANES)) + (plane,) * 4
     return call(pre1_kernel, out, scratch, "pre1", *pieces)
 
 
 def finish(*pieces):
     plane2 = buffer(DEPTH2, ROWS2, LANES)
     plane1 = buffer(DEPTH1, ROWS1, LANES)
-    plane0 = buffer(18, ROWS0, LANES)
+    plane0 = buffer(KEPT0, ROWS0, LANES)
     scratch = [buffer(3, DEPTH2, ROWS2, LANES)] + [plane2] * 7 + [buffer(3, 128, LANES)]
-    scratch += [buffer(3, DEPTH1, ROWS1, LANES)] + [plane1] * 6
-    scratch += [buffer(DEPTH2 + 6, 24, LANES), buffer(8, 32, LANES)]
-    scratch += [buffer(12, 3, 2, ROWS0, LANES)] + [plane0] * 7 + [buffer(5, ROWS0, LANES)]
+    scratch += [plane1] * 2 + [buffer(DEPTH2 + 6, 24, LANES), buffer(8, 32, LANES)]
+    scratch += [plane0] * 2 + [buffer(5, ROWS0, LANES)]
     return call(finish_kernel, f32(2, 16, LANES), scratch, "finish", *pieces)
 
 
@@ -540,11 +540,16 @@
 
 def body(source, absorb, beta):
     members = lax.axis_size("gx")
-    across_y = lax.axis_size("gy")
+    wide = lax.axis_size("gy")
     layers = members // LAYER
     near = [[LAYER * z + c for c in range(LAYER)] for z in range(layers)]
     chips = [[2 * chip, 2 * chip + 1] for chip in range(members // 2)]
     column = [[LAYER * z + c for z in range(layers)] for c in range(LAYER)]
+    cores = [
+        [(LAYER * z + 2 * chip + core) * wide + y for chip in range(2) for y in range(wide)]
+        for z in range(layers)
+        for core in range(2)
+    ]
     first_core = lax.axis_index("gx") % 2 == 0
 
     def both(value):
@@ -552,23 +557,22 @@
 
     local = jnp.stack([source, absorb, beta])
     own = lax.all_gather(local, "gx", axis_index_groups=near)
-    outer = both(layers_apart(own, 1))
-    edges = [jnp.where(first_core, x[..., 8:, :], x[..., :8, :]) for x in (outer[0], own, outer[1])]
-    sides0 = both(columns_apart(jnp.stack(edges)))
-    pieces0 = (own, outer, sides0)
-    field0, tile, absorb1 = pre0(*pieces0)
-
-    tiles = both(jnp.stack([layers_apart(tile, 1), layers_apart(tile, 2)]))
-    middle = jnp.concatenate(
-        [tiles[0, 1, 0:5], tiles[0, 0, 1:5], tile[1:5], tiles[1, 0, 1:5], tiles[1, 1, 1:6]]
-    )
-    pieces1 = (middle, both(columns_apart(middle)))
-    pay, field1 = pre1(*pieces1, absorb1)
+    edges = jnp.where(first_core, own[..., 8:, :], own[..., :8, :])
+    sides = both(columns_apart(edges))
+    layer = jnp.concatenate([sides[0], own, sides[1]], axis=-2)
+    kept0, tile, absorb1 = pre0(layer, both(layers_apart(layer, 1)))
+
+    sides = both(columns_apart(tile))
+    tall = jnp.concatenate([sides[0, ..., 0:6, :], tile[..., 2:6, :], sides[1, ..., 2:8, :]], axis=-2)
+    tiles = [layers_apart(tall[1:5], 1), layers_apart(tall[..., 4:12, :], 2)]
+    tiles = jnp.concatenate([x.reshape(-1, 8, LANES) for x in tiles])
+    pay, *kept1 = pre1(tall, both(tiles), absorb1)
 
     rows = lax.all_to_all(pay, "gx", 0, 0, axis_index_groups=column)
-    rows = jnp.broadcast_to(rows, (across_y,) + rows.shape)
-    packed = lax.all_to_all(rows, "gy", 0, 0).reshape(-1, LANES)
-    return finish(packed, *pieces1, field1, *pieces0, field0)
+    rows = jnp.broadcast_to(rows, (2 * wide,) + rows.shape)
+    rows = lax.all_to_all(rows, ("gx", "gy"), 0, 0, axis_index_groups=cores)
+    packed = both(rows).reshape(-1, LANES)
+    return finish(packed, *kept1, kept0)
 
 
 def solution(mesh):

time: 112 us -> 113 us (level)
  blocking collectives: 68.2 us -> 72.4 us
  waiting for transfers between devices: 22.4 us -> 19.8 us
    all_gather x4 -> x5, blocking collectives: 9.18 us -> 14.6 us  [both(): return lax.all_gather(value, 'gx', axis_index_groups=chips)]
    ppermute x2, waiting for transfers between devices: 12.8 us -> 7.84 us  [columns_apart(): return lax.ppermute(value, ('gx', 'gy'), ways)]
    ppermute x3, waiting for transfers between devices: 9.63 us -> 11.9 us  [layers_apart(): lax.ppermute(value, 'gx', [(i, j) for i, j in ways if 0 <= j < count])]
    all_to_all x1, blocking collectives: 21.1 us -> 19.3 us  [body(): rows = lax.all_to_all(rows, ('gx', 'gy'), 0, 0, axis_index_groups=cores)]
  transfers between devices with their start and end apart: 5 -> 5, of which waited for: 5 -> 4; matrix products, arithmetic and copies ran while one was open for 0% -> 0% of each run, Pallas kernels for 0% -> 0%
where the time goes in v4:
time: 113 us; the launch traced here: 112 us
  blocking collectives  72.4 us (64%)
  waiting for transfers between devices  19.8 us (18%)
  Pallas kernels  12.4 us (11%)
  starting transfers between devices  6.46 us (6%)
    all_to_all x1, blocking collectives, body(): rows = lax.all_to_all(pay, 'gx', 0, 0, axis_index_groups=column)  26.1 us
    all_to_all x1, blocking collectives, body(): rows = lax.all_to_all(rows, ('gx', 'gy'), 0, 0, axis_index_groups=cores)  19.3 us
    all_gather x5, blocking collectives, both(): return lax.all_gather(value, 'gx', axis_index_groups=chips)  14.6 us
    pallas_call x3, Pallas kernels, call(): pl.pallas_call(kernel, out_shape=out, scratch_shapes=scratch, name=name,...  12.4 us
    all_gather x1, blocking collectives, body(): own = lax.all_gather(local, 'gx', axis_index_groups=near)  12.3 us
    ppermute x3, waiting for transfers between devices, layers_apart(): lax.ppermute(value, 'gx', [(i, j) for i, j in ways if 0 <= j < count])  11.9 us
    ppermute x2, waiting for transfers between devices, columns_apart(): return lax.ppermute(value, ('gx', 'gy'), ways)  7.84 us
    ppermute x3, starting transfers between devices, layers_apart(): lax.ppermute(value, 'gx', [(i, j) for i, j in ways if 0 <= j < count])  3.88 us
  transfers between devices with their start and end apart: 5, of which 4 were waited for; matrix products, arithmetic and copies ran while one was open for 0% of the time, Pallas kernels for 0%

profile of v4, /device:TPU:1, one launch (start us, length us, event | category | flops | bytes accessed | tf_op | source)
XLA Modules:
  0.0 112.3 jit_solution(7401185569608626221)
XLA Ops:
  0.0 0.8 pad_maximum_fusion.3
  0.8 12.3 %all-gather = f32[12,2,16,128]{3,2,1,0:T(8,128)S(1)} all-gather(f32[3,2,16,128]{3,2,1,0:T(8,128)S(1)} %pad_maximum_fusion.3), channel_id=2, replica_groups={{0,8,16,24},{32,40,48,56},{64,72,80,88},{96,104,112,120},{128,136,144,1..., dimensions={0}, use_global_device_ids=true | all-gather | bytes 245760 | tf_op jit(solution)/shard_map/all_gather | solution.py:559
  13.1 1.3 %collective-permute-start = (f32[4,3,2,8,128]{4,3,2,1,0:T(8,128)S(1)}, f32[4,3,2,8,128]{4,3,2,1,0:T(8,128)S(1)}, u32[]{:S(2)}, u32[]{:S(2)}) collective-permute-start(f32[4,3,2,8,128]{4,3,2,1,0:T(8,128)S(1)} %slice_select_fusion), channel_id=1, source_target_pairs={{0,1},{1,2},{2,3},{3,4},{4,5},{5,6},{6,7},{9,8},{10,9},{11,10},{12... | collective-permute-start | bytes 294920 | tf_op jit(solution)/shard_map/ppermute | solution.py:538
  14.4 4.1 %collective-permute-done = f32[4,3,2,8,128]{4,3,2,1,0:T(8,128)S(1)} collective-permute-done((f32[4,3,2,8,128]{4,3,2,1,0:T(8,128)S(1)}, f32[4,3,2,8,128]{4,3,2,1,0:T(8,128)S(1)}, u32[]{:S(2)}, u32[]{:S(2)}) %collective-permute-start) | collective-permute-done | bytes 98336 | tf_op jit(solution)/shard_map/ppermute | solution.py:538
  18.4 1.9 %all-gather.1 = f32[8,3,2,8,128]{4,3,2,1,0:T(8,128)S(1)} all-gather(f32[4,3,2,8,128]{4,3,2,1,0:T(8,128)S(1)} %collective-permute-done), channel_id=3, replica_groups={{0,8},{16,24},{32,40},{48,56},{64,72},{80,88},{96,104},{112,120},{128,1..., dimensions={0}, use_global_device_ids=true | all-gather | bytes 294912 | tf_op jit(solution)/shard_map/all_gather | solution.py:556
  20.4 1.3 %collective-permute-start.1 = (f32[4,3,2,32,128]{4,3,2,1,0:T(8,128)S(1)}, f32[4,3,2,32,128]{4,3,2,1,0:T(8,128)S(1)}, u32[]{:S(2)}, u32[]{:S(2)}) collective-permute-start(f32[4,3,2,32,128]{4,3,2,1,0:T(8,128)S(1)} %pad_maximum_fusion.own), channel_id=1, source_target_pairs={{0,32},{16,48},{32,64},{40,8},{48,80},{56,24},{64,96},{72,40},{80,... | collective-permute-start | bytes 1179656 | tf_op jit(solution)/shard_map/ppermute | solution.py:527
  21.7 7.2 %collective-permute-done.1 = f32[4,3,2,32,128]{4,3,2,1,0:T(8,128)S(1)} collective-permute-done((f32[4,3,2,32,128]{4,3,2,1,0:T(8,128)S(1)}, f32[4,3,2,32,128]{4,3,2,1,0:T(8,128)S(1)}, u32[]{:S(2)}, u32[]{:S(2)}) %collective-permute-start.1) | collective-permute-done | bytes 393248 | tf_op jit(solution)/shard_map/ppermute | solution.py:527
  28.9 2.4 %all-gather.2 = f32[8,3,2,32,128]{4,3,2,1,0:T(8,128)S(1)} all-gather(f32[4,3,2,32,128]{4,3,2,1,0:T(8,128)S(1)} %collective-permute-done.1), channel_id=4, replica_groups={{0,8},{16,24},{32,40},{48,56},{64,72},{80,88},{96,104},{112,120},{128,1..., dimensions={0}, use_global_device_ids=true | all-gather | bytes 1179648 | tf_op jit(solution)/shard_map/all_gather | solution.py:556
  31.3 1.8 %pre0.1 = (f32[7,10,32,128]{3,2,1,0:T(8,128)S(1)}, f32[6,3,8,128]{3,2,1,0:T(8,128)S(1)}, f32[4,8,128]{2,1,0:T(8,128)S(1)}) custom-call(f32[4,3,2,32,128]{4,3,2,1,0:T(8,128)S(1)} %pad_maximum_fusion.own, f32[2,4,3,2,32,128]{5,4,3,2,1,0:T(8,128)S(1)} %bitcast.14), custom_call_target="tpu_custom_call" | custom-call | tf_op jit(solution)/shard_map/pre0/pallas_call | solution.py:491
  33.1 1.3 %collective-permute-start.2 = (f32[6,3,8,128]{3,2,1,0:T(8,128)S(1)}, f32[6,3,8,128]{3,2,1,0:T(8,128)S(1)}, u32[]{:S(2)}, u32[]{:S(2)}) collective-permute-start(f32[6,3,8,128]{3,2,1,0:T(8,128)S(1)} %get-tuple-element.15), channel_id=1, source_target_pairs={{0,1},{1,2},{2,3},{3,4},{4,5},{5,6},{6,7},{9,8},{10,9},{11,10},{12... | collective-permute-start | bytes 221192 | tf_op jit(solution)/shard_map/ppermute | solution.py:538
  34.4 3.8 %collective-permute-done.2 = f32[6,3,8,128]{3,2,1,0:T(8,128)S(1)} collective-permute-done((f32[6,3,8,128]{3,2,1,0:T(8,128)S(1)}, f32[6,3,8,128]{3,2,1,0:T(8,128)S(1)}, u32[]{:S(2)}, u32[]{:S(2)}) %collective-permute-start.2) | collective-permute-done | bytes 73760 | tf_op jit(solution)/shard_map/ppermute | solution.py:538
  38.2 1.9 %all-gather.3 = f32[12,3,8,128]{3,2,1,0:T(8,128)S(1)} all-gather(f32[6,3,8,128]{3,2,1,0:T(8,128)S(1)} %collective-permute-done.2), channel_id=5, replica_groups={{0,8},{16,24},{32,40},{48,56},{64,72},{80,88},{96,104},{112,120},{128,1..., dimensions={0}, use_global_device_ids=true | all-gather | bytes 221184 | tf_op jit(solution)/shard_map/all_gather | solution.py:556
  40.2 1.3 %collective-permute-start.3 = (f32[4,3,16,128]{3,2,1,0:T(8,128)S(1)}, f32[4,3,16,128]{3,2,1,0:T(8,128)S(1)}, u32[]{:S(2)}, u32[]{:S(2)}) collective-permute-start(f32[4,3,16,128]{3,2,1,0:T(8,128)S(1)} %slice.44), channel_id=1, source_target_pairs={{0,32},{16,48},{32,64},{40,8},{48,80},{56,24},{64,96},{72,40},{80,... | collective-permute-start | bytes 294920 | tf_op jit(solution)/shard_map/ppermute | solution.py:527
  41.5 1.3 %collective-permute-start.4 = (f32[6,3,8,128]{3,2,1,0:T(8,128)S(1)}, f32[6,3,8,128]{3,2,1,0:T(8,128)S(1)}, u32[]{:S(2)}, u32[]{:S(2)}) collective-permute-start(f32[6,3,8,128]{3,2,1,0:T(8,128)S(1)} %slice.45), channel_id=1, source_target_pairs={{0,64},{16,80},{32,96},{48,112},{64,128},{72,8},{80,144},{88,24},{... | collective-permute-start | bytes 221192 | tf_op jit(solution)/shard_map/ppermute | solution.py:527
  42.8 4.7 %collective-permute-done.4 = f32[6,3,8,128]{3,2,1,0:T(8,128)S(1)} collective-permute-done((f32[6,3,8,128]{3,2,1,0:T(8,128)S(1)}, f32[6,3,8,128]{3,2,1,0:T(8,128)S(1)}, u32[]{:S(2)}, u32[]{:S(2)}) %collective-permute-start.4) | collective-permute-done | bytes 73760 | tf_op jit(solution)/shard_map/ppermute | solution.py:527
  47.5 0.0 collective-permute-done.3
  47.5 3.5 %all-gather.4 = f32[84,8,128]{2,1,0:T(8,128)S(1)} all-gather(f32[42,8,128]{2,1,0:T(8,128)S(1)} %pad_maximum_fusion.1), channel_id=6, replica_groups={{0,8},{16,24},{32,40},{48,56},{64,72},{80,88},{96,104},{112,120},{128,1..., dimensions={0}, use_global_device_ids=true | all-gather | bytes 516096 | tf_op jit(solution)/shard_map/all_gather | solution.py:556
  51.0 1.1 %pre1.1 = (f32[16,2,128]{2,1,0:T(2,128)S(1)}, f32[22,16,128]{2,1,0:T(8,128)S(1)}, f32[3,22,16,128]{3,2,1,0:T(8,128)S(1)}, f32[22,16,128]{2,1,0:T(8,128)S(1)}, f3...) custom-call(f32[6,3,16,128]{3,2,1,0:T(8,128)S(1)} %pad_maximum_fusion.2.own, ...), custom_call_target="tpu_custom_call" | custom-call | tf_op jit(solution)/shard_map/pre1/pallas_call | solution.py:491
  52.1 26.1 %all_to_all.10 = f32[16,2,128]{2,1,0:T(2,128)S(1)} all-to-all(f32[16,2,128]{2,1,0:T(2,128)S(1)} %get-tuple-element.17), channel_id=1, replica_groups={{0,32,64,96,128,160,192,224,256,288,320,352,384,416,448,480},{8,40,72,1..., dimensions={0} | all-to-all | bytes 32768 | tf_op jit(solution)/shard_map/all_to_all | solution.py:571
  78.3 19.3 %all_to_all.11 = f32[16,16,2,128]{3,1,2,0:T(8,128)S(1)} all-to-all(f32[16,16,2,128]{3,1,2,0:T(8,128)S(1)} %broadcast_in_dim.3), channel_id=1, replica_groups={{0,1,2,3,4,5,6,7,16,17,18,19,20,21,22,23},{8,9,10,11,12,13,14,15,24,25,..., dimensions={0} | all-to-all | bytes 524288 | tf_op jit(solution)/shard_map/all_to_all | solution.py:573
  97.6 5.0 %all-gather.5 = f32[32,16,2,128]{3,1,2,0:T(8,128)S(1)} all-gather(f32[16,16,2,128]{3,1,2,0:T(8,128)S(1)} %all_to_all.11), channel_id=7, replica_groups={{0,8},{16,24},{32,40},{48,56},{64,72},{80,88},{96,104},{112,120},{128,1..., dimensions={0}, use_global_device_ids=true | all-gather | bytes 786432 | tf_op jit(solution)/shard_map/all_gather | solution.py:556
  102.6 0.3 copy.5
  102.8 9.5 %finish.1 = f32[2,16,128]{2,1,0:T(8,128)} custom-call(f32[1024,128]{1,0:T(8,128)S(1)} %bitcast.15, f32[22,16,128]{2,1,0:T(8,128)S(1)} %get-tuple-element.18.field1, f32[3,22,16,128]{3,2,1,0:T(8,128)S(1)} %get-tuple-element.19.region1, f32[22,16,128]{2,1,0:T(8,128)S(1)} %get-tuple-element.20.inverse1, f32[22,16,128]{2,1,0:T(8,128)S(1)} %get-tuple-element.21.first1, ...), custom_call_target="tpu_custom_call" | custom-call | tf_op jit(solution)/shard_map/finish/pallas_call | solution.py:491
  (11 shorter events, 0.2 us)
Async XLA Ops:
  13.1 5.4 %collective-permute-start = (f32[4,3,2,8,128]{4,3,2,1,0:T(8,128)S(1)}, f32[4,3,2,8,128]{4,3,2,1,0:T(8,128)S(1)}, u32[]{:S(2)}, u32[]{:S(2)}) collective-permute-start(f32[4,3,2,8,128]{4,3,2,1,0:T(8,128)S(1)} %slice_select_fusion), channel_id=1, source_target_pairs={{0,1},{1,2},{2,3},{3,4},{4,5},{5,6},{6,7},{9,8},{10,9},{11,10},{12... | collective-permute-start | bytes 294920 | tf_op jit(solution)/shard_map/ppermute | solution.py:538
  20.4 8.5 %collective-permute-start.1 = (f32[4,3,2,32,128]{4,3,2,1,0:T(8,128)S(1)}, f32[4,3,2,32,128]{4,3,2,1,0:T(8,128)S(1)}, u32[]{:S(2)}, u32[]{:S(2)}) collective-permute-start(f32[4,3,2,32,128]{4,3,2,1,0:T(8,128)S(1)} %pad_maximum_fusion.own), channel_id=1, source_target_pairs={{0,32},{16,48},{32,64},{40,8},{48,80},{56,24},{64,96},{72,40},{80,... | collective-permute-start | bytes 1179656 | tf_op jit(solution)/shard_map/ppermute | solution.py:527
  33.1 5.1 %collective-permute-start.2 = (f32[6,3,8,128]{3,2,1,0:T(8,128)S(1)}, f32[6,3,8,128]{3,2,1,0:T(8,128)S(1)}, u32[]{:S(2)}, u32[]{:S(2)}) collective-permute-start(f32[6,3,8,128]{3,2,1,0:T(8,128)S(1)} %get-tuple-element.15), channel_id=1, source_target_pairs={{0,1},{1,2},{2,3},{3,4},{4,5},{5,6},{6,7},{9,8},{10,9},{11,10},{12... | collective-permute-start | bytes 221192 | tf_op jit(solution)/shard_map/ppermute | solution.py:538
  40.2 7.3 %collective-permute-start.3 = (f32[4,3,16,128]{3,2,1,0:T(8,128)S(1)}, f32[4,3,16,128]{3,2,1,0:T(8,128)S(1)}, u32[]{:S(2)}, u32[]{:S(2)}) collective-permute-start(f32[4,3,16,128]{3,2,1,0:T(8,128)S(1)} %slice.44), channel_id=1, source_target_pairs={{0,32},{16,48},{32,64},{40,8},{48,80},{56,24},{64,96},{72,40},{80,... | collective-permute-start | bytes 294920 | tf_op jit(solution)/shard_map/ppermute | solution.py:527
  41.5 6.0 %collective-permute-start.4 = (f32[6,3,8,128]{3,2,1,0:T(8,128)S(1)}, f32[6,3,8,128]{3,2,1,0:T(8,128)S(1)}, u32[]{:S(2)}, u32[]{:S(2)}) collective-permute-start(f32[6,3,8,128]{3,2,1,0:T(8,128)S(1)} %slice.45), channel_id=1, source_target_pairs={{0,64},{16,80},{32,96},{48,112},{64,128},{72,8},{80,144},{88,24},{... | collective-permute-start | bytes 221192 | tf_op jit(solution)/shard_map/ppermute | solution.py:527

commit v5 on v4

v5 whole, which is shorter than its diff:
```python
import jax
import jax.numpy as jnp
from jax import lax
from jax.experimental import pallas as pl
from jax.experimental.pallas import tpu as pltpu
from jax.sharding import PartitionSpec as P

SWEEPS = 4
BOTTOM = 8
LANES = 128
VMEM = 24 * 1024 * 1024

LAYER = 4
PACK = (1, 2, 4, 8)


def face(level):
    return 0.5 * 0.25**level


def chebyshev_table(count):
    centre = 1.125
    half_width = 0.875
    ratio = centre / half_width
    factor = 1.0 / ratio
    table = [(0.0, 1.0 / centre)]
    for order in range(1, count):
        fresh_factor = 1.0 / (2.0 * ratio - factor)
        table.append((fresh_factor * factor, 2.0 * fresh_factor / half_width))
        factor = fresh_factor
    return table


def position():
    return lax.axis_index("gx")


def column_position():
    return lax.axis_index("gy")


def lanes_of(rows):
    return lax.broadcasted_iota(jnp.int32, (rows, LANES), 1)


def rows_of(rows):
    return lax.broadcasted_iota(jnp.int32, (rows, LANES), 0)


def along(value, steps):
    return pltpu.roll(value, (-steps) % LANES, value.ndim - 1)


def across(value, steps):
    rows = value.shape[-2]
    return pltpu.roll(value, (-steps) % rows, value.ndim - 2)


class Packed:
    def __init__(self, pack, period, whole):
        self.pack = pack
        self.period = period
        self.whole = whole
        self.kept = {}

    def masks(self, value):
        if value.shape not in self.kept:
            pack, dims = self.pack, value.ndim
            lane = lax.broadcasted_iota(jnp.int32, value.shape, dims - 1)
            row = lax.broadcasted_iota(jnp.int32, value.shape, dims - 2) & (self.period - 1)
            inner = lane & (pack - 1)
            self.kept[value.shape] = dict(
                up=inner < pack - 1,
                down=inner > 0,
                third_last=lane >= LANES - pack,
                third_first=lane < pack,
                second_last=(row == self.period - 1) & (inner == pack - 1),
                second_first=(row == 0) & (inner == 0),
            )
        return self.kept[value.shape]

    def second_up(self, value):
        if self.pack == 1:
            return across(value, 1)
        mask = self.masks(value)["up"]
        return jnp.where(mask, along(value, 1), across(along(value, 1 - self.pack), 1))

    def second_down(self, value):
        if self.pack == 1:
            return across(value, -1)
        mask = self.masks(value)["down"]
        return jnp.where(mask, along(value, -1), across(along(value, self.pack - 1), -1))

    def faces(self, beta, half):
        mask = self.masks(beta)
        up = self.second_up(beta)
        if self.whole:
            up = jnp.where(mask["second_last"], 0.0, up)
        second = half * (beta + up)
        down = self.second_down(beta)
        if self.whole:
            down = jnp.where(mask["second_first"], 0.0, down)
        share = half * (beta + down) + second
        if self.whole:
            second = jnp.where(mask["second_last"], 0.0, second)
        third_up = jnp.where(mask["third_last"], 0.0, along(beta, self.pack))
        third = half * (beta + third_up)
        third_down = jnp.where(mask["third_first"], 0.0, along(beta, -self.pack))
        share = share + half * (beta + third_down) + third
        return second, jnp.where(mask["third_last"], 0.0, third), share

    def coupled(self, value, second, third):
        total = second * self.second_up(value) + self.second_down(second * value)
        total = total + third * along(value, self.pack)
        return total + along(third * value, -self.pack)


def pair_sum(value, width):
    low = (lax.broadcasted_iota(jnp.int32, value.shape, value.ndim - 1) & width) == 0
    return value + jnp.where(low, along(value, width), along(value, -width))


def residual(shape, source, parts, field, start, stop):
    diag, _, first, second, third = parts
    here = field[start:stop]
    total = source(start, stop) - diag[start:stop] * here
    total = total + first[start:stop] * field[start + 1 : stop + 1]
    total = total + first[start - 1 : stop - 1] * field[start - 1 : stop - 1]
    return total + shape.coupled(here, second[start:stop], third[start:stop])


def sweep(shape, orders, source, parts, buffers, ranges, chunk):
    inverse = parts[1]
    current, previous = buffers
    for (order, (carry, push)), (low, high) in zip(orders, ranges):
        for start in range(low, high, chunk):
            stop = min(start + chunk, high)
            rest = residual(shape, source, parts, current, start, stop)
            here = current[start:stop]
            fresh = here + push * (inverse[start:stop] * rest)
            if order > 0:
                fresh = fresh + carry * (here - previous[start:stop])
            previous[start:stop] = fresh
        current, previous = previous, current
    return current, previous


def begin(table, inverse, source, buffers, low, high, chunk):
    for start in range(low, high, chunk):
        stop = min(start + chunk, high)
        fresh = table[0][1] * (inverse[start:stop] * source(start, stop))
        buffers[0][start:stop] = fresh
        buffers[1][start:stop] = jnp.zeros_like(fresh)


ROWS0 = 32


CHUNK0 = 2


def level0_parts(shape, beta, absorb, parts, low, high):
    diag, inverse, first, second, third = parts
    half = face(0)
    first[low - 1 : low] = half * (beta(low - 1, low) + beta(low, low + 1))
    for start in range(low, high, CHUNK0):
        stop = min(start + CHUNK0, high)
        here = beta(start, stop)
        first[start:stop] = half * (here + beta(start + 1, stop + 1))
        lower = half * (beta(start - 1, stop - 1) + here)
        second[start:stop], third[start:stop], share = shape.faces(here, half)
        total = absorb(start, stop) + lower + first[start:stop] + share
        diag[start:stop] = total
        inverse[start:stop] = jnp.where(here > 0.0, 1.0 / total, 0.0)


def pairs(value):
    return jnp.stack([value[at] + value[at + 1] for at in range(0, value.shape[0], 2)])


def coarse_rows(ref, value):
    count = value.shape[0]
    ref[0:count] = pair_sum(value, 1)
    take = lambda offset: jnp.stack([ref[at, pl.ds(offset, 8, stride=4), :] for at in range(count)])
    even = (lax.broadcasted_iota(jnp.int32, (count, 8, LANES), 2) & 1) == 0
    return 0.125 * jnp.where(even, take(0) + take(1), take(2) + take(3))


KEPT0 = 10


def pre0_kernel(
    own, outer, kept_out, tile_out, absorb_out,
    diag, inverse, first, second, third, one, two, tmp,
):
    def piece(kind):
        def planes(start, stop):
            found = []
            for plane in range(start, stop):
                part, member = plane // 8, plane % 8 // 2
                block = own.at[member] if part == 1 else outer.at[part // 2, member]
                found.append(block[kind, plane % 2])
            return jnp.stack(found)

        return planes

    source, absorb, beta = piece(0), piece(1), piece(2)
    shape = Packed(1, ROWS0, False)
    parts = (diag, inverse, first, second, third)
    level0_parts(shape, beta, absorb, parts, 1, 23)
    table = chebyshev_table(SWEEPS)
    begin(table, inverse, source, (one, two), 1, 23, CHUNK0)
    ranges = [(1 + order, 23 - order) for order in range(1, SWEEPS)]
    current, previous = sweep(
        shape, list(enumerate(table))[1:], source, parts, (one, two), ranges, CHUNK0
    )
    previous[4:20] = source(4, 20)
    base = 2 * (position() % LAYER) + 4
    for plane in range(KEPT0):
        for number, kept in enumerate((current, previous) + parts):
            kept_out[number, plane] = kept[base + plane]
    coarse = Packed(2, 8, False)
    half = face(1)
    betas = coarse_rows(tmp.at[0:8], pairs(beta(4, 20)))
    wide = coarse_rows(tmp.at[8:14], pairs(absorb(6, 18)))
    rest = [residual(shape, source, parts, current, p, p + 2) for p in range(6, 18, 2)]
    tile_out[:, 0] = coarse_rows(tmp.at[14:20], jnp.stack([x[0] + x[1] for x in rest]))
    here = betas[1:7]
    _, _, share = coarse.faces(here, half)
    tile_out[:, 1] = here
    tile_out[:, 2] = wide + half * (here + betas[0:6]) + half * (here + betas[2:8]) + share
    absorb_out[...] = wide[1:5]


DEPTH1 = 22
ROWS1 = 16


def gather_level1(region, own, outer):
    zero = jnp.zeros((4, LANES), jnp.float32)
    for plane in range(DEPTH1):
        for kind in range(3):
            if 5 <= plane < 17:
                part, index = divmod(plane - 5, 4)
                if part == 1:
                    region[kind, plane] = own[index + 1, kind]
                else:
                    at = 6 * index + 2 * kind
                    region[kind, plane, 0:8, :] = outer[part // 2, at]
                    region[kind, plane, 8:16, :] = outer[part // 2, at + 1]
            else:
                part, index = (0, plane) if plane < 5 else (1, plane - 16)
                region[kind, plane, 0:4, :] = zero
                region[kind, plane, 4:12, :] = outer[part, 24 + 3 * index + kind]
                region[kind, plane, 12:16, :] = zero


CHUNK1 = 4


def level1_parts(shape, region, inverse, first, second, third):
    half = face(1)
    beta = region.at[1]
    for start in range(0, DEPTH1, CHUNK1):
        stop = min(start + CHUNK1, DEPTH1)
        here = beta[start:stop]
        second[start:stop], third[start:stop], _ = shape.faces(here, half)
        inverse[start:stop] = jnp.where(here > 0.0, 1.0 / region[2, start:stop], 0.0)
        stop = min(stop, DEPTH1 - 1)
        first[start:stop] = half * (beta[start:stop] + beta[start + 1 : stop + 1])


def coarser_rows(ref, value, start):
    ref[...] = pair_sum(pair_sum(value, 1), 2)
    inner = lanes_of(1) & 3
    rows = []
    for at in range(value.shape[0]):
        row = ref[at, start : start + 1, :]
        for offset in range(1, 4):
            row = jnp.where(inner == offset, ref[at, start + offset : start + offset + 1, :], row)
        rows.append(0.125 * row)
    return rows


def pre1_kernel(
    own, outer, absorb, pay_out, field, region, inverse, first, second, third,
    two, tmp, small, tile,
):
    gather_level1(region, own, outer)
    shape = Packed(2, ROWS1, False)
    level1_parts(shape, region, inverse, first, second, third)
    source = lambda start, stop: region[0, start:stop]
    parts = (region.at[2], inverse, first, second, third)
    table = chebyshev_table(SWEEPS)
    begin(table, inverse, source, (two, field), 0, DEPTH1, CHUNK1)
    ranges = [(order, DEPTH1 - order) for order in range(1, SWEEPS)]
    current, _ = sweep(
        shape, list(enumerate(table))[1:], source, parts, (two, field), ranges, CHUNK1
    )
    rest = residual(shape, source, parts, current, 9, 13)
    rows = coarser_rows(tmp, jnp.concatenate([pairs(rest), pairs(region[1, 9:13])]), 6)
    rows += coarser_rows(small, pairs(absorb[...]), 2)
    for at in range(6):
        tile[at : at + 1, :] = rows[at]
    tile[6:8, :] = jnp.zeros((2, LANES), jnp.float32)
    kind = 2 * (position() % LAYER)
    for side in range(2):
        part = tile[pl.ds(kind + side, 1), :]
        pay_out[:, side * LANES : (side + 1) * LANES] = jnp.broadcast_to(part, (16, LANES))


DEPTH2 = 32
KIND_AT = (0, 2, 1)
ROWS2 = 8


CHUNK2 = 4


def level2_parts(shape, beta, absorb, parts):
    diag, inverse, first, second, third = parts
    half = face(2)
    first[0:1] = jnp.zeros((1, ROWS2, LANES), jnp.float32)
    for start in range(1, DEPTH2 + 1, CHUNK2):
        stop = start + CHUNK2
        here = beta[start:stop]
        upper = half * (here + beta[start + 1 : stop + 1])
        lower = half * (here + beta[start - 1 : stop - 1])
        second[start:stop], third[start:stop], share = shape.faces(here, half)
        total = absorb[start:stop] + lower + upper + share
        first[start:stop] = upper
        diag[start:stop] = total
        inverse[start:stop] = 1.0 / total


def bottom_rows(ref, planes):
    value = planes(1, DEPTH2 + 1)
    value = jnp.concatenate([value[at] + value[at + 1] for at in range(0, DEPTH2, 2)])
    ref[...] = pair_sum(pair_sum(value, 1), 4)
    inner = lanes_of(32) & 7
    total = None
    for offset in range(4):
        value = jnp.concatenate(
            [ref[pl.ds(32 * block + offset, 8, stride=4), :] for block in range(4)]
        )
        moved = along(value, 1 if offset % 2 == 0 else -1)
        same = 2 * offset + offset % 2
        value = jnp.where(inner == same, value, moved)
        total = value if total is None else jnp.where(inner >> 1 == offset, value, total)
    return 0.125 * total


def bottom_solve(source, absorb, beta):
    shape = Packed(8, 2, True)
    half = face(3)
    row = rows_of(32)
    last, initial = row >= 30, row < 2
    up = jnp.where(last, 0.0, across(beta, 2))
    down = jnp.where(initial, 0.0, across(beta, -2))
    second, third, share = shape.faces(beta, half)
    upper = half * (beta + up)
    diag = absorb + half * (beta + down) + upper + share
    first = jnp.where(last, 0.0, upper)
    inverse = 1.0 / diag
    table = chebyshev_table(BOTTOM)
    current = table[0][1] * (inverse * source)
    previous = jnp.zeros_like(current)
    for carry, push in table[1:]:
        rest = source - diag * current + first * across(current, 2) + across(first * current, -2)
        rest = rest + shape.coupled(current, second, third)
        fresh = current + carry * (current - previous) + push * (inverse * rest)
        current, previous = fresh, current
    return current


def bottom_prolong(ref, value):
    inner = lanes_of(32) & 7
    part = inner & 3
    back1, back2 = along(value, -1), along(value, -2)
    fore1, fore2 = along(value, 1), along(value, 2)
    low = jnp.where(part == 0, value, jnp.where(part == 3, back2, back1))
    high = jnp.where(part == 3, value, jnp.where(part == 0, fore2, fore1))
    left = inner < 4
    for offset in range(4):
        base = low if offset % 2 == 0 else high
        if offset < 2:
            moved = jnp.where(left, base, along(base, -4))
        else:
            moved = jnp.where(left, along(base, 4), base)
        for block in range(4):
            ref[pl.ds(32 * block + offset, 8, stride=4), :] = moved[8 * block : 8 * block + 8]


def solve23(packed, halves, rows2, parts2, one2, two2, tall):
    shape = Packed(4, ROWS2, True)
    zero = jnp.zeros((ROWS2, LANES), jnp.float32)
    for side in range(2):
        halves[side] = packed[:, side * LANES : (side + 1) * LANES]
    for number in range(3):
        for plane in range(DEPTH2):
            at = 128 * KIND_AT[number] + plane // 2
            rows2[number, plane + 1] = halves[plane % 2, pl.ds(at, 8, stride=16), :]
    for ref in (rows2.at[1], one2, two2):
        ref[0] = zero
        ref[DEPTH2 + 1] = zero

    source2 = lambda start, stop: rows2[0, start:stop]
    level2_parts(shape, rows2.at[1], rows2.at[2], parts2)
    table = chebyshev_table(SWEEPS)
    begin(table, parts2[1], source2, (one2, two2), 1, DEPTH2 + 1, CHUNK2)
    everywhere = [(1, DEPTH2 + 1)] * SWEEPS
    current, previous = sweep(
        shape, list(enumerate(table))[1:], source2, parts2, (one2, two2), everywhere, CHUNK2
    )
    source3 = bottom_rows(
        tall.at[0], lambda start, stop: residual(shape, source2, parts2, current, start, stop)
    )
    absorb3 = bottom_rows(tall.at[1], lambda start, stop: rows2[2, start:stop])
    beta3 = bottom_rows(tall.at[2], lambda start, stop: rows2[1, start:stop])
    bottom_prolong(tall.at[0], bottom_solve(source3, absorb3, beta3))
    for plane in range(DEPTH2):
        pair = plane // 2
        current[plane + 1] = current[plane + 1] + tall[0, 8 * pair : 8 * pair + 8, :]
    current, previous = sweep(
        shape, list(enumerate(table)), source2, parts2, (current, previous), everywhere, CHUNK2
    )
    return current


def post1(field, whole, region, parts, one, two, wide, tmp):
    inverse, first, second, third = parts
    shape = Packed(2, ROWS1, False)
    layer = position() // LAYER
    row = column_position() + 6
    zero = jnp.zeros((8, LANES), jnp.float32)
    for plane in range(DEPTH2 + 6):
        wide[plane, 0:8, :] = zero
        wide[plane, 16:24, :] = zero
        inside = 3 <= plane < DEPTH2 + 3
        wide[plane, 8:16, :] = whole[plane - 2] if inside else zero
    value = jnp.stack([wide[2 * layer + pair, pl.ds(row, 8), :] for pair in range(8)])
    inner = lax.broadcasted_iota(jnp.int32, value.shape, 2) & 3
    moved = {steps: along(value, steps) for steps in range(-3, 4) if steps}
    moved[0] = value
    for offset in range(4):
        picked = moved[offset]
        for lane in range(1, 4):
            picked = jnp.where(inner == lane, moved[offset - lane], picked)
        for pair in range(8):
            tmp[pair, pl.ds(offset, 8, stride=4), :] = picked[pair]
    for plane in range(3, 19):
        one[plane] = field[plane] + tmp[(plane - 3) // 2, 2:18, :]
    table = chebyshev_table(SWEEPS)
    ranges = [(3 + order, 19 - order) for order in range(1, SWEEPS + 1)]
    current, _ = sweep(
        shape, list(enumerate(table)), lambda start, stop: region[0, start:stop],
        (region.at[2], inverse, first, second, third), (one, two), ranges, CHUNK1,
    )
    return current


def post0(kept, coarse, out, one, two, tmp):
    field, source = kept.at[0], kept.at[1]
    parts = tuple(kept.at[number] for number in range(2, 7))
    member = position() % LAYER
    shape = Packed(1, ROWS0, False)
    value = jnp.stack([coarse[7 + member + pair, 4:12, :] for pair in range(5)])
    even = (lax.broadcasted_iota(jnp.int32, value.shape, 2) & 1) == 0
    upper_rows = jnp.where(even, value, along(value, -1))
    lower_rows = jnp.where(even, along(value, 1), value)
    for pair in range(5):
        for offset in range(4):
            rows = upper_rows if offset < 2 else lower_rows
            tmp[pair, pl.ds(offset, 8, stride=4), :] = rows[pair]
    for plane in range(KEPT0):
        one[plane] = field[plane] + tmp[plane // 2]
    table = chebyshev_table(SWEEPS)
    ranges = [(1 + order, KEPT0 - 1 - order) for order in range(SWEEPS)]
    current, _ = sweep(
        shape, list(enumerate(table)), lambda start, stop: source[start:stop], parts,
        (one, two), ranges, CHUNK0,
    )
    for plane in (4, 5):
        out[plane - 4] = current[plane][8:24, :]


def finish_kernel(
    packed, field1, region1, inverse1, first1, second1, third1, kept0, out,
    halves, rows2, diag2, inverse2, first2, second2, third2, one2, two2, tall,
    one1, two1, wide1, tmp1, one0, two0, tmp0,
):
    parts2 = (diag2, inverse2, first2, second2, third2)
    whole = solve23(packed, halves, rows2, parts2, one2, two2, tall)
    parts1 = (inverse1, first1, second1, third1)
    coarse = post1(field1, whole, region1, parts1, one1, two1, wide1, tmp1)
    post0(kept0, coarse, out, one0, two0, tmp0)


def f32(*shape):
    return jax.ShapeDtypeStruct(shape, jnp.float32)


def buffer(*shape):
    return pltpu.VMEM(shape, jnp.float32)


def call(kernel, out, scratch, name, *operands):
    return pl.pallas_call(
        kernel,
        out_shape=out,
        scratch_shapes=scratch,
        name=name,
        compiler_params=pltpu.CompilerParams(vmem_limit_bytes=VMEM),
    )(*operands)


def pre0(*pieces):
    plane = buffer(24, ROWS0, LANES)
    scratch = [plane] * 7 + [buffer(20, ROWS0, LANES)]
    out = (f32(7, KEPT0, ROWS0, LANES), f32(6, 3, 8, LANES), f32(4, 8, LANES))
    return call(pre0_kernel, out, scratch, "pre0", *pieces)


def pre1(*pieces):
    plane = f32(DEPTH1, ROWS1, LANES)
    scratch = [buffer(DEPTH1, ROWS1, LANES), buffer(4, ROWS1, LANES), buffer(2, 8, LANES)]
    scratch += [buffer(8, LANES)]
    out = (f32(16, 2 * LANES), plane, f32(3, DEPTH1, ROWS1, LANES)) + (plane,) * 4
    return call(pre1_kernel, out, scratch, "pre1", *pieces)


def finish(*pieces):
    plane2 = buffer(DEPTH2 + 2, ROWS2, LANES)
    plane1 = buffer(DEPTH1, ROWS1, LANES)
    plane0 = buffer(KEPT0, ROWS0, LANES)
    scratch = [buffer(2, 512, LANES), buffer(3, DEPTH2 + 2, ROWS2, LANES)] + [plane2] * 7 + [buffer(3, 128, LANES)]
    scratch += [plane1] * 2 + [buffer(DEPTH2 + 6, 24, LANES), buffer(8, 32, LANES)]
    scratch += [plane0] * 2 + [buffer(5, ROWS0, LANES)]
    return call(finish_kernel, f32(2, 16, LANES), scratch, "finish", *pieces)


def layers_apart(value, steps):
    count = lax.axis_size("gx")
    ways = [(i, i + (LAYER * steps if i % 2 == 0 else -LAYER * steps)) for i in range(count)]
    return lax.ppermute(value, "gx", [(i, j) for i, j in ways if 0 <= j < count])


def columns_apart(value):
    count, wide = lax.axis_size("gx"), lax.axis_size("gy")
    ways = [
        (i * wide + j, i * wide + j + (1 if i % 2 == 0 else -1))
        for i in range(count)
        for j in range(wide)
        if 0 <= j + (1 if i % 2 == 0 else -1) < wide
    ]
    return lax.ppermute(value, ("gx", "gy"), ways)


def body(source, absorb, beta):
    members = lax.axis_size("gx")
    wide = lax.axis_size("gy")
    layers = members // LAYER
    near = [[LAYER * z + c for c in range(LAYER)] for z in range(layers)]
    chips = [[2 * chip, 2 * chip + 1] for chip in range(members // 2)]
    column = [[LAYER * z + c for z in range(layers)] for c in range(LAYER)]
    cores = [
        [(LAYER * z + 2 * chip + core) * wide + y for chip in range(2) for y in range(wide)]
        for z in range(layers)
        for core in range(2)
    ]
    first_core = lax.axis_index("gx") % 2 == 0

    def both(value):
        return lax.all_gather(value, "gx", axis_index_groups=chips)

    local = jnp.stack([source, absorb, beta])
    own = lax.all_gather(local, "gx", axis_index_groups=near)
    edges = jnp.where(first_core, own[..., 8:, :], own[..., :8, :])
    sides = both(columns_apart(edges))
    layer = jnp.concatenate([sides[0], own, sides[1]], axis=-2)
    kept0, tile, absorb1 = pre0(layer, both(layers_apart(layer, 1)))

    sides = both(columns_apart(tile))
    tall = jnp.concatenate([sides[0, ..., 0:6, :], tile[..., 2:6, :], sides[1, ..., 2:8, :]], axis=-2)
    tiles = [layers_apart(tall[1:5], 1), layers_apart(tall[..., 4:12, :], 2)]
    tiles = jnp.concatenate([x.reshape(-1, 8, LANES) for x in tiles])
    pay, *kept1 = pre1(tall, both(tiles), absorb1)

    rows = lax.all_to_all(pay, "gx", 0, 0, axis_index_groups=column)
    rows = jnp.broadcast_to(rows, (2 * wide,) + rows.shape)
    rows = lax.all_to_all(rows, ("gx", "gy"), 0, 0, axis_index_groups=cores)
    packed = both(rows).reshape(-1, 2 * LANES)
    return finish(packed, *kept1, kept0)


def solution(mesh):
    placed = (P("gx", "gy", None), P("gx", "gy", None), P("gx", "gy", None))
    return jax.shard_map(
        body, mesh=mesh, in_specs=placed, out_specs=P("gx", "gy", None), check_vma=False
    )
```

time: 113 us -> 108 us (0.956)
  Pallas kernels: 12.4 us -> 8.25 us
    pallas_call x3, Pallas kernels: 12.4 us -> 8.25 us  [call(): pl.pallas_call(kernel, out_shape=out, scratch_shapes=scratch, name=name,...]
where the time goes in v5:
time: 108 us
  blocking collectives  72.4 us (67%)
  waiting for transfers between devices  19.8 us (18%)
  Pallas kernels  8.25 us (8%)
  starting transfers between devices  6.46 us (6%)
    all_to_all x1, blocking collectives, body(): rows = lax.all_to_all(pay, 'gx', 0, 0, axis_index_groups=column)  26.1 us
    all_to_all x1, blocking collectives, body(): rows = lax.all_to_all(rows, ('gx', 'gy'), 0, 0, axis_index_groups=cores)  19.3 us
    all_gather x5, blocking collectives, both(): return lax.all_gather(value, 'gx', axis_index_groups=chips)  14.6 us
    all_gather x1, blocking collectives, body(): own = lax.all_gather(local, 'gx', axis_index_groups=near)  12.3 us
    ppermute x3, waiting for transfers between devices, layers_apart(): lax.ppermute(value, 'gx', [(i, j) for i, j in ways if 0 <= j < count])  11.9 us
    pallas_call x3, Pallas kernels, call(): pl.pallas_call(kernel, out_shape=out, scratch_shapes=scratch, name=name,...  8.25 us
    ppermute x2, waiting for transfers between devices, columns_apart(): return lax.ppermute(value, ('gx', 'gy'), ways)  7.84 us
    ppermute x3, starting transfers between devices, layers_apart(): lax.ppermute(value, 'gx', [(i, j) for i, j in ways if 0 <= j < count])  3.88 us
  transfers between devices with their start and end apart: 5, of which 4 were waited for; matrix products, arithmetic and copies ran while one was open for 0% of the time, Pallas kernels for 0%

profile of v5, /device:TPU:1, one launch (start us, length us, event | category | flops | bytes accessed | tf_op | source)
XLA Modules:
  0.0 107.9 jit_solution(7786030714879155668)
XLA Ops:
  0.0 0.8 pad_maximum_fusion.3
  0.8 12.3 %all-gather = f32[12,2,16,128]{3,2,1,0:T(8,128)S(1)} all-gather(f32[3,2,16,128]{3,2,1,0:T(8,128)S(1)} %pad_maximum_fusion.3), channel_id=2, replica_groups={{0,8,16,24},{32,40,48,56},{64,72,80,88},{96,104,112,120},{128,136,144,1..., dimensions={0}, use_global_device_ids=true | all-gather | bytes 245760 | tf_op jit(solution)/shard_map/all_gather | solution.py:577
  13.1 1.3 %collective-permute-start = (f32[4,3,2,8,128]{4,3,2,1,0:T(8,128)S(1)}, f32[4,3,2,8,128]{4,3,2,1,0:T(8,128)S(1)}, u32[]{:S(2)}, u32[]{:S(2)}) collective-permute-start(f32[4,3,2,8,128]{4,3,2,1,0:T(8,128)S(1)} %slice_select_fusion), channel_id=1, source_target_pairs={{0,1},{1,2},{2,3},{3,4},{4,5},{5,6},{6,7},{9,8},{10,9},{11,10},{12... | collective-permute-start | bytes 294920 | tf_op jit(solution)/shard_map/ppermute | solution.py:556
  14.4 4.1 %collective-permute-done = f32[4,3,2,8,128]{4,3,2,1,0:T(8,128)S(1)} collective-permute-done((f32[4,3,2,8,128]{4,3,2,1,0:T(8,128)S(1)}, f32[4,3,2,8,128]{4,3,2,1,0:T(8,128)S(1)}, u32[]{:S(2)}, u32[]{:S(2)}) %collective-permute-start) | collective-permute-done | bytes 98336 | tf_op jit(solution)/shard_map/ppermute | solution.py:556
  18.4 1.9 %all-gather.1 = f32[8,3,2,8,128]{4,3,2,1,0:T(8,128)S(1)} all-gather(f32[4,3,2,8,128]{4,3,2,1,0:T(8,128)S(1)} %collective-permute-done), channel_id=3, replica_groups={{0,8},{16,24},{32,40},{48,56},{64,72},{80,88},{96,104},{112,120},{128,1..., dimensions={0}, use_global_device_ids=true | all-gather | bytes 294912 | tf_op jit(solution)/shard_map/all_gather | solution.py:574
  20.4 1.3 %collective-permute-start.1 = (f32[4,3,2,32,128]{4,3,2,1,0:T(8,128)S(1)}, f32[4,3,2,32,128]{4,3,2,1,0:T(8,128)S(1)}, u32[]{:S(2)}, u32[]{:S(2)}) collective-permute-start(f32[4,3,2,32,128]{4,3,2,1,0:T(8,128)S(1)} %pad_maximum_fusion.own), channel_id=1, source_target_pairs={{0,32},{16,48},{32,64},{40,8},{48,80},{56,24},{64,96},{72,40},{80,... | collective-permute-start | bytes 1179656 | tf_op jit(solution)/shard_map/ppermute | solution.py:545
  21.7 7.2 %collective-permute-done.1 = f32[4,3,2,32,128]{4,3,2,1,0:T(8,128)S(1)} collective-permute-done((f32[4,3,2,32,128]{4,3,2,1,0:T(8,128)S(1)}, f32[4,3,2,32,128]{4,3,2,1,0:T(8,128)S(1)}, u32[]{:S(2)}, u32[]{:S(2)}) %collective-permute-start.1) | collective-permute-done | bytes 393248 | tf_op jit(solution)/shard_map/ppermute | solution.py:545
  28.9 2.4 %all-gather.2 = f32[8,3,2,32,128]{4,3,2,1,0:T(8,128)S(1)} all-gather(f32[4,3,2,32,128]{4,3,2,1,0:T(8,128)S(1)} %collective-permute-done.1), channel_id=4, replica_groups={{0,8},{16,24},{32,40},{48,56},{64,72},{80,88},{96,104},{112,120},{128,1..., dimensions={0}, use_global_device_ids=true | all-gather | bytes 1179648 | tf_op jit(solution)/shard_map/all_gather | solution.py:574
  31.3 1.6 %pre0.1 = (f32[7,10,32,128]{3,2,1,0:T(8,128)S(1)}, f32[6,3,8,128]{3,2,1,0:T(8,128)S(1)}, f32[4,8,128]{2,1,0:T(8,128)S(1)}) custom-call(f32[4,3,2,32,128]{4,3,2,1,0:T(8,128)S(1)} %pad_maximum_fusion.own, f32[2,4,3,2,32,128]{5,4,3,2,1,0:T(8,128)S(1)} %bitcast.18), custom_call_target="tpu_custom_call" | custom-call | tf_op jit(solution)/shard_map/pre0/pallas_call | solution.py:508
  32.9 1.3 %collective-permute-start.2 = (f32[6,3,8,128]{3,2,1,0:T(8,128)S(1)}, f32[6,3,8,128]{3,2,1,0:T(8,128)S(1)}, u32[]{:S(2)}, u32[]{:S(2)}) collective-permute-start(f32[6,3,8,128]{3,2,1,0:T(8,128)S(1)} %get-tuple-element.15), channel_id=1, source_target_pairs={{0,1},{1,2},{2,3},{3,4},{4,5},{5,6},{6,7},{9,8},{10,9},{11,10},{12... | collective-permute-start | bytes 221192 | tf_op jit(solution)/shard_map/ppermute | solution.py:556
  34.2 3.8 %collective-permute-done.2 = f32[6,3,8,128]{3,2,1,0:T(8,128)S(1)} collective-permute-done((f32[6,3,8,128]{3,2,1,0:T(8,128)S(1)}, f32[6,3,8,128]{3,2,1,0:T(8,128)S(1)}, u32[]{:S(2)}, u32[]{:S(2)}) %collective-permute-start.2) | collective-permute-done | bytes 73760 | tf_op jit(solution)/shard_map/ppermute | solution.py:556
  38.0 1.9 %all-gather.3 = f32[12,3,8,128]{3,2,1,0:T(8,128)S(1)} all-gather(f32[6,3,8,128]{3,2,1,0:T(8,128)S(1)} %collective-permute-done.2), channel_id=5, replica_groups={{0,8},{16,24},{32,40},{48,56},{64,72},{80,88},{96,104},{112,120},{128,1..., dimensions={0}, use_global_device_ids=true | all-gather | bytes 221184 | tf_op jit(solution)/shard_map/all_gather | solution.py:574
  40.0 1.3 %collective-permute-start.3 = (f32[4,3,16,128]{3,2,1,0:T(8,128)S(1)}, f32[4,3,16,128]{3,2,1,0:T(8,128)S(1)}, u32[]{:S(2)}, u32[]{:S(2)}) collective-permute-start(f32[4,3,16,128]{3,2,1,0:T(8,128)S(1)} %slice.44), channel_id=1, source_target_pairs={{0,32},{16,48},{32,64},{40,8},{48,80},{56,24},{64,96},{72,40},{80,... | collective-permute-start | bytes 294920 | tf_op jit(solution)/shard_map/ppermute | solution.py:545
  41.3 1.3 %collective-permute-start.4 = (f32[6,3,8,128]{3,2,1,0:T(8,128)S(1)}, f32[6,3,8,128]{3,2,1,0:T(8,128)S(1)}, u32[]{:S(2)}, u32[]{:S(2)}) collective-permute-start(f32[6,3,8,128]{3,2,1,0:T(8,128)S(1)} %slice.45), channel_id=1, source_target_pairs={{0,64},{16,80},{32,96},{48,112},{64,128},{72,8},{80,144},{88,24},{... | collective-permute-start | bytes 221192 | tf_op jit(solution)/shard_map/ppermute | solution.py:545
  42.6 4.7 %collective-permute-done.4 = f32[6,3,8,128]{3,2,1,0:T(8,128)S(1)} collective-permute-done((f32[6,3,8,128]{3,2,1,0:T(8,128)S(1)}, f32[6,3,8,128]{3,2,1,0:T(8,128)S(1)}, u32[]{:S(2)}, u32[]{:S(2)}) %collective-permute-start.4) | collective-permute-done | bytes 73760 | tf_op jit(solution)/shard_map/ppermute | solution.py:545
  47.3 0.0 collective-permute-done.3
  47.3 3.5 %all-gather.4 = f32[84,8,128]{2,1,0:T(8,128)S(1)} all-gather(f32[42,8,128]{2,1,0:T(8,128)S(1)} %pad_maximum_fusion.1), channel_id=6, replica_groups={{0,8},{16,24},{32,40},{48,56},{64,72},{80,88},{96,104},{112,120},{128,1..., dimensions={0}, use_global_device_ids=true | all-gather | bytes 516096 | tf_op jit(solution)/shard_map/all_gather | solution.py:574
  50.8 1.2 %pre1.1 = (f32[16,256]{1,0:T(8,128)S(1)}, f32[22,16,128]{2,1,0:T(8,128)S(1)}, f32[3,22,16,128]{3,2,1,0:T(8,128)S(1)}, f32[22,16,128]{2,1,0:T(8,128)S(1)}, f32[22...) custom-call(f32[6,3,16,128]{3,2,1,0:T(8,128)S(1)} %pad_maximum_fusion.2.own, ...), custom_call_target="tpu_custom_call" | custom-call | tf_op jit(solution)/shard_map/pre1/pallas_call | solution.py:508
  52.0 26.1 %all_to_all.17 = f32[16,1,256]{2,1,0:T(1,128)S(1)} all-to-all(f32[16,1,256]{2,1,0:T(1,128)S(1)} %copy.4), channel_id=1, replica_groups={{0,32,64,96,128,160,192,224,256,288,320,352,384,416,448,480},{8,40,72,1..., dimensions={0} | all-to-all | bytes 32768 | tf_op jit(solution)/shard_map/all_to_all | solution.py:589
  78.1 19.3 %all_to_all.18 = f32[16,16,256]{2,1,0:T(8,128)S(1)} all-to-all(f32[16,16,256]{2,1,0:T(8,128)S(1)} %broadcast_in_dim.3), channel_id=1, replica_groups={{0,1,2,3,4,5,6,7,16,17,18,19,20,21,22,23},{8,9,10,11,12,13,14,15,24,25,..., dimensions={0} | all-to-all | bytes 524288 | tf_op jit(solution)/shard_map/all_to_all | solution.py:591
  97.4 5.0 %all-gather.5 = f32[32,16,256]{2,1,0:T(8,128)S(1)} all-gather(f32[16,16,256]{2,1,0:T(8,128)S(1)} %all_to_all.18), channel_id=7, replica_groups={{0,8},{16,24},{32,40},{48,56},{64,72},{80,88},{96,104},{112,120},{128,1..., dimensions={0}, use_global_device_ids=true | all-gather | bytes 786432 | tf_op jit(solution)/shard_map/all_gather | solution.py:574
  102.4 5.5 %finish.1 = f32[2,16,128]{2,1,0:T(8,128)} custom-call(f32[512,256]{1,0:T(8,128)S(1)} %bitcast.19, f32[22,16,128]{2,1,0:T(8,128)S(1)} %get-tuple-element.18.field1, f32[3,22,16,128]{3,2,1,0:T(8,128)S(1)} %get-tuple-element.19.region1, f32[22,16,128]{2,1,0:T(8,128)S(1)} %get-tuple-element.20.inverse1, f32[22,16,128]{2,1,0:T(8,128)S(1)} %get-tuple-element.21.first1, ...), custom_call_target="tpu_custom_call" | custom-call | tf_op jit(solution)/shard_map/finish/pallas_call | solution.py:508
  (12 shorter events, 0.2 us)
Async XLA Ops:
  13.1 5.4 %collective-permute-start = (f32[4,3,2,8,128]{4,3,2,1,0:T(8,128)S(1)}, f32[4,3,2,8,128]{4,3,2,1,0:T(8,128)S(1)}, u32[]{:S(2)}, u32[]{:S(2)}) collective-permute-start(f32[4,3,2,8,128]{4,3,2,1,0:T(8,128)S(1)} %slice_select_fusion), channel_id=1, source_target_pairs={{0,1},{1,2},{2,3},{3,4},{4,5},{5,6},{6,7},{9,8},{10,9},{11,10},{12... | collective-permute-start | bytes 294920 | tf_op jit(solution)/shard_map/ppermute | solution.py:556
  20.4 8.5 %collective-permute-start.1 = (f32[4,3,2,32,128]{4,3,2,1,0:T(8,128)S(1)}, f32[4,3,2,32,128]{4,3,2,1,0:T(8,128)S(1)}, u32[]{:S(2)}, u32[]{:S(2)}) collective-permute-start(f32[4,3,2,32,128]{4,3,2,1,0:T(8,128)S(1)} %pad_maximum_fusion.own), channel_id=1, source_target_pairs={{0,32},{16,48},{32,64},{40,8},{48,80},{56,24},{64,96},{72,40},{80,... | collective-permute-start | bytes 1179656 | tf_op jit(solution)/shard_map/ppermute | solution.py:545
  32.9 5.1 %collective-permute-start.2 = (f32[6,3,8,128]{3,2,1,0:T(8,128)S(1)}, f32[6,3,8,128]{3,2,1,0:T(8,128)S(1)}, u32[]{:S(2)}, u32[]{:S(2)}) collective-permute-start(f32[6,3,8,128]{3,2,1,0:T(8,128)S(1)} %get-tuple-element.15), channel_id=1, source_target_pairs={{0,1},{1,2},{2,3},{3,4},{4,5},{5,6},{6,7},{9,8},{10,9},{11,10},{12... | collective-permute-start | bytes 221192 | tf_op jit(solution)/shard_map/ppermute | solution.py:556
  40.0 7.3 %collective-permute-start.3 = (f32[4,3,16,128]{3,2,1,0:T(8,128)S(1)}, f32[4,3,16,128]{3,2,1,0:T(8,128)S(1)}, u32[]{:S(2)}, u32[]{:S(2)}) collective-permute-start(f32[4,3,16,128]{3,2,1,0:T(8,128)S(1)} %slice.44), channel_id=1, source_target_pairs={{0,32},{16,48},{32,64},{40,8},{48,80},{56,24},{64,96},{72,40},{80,... | collective-permute-start | bytes 294920 | tf_op jit(solution)/shard_map/ppermute | solution.py:545
  41.3 6.0 %collective-permute-start.4 = (f32[6,3,8,128]{3,2,1,0:T(8,128)S(1)}, f32[6,3,8,128]{3,2,1,0:T(8,128)S(1)}, u32[]{:S(2)}, u32[]{:S(2)}) collective-permute-start(f32[6,3,8,128]{3,2,1,0:T(8,128)S(1)} %slice.45), channel_id=1, source_target_pairs={{0,64},{16,80},{32,96},{48,112},{64,128},{72,8},{80,144},{88,24},{... | collective-permute-start | bytes 221192 | tf_op jit(solution)/shard_map/ppermute | solution.py:545

commit v6 on v5

--- a/solution.py
+++ b/solution.py
@@ -153,7 +153,7 @@
         buffers[1][start:stop] = jnp.zeros_like(fresh)
 
 
-ROWS0 = 32
+ROWS0 = 48
 
 
 CHUNK0 = 2
@@ -180,13 +180,24 @@
 
 def coarse_rows(ref, value):
     count = value.shape[0]
-    ref[0:count] = pair_sum(value, 1)
-    take = lambda offset: jnp.stack([ref[at, pl.ds(offset, 8, stride=4), :] for at in range(count)])
-    even = (lax.broadcasted_iota(jnp.int32, (count, 8, LANES), 2) & 1) == 0
+    zero = jnp.zeros((count, 8, LANES), jnp.float32)
+    ref[0:count, 0:8, :] = zero
+    ref[0:count, 8:56, :] = pair_sum(value, 1)
+    ref[0:count, 56:64, :] = zero
+
+    def take(offset):
+        halves = [
+            [ref[at, pl.ds(32 * half + offset, 8, stride=4), :] for half in range(2)]
+            for at in range(count)
+        ]
+        return jnp.stack([jnp.concatenate(both) for both in halves])
+
+    even = (lax.broadcasted_iota(jnp.int32, (count, ROWS1, LANES), 2) & 1) == 0
     return 0.125 * jnp.where(even, take(0) + take(1), take(2) + take(3))
 
 
 KEPT0 = 10
+KEPT_ROWS0 = 32
 
 
 def pre0_kernel(
@@ -218,8 +229,8 @@
     base = 2 * (position() % LAYER) + 4
     for plane in range(KEPT0):
         for number, kept in enumerate((current, previous) + parts):
-            kept_out[number, plane] = kept[base + plane]
-    coarse = Packed(2, 8, False)
+            kept_out[number, plane] = kept[base + plane, 8:40, :]
+    coarse = Packed(2, ROWS1, False)
     half = face(1)
     betas = coarse_rows(tmp.at[0:8], pairs(beta(4, 20)))
     wide = coarse_rows(tmp.at[8:14], pairs(absorb(6, 18)))
@@ -283,8 +294,8 @@
 
 
 def pre1_kernel(
-    own, outer, absorb, pay_out, field, region, inverse, first, second, third,
-    two, tmp, small, tile,
+    own, outer, absorb, pay_out, rows_out, field, region, inverse, first, second, third,
+    two, tmp, tile,
 ):
     gather_level1(region, own, outer)
     shape = Packed(2, ROWS1, False)
@@ -298,8 +309,8 @@
         shape, list(enumerate(table))[1:], source, parts, (two, field), ranges, CHUNK1
     )
     rest = residual(shape, source, parts, current, 9, 13)
-    rows = coarser_rows(tmp, jnp.concatenate([pairs(rest), pairs(region[1, 9:13])]), 6)
-    rows += coarser_rows(small, pairs(absorb[...]), 2)
+    totals = [pairs(rest), pairs(region[1, 9:13]), pairs(absorb[...])]
+    rows = coarser_rows(tmp, jnp.concatenate(totals), 6)
     for at in range(6):
         tile[at : at + 1, :] = rows[at]
     tile[6:8, :] = jnp.zeros((2, LANES), jnp.float32)
@@ -307,6 +318,10 @@
     for side in range(2):
         part = tile[pl.ds(kind + side, 1), :]
         pay_out[:, side * LANES : (side + 1) * LANES] = jnp.broadcast_to(part, (16, LANES))
+    base = 3 + 4 * (position() % LAYER)
+    for plane in range(4):
+        row, lane = 4 * (plane % 2), plane // 2 * LANES
+        rows_out[row : row + 4, lane : lane + LANES] = current[base + plane, 6:10, :]
 
 
 DEPTH2 = 32
@@ -394,8 +409,11 @@
 def solve23(packed, halves, rows2, parts2, one2, two2, tall):
     shape = Packed(4, ROWS2, True)
     zero = jnp.zeros((ROWS2, LANES), jnp.float32)
-    for side in range(2):
-        halves[side] = packed[:, side * LANES : (side + 1) * LANES]
+    for peer in range(32):
+        for side in range(2):
+            halves[side, 16 * peer : 16 * peer + 16, :] = packed[
+                peer, 0:16, side * LANES : (side + 1) * LANES
+            ]
     for number in range(3):
         for plane in range(DEPTH2):
             at = 128 * KIND_AT[number] + plane // 2
@@ -427,7 +445,7 @@
     return current
 
 
-def post1(field, whole, region, parts, one, two, wide, tmp):
+def post1(packed, field, whole, region, parts, one, two, wide, tmp):
     inverse, first, second, third = parts
     shape = Packed(2, ROWS1, False)
     layer = position() // LAYER
@@ -448,8 +466,24 @@
             picked = jnp.where(inner == lane, moved[offset - lane], picked)
         for pair in range(8):
             tmp[pair, pl.ds(offset, 8, stride=4), :] = picked[pair]
-    for plane in range(3, 19):
-        one[plane] = field[plane] + tmp[(plane - 3) // 2, 2:18, :]
+    place = column_position()
+    before, after = jnp.maximum(place - 1, 0), jnp.minimum(place + 1, 7)
+    has_before = jnp.where(place > 0, 1.0, 0.0)
+    has_after = jnp.where(place < 7, 1.0, 0.0)
+    row = lax.broadcasted_iota(jnp.int32, (2, 8, LANES), 1)
+    inside = (row >= 2) & (row < 6)
+
+    def neighbour(start, who, there):
+        member, half = divmod((start - 3) // 2, 2)
+        at = 16 * (member % 2) + 8 * (member // 2)
+        value = there * packed[at + who, 16:24, half * LANES : (half + 1) * LANES]
+        return jnp.stack([across(value, -2), across(value, 2)])
+
+    for start in range(3, 19, 2):
+        here = field[start : start + 2]
+        upper = jnp.where(inside, neighbour(start, before, has_before), here[:, 0:8])
+        lower = jnp.where(inside, neighbour(start, after, has_after), here[:, 8:16])
+        one[start : start + 2] = jnp.concatenate([upper, lower], 1) + tmp[(start - 3) // 2, 2:18, :]
     table = chebyshev_table(SWEEPS)
     ranges = [(3 + order, 19 - order) for order in range(1, SWEEPS + 1)]
     current, _ = sweep(
@@ -480,8 +514,7 @@
         shape, list(enumerate(table)), lambda start, stop: source[start:stop], parts,
         (one, two), ranges, CHUNK0,
     )
-    for plane in (4, 5):
-        out[plane - 4] = current[plane][8:24, :]
+    out[...] = current[4:6, 8:24, :]
 
 
 def finish_kernel(
@@ -492,7 +525,7 @@
     parts2 = (diag2, inverse2, first2, second2, third2)
     whole = solve23(packed, halves, rows2, parts2, one2, two2, tall)
     parts1 = (inverse1, first1, second1, third1)
-    coarse = post1(field1, whole, region1, parts1, one1, two1, wide1, tmp1)
+    coarse = post1(packed, field1, whole, region1, parts1, one1, two1, wide1, tmp1)
     post0(kept0, coarse, out, one0, two0, tmp0)
 
 
@@ -516,26 +549,25 @@
 
 def pre0(*pieces):
     plane = buffer(24, ROWS0, LANES)
-    scratch = [plane] * 7 + [buffer(20, ROWS0, LANES)]
-    out = (f32(7, KEPT0, ROWS0, LANES), f32(6, 3, 8, LANES), f32(4, 8, LANES))
+    scratch = [plane] * 7 + [buffer(20, 64, LANES)]
+    out = (f32(7, KEPT0, KEPT_ROWS0, LANES), f32(6, 3, ROWS1, LANES), f32(4, ROWS1, LANES))
     return call(pre0_kernel, out, scratch, "pre0", *pieces)
 
 
 def pre1(*pieces):
     plane = f32(DEPTH1, ROWS1, LANES)
-    scratch = [buffer(DEPTH1, ROWS1, LANES), buffer(4, ROWS1, LANES), buffer(2, 8, LANES)]
-    scratch += [buffer(8, LANES)]
-    out = (f32(16, 2 * LANES), plane, f32(3, DEPTH1, ROWS1, LANES)) + (plane,) * 4
+    scratch = [buffer(DEPTH1, ROWS1, LANES), buffer(6, ROWS1, LANES), buffer(8, LANES)]
+    out = (f32(16, 2 * LANES), f32(8, 2 * LANES), plane, f32(3, DEPTH1, ROWS1, LANES)) + (plane,) * 4
     return call(pre1_kernel, out, scratch, "pre1", *pieces)
 
 
 def finish(*pieces):
     plane2 = buffer(DEPTH2 + 2, ROWS2, LANES)
     plane1 = buffer(DEPTH1, ROWS1, LANES)
-    plane0 = buffer(KEPT0, ROWS0, LANES)
+    plane0 = buffer(KEPT0, KEPT_ROWS0, LANES)
     scratch = [buffer(2, 512, LANES), buffer(3, DEPTH2 + 2, ROWS2, LANES)] + [plane2] * 7 + [buffer(3, 128, LANES)]
     scratch += [plane1] * 2 + [buffer(DEPTH2 + 6, 24, LANES), buffer(8, 32, LANES)]
-    scratch += [plane0] * 2 + [buffer(5, ROWS0, LANES)]
+    scratch += [plane0] * 2 + [buffer(5, KEPT_ROWS0, LANES)]
     return call(finish_kernel, f32(2, 16, LANES), scratch, "finish", *pieces)
 
 
@@ -568,28 +600,24 @@
         for z in range(layers)
         for core in range(2)
     ]
-    first_core = lax.axis_index("gx") % 2 == 0
-
     def both(value):
         return lax.all_gather(value, "gx", axis_index_groups=chips)
 
     local = jnp.stack([source, absorb, beta])
     own = lax.all_gather(local, "gx", axis_index_groups=near)
-    edges = jnp.where(first_core, own[..., 8:, :], own[..., :8, :])
-    sides = both(columns_apart(edges))
+    sides = both(columns_apart(own))
     layer = jnp.concatenate([sides[0], own, sides[1]], axis=-2)
     kept0, tile, absorb1 = pre0(layer, both(layers_apart(layer, 1)))
 
-    sides = both(columns_apart(tile))
-    tall = jnp.concatenate([sides[0, ..., 0:6, :], tile[..., 2:6, :], sides[1, ..., 2:8, :]], axis=-2)
-    tiles = [layers_apart(tall[1:5], 1), layers_apart(tall[..., 4:12, :], 2)]
+    tiles = [layers_apart(tile[1:5], 1), layers_apart(tile[..., 4:12, :], 2)]
     tiles = jnp.concatenate([x.reshape(-1, 8, LANES) for x in tiles])
-    pay, *kept1 = pre1(tall, both(tiles), absorb1)
+    pay, rows1, *kept1 = pre1(tile, both(tiles), absorb1)
 
     rows = lax.all_to_all(pay, "gx", 0, 0, axis_index_groups=column)
+    rows = jnp.concatenate([rows, rows1])
     rows = jnp.broadcast_to(rows, (2 * wide,) + rows.shape)
     rows = lax.all_to_all(rows, ("gx", "gy"), 0, 0, axis_index_groups=cores)
-    packed = both(rows).reshape(-1, 2 * LANES)
+    packed = both(rows).reshape(-1, *rows.shape[1:])
     return finish(packed, *kept1, kept0)
 
 

time: 108 us -> 136 us (1.26)
  waiting for transfers between devices: 19.8 us -> 43.5 us
  between operations: 0.13 us -> 13.5 us
  blocking collectives: 72.4 us -> 61.6 us
  local copies, waits for them, and re-layouts: 0.1 us -> 2.2 us
    all_gather x0 -> x1, waiting for transfers between devices: none -> 24.4 us  [both(): return lax.all_gather(value, 'gx', axis_index_groups=chips)]
    all_to_all x1, blocking collectives: 19.3 us -> 14.6 us  [body(): rows = lax.all_to_all(rows, ('gx', 'gy'), 0, 0, axis_index_groups=cores)]
    all_gather x5 -> x3, blocking collectives: 14.6 us -> 10.5 us  [both(): return lax.all_gather(value, 'gx', axis_index_groups=chips)]
    ppermute x2 -> x1, waiting for transfers between devices: 7.84 us -> 5.11 us  [columns_apart(): return lax.ppermute(value, ('gx', 'gy'), ways)]
    unnamed x1 -> x5, local copies, waits for them, and re-layouts: 0.01 us -> 2.11 us
    ppermute x3, waiting for transfers between devices: 11.9 us -> 14 us  [layers_apart(): lax.ppermute(value, 'gx', [(i, j) for i, j in ways if 0 <= j < count])]
    all_to_all x1, blocking collectives: 26.1 us -> 24.2 us  [body(): rows = lax.all_to_all(pay, 'gx', 0, 0, axis_index_groups=column)]
where the time goes in v6:
time: 136 us
  blocking collectives  61.6 us (45%)
  waiting for transfers between devices  43.5 us (32%)
  between operations  13.5 us (10%)
  Pallas kernels  9.09 us (7%)
  starting transfers between devices  5.16 us (4%)
  local copies, waits for them, and re-layouts  2.2 us (2%)
    all_gather x1, waiting for transfers between devices, both(): return lax.all_gather(value, 'gx', axis_index_groups=chips)  24.4 us
    all_to_all x1, blocking collectives, body(): rows = lax.all_to_all(pay, 'gx', 0, 0, axis_index_groups=column)  24.2 us
    all_to_all x1, blocking collectives, body(): rows = lax.all_to_all(rows, ('gx', 'gy'), 0, 0, axis_index_groups=cores)  14.6 us
    ppermute x3, waiting for transfers between devices, layers_apart(): lax.ppermute(value, 'gx', [(i, j) for i, j in ways if 0 <= j < count])  14 us
    all_gather x1, blocking collectives, body(): own = lax.all_gather(local, 'gx', axis_index_groups=near)  12.3 us
    all_gather x3, blocking collectives, both(): return lax.all_gather(value, 'gx', axis_index_groups=chips)  10.5 us
    pallas_call x3, Pallas kernels, call(): pl.pallas_call(kernel, out_shape=out, scratch_shapes=scratch, name=name,...  9.09 us
    ppermute x1, waiting for transfers between devices, columns_apart(): return lax.ppermute(value, ('gx', 'gy'), ways)  5.11 us
  transfers between devices with their start and end apart: 5, of which 4 were waited for; matrix products, arithmetic and copies ran while one was open for 0% of the time, Pallas kernels for 0%

profile of v6, /device:TPU:1, one launch (start us, length us, event | category | flops | bytes accessed | tf_op | source)
XLA Modules:
  0.0 135.9 jit_solution(10875111732964754375)
XLA Ops:
  6.5 0.0 all-gather.7.cloned.1.call-start
  6.5 0.8 pad_maximum_fusion.2
  7.3 12.3 %all-gather = f32[12,2,16,128]{3,2,1,0:T(8,128)S(1)} all-gather(f32[3,2,16,128]{3,2,1,0:T(8,128)S(1)} %pad_maximum_fusion.2), channel_id=2, replica_groups={{0,8,16,24},{32,40,48,56},{64,72,80,88},{96,104,112,120},{128,136,144,1..., dimensions={0}, use_global_device_ids=true | all-gather | bytes 245760 | tf_op jit(solution)/shard_map/all_gather | solution.py:607
  19.6 1.3 collective-permute-start
  20.9 5.1 %collective-permute-done = f32[4,3,2,16,128]{4,3,2,1,0:T(8,128)S(1)} collective-permute-done((f32[4,3,2,16,128]{4,3,2,1,0:T(8,128)S(1)}, f32[4,3,2,16,128]{4,3,2,1,0:T(8,128)S(1)}, u32[]{:S(2)}, u32[]{:S(2)}) %collective-permute-start) | collective-permute-done | bytes 196640 | tf_op jit(solution)/shard_map/ppermute | solution.py:588
  26.0 2.1 %all-gather.1 = f32[8,3,2,16,128]{4,3,2,1,0:T(8,128)S(1)} all-gather(f32[4,3,2,16,128]{4,3,2,1,0:T(8,128)S(1)} %collective-permute-done), channel_id=3, replica_groups={{0,8},{16,24},{32,40},{48,56},{64,72},{80,88},{96,104},{112,120},{128,1..., dimensions={0}, use_global_device_ids=true | all-gather | bytes 589824 | tf_op jit(solution)/shard_map/all_gather | solution.py:604
  28.2 1.3 collective-permute-start.1
  29.5 9.3 %collective-permute-done.1 = f32[4,3,2,48,128]{4,3,2,1,0:T(8,128)S(1)} collective-permute-done((f32[4,3,2,48,128]{4,3,2,1,0:T(8,128)S(1)}, f32[4,3,2,48,128]{4,3,2,1,0:T(8,128)S(1)}, u32[]{:S(2)}, u32[]{:S(2)}) %collective-permute-start.1) | collective-permute-done | bytes 589856 | tf_op jit(solution)/shard_map/ppermute | solution.py:577
  38.8 0.0 copy-start.1
  38.8 0.8 copy-done.1
  39.6 0.0 all-gather.7.cloned.1.call-update
  39.6 24.4 %all-gather.7.cloned.1.call-done = f32[8,3,2,48,128]{4,3,2,1,0:T(8,128)} async-done(((f32[4,3,2,48,128]{4,3,2,1,0:T(8,128)}), f32[8,3,2,48,128]{4,3,2,1,0:T(8,128)}) %all-gather.7.cloned.1.call-update) | async-done | bytes 1179664 | tf_op jit(solution)/shard_map/all_gather | solution.py:604
  64.0 0.0 copy-start
  64.0 1.3 copy-done
  65.3 2.3 %pre0.1 = (f32[7,10,32,128]{3,2,1,0:T(8,128)S(1)}, f32[6,3,16,128]{3,2,1,0:T(8,128)S(1)}, f32[4,16,128]{2,1,0:T(8,128)S(1)}) custom-call(f32[4,3,2,48,128]{4,3,2,1,0:T(8,128)S(1)} %pad_maximum_fusion.own, f32[2,4,3,2,48,128]{5,4,3,2,1,0:T(8,128)S(1)} %bitcast.13), custom_call_target="tpu_custom_call" | custom-call | tf_op jit(solution)/shard_map/pre0/pallas_call | solution.py:541
  67.6 1.3 collective-permute-start.2
  69.0 1.3 collective-permute-start.3
  70.3 4.7 %collective-permute-done.3 = f32[6,3,8,128]{3,2,1,0:T(8,128)S(1)} collective-permute-done((f32[6,3,8,128]{3,2,1,0:T(8,128)S(1)}, f32[6,3,8,128]{3,2,1,0:T(8,128)S(1)}, u32[]{:S(2)}, u32[]{:S(2)}) %collective-permute-start.3) | collective-permute-done | bytes 73760 | tf_op jit(solution)/shard_map/ppermute | solution.py:577
  74.9 0.0 collective-permute-done.2
  75.0 3.5 %all-gather.3 = f32[84,8,128]{2,1,0:T(8,128)S(1)} all-gather(f32[42,8,128]{2,1,0:T(8,128)S(1)} %pad_maximum_fusion.1), channel_id=5, replica_groups={{0,8},{16,24},{32,40},{48,56},{64,72},{80,88},{96,104},{112,120},{128,1..., dimensions={0}, use_global_device_ids=true | all-gather | bytes 516096 | tf_op jit(solution)/shard_map/all_gather | solution.py:604
  78.5 1.3 pre1.1
  79.7 24.2 %all_to_all.17 = f32[16,1,256]{2,1,0:T(1,128)S(1)} all-to-all(f32[16,1,256]{2,1,0:T(1,128)S(1)} %copy.4), channel_id=1, replica_groups={{0,32,64,96,128,160,192,224,256,288,320,352,384,416,448,480},{8,40,72,1..., dimensions={0} | all-to-all | bytes 32768 | tf_op jit(solution)/shard_map/all_to_all | solution.py:616
  104.0 14.6 %all_to_all.18 = f32[16,24,256]{2,1,0:T(8,128)S(1)} all-to-all(f32[16,24,256]{2,1,0:T(8,128)S(1)} %broadcast_in_dim.3), channel_id=1, replica_groups={{0,1,2,3,4,5,6,7,16,17,18,19,20,21,22,23},{8,9,10,11,12,13,14,15,24,25,..., dimensions={0} | all-to-all | bytes 786432 | tf_op jit(solution)/shard_map/all_to_all | solution.py:619
  118.6 4.9 %all-gather.4.packed = f32[32,24,256]{2,1,0:T(8,128)S(1)} all-gather(f32[16,24,256]{2,1,0:T(8,128)S(1)} %all_to_all.18), channel_id=6, replica_groups={{0,8},{16,24},{32,40},{48,56},{64,72},{80,88},{96,104},{112,120},{128,1..., dimensions={0}, use_global_device_ids=true | all-gather | bytes 1179648 | tf_op jit(solution)/shard_map/all_gather | solution.py:604
  123.5 5.5 %finish.1 = f32[2,16,128]{2,1,0:T(8,128)} custom-call(f32[32,24,256]{2,1,0:T(8,128)S(1)} %all-gather.4.packed, f32[22,16,128]{2,1,0:T(8,128)S(1)} %get-tuple-element.20.field1, f32[3,22,16,128]{3,2,1,0:T(8,128)S(1)} %get-tuple-element.21.region1, f32[22,16,128]{2,1,0:T(8,128)S(1)} %get-tuple-element.22.inverse1, ...), custom_call_target="tpu_custom_call" | custom-call | tf_op jit(solution)/shard_map/finish/pallas_call | solution.py:541
  (9 shorter events, 0.2 us)
Async XLA Ops:
  6.5 57.5 %all-gather.7.cloned.1.call-start = ((), (), s32[]{:S(2)}) async-start(), calls=%async_computation.2 | async-start | bytes 1769472 | tf_op jit(solution)/shard_map/all_gather | solution.py:604
  19.6 6.4 %collective-permute-start = (f32[4,3,2,16,128]{4,3,2,1,0:T(8,128)S(1)}, f32[4,3,2,16,128]{4,3,2,1,0:T(8,128)S(1)}, u32[]{:S(2)}, u32[]{:S(2)}) collective-permute-start(f32[4,3,2,16,128]{4,3,2,1,0:T(8,128)S(1)} %bitcast.15), channel_id=1, source_target_pairs={{0,1},{1,2},{2,3},{3,4},{4,5},{5,6},{6,7},{9,8},{10,9},{11,10},{12... | collective-permute-start | bytes 589832 | tf_op jit(solution)/shard_map/ppermute | solution.py:588
  28.2 10.6 %collective-permute-start.1 = (f32[4,3,2,48,128]{4,3,2,1,0:T(8,128)S(1)}, f32[4,3,2,48,128]{4,3,2,1,0:T(8,128)S(1)}, u32[]{:S(2)}, u32[]{:S(2)}) collective-permute-start(f32[4,3,2,48,128]{4,3,2,1,0:T(8,128)S(1)} %pad_maximum_fusion.own), channel_id=1, source_target_pairs={{0,32},{16,48},{32,64},{40,8},{48,80},{56,24},{64,96},{72,40},{80,... | collective-permute-start | bytes 1769480 | tf_op jit(solution)/shard_map/ppermute | solution.py:577
  38.8 0.8 copy-start.1
  64.0 1.3 copy-start
  67.6 7.3 %collective-permute-start.2 = (f32[4,3,16,128]{3,2,1,0:T(8,128)S(1)}, f32[4,3,16,128]{3,2,1,0:T(8,128)S(1)}, u32[]{:S(2)}, u32[]{:S(2)}) collective-permute-start(f32[4,3,16,128]{3,2,1,0:T(8,128)S(1)} %slice.14), channel_id=1, source_target_pairs={{0,32},{16,48},{32,64},{40,8},{48,80},{56,24},{64,96},{72,40},{80,... | collective-permute-start | bytes 294920 | tf_op jit(solution)/shard_map/ppermute | solution.py:577
  69.0 6.0 %collective-permute-start.3 = (f32[6,3,8,128]{3,2,1,0:T(8,128)S(1)}, f32[6,3,8,128]{3,2,1,0:T(8,128)S(1)}, u32[]{:S(2)}, u32[]{:S(2)}) collective-permute-start(f32[6,3,8,128]{3,2,1,0:T(8,128)S(1)} %slice.15), channel_id=1, source_target_pairs={{0,64},{16,80},{32,96},{48,112},{64,128},{72,8},{80,144},{88,24},{... | collective-permute-start | bytes 221192 | tf_op jit(solution)/shard_map/ppermute | solution.py:577
Sparse Core Ops, SparseCore 0:
  39.8 24.2 all-gather.6

commit v7 on v6

--- a/solution.py
+++ b/solution.py
@@ -204,13 +204,27 @@
     own, outer, kept_out, tile_out, absorb_out,
     diag, inverse, first, second, third, one, two, tmp,
 ):
+    zero = jnp.zeros((8, LANES), jnp.float32)
+
     def piece(kind):
         def planes(start, stop):
             found = []
             for plane in range(start, stop):
                 part, member = plane // 8, plane % 8 // 2
-                block = own.at[member] if part == 1 else outer.at[part // 2, member]
-                found.append(block[kind, plane % 2])
+                if part == 1:
+                    found.append(own[member, kind, plane % 2])
+                    continue
+                side = part // 2
+                at = 4 * (6 * member + 2 * kind + plane % 2)
+                middle = [outer[side, at + tile] for tile in range(4)]
+                reach = 3 if kind == 2 else 2
+                near = member - (LAYER - reach) if side == 0 else member
+                if 0 <= near < reach:
+                    at = 96 + 2 * (2 * (2 * kind + near) + plane % 2)
+                    ends = outer[side, at], outer[side, at + 1]
+                else:
+                    ends = zero, zero
+                found.append(jnp.concatenate([ends[0], *middle, ends[1]]))
             return jnp.stack(found)
 
         return planes
@@ -600,6 +614,8 @@
         for z in range(layers)
         for core in range(2)
     ]
+    first_core = lax.axis_index("gx") % 2 == 0
+
     def both(value):
         return lax.all_gather(value, "gx", axis_index_groups=chips)
 
@@ -607,7 +623,12 @@
     own = lax.all_gather(local, "gx", axis_index_groups=near)
     sides = both(columns_apart(own))
     layer = jnp.concatenate([sides[0], own, sides[1]], axis=-2)
-    kept0, tile, absorb1 = pre0(layer, both(layers_apart(layer, 1)))
+    ends = jnp.concatenate([sides[0, ..., :8, :], sides[1, ..., 8:, :]], axis=-2)
+    near2 = jnp.where(first_core, ends[2:, :2], ends[:2, :2])
+    near3 = jnp.where(first_core, ends[1:, 2], ends[:3, 2])
+    sent = [layer[..., 8:40, :], near2[:, 0], near2[:, 1], near3]
+    sent = jnp.concatenate([x.reshape(-1, 8, LANES) for x in sent])
+    kept0, tile, absorb1 = pre0(layer, both(layers_apart(sent, 1)))
 
     tiles = [layers_apart(tile[1:5], 1), layers_apart(tile[..., 4:12, :], 2)]
     tiles = jnp.concatenate([x.reshape(-1, 8, LANES) for x in tiles])

time: 136 us -> 101 us (0.74)
  waiting for transfers between devices: 43.5 us -> 18.3 us
  between operations: 13.5 us -> 0.16 us
  blocking collectives: 61.6 us -> 66.8 us
  local copies, waits for them, and re-layouts: 2.2 us -> 0.15 us
    all_gather x1 -> x0, waiting for transfers between devices: 24.4 us -> none  [both(): return lax.all_gather(value, 'gx', axis_index_groups=chips)]
    all_to_all x1, blocking collectives: 14.6 us -> 16.7 us  [body(): rows = lax.all_to_all(rows, ('gx', 'gy'), 0, 0, axis_index_groups=cores)]
    unnamed x5 -> x1, local copies, waits for them, and re-layouts: 2.11 us -> 0.01 us
    all_to_all x1, blocking collectives: 24.2 us -> 26.1 us  [body(): rows = lax.all_to_all(pay, 'gx', 0, 0, axis_index_groups=column)]
    all_gather x3 -> x4, blocking collectives: 10.5 us -> 11.7 us  [both(): return lax.all_gather(value, 'gx', axis_index_groups=chips)]
  transfers between devices with their start and end apart: 5 -> 4, of which waited for: 4 -> 3; matrix products, arithmetic and copies ran while one was open for 0% -> 0% of each run, Pallas kernels for 0% -> 0%
where the time goes in v7:
time: 101 us; the launch traced here: 100 us
  blocking collectives  66.8 us (66%)
  waiting for transfers between devices  18.3 us (18%)
  Pallas kernels  9.06 us (9%)
  starting transfers between devices  5.16 us (5%)
    all_to_all x1, blocking collectives, body(): rows = lax.all_to_all(pay, 'gx', 0, 0, axis_index_groups=column)  26.1 us
    all_to_all x1, blocking collectives, body(): rows = lax.all_to_all(rows, ('gx', 'gy'), 0, 0, axis_index_groups=cores)  16.7 us
    ppermute x3, waiting for transfers between devices, layers_apart(): lax.ppermute(value, 'gx', [(i, j) for i, j in ways if 0 <= j < count])  13.1 us
    all_gather x1, blocking collectives, body(): own = lax.all_gather(local, 'gx', axis_index_groups=near)  12.3 us
    all_gather x4, blocking collectives, both(): return lax.all_gather(value, 'gx', axis_index_groups=chips)  11.7 us
    pallas_call x3, Pallas kernels, call(): pl.pallas_call(kernel, out_shape=out, scratch_shapes=scratch, name=name,...  9.06 us
    ppermute x1, waiting for transfers between devices, columns_apart(): return lax.ppermute(value, ('gx', 'gy'), ways)  5.1 us
    ppermute x3, starting transfers between devices, layers_apart(): lax.ppermute(value, 'gx', [(i, j) for i, j in ways if 0 <= j < count])  3.88 us
  transfers between devices with their start and end apart: 4, of which 3 were waited for; matrix products, arithmetic and copies ran while one was open for 0% of the time, Pallas kernels for 0%

profile of v7, /device:TPU:1, one launch (start us, length us, event | category | flops | bytes accessed | tf_op | source)
XLA Modules:
  0.0 100.5 jit_solution(10024513224530073774)
XLA Ops:
  0.0 0.8 pad_maximum_fusion.4
  0.8 12.3 %all-gather = f32[12,2,16,128]{3,2,1,0:T(8,128)S(1)} all-gather(f32[3,2,16,128]{3,2,1,0:T(8,128)S(1)} %pad_maximum_fusion.4), channel_id=2, replica_groups={{0,8,16,24},{32,40,48,56},{64,72,80,88},{96,104,112,120},{128,136,144,1..., dimensions={0}, use_global_device_ids=true | all-gather | bytes 245760 | tf_op jit(solution)/shard_map/all_gather | solution.py:623
  13.1 1.3 %collective-permute-start = (f32[4,3,2,16,128]{4,3,2,1,0:T(8,128)S(1)}, f32[4,3,2,16,128]{4,3,2,1,0:T(8,128)S(1)}, u32[]{:S(2)}, u32[]{:S(2)}) collective-permute-start(f32[4,3,2,16,128]{4,3,2,1,0:T(8,128)S(1)} %bitcast.26), channel_id=1, source_target_pairs={{0,1},{1,2},{2,3},{3,4},{4,5},{5,6},{6,7},{9,8},{10,9},{11,10},{12... | collective-permute-start | bytes 589832 | tf_op jit(solution)/shard_map/ppermute | solution.py:602
  14.4 5.1 %collective-permute-done = f32[4,3,2,16,128]{4,3,2,1,0:T(8,128)S(1)} collective-permute-done((f32[4,3,2,16,128]{4,3,2,1,0:T(8,128)S(1)}, f32[4,3,2,16,128]{4,3,2,1,0:T(8,128)S(1)}, u32[]{:S(2)}, u32[]{:S(2)}) %collective-permute-start) | collective-permute-done | bytes 196640 | tf_op jit(solution)/shard_map/ppermute | solution.py:602
  19.5 2.1 %all-gather.1 = f32[8,3,2,16,128]{4,3,2,1,0:T(8,128)S(1)} all-gather(f32[4,3,2,16,128]{4,3,2,1,0:T(8,128)S(1)} %collective-permute-done), channel_id=3, replica_groups={{0,8},{16,24},{32,40},{48,56},{64,72},{80,88},{96,104},{112,120},{128,1..., dimensions={0}, use_global_device_ids=true | all-gather | bytes 589824 | tf_op jit(solution)/shard_map/all_gather | solution.py:620
  21.8 1.3 %collective-permute-start.1 = (f32[124,8,128]{2,1,0:T(8,128)S(1)}, f32[124,8,128]{2,1,0:T(8,128)S(1)}, u32[]{:S(2)}, u32[]{:S(2)}) collective-permute-start(f32[124,8,128]{2,1,0:T(8,128)S(1)} %pad_maximum_fusion.1), channel_id=1, source_target_pairs={{0,32},{16,48},{32,64},{40,8},{48,80},{56,24},{64,96},{72,40},{80,... | collective-permute-start | bytes 1523720 | tf_op jit(solution)/shard_map/ppermute | solution.py:591
  23.1 8.4 %collective-permute-done.1 = f32[124,8,128]{2,1,0:T(8,128)S(1)} collective-permute-done((f32[124,8,128]{2,1,0:T(8,128)S(1)}, f32[124,8,128]{2,1,0:T(8,128)S(1)}, u32[]{:S(2)}, u32[]{:S(2)}) %collective-permute-start.1) | collective-permute-done | bytes 507936 | tf_op jit(solution)/shard_map/ppermute | solution.py:591
  31.5 2.5 %all-gather.2 = f32[248,8,128]{2,1,0:T(8,128)S(1)} all-gather(f32[124,8,128]{2,1,0:T(8,128)S(1)} %collective-permute-done.1), channel_id=4, replica_groups={{0,8},{16,24},{32,40},{48,56},{64,72},{80,88},{96,104},{112,120},{128,1..., dimensions={0}, use_global_device_ids=true | all-gather | bytes 1523712 | tf_op jit(solution)/shard_map/all_gather | solution.py:620
  34.0 2.3 %pre0.1 = (f32[7,10,32,128]{3,2,1,0:T(8,128)S(1)}, f32[6,3,16,128]{3,2,1,0:T(8,128)S(1)}, f32[4,16,128]{2,1,0:T(8,128)S(1)}) custom-call(f32[4,3,2,48,128]{4,3,2,1,0:T(8,128)S(1)} %pad_maximum_fusion.own, f32[2,124,8,128]{3,2,1,0:T(8,128)S(1)} %bitcast.21), custom_call_target="tpu_custom_call" | custom-call | tf_op jit(solution)/shard_map/pre0/pallas_call | solution.py:555
  36.3 1.3 %collective-permute-start.2 = (f32[4,3,16,128]{3,2,1,0:T(8,128)S(1)}, f32[4,3,16,128]{3,2,1,0:T(8,128)S(1)}, u32[]{:S(2)}, u32[]{:S(2)}) collective-permute-start(f32[4,3,16,128]{3,2,1,0:T(8,128)S(1)} %slice.50), channel_id=1, source_target_pairs={{0,32},{16,48},{32,64},{40,8},{48,80},{56,24},{64,96},{72,40},{80,... | collective-permute-start | bytes 294920 | tf_op jit(solution)/shard_map/ppermute | solution.py:591
  37.7 1.3 %collective-permute-start.3 = (f32[6,3,8,128]{3,2,1,0:T(8,128)S(1)}, f32[6,3,8,128]{3,2,1,0:T(8,128)S(1)}, u32[]{:S(2)}, u32[]{:S(2)}) collective-permute-start(f32[6,3,8,128]{3,2,1,0:T(8,128)S(1)} %slice.51), channel_id=1, source_target_pairs={{0,64},{16,80},{32,96},{48,112},{64,128},{72,8},{80,144},{88,24},{... | collective-permute-start | bytes 221192 | tf_op jit(solution)/shard_map/ppermute | solution.py:591
  39.0 4.7 %collective-permute-done.3 = f32[6,3,8,128]{3,2,1,0:T(8,128)S(1)} collective-permute-done((f32[6,3,8,128]{3,2,1,0:T(8,128)S(1)}, f32[6,3,8,128]{3,2,1,0:T(8,128)S(1)}, u32[]{:S(2)}, u32[]{:S(2)}) %collective-permute-start.3) | collective-permute-done | bytes 73760 | tf_op jit(solution)/shard_map/ppermute | solution.py:591
  43.7 0.0 collective-permute-done.2
  43.7 2.2 %all-gather.3 = f32[84,8,128]{2,1,0:T(8,128)S(1)} all-gather(f32[42,8,128]{2,1,0:T(8,128)S(1)} %pad_maximum_fusion.2), channel_id=5, replica_groups={{0,8},{16,24},{32,40},{48,56},{64,72},{80,88},{96,104},{112,120},{128,1..., dimensions={0}, use_global_device_ids=true | all-gather | bytes 516096 | tf_op jit(solution)/shard_map/all_gather | solution.py:620
  45.9 1.3 %pre1.1 = (f32[16,256]{1,0:T(8,128)S(1)}, f32[8,256]{1,0:T(8,128)S(1)}, f32[22,16,128]{2,1,0:T(8,128)S(1)}, f32[3,22,16,128]{3,2,1,0:T(8,128)S(1)}, f32[22,16,12...) custom-call(f32[6,3,16,128]{3,2,1,0:T(8,128)S(1)} %get-tuple-element.16.ow, ...), custom_call_target="tpu_custom_call" | custom-call | tf_op jit(solution)/shard_map/pre1/pallas_call | solution.py:555
  47.2 26.1 %all_to_all.17 = f32[16,1,256]{2,1,0:T(1,128)S(1)} all-to-all(f32[16,1,256]{2,1,0:T(1,128)S(1)} %copy.4), channel_id=1, replica_groups={{0,32,64,96,128,160,192,224,256,288,320,352,384,416,448,480},{8,40,72,1..., dimensions={0} | all-to-all | bytes 32768 | tf_op jit(solution)/shard_map/all_to_all | solution.py:637
  73.3 16.7 %all_to_all.18 = f32[16,24,256]{2,1,0:T(8,128)S(1)} all-to-all(f32[16,24,256]{2,1,0:T(8,128)S(1)} %broadcast_in_dim.3), channel_id=1, replica_groups={{0,1,2,3,4,5,6,7,16,17,18,19,20,21,22,23},{8,9,10,11,12,13,14,15,24,25,..., dimensions={0} | all-to-all | bytes 786432 | tf_op jit(solution)/shard_map/all_to_all | solution.py:640
  90.0 4.9 %all-gather.4.packed = f32[32,24,256]{2,1,0:T(8,128)S(1)} all-gather(f32[16,24,256]{2,1,0:T(8,128)S(1)} %all_to_all.18), channel_id=6, replica_groups={{0,8},{16,24},{32,40},{48,56},{64,72},{80,88},{96,104},{112,120},{128,1..., dimensions={0}, use_global_device_ids=true | all-gather | bytes 1179648 | tf_op jit(solution)/shard_map/all_gather | solution.py:620
  94.9 5.5 %finish.1 = f32[2,16,128]{2,1,0:T(8,128)} custom-call(f32[32,24,256]{2,1,0:T(8,128)S(1)} %all-gather.4.packed, f32[22,16,128]{2,1,0:T(8,128)S(1)} %get-tuple-element.20.field1, f32[3,22,16,128]{3,2,1,0:T(8,128)S(1)} %get-tuple-element.21.region1, f32[22,16,128]{2,1,0:T(8,128)S(1)} %get-tuple-element.22.inverse1, ...), custom_call_target="tpu_custom_call" | custom-call | tf_op jit(solution)/shard_map/finish/pallas_call | solution.py:555
  (15 shorter events, 0.3 us)
Async XLA Ops:
  13.1 6.4 %collective-permute-start = (f32[4,3,2,16,128]{4,3,2,1,0:T(8,128)S(1)}, f32[4,3,2,16,128]{4,3,2,1,0:T(8,128)S(1)}, u32[]{:S(2)}, u32[]{:S(2)}) collective-permute-start(f32[4,3,2,16,128]{4,3,2,1,0:T(8,128)S(1)} %bitcast.26), channel_id=1, source_target_pairs={{0,1},{1,2},{2,3},{3,4},{4,5},{5,6},{6,7},{9,8},{10,9},{11,10},{12... | collective-permute-start | bytes 589832 | tf_op jit(solution)/shard_map/ppermute | solution.py:602
  21.8 9.8 %collective-permute-start.1 = (f32[124,8,128]{2,1,0:T(8,128)S(1)}, f32[124,8,128]{2,1,0:T(8,128)S(1)}, u32[]{:S(2)}, u32[]{:S(2)}) collective-permute-start(f32[124,8,128]{2,1,0:T(8,128)S(1)} %pad_maximum_fusion.1), channel_id=1, source_target_pairs={{0,32},{16,48},{32,64},{40,8},{48,80},{56,24},{64,96},{72,40},{80,... | collective-permute-start | bytes 1523720 | tf_op jit(solution)/shard_map/ppermute | solution.py:591
  36.3 7.3 %collective-permute-start.2 = (f32[4,3,16,128]{3,2,1,0:T(8,128)S(1)}, f32[4,3,16,128]{3,2,1,0:T(8,128)S(1)}, u32[]{:S(2)}, u32[]{:S(2)}) collective-permute-start(f32[4,3,16,128]{3,2,1,0:T(8,128)S(1)} %slice.50), channel_id=1, source_target_pairs={{0,32},{16,48},{32,64},{40,8},{48,80},{56,24},{64,96},{72,40},{80,... | collective-permute-start | bytes 294920 | tf_op jit(solution)/shard_map/ppermute | solution.py:591
  37.7 6.0 %collective-permute-start.3 = (f32[6,3,8,128]{3,2,1,0:T(8,128)S(1)}, f32[6,3,8,128]{3,2,1,0:T(8,128)S(1)}, u32[]{:S(2)}, u32[]{:S(2)}) collective-permute-start(f32[6,3,8,128]{3,2,1,0:T(8,128)S(1)} %slice.51), channel_id=1, source_target_pairs={{0,64},{16,80},{32,96},{48,112},{64,128},{72,8},{80,144},{88,24},{... | collective-permute-start | bytes 221192 | tf_op jit(solution)/shard_map/ppermute | solution.py:591

commit v8 on v7

--- a/solution.py
+++ b/solution.py
@@ -215,8 +215,8 @@
                     found.append(own[member, kind, plane % 2])
                     continue
                 side = part // 2
-                at = 4 * (6 * member + 2 * kind + plane % 2)
-                middle = [outer[side, at + tile] for tile in range(4)]
+                at = 2 * (6 * member + 2 * kind + plane % 2)
+                rows = [outer[side, at + tile] for tile in (48, 0, 1, 49)]
                 reach = 3 if kind == 2 else 2
                 near = member - (LAYER - reach) if side == 0 else member
                 if 0 <= near < reach:
@@ -224,7 +224,7 @@
                     ends = outer[side, at], outer[side, at + 1]
                 else:
                     ends = zero, zero
-                found.append(jnp.concatenate([ends[0], *middle, ends[1]]))
+                found.append(jnp.concatenate([ends[0], *rows, ends[1]]))
             return jnp.stack(found)
 
         return planes
@@ -621,17 +621,21 @@
 
     local = jnp.stack([source, absorb, beta])
     own = lax.all_gather(local, "gx", axis_index_groups=near)
-    sides = both(columns_apart(own))
+    def tiles_of(arrays):
+        return jnp.concatenate([x.reshape(-1, 8, LANES) for x in arrays])
+
+    sides = columns_apart(own)
+    outer = layers_apart(own, 1)
+    sides = both(sides)
     layer = jnp.concatenate([sides[0], own, sides[1]], axis=-2)
+    rims = jnp.concatenate([sides[0, ..., 8:, :], sides[1, ..., :8, :]], axis=-2)
     ends = jnp.concatenate([sides[0, ..., :8, :], sides[1, ..., 8:, :]], axis=-2)
     near2 = jnp.where(first_core, ends[2:, :2], ends[:2, :2])
     near3 = jnp.where(first_core, ends[1:, 2], ends[:3, 2])
-    sent = [layer[..., 8:40, :], near2[:, 0], near2[:, 1], near3]
-    sent = jnp.concatenate([x.reshape(-1, 8, LANES) for x in sent])
-    kept0, tile, absorb1 = pre0(layer, both(layers_apart(sent, 1)))
-
-    tiles = [layers_apart(tile[1:5], 1), layers_apart(tile[..., 4:12, :], 2)]
-    tiles = jnp.concatenate([x.reshape(-1, 8, LANES) for x in tiles])
+    rest = layers_apart(tiles_of([rims, near2[:, 0], near2[:, 1], near3]), 1)
+    kept0, tile, absorb1 = pre0(layer, both(tiles_of([outer, rest])))
+
+    tiles = tiles_of([layers_apart(tile[1:5], 1), layers_apart(tile[..., 4:12, :], 2)])
     pay, rows1, *kept1 = pre1(tile, both(tiles), absorb1)
 
     rows = lax.all_to_all(pay, "gx", 0, 0, axis_index_groups=column)

time: 101 us -> 98.8 us (0.978)
  waiting for transfers between devices: 18.3 us -> 14.8 us
  starting transfers between devices: 5.16 us -> 6.45 us
    ppermute x3 -> x4, waiting for transfers between devices: 13.1 us -> 10.9 us  [layers_apart(): lax.ppermute(value, 'gx', [(i, j) for i, j in ways if 0 <= j < count])]
    ppermute x1, waiting for transfers between devices: 5.1 us -> 3.8 us  [columns_apart(): return lax.ppermute(value, ('gx', 'gy'), ways)]
    ppermute x3 -> x4, starting transfers between devices: 3.88 us -> 5.17 us  [layers_apart(): lax.ppermute(value, 'gx', [(i, j) for i, j in ways if 0 <= j < count])]
    all_gather x4, blocking collectives: 11.7 us -> 13 us  [both(): return lax.all_gather(value, 'gx', axis_index_groups=chips)]
    all_to_all x1, blocking collectives: 26.1 us -> 24.8 us  [body(): rows = lax.all_to_all(pay, 'gx', 0, 0, axis_index_groups=column)]
  transfers between devices with their start and end apart: 4 -> 5, of which waited for: 3 -> 3; matrix products, arithmetic and copies ran while one was open for 0% -> 0% of each run, Pallas kernels for 0% -> 0%
where the time goes in v8:
time: 98.8 us; the launch traced here: 98.3 us
  blocking collectives  66.8 us (68%)
  waiting for transfers between devices  14.8 us (15%)
  Pallas kernels  9.06 us (9%)
  starting transfers between devices  6.45 us (7%)
    all_to_all x1, blocking collectives, body(): rows = lax.all_to_all(pay, 'gx', 0, 0, axis_index_groups=column)  24.8 us
    all_to_all x1, blocking collectives, body(): rows = lax.all_to_all(rows, ('gx', 'gy'), 0, 0, axis_index_groups=cores)  16.7 us
    all_gather x4, blocking collectives, both(): return lax.all_gather(value, 'gx', axis_index_groups=chips)  13 us
    all_gather x1, blocking collectives, body(): own = lax.all_gather(local, 'gx', axis_index_groups=near)  12.3 us
    ppermute x4, waiting for transfers between devices, layers_apart(): lax.ppermute(value, 'gx', [(i, j) for i, j in ways if 0 <= j < count])  10.9 us
    pallas_call x3, Pallas kernels, call(): pl.pallas_call(kernel, out_shape=out, scratch_shapes=scratch, name=name,...  9.06 us
    ppermute x4, starting transfers between devices, layers_apart(): lax.ppermute(value, 'gx', [(i, j) for i, j in ways if 0 <= j < count])  5.17 us
    ppermute x1, waiting for transfers between devices, columns_apart(): return lax.ppermute(value, ('gx', 'gy'), ways)  3.8 us
  transfers between devices with their start and end apart: 5, of which 3 were waited for; matrix products, arithmetic and copies ran while one was open for 0% of the time, Pallas kernels for 0%

profile of v8, /device:TPU:1, one launch (start us, length us, event | category | flops | bytes accessed | tf_op | source)
XLA Modules:
  0.0 98.3 jit_solution(6826116280866908153)
XLA Ops:
  0.0 0.8 pad_maximum_fusion.6
  0.8 12.3 %all-gather = f32[12,2,16,128]{3,2,1,0:T(8,128)S(1)} all-gather(f32[3,2,16,128]{3,2,1,0:T(8,128)S(1)} %pad_maximum_fusion.6), channel_id=2, replica_groups={{0,8,16,24},{32,40,48,56},{64,72,80,88},{96,104,112,120},{128,136,144,1..., dimensions={0}, use_global_device_ids=true | all-gather | bytes 245760 | tf_op jit(solution)/shard_map/all_gather | solution.py:623
  13.1 1.3 %collective-permute-start = (f32[4,3,2,16,128]{4,3,2,1,0:T(8,128)S(1)}, f32[4,3,2,16,128]{4,3,2,1,0:T(8,128)S(1)}, u32[]{:S(2)}, u32[]{:S(2)}) collective-permute-start(f32[4,3,2,16,128]{4,3,2,1,0:T(8,128)S(1)} %bitcast.31), channel_id=1, source_target_pairs={{0,1},{1,2},{2,3},{3,4},{4,5},{5,6},{6,7},{9,8},{10,9},{11,10},{12... | collective-permute-start | bytes 589832 | tf_op jit(solution)/shard_map/ppermute | solution.py:602
  14.3 1.3 %collective-permute-start.1 = (f32[4,3,2,16,128]{4,3,2,1,0:T(8,128)S(1)}, f32[4,3,2,16,128]{4,3,2,1,0:T(8,128)S(1)}, u32[]{:S(2)}, u32[]{:S(2)}) collective-permute-start(f32[4,3,2,16,128]{4,3,2,1,0:T(8,128)S(1)} %bitcast.32), channel_id=1, source_target_pairs={{0,32},{16,48},{32,64},{40,8},{48,80},{56,24},{64,96},{72,40},{80,... | collective-permute-start | bytes 589832 | tf_op jit(solution)/shard_map/ppermute | solution.py:591
  15.7 3.8 %collective-permute-done = f32[4,3,2,16,128]{4,3,2,1,0:T(8,128)S(1)} collective-permute-done((f32[4,3,2,16,128]{4,3,2,1,0:T(8,128)S(1)}, f32[4,3,2,16,128]{4,3,2,1,0:T(8,128)S(1)}, u32[]{:S(2)}, u32[]{:S(2)}) %collective-permute-start) | collective-permute-done | bytes 196640 | tf_op jit(solution)/shard_map/ppermute | solution.py:602
  19.5 2.1 %all-gather.1 = f32[8,3,2,16,128]{4,3,2,1,0:T(8,128)S(1)} all-gather(f32[4,3,2,16,128]{4,3,2,1,0:T(8,128)S(1)} %collective-permute-done), channel_id=3, replica_groups={{0,8},{16,24},{32,40},{48,56},{64,72},{80,88},{96,104},{112,120},{128,1..., dimensions={0}, use_global_device_ids=true | all-gather | bytes 589824 | tf_op jit(solution)/shard_map/all_gather | solution.py:620
  21.7 1.3 %collective-permute-start.2 = (f32[76,8,128]{2,1,0:T(8,128)S(1)}, f32[76,8,128]{2,1,0:T(8,128)S(1)}, u32[]{:S(2)}, u32[]{:S(2)}) collective-permute-start(f32[76,8,128]{2,1,0:T(8,128)S(1)} %pad_maximum_fusion.2), channel_id=1, source_target_pairs={{0,32},{16,48},{32,64},{40,8},{48,80},{56,24},{64,96},{72,40},{80,... | collective-permute-start | bytes 933896 | tf_op jit(solution)/shard_map/ppermute | solution.py:591
  23.1 0.0 collective-permute-done.1
  23.1 6.2 %collective-permute-done.2 = f32[76,8,128]{2,1,0:T(8,128)S(1)} collective-permute-done((f32[76,8,128]{2,1,0:T(8,128)S(1)}, f32[76,8,128]{2,1,0:T(8,128)S(1)}, u32[]{:S(2)}, u32[]{:S(2)}) %collective-permute-start.2) | collective-permute-done | bytes 311328 | tf_op jit(solution)/shard_map/ppermute | solution.py:591
  29.4 2.5 %all-gather.2 = f32[248,8,128]{2,1,0:T(8,128)S(1)} all-gather(f32[124,8,128]{2,1,0:T(8,128)S(1)} %pad_maximum_fusion.1), channel_id=4, replica_groups={{0,8},{16,24},{32,40},{48,56},{64,72},{80,88},{96,104},{112,120},{128,1..., dimensions={0}, use_global_device_ids=true | all-gather | bytes 1523712 | tf_op jit(solution)/shard_map/all_gather | solution.py:620
  31.9 2.3 %pre0.1 = (f32[7,10,32,128]{3,2,1,0:T(8,128)S(1)}, f32[6,3,16,128]{3,2,1,0:T(8,128)S(1)}, f32[4,16,128]{2,1,0:T(8,128)S(1)}) custom-call(f32[4,3,2,48,128]{4,3,2,1,0:T(8,128)S(1)} %pad_maximum_fusion.own, f32[2,124,8,128]{3,2,1,0:T(8,128)S(1)} %bitcast.26), custom_call_target="tpu_custom_call" | custom-call | tf_op jit(solution)/shard_map/pre0/pallas_call | solution.py:555
  34.2 1.3 %collective-permute-start.3 = (f32[4,3,16,128]{3,2,1,0:T(8,128)S(1)}, f32[4,3,16,128]{3,2,1,0:T(8,128)S(1)}, u32[]{:S(2)}, u32[]{:S(2)}) collective-permute-start(f32[4,3,16,128]{3,2,1,0:T(8,128)S(1)} %slice.54), channel_id=1, source_target_pairs={{0,32},{16,48},{32,64},{40,8},{48,80},{56,24},{64,96},{72,40},{80,... | collective-permute-start | bytes 294920 | tf_op jit(solution)/shard_map/ppermute | solution.py:591
  35.5 1.3 %collective-permute-start.4 = (f32[6,3,8,128]{3,2,1,0:T(8,128)S(1)}, f32[6,3,8,128]{3,2,1,0:T(8,128)S(1)}, u32[]{:S(2)}, u32[]{:S(2)}) collective-permute-start(f32[6,3,8,128]{3,2,1,0:T(8,128)S(1)} %slice.55), channel_id=1, source_target_pairs={{0,64},{16,80},{32,96},{48,112},{64,128},{72,8},{80,144},{88,24},{... | collective-permute-start | bytes 221192 | tf_op jit(solution)/shard_map/ppermute | solution.py:591
  36.8 4.7 %collective-permute-done.4 = f32[6,3,8,128]{3,2,1,0:T(8,128)S(1)} collective-permute-done((f32[6,3,8,128]{3,2,1,0:T(8,128)S(1)}, f32[6,3,8,128]{3,2,1,0:T(8,128)S(1)}, u32[]{:S(2)}, u32[]{:S(2)}) %collective-permute-start.4) | collective-permute-done | bytes 73760 | tf_op jit(solution)/shard_map/ppermute | solution.py:591
  41.5 0.0 collective-permute-done.3
  41.5 3.5 %all-gather.3 = f32[84,8,128]{2,1,0:T(8,128)S(1)} all-gather(f32[42,8,128]{2,1,0:T(8,128)S(1)} %pad_maximum_fusion.4), channel_id=5, replica_groups={{0,8},{16,24},{32,40},{48,56},{64,72},{80,88},{96,104},{112,120},{128,1..., dimensions={0}, use_global_device_ids=true | all-gather | bytes 516096 | tf_op jit(solution)/shard_map/all_gather | solution.py:620
  45.0 1.3 %pre1.1 = (f32[16,256]{1,0:T(8,128)S(1)}, f32[8,256]{1,0:T(8,128)S(1)}, f32[22,16,128]{2,1,0:T(8,128)S(1)}, f32[3,22,16,128]{3,2,1,0:T(8,128)S(1)}, f32[22,16,12...) custom-call(f32[6,3,16,128]{3,2,1,0:T(8,128)S(1)} %get-tuple-element.16.ow, ...), custom_call_target="tpu_custom_call" | custom-call | tf_op jit(solution)/shard_map/pre1/pallas_call | solution.py:555
  46.3 24.8 %all_to_all.17 = f32[16,1,256]{2,1,0:T(1,128)S(1)} all-to-all(f32[16,1,256]{2,1,0:T(1,128)S(1)} %copy.4), channel_id=1, replica_groups={{0,32,64,96,128,160,192,224,256,288,320,352,384,416,448,480},{8,40,72,1..., dimensions={0} | all-to-all | bytes 32768 | tf_op jit(solution)/shard_map/all_to_all | solution.py:641
  71.2 16.7 %all_to_all.18 = f32[16,24,256]{2,1,0:T(8,128)S(1)} all-to-all(f32[16,24,256]{2,1,0:T(8,128)S(1)} %broadcast_in_dim.3), channel_id=1, replica_groups={{0,1,2,3,4,5,6,7,16,17,18,19,20,21,22,23},{8,9,10,11,12,13,14,15,24,25,..., dimensions={0} | all-to-all | bytes 786432 | tf_op jit(solution)/shard_map/all_to_all | solution.py:644
  87.9 4.9 %all-gather.4.packed = f32[32,24,256]{2,1,0:T(8,128)S(1)} all-gather(f32[16,24,256]{2,1,0:T(8,128)S(1)} %all_to_all.18), channel_id=6, replica_groups={{0,8},{16,24},{32,40},{48,56},{64,72},{80,88},{96,104},{112,120},{128,1..., dimensions={0}, use_global_device_ids=true | all-gather | bytes 1179648 | tf_op jit(solution)/shard_map/all_gather | solution.py:620
  92.8 5.5 %finish.1 = f32[2,16,128]{2,1,0:T(8,128)} custom-call(f32[32,24,256]{2,1,0:T(8,128)S(1)} %all-gather.4.packed, f32[22,16,128]{2,1,0:T(8,128)S(1)} %get-tuple-element.20.field1, f32[3,22,16,128]{3,2,1,0:T(8,128)S(1)} %get-tuple-element.21.region1, f32[22,16,128]{2,1,0:T(8,128)S(1)} %get-tuple-element.22.inverse1, ...), custom_call_target="tpu_custom_call" | custom-call | tf_op jit(solution)/shard_map/finish/pallas_call | solution.py:555
  (16 shorter events, 0.3 us)
Async XLA Ops:
  13.1 6.4 %collective-permute-start = (f32[4,3,2,16,128]{4,3,2,1,0:T(8,128)S(1)}, f32[4,3,2,16,128]{4,3,2,1,0:T(8,128)S(1)}, u32[]{:S(2)}, u32[]{:S(2)}) collective-permute-start(f32[4,3,2,16,128]{4,3,2,1,0:T(8,128)S(1)} %bitcast.31), channel_id=1, source_target_pairs={{0,1},{1,2},{2,3},{3,4},{4,5},{5,6},{6,7},{9,8},{10,9},{11,10},{12... | collective-permute-start | bytes 589832 | tf_op jit(solution)/shard_map/ppermute | solution.py:602
  14.3 8.7 %collective-permute-start.1 = (f32[4,3,2,16,128]{4,3,2,1,0:T(8,128)S(1)}, f32[4,3,2,16,128]{4,3,2,1,0:T(8,128)S(1)}, u32[]{:S(2)}, u32[]{:S(2)}) collective-permute-start(f32[4,3,2,16,128]{4,3,2,1,0:T(8,128)S(1)} %bitcast.32), channel_id=1, source_target_pairs={{0,32},{16,48},{32,64},{40,8},{48,80},{56,24},{64,96},{72,40},{80,... | collective-permute-start | bytes 589832 | tf_op jit(solution)/shard_map/ppermute | solution.py:591
  21.7 7.6 %collective-permute-start.2 = (f32[76,8,128]{2,1,0:T(8,128)S(1)}, f32[76,8,128]{2,1,0:T(8,128)S(1)}, u32[]{:S(2)}, u32[]{:S(2)}) collective-permute-start(f32[76,8,128]{2,1,0:T(8,128)S(1)} %pad_maximum_fusion.2), channel_id=1, source_target_pairs={{0,32},{16,48},{32,64},{40,8},{48,80},{56,24},{64,96},{72,40},{80,... | collective-permute-start | bytes 933896 | tf_op jit(solution)/shard_map/ppermute | solution.py:591
  34.2 7.3 %collective-permute-start.3 = (f32[4,3,16,128]{3,2,1,0:T(8,128)S(1)}, f32[4,3,16,128]{3,2,1,0:T(8,128)S(1)}, u32[]{:S(2)}, u32[]{:S(2)}) collective-permute-start(f32[4,3,16,128]{3,2,1,0:T(8,128)S(1)} %slice.54), channel_id=1, source_target_pairs={{0,32},{16,48},{32,64},{40,8},{48,80},{56,24},{64,96},{72,40},{80,... | collective-permute-start | bytes 294920 | tf_op jit(solution)/shard_map/ppermute | solution.py:591
  35.5 6.0 %collective-permute-start.4 = (f32[6,3,8,128]{3,2,1,0:T(8,128)S(1)}, f32[6,3,8,128]{3,2,1,0:T(8,128)S(1)}, u32[]{:S(2)}, u32[]{:S(2)}) collective-permute-start(f32[6,3,8,128]{3,2,1,0:T(8,128)S(1)} %slice.55), channel_id=1, source_target_pairs={{0,64},{16,80},{32,96},{48,112},{64,128},{72,8},{80,144},{88,24},{... | collective-permute-start | bytes 221192 | tf_op jit(solution)/shard_map/ppermute | solution.py:591

commit v9 on v8

--- a/solution.py
+++ b/solution.py
@@ -201,7 +201,7 @@
 
 
 def pre0_kernel(
-    own, outer, kept_out, tile_out, absorb_out,
+    own, outer, kept_out, rest_out, beta_out, diag_out, absorb_out,
     diag, inverse, first, second, third, one, two, tmp,
 ):
     zero = jnp.zeros((8, LANES), jnp.float32)
@@ -249,35 +249,28 @@
     betas = coarse_rows(tmp.at[0:8], pairs(beta(4, 20)))
     wide = coarse_rows(tmp.at[8:14], pairs(absorb(6, 18)))
     rest = [residual(shape, source, parts, current, p, p + 2) for p in range(6, 18, 2)]
-    tile_out[:, 0] = coarse_rows(tmp.at[14:20], jnp.stack([x[0] + x[1] for x in rest]))
+    rest_out[...] = coarse_rows(tmp.at[14:20], jnp.stack([x[0] + x[1] for x in rest]))
     here = betas[1:7]
     _, _, share = coarse.faces(here, half)
-    tile_out[:, 1] = here
-    tile_out[:, 2] = wide + half * (here + betas[0:6]) + half * (here + betas[2:8]) + share
+    beta_out[...] = betas
+    diag_out[...] = wide + half * (here + betas[0:6]) + half * (here + betas[2:8]) + share
     absorb_out[...] = wide[1:5]
 
 
-DEPTH1 = 22
+DEPTH1 = 16
 ROWS1 = 16
 
 
-def gather_level1(region, own, outer):
-    zero = jnp.zeros((4, LANES), jnp.float32)
-    for plane in range(DEPTH1):
-        for kind in range(3):
-            if 5 <= plane < 17:
-                part, index = divmod(plane - 5, 4)
-                if part == 1:
-                    region[kind, plane] = own[index + 1, kind]
-                else:
-                    at = 6 * index + 2 * kind
-                    region[kind, plane, 0:8, :] = outer[part // 2, at]
-                    region[kind, plane, 8:16, :] = outer[part // 2, at + 1]
-            else:
-                part, index = (0, plane) if plane < 5 else (1, plane - 16)
-                region[kind, plane, 0:4, :] = zero
-                region[kind, plane, 4:12, :] = outer[part, 24 + 3 * index + kind]
-                region[kind, plane, 12:16, :] = zero
+def gather_level1(region, rest, beta, diag, outer):
+    region[0, 1:6] = outer[0, 0:5]
+    region[0, 6:10] = rest[1:5]
+    region[0, 10:15] = outer[1, 0:5]
+    region[1, 0:6] = outer[0, 5:11]
+    region[1, 6:10] = beta[2:6]
+    region[1, 10:16] = outer[1, 5:11]
+    region[2, 1:6] = outer[0, 11:16]
+    region[2, 6:10] = diag[1:5]
+    region[2, 10:15] = outer[1, 11:16]
 
 
 CHUNK1 = 4
@@ -286,13 +279,13 @@
 def level1_parts(shape, region, inverse, first, second, third):
     half = face(1)
     beta = region.at[1]
-    for start in range(0, DEPTH1, CHUNK1):
-        stop = min(start + CHUNK1, DEPTH1)
+    first[0:1] = half * (beta[0:1] + beta[1:2])
+    for start in range(1, DEPTH1 - 1, CHUNK1):
+        stop = min(start + CHUNK1, DEPTH1 - 1)
         here = beta[start:stop]
         second[start:stop], third[start:stop], _ = shape.faces(here, half)
         inverse[start:stop] = jnp.where(here > 0.0, 1.0 / region[2, start:stop], 0.0)
-        stop = min(stop, DEPTH1 - 1)
-        first[start:stop] = half * (beta[start:stop] + beta[start + 1 : stop + 1])
+        first[start:stop] = half * (here + beta[start + 1 : stop + 1])
 
 
 def coarser_rows(ref, value, start):
@@ -308,37 +301,37 @@
 
 
 def pre1_kernel(
-    own, outer, absorb, pay_out, rows_out, field, region, inverse, first, second, third,
-    two, tmp, tile,
+    rest1, beta1, diag1, outer, absorb, pay_out, region, inverse, first, second, third,
+    one, two, tmp, tile,
 ):
-    gather_level1(region, own, outer)
+    gather_level1(region, rest1, beta1, diag1, outer)
     shape = Packed(2, ROWS1, False)
     level1_parts(shape, region, inverse, first, second, third)
     source = lambda start, stop: region[0, start:stop]
     parts = (region.at[2], inverse, first, second, third)
     table = chebyshev_table(SWEEPS)
-    begin(table, inverse, source, (two, field), 0, DEPTH1, CHUNK1)
-    ranges = [(order, DEPTH1 - order) for order in range(1, SWEEPS)]
+    begin(table, inverse, source, (one, two), 2, 14, CHUNK1)
+    ranges = [(2 + order, 14 - order) for order in range(1, SWEEPS)]
     current, _ = sweep(
-        shape, list(enumerate(table))[1:], source, parts, (two, field), ranges, CHUNK1
-    )
-    rest = residual(shape, source, parts, current, 9, 13)
-    totals = [pairs(rest), pairs(region[1, 9:13]), pairs(absorb[...])]
+        shape, list(enumerate(table))[1:], source, parts, (one, two), ranges, CHUNK1
+    )
+    rest = residual(shape, source, parts, current, 6, 10)
+    totals = [pairs(rest), pairs(region[1, 6:10]), pairs(absorb[...])]
     rows = coarser_rows(tmp, jnp.concatenate(totals), 6)
     for at in range(6):
         tile[at : at + 1, :] = rows[at]
     tile[6:8, :] = jnp.zeros((2, LANES), jnp.float32)
-    kind = 2 * (position() % LAYER)
-    for side in range(2):
-        part = tile[pl.ds(kind + side, 1), :]
-        pay_out[:, side * LANES : (side + 1) * LANES] = jnp.broadcast_to(part, (16, LANES))
-    base = 3 + 4 * (position() % LAYER)
-    for plane in range(4):
-        row, lane = 4 * (plane % 2), plane // 2 * LANES
-        rows_out[row : row + 4, lane : lane + LANES] = current[base + plane, 6:10, :]
+    member = position() % LAYER
+    tile[8:10, :] = tile[pl.ds(2 * member, 2), :]
+    tile[10:12, :] = jnp.zeros((2, LANES), jnp.float32)
+    tile[12:16, :] = current[6 + member, 6:10, :]
+    whole = tile[8:16, :]
+    for slot in range(16):
+        pay_out[slot] = whole
 
 
 DEPTH2 = 32
+SLOT = 48
 KIND_AT = (0, 2, 1)
 ROWS2 = 8
 
@@ -420,18 +413,13 @@
             ref[pl.ds(32 * block + offset, 8, stride=4), :] = moved[8 * block : 8 * block + 8]
 
 
-def solve23(packed, halves, rows2, parts2, one2, two2, tall):
+def solve23(gathered, rows2, parts2, one2, two2, tall):
     shape = Packed(4, ROWS2, True)
     zero = jnp.zeros((ROWS2, LANES), jnp.float32)
-    for peer in range(32):
-        for side in range(2):
-            halves[side, 16 * peer : 16 * peer + 16, :] = packed[
-                peer, 0:16, side * LANES : (side + 1) * LANES
-            ]
     for number in range(3):
         for plane in range(DEPTH2):
-            at = 128 * KIND_AT[number] + plane // 2
-            rows2[number, plane + 1] = halves[plane % 2, pl.ds(at, 8, stride=16), :]
+            at = SLOT * 8 * KIND_AT[number] + plane
+            rows2[number, plane + 1] = gathered[pl.ds(at, 8, stride=SLOT), :]
     for ref in (rows2.at[1], one2, two2):
         ref[0] = zero
         ref[DEPTH2 + 1] = zero
@@ -459,7 +447,7 @@
     return current
 
 
-def post1(packed, field, whole, region, parts, one, two, wide, tmp):
+def post1(packed, whole, region, parts, one, two, wide, tmp):
     inverse, first, second, third = parts
     shape = Packed(2, ROWS1, False)
     layer = position() // LAYER
@@ -481,25 +469,25 @@
         for pair in range(8):
             tmp[pair, pl.ds(offset, 8, stride=4), :] = picked[pair]
     place = column_position()
-    before, after = jnp.maximum(place - 1, 0), jnp.minimum(place + 1, 7)
-    has_before = jnp.where(place > 0, 1.0, 0.0)
-    has_after = jnp.where(place < 7, 1.0, 0.0)
-    row = lax.broadcasted_iota(jnp.int32, (2, 8, LANES), 1)
-    inside = (row >= 2) & (row < 6)
-
-    def neighbour(start, who, there):
-        member, half = divmod((start - 3) // 2, 2)
+    columns = (
+        (jnp.maximum(place - 1, 0), jnp.where(place > 0, 1.0, 0.0)),
+        (place, 1.0),
+        (jnp.minimum(place + 1, 7), jnp.where(place < 7, 1.0, 0.0)),
+    )
+    blank = jnp.zeros((2, LANES), jnp.float32)
+    for plane in range(DEPTH1):
+        member = (plane - 6) % LAYER
         at = 16 * (member % 2) + 8 * (member // 2)
-        value = there * packed[at + who, 16:24, half * LANES : (half + 1) * LANES]
-        return jnp.stack([across(value, -2), across(value, 2)])
-
-    for start in range(3, 19, 2):
-        here = field[start : start + 2]
-        upper = jnp.where(inside, neighbour(start, before, has_before), here[:, 0:8])
-        lower = jnp.where(inside, neighbour(start, after, has_after), here[:, 8:16])
-        one[start : start + 2] = jnp.concatenate([upper, lower], 1) + tmp[(start - 3) // 2, 2:18, :]
+        row = 32 + 4 * (plane // LAYER)
+        one[plane, 0:2, :] = blank
+        for number, (who, there) in enumerate(columns):
+            start = 2 + 4 * number
+            one[plane, start : start + 4, :] = there * packed[at + who, row : row + 4, :]
+        one[plane, 14:16, :] = blank
+    for plane in range(DEPTH1):
+        one[plane] = one[plane] + tmp[plane // 2, 2:18, :]
     table = chebyshev_table(SWEEPS)
-    ranges = [(3 + order, 19 - order) for order in range(1, SWEEPS + 1)]
+    ranges = [(order, DEPTH1 - order) for order in range(1, SWEEPS + 1)]
     current, _ = sweep(
         shape, list(enumerate(table)), lambda start, stop: region[0, start:stop],
         (region.at[2], inverse, first, second, third), (one, two), ranges, CHUNK1,
@@ -512,7 +500,7 @@
     parts = tuple(kept.at[number] for number in range(2, 7))
     member = position() % LAYER
     shape = Packed(1, ROWS0, False)
-    value = jnp.stack([coarse[7 + member + pair, 4:12, :] for pair in range(5)])
+    value = jnp.stack([coarse[4 + member + pair, 4:12, :] for pair in range(5)])
     even = (lax.broadcasted_iota(jnp.int32, value.shape, 2) & 1) == 0
     upper_rows = jnp.where(even, value, along(value, -1))
     lower_rows = jnp.where(even, along(value, 1), value)
@@ -532,14 +520,14 @@
 
 
 def finish_kernel(
-    packed, field1, region1, inverse1, first1, second1, third1, kept0, out,
-    halves, rows2, diag2, inverse2, first2, second2, third2, one2, two2, tall,
+    gathered, packed, region1, inverse1, first1, second1, third1, kept0, out,
+    rows2, diag2, inverse2, first2, second2, third2, one2, two2, tall,
     one1, two1, wide1, tmp1, one0, two0, tmp0,
 ):
     parts2 = (diag2, inverse2, first2, second2, third2)
-    whole = solve23(packed, halves, rows2, parts2, one2, two2, tall)
+    whole = solve23(gathered, rows2, parts2, one2, two2, tall)
     parts1 = (inverse1, first1, second1, third1)
-    coarse = post1(packed, field1, whole, region1, parts1, one1, two1, wide1, tmp1)
+    coarse = post1(packed, whole, region1, parts1, one1, two1, wide1, tmp1)
     post0(kept0, coarse, out, one0, two0, tmp0)
 
 
@@ -564,14 +552,15 @@
 def pre0(*pieces):
     plane = buffer(24, ROWS0, LANES)
     scratch = [plane] * 7 + [buffer(20, 64, LANES)]
-    out = (f32(7, KEPT0, KEPT_ROWS0, LANES), f32(6, 3, ROWS1, LANES), f32(4, ROWS1, LANES))
+    coarse = lambda count: f32(count, ROWS1, LANES)
+    out = (f32(7, KEPT0, KEPT_ROWS0, LANES), coarse(6), coarse(8), coarse(6), coarse(4))
     return call(pre0_kernel, out, scratch, "pre0", *pieces)
 
 
 def pre1(*pieces):
-    plane = f32(DEPTH1, ROWS1, LANES)
-    scratch = [buffer(DEPTH1, ROWS1, LANES), buffer(6, ROWS1, LANES), buffer(8, LANES)]
-    out = (f32(16, 2 * LANES), f32(8, 2 * LANES), plane, f32(3, DEPTH1, ROWS1, LANES)) + (plane,) * 4
+    plane, work = f32(DEPTH1, ROWS1, LANES), buffer(DEPTH1, ROWS1, LANES)
+    scratch = [work, work, buffer(6, ROWS1, LANES), buffer(16, LANES)]
+    out = (f32(16, 8, LANES), f32(3, DEPTH1, ROWS1, LANES)) + (plane,) * 4
     return call(pre1_kernel, out, scratch, "pre1", *pieces)
 
 
@@ -579,7 +568,7 @@
     plane2 = buffer(DEPTH2 + 2, ROWS2, LANES)
     plane1 = buffer(DEPTH1, ROWS1, LANES)
     plane0 = buffer(KEPT0, KEPT_ROWS0, LANES)
-    scratch = [buffer(2, 512, LANES), buffer(3, DEPTH2 + 2, ROWS2, LANES)] + [plane2] * 7 + [buffer(3, 128, LANES)]
+    scratch = [buffer(3, DEPTH2 + 2, ROWS2, LANES)] + [plane2] * 7 + [buffer(3, 128, LANES)]
     scratch += [plane1] * 2 + [buffer(DEPTH2 + 6, 24, LANES), buffer(8, 32, LANES)]
     scratch += [plane0] * 2 + [buffer(5, KEPT_ROWS0, LANES)]
     return call(finish_kernel, f32(2, 16, LANES), scratch, "finish", *pieces)
@@ -633,17 +622,23 @@
     near2 = jnp.where(first_core, ends[2:, :2], ends[:2, :2])
     near3 = jnp.where(first_core, ends[1:, 2], ends[:3, 2])
     rest = layers_apart(tiles_of([rims, near2[:, 0], near2[:, 1], near3]), 1)
-    kept0, tile, absorb1 = pre0(layer, both(tiles_of([outer, rest])))
-
-    tiles = tiles_of([layers_apart(tile[1:5], 1), layers_apart(tile[..., 4:12, :], 2)])
-    pay, rows1, *kept1 = pre1(tile, both(tiles), absorb1)
+    kept0, rest1, beta1, diag1, absorb1 = pre0(layer, both(tiles_of([outer, rest])))
+
+    upwards = jnp.concatenate([rest1[0:5], beta1[0:6], diag1[0:5]])
+    downwards = jnp.concatenate([rest1[1:6], beta1[2:8], diag1[1:6]])
+    outer = both(layers_apart(jnp.where(first_core, upwards, downwards), 1))
+    pay, *kept1 = pre1(rest1, beta1, diag1, outer, absorb1)
 
     rows = lax.all_to_all(pay, "gx", 0, 0, axis_index_groups=column)
-    rows = jnp.concatenate([rows, rows1])
+    place = lax.axis_index("gx")
+    start = place // LAYER + jnp.where(place % LAYER < 2, 1, 0)
+    fields = jnp.pad(rows[:, 4:8], ((2, 2), (0, 0), (0, 0)))
+    fields = lax.dynamic_slice_in_dim(fields, start, 4)
+    rows = jnp.concatenate([rows[:, 0:2].reshape(-1, LANES), fields.reshape(-1, LANES)])
     rows = jnp.broadcast_to(rows, (2 * wide,) + rows.shape)
     rows = lax.all_to_all(rows, ("gx", "gy"), 0, 0, axis_index_groups=cores)
-    packed = both(rows).reshape(-1, *rows.shape[1:])
-    return finish(packed, *kept1, kept0)
+    packed = both(rows).reshape(-1, SLOT, LANES)
+    return finish(packed.reshape(-1, LANES), packed, *kept1, kept0)
 
 
 def solution(mesh):

time: 98.8 us -> 97.3 us (0.985)
  blocking collectives: 66.8 us -> 40.7 us
  starting transfers between devices: 6.45 us -> 19.5 us
  waiting for transfers between devices: 14.8 us -> 26.1 us
    all_to_all x1 -> x0, blocking collectives: 24.8 us -> none  [body(): rows = lax.all_to_all(pay, 'gx', 0, 0, axis_index_groups=column)]
    all_to_all x0 -> x1, starting transfers between devices: none -> 14.3 us  [body(): rows = lax.all_to_all(pay, 'gx', 0, 0, axis_index_groups=column)]
    all_to_all x0 -> x1, waiting for transfers between devices: none -> 11.7 us  [body(): rows = lax.all_to_all(pay, 'gx', 0, 0, axis_index_groups=column)]
    ppermute x4 -> x3, starting transfers between devices: 5.17 us -> 3.88 us  [layers_apart(): lax.ppermute(value, 'gx', [(i, j) for i, j in ways if 0 <= j < count])]
    all_gather x4, blocking collectives: 13 us -> 11.8 us  [both(): return lax.all_gather(value, 'gx', axis_index_groups=chips)]
    ppermute x4 -> x3, waiting for transfers between devices: 10.9 us -> 10.7 us  [layers_apart(): lax.ppermute(value, 'gx', [(i, j) for i, j in ways if 0 <= j < count])]
  transfers between devices with their start and end apart: 5 -> 5, of which waited for: 3 -> 4; matrix products, arithmetic and copies ran while one was open for 0% -> 0% of each run, Pallas kernels for 0% -> 0%
where the time goes in v9:
time: 97.3 us; the launch traced here: 96.8 us
  blocking collectives  40.7 us (42%)
  waiting for transfers between devices  26.1 us (27%)
  starting transfers between devices  19.5 us (20%)
  Pallas kernels  9.22 us (9%)
    all_to_all x1, blocking collectives, body(): rows = lax.all_to_all(rows, ('gx', 'gy'), 0, 0, axis_index_groups=cores)  16.6 us
    all_to_all x1, starting transfers between devices, body(): rows = lax.all_to_all(pay, 'gx', 0, 0, axis_index_groups=column)  14.3 us
    all_gather x1, blocking collectives, body(): own = lax.all_gather(local, 'gx', axis_index_groups=near)  12.3 us
    all_gather x4, blocking collectives, both(): return lax.all_gather(value, 'gx', axis_index_groups=chips)  11.8 us
    all_to_all x1, waiting for transfers between devices, body(): rows = lax.all_to_all(pay, 'gx', 0, 0, axis_index_groups=column)  11.7 us
    ppermute x3, waiting for transfers between devices, layers_apart(): lax.ppermute(value, 'gx', [(i, j) for i, j in ways if 0 <= j < count])  10.7 us
    pallas_call x3, Pallas kernels, call(): pl.pallas_call(kernel, out_shape=out, scratch_shapes=scratch, name=name,...  9.22 us
    ppermute x3, starting transfers between devices, layers_apart(): lax.ppermute(value, 'gx', [(i, j) for i, j in ways if 0 <= j < count])  3.88 us
  transfers between devices with their start and end apart: 5, of which 4 were waited for; matrix products, arithmetic and copies ran while one was open for 0% of the time, Pallas kernels for 0%

profile of v9, /device:TPU:1, one launch (start us, length us, event | category | flops | bytes accessed | tf_op | source)
XLA Modules:
  0.0 96.8 jit_solution(5743348559000230602)
XLA Ops:
  0.0 0.8 pad_maximum_fusion.5
  0.8 12.3 %all-gather = f32[12,2,16,128]{3,2,1,0:T(8,128)S(1)} all-gather(f32[3,2,16,128]{3,2,1,0:T(8,128)S(1)} %pad_maximum_fusion.5), channel_id=2, replica_groups={{0,8,16,24},{32,40,48,56},{64,72,80,88},{96,104,112,120},{128,136,144,1..., dimensions={0}, use_global_device_ids=true | all-gather | bytes 245760 | tf_op jit(solution)/shard_map/all_gather | solution.py:612
  13.1 1.3 %collective-permute-start = (f32[4,3,2,16,128]{4,3,2,1,0:T(8,128)S(1)}, f32[4,3,2,16,128]{4,3,2,1,0:T(8,128)S(1)}, u32[]{:S(2)}, u32[]{:S(2)}) collective-permute-start(f32[4,3,2,16,128]{4,3,2,1,0:T(8,128)S(1)} %bitcast.28), channel_id=1, source_target_pairs={{0,1},{1,2},{2,3},{3,4},{4,5},{5,6},{6,7},{9,8},{10,9},{11,10},{12... | collective-permute-start | bytes 589832 | tf_op jit(solution)/shard_map/ppermute | solution.py:591
  14.3 1.3 %collective-permute-start.1 = (f32[4,3,2,16,128]{4,3,2,1,0:T(8,128)S(1)}, f32[4,3,2,16,128]{4,3,2,1,0:T(8,128)S(1)}, u32[]{:S(2)}, u32[]{:S(2)}) collective-permute-start(f32[4,3,2,16,128]{4,3,2,1,0:T(8,128)S(1)} %bitcast.29), channel_id=1, source_target_pairs={{0,32},{16,48},{32,64},{40,8},{48,80},{56,24},{64,96},{72,40},{80,... | collective-permute-start | bytes 589832 | tf_op jit(solution)/shard_map/ppermute | solution.py:580
  15.7 3.8 %collective-permute-done = f32[4,3,2,16,128]{4,3,2,1,0:T(8,128)S(1)} collective-permute-done((f32[4,3,2,16,128]{4,3,2,1,0:T(8,128)S(1)}, f32[4,3,2,16,128]{4,3,2,1,0:T(8,128)S(1)}, u32[]{:S(2)}, u32[]{:S(2)}) %collective-permute-start) | collective-permute-done | bytes 196640 | tf_op jit(solution)/shard_map/ppermute | solution.py:591
  19.5 2.1 %all-gather.1 = f32[8,3,2,16,128]{4,3,2,1,0:T(8,128)S(1)} all-gather(f32[4,3,2,16,128]{4,3,2,1,0:T(8,128)S(1)} %collective-permute-done), channel_id=3, replica_groups={{0,8},{16,24},{32,40},{48,56},{64,72},{80,88},{96,104},{112,120},{128,1..., dimensions={0}, use_global_device_ids=true | all-gather | bytes 589824 | tf_op jit(solution)/shard_map/all_gather | solution.py:609
  21.7 1.3 %collective-permute-start.2 = (f32[76,8,128]{2,1,0:T(8,128)S(1)}, f32[76,8,128]{2,1,0:T(8,128)S(1)}, u32[]{:S(2)}, u32[]{:S(2)}) collective-permute-start(f32[76,8,128]{2,1,0:T(8,128)S(1)} %pad_maximum_fusion.2), channel_id=1, source_target_pairs={{0,32},{16,48},{32,64},{40,8},{48,80},{56,24},{64,96},{72,40},{80,... | collective-permute-start | bytes 933896 | tf_op jit(solution)/shard_map/ppermute | solution.py:580
  23.1 0.0 collective-permute-done.1
  23.1 6.2 %collective-permute-done.2 = f32[76,8,128]{2,1,0:T(8,128)S(1)} collective-permute-done((f32[76,8,128]{2,1,0:T(8,128)S(1)}, f32[76,8,128]{2,1,0:T(8,128)S(1)}, u32[]{:S(2)}, u32[]{:S(2)}) %collective-permute-start.2) | collective-permute-done | bytes 311328 | tf_op jit(solution)/shard_map/ppermute | solution.py:580
  29.4 2.5 %all-gather.2 = f32[248,8,128]{2,1,0:T(8,128)S(1)} all-gather(f32[124,8,128]{2,1,0:T(8,128)S(1)} %pad_maximum_fusion.1), channel_id=4, replica_groups={{0,8},{16,24},{32,40},{48,56},{64,72},{80,88},{96,104},{112,120},{128,1..., dimensions={0}, use_global_device_ids=true | all-gather | bytes 1523712 | tf_op jit(solution)/shard_map/all_gather | solution.py:609
  31.9 2.3 %pre0.1 = (f32[7,10,32,128]{3,2,1,0:T(8,128)S(1)}, f32[6,16,128]{2,1,0:T(8,128)S(1)}, f32[8,16,128]{2,1,0:T(8,128)S(1)}, f32[6,16,128]{2,1,0:T(8,128)S(1)}, f32[4,16,128]{2,1,0:T(8,128)S(1)}) custom-call(f32[4,3,2,48,128]{4,3,2,1,0:T(8,128)S(1)} %pad_maximum_fusion.own, f32[2,124,8,128]{3,2,1,0:T(8,128)S(1)} %bitcast.24), custom_call_target="tpu_custom_call" | custom-call | tf_op jit(solution)/shard_map/pre0/pallas_call | solution.py:543
  34.2 1.3 %collective-permute-start.3 = (f32[16,16,128]{2,1,0:T(8,128)S(1)}, f32[16,16,128]{2,1,0:T(8,128)S(1)}, u32[]{:S(2)}, u32[]{:S(2)}) collective-permute-start(f32[16,16,128]{2,1,0:T(8,128)S(1)} %maximum_select_fusion), channel_id=1, source_target_pairs={{0,32},{16,48},{32,64},{40,8},{48,80},{56,24},{64,96},{72,40},{80,... | collective-permute-start | bytes 393224 | tf_op jit(solution)/shard_map/ppermute | solution.py:580
  35.5 4.4 %collective-permute-done.3 = f32[16,16,128]{2,1,0:T(8,128)S(1)} collective-permute-done((f32[16,16,128]{2,1,0:T(8,128)S(1)}, f32[16,16,128]{2,1,0:T(8,128)S(1)}, u32[]{:S(2)}, u32[]{:S(2)}) %collective-permute-start.3) | collective-permute-done | bytes 131104 | tf_op jit(solution)/shard_map/ppermute | solution.py:580
  39.9 2.0 %all-gather.3 = f32[32,16,128]{2,1,0:T(8,128)S(1)} all-gather(f32[16,16,128]{2,1,0:T(8,128)S(1)} %collective-permute-done.3), channel_id=5, replica_groups={{0,8},{16,24},{32,40},{48,56},{64,72},{80,88},{96,104},{112,120},{128,1..., dimensions={0}, use_global_device_ids=true | all-gather | bytes 393216 | tf_op jit(solution)/shard_map/all_gather | solution.py:609
  41.9 1.5 %pre1.1 = (f32[16,8,128]{2,1,0:T(8,128)}, f32[3,16,16,128]{3,2,1,0:T(8,128)S(1)}, f32[16,16,128]{2,1,0:T(8,128)S(1)}, f32[16,16,128]{2,1,0:T(8,128)S(1)}, f32[16...) custom-call(f32[6,16,128]{2,1,0:T(8,128)S(1)} %get-tuple-element.16.rest1, f32[8,16,128]{2,1,0:T(8,128)S(1)} %get-tuple-element.17.beta1, ...), custom_call_target="tpu_custom_call" | custom-call | tf_op jit(solution)/shard_map/pre1/pallas_call | solution.py:543
  43.4 14.3 %all-to-all-start = ((f32[16,8,128]{2,1,0:T(8,128)}), f32[16,8,128]{2,1,0:T(8,128)S(1)}, u32[]{:S(2)}, u32[]{:S(2)}) async-start(f32[16,8,128]{2,1,0:T(8,128)} %get-tuple-element.20), calls=%async_computation | async-start | bytes 131072 | tf_op jit(solution)/shard_map/all_to_all | solution.py:632
  57.7 11.7 %all-to-all-done = f32[16,8,128]{2,1,0:T(8,128)S(1)} async-done(((f32[16,8,128]{2,1,0:T(8,128)}), f32[16,8,128]{2,1,0:T(8,128)S(1)}, u32[]{:S(2)}, u32[]{:S(2)}) %all-to-all-start) | async-done | bytes 65568 | tf_op jit(solution)/shard_map/all_to_all | solution.py:632
  69.5 16.6 %all_to_all.10 = f32[16,48,128]{2,1,0:T(8,128)S(1)} all-to-all(f32[16,48,128]{2,1,0:T(8,128)S(1)} %broadcast_in_dim.3), channel_id=1, replica_groups={{0,1,2,3,4,5,6,7,16,17,18,19,20,21,22,23},{8,9,10,11,12,13,14,15,24,25,..., dimensions={0} | all-to-all | bytes 786432 | tf_op jit(solution)/shard_map/all_to_all | solution.py:639
  86.1 5.3 %all-gather.4.packed = f32[32,48,128]{2,1,0:T(8,128)S(1)} all-gather(f32[16,48,128]{2,1,0:T(8,128)S(1)} %all_to_all.10), channel_id=6, replica_groups={{0,8},{16,24},{32,40},{48,56},{64,72},{80,88},{96,104},{112,120},{128,1..., dimensions={0}, use_global_device_ids=true | all-gather | bytes 1179648 | tf_op jit(solution)/shard_map/all_gather | solution.py:609
  91.3 5.5 %finish.1 = f32[2,16,128]{2,1,0:T(8,128)} custom-call(f32[1536,128]{1,0:T(8,128)S(1)} %bitcast.23, f32[32,48,128]{2,1,0:T(8,128)S(1)} %all-gather.4.packed, f32[3,16,16,128]{3,2,1,0:T(8,128)S(1)} %get-tuple-element.21.region1, f32[16,16,128]{2,1,0:T(8,128)S(1)} %get-tuple-element.22.inverse1, f32[16,16,128]{2,1,0:T(8,128)S(1)} %get-tuple-element.23.first1, ...), custom_call_target="tpu_custom_call" | custom-call | tf_op jit(solution)/shard_map/finish/pallas_call | solution.py:543
  (17 shorter events, 0.3 us)
Async XLA Ops:
  13.1 6.4 %collective-permute-start = (f32[4,3,2,16,128]{4,3,2,1,0:T(8,128)S(1)}, f32[4,3,2,16,128]{4,3,2,1,0:T(8,128)S(1)}, u32[]{:S(2)}, u32[]{:S(2)}) collective-permute-start(f32[4,3,2,16,128]{4,3,2,1,0:T(8,128)S(1)} %bitcast.28), channel_id=1, source_target_pairs={{0,1},{1,2},{2,3},{3,4},{4,5},{5,6},{6,7},{9,8},{10,9},{11,10},{12... | collective-permute-start | bytes 589832 | tf_op jit(solution)/shard_map/ppermute | solution.py:591
  14.3 8.7 %collective-permute-start.1 = (f32[4,3,2,16,128]{4,3,2,1,0:T(8,128)S(1)}, f32[4,3,2,16,128]{4,3,2,1,0:T(8,128)S(1)}, u32[]{:S(2)}, u32[]{:S(2)}) collective-permute-start(f32[4,3,2,16,128]{4,3,2,1,0:T(8,128)S(1)} %bitcast.29), channel_id=1, source_target_pairs={{0,32},{16,48},{32,64},{40,8},{48,80},{56,24},{64,96},{72,40},{80,... | collective-permute-start | bytes 589832 | tf_op jit(solution)/shard_map/ppermute | solution.py:580
  21.7 7.6 %collective-permute-start.2 = (f32[76,8,128]{2,1,0:T(8,128)S(1)}, f32[76,8,128]{2,1,0:T(8,128)S(1)}, u32[]{:S(2)}, u32[]{:S(2)}) collective-permute-start(f32[76,8,128]{2,1,0:T(8,128)S(1)} %pad_maximum_fusion.2), channel_id=1, source_target_pairs={{0,32},{16,48},{32,64},{40,8},{48,80},{56,24},{64,96},{72,40},{80,... | collective-permute-start | bytes 933896 | tf_op jit(solution)/shard_map/ppermute | solution.py:580
  34.2 5.7 %collective-permute-start.3 = (f32[16,16,128]{2,1,0:T(8,128)S(1)}, f32[16,16,128]{2,1,0:T(8,128)S(1)}, u32[]{:S(2)}, u32[]{:S(2)}) collective-permute-start(f32[16,16,128]{2,1,0:T(8,128)S(1)} %maximum_select_fusion), channel_id=1, source_target_pairs={{0,32},{16,48},{32,64},{40,8},{48,80},{56,24},{64,96},{72,40},{80,... | collective-permute-start | bytes 393224 | tf_op jit(solution)/shard_map/ppermute | solution.py:580
  43.4 26.0 %all-to-all-start = ((f32[16,8,128]{2,1,0:T(8,128)}), f32[16,8,128]{2,1,0:T(8,128)S(1)}, u32[]{:S(2)}, u32[]{:S(2)}) async-start(f32[16,8,128]{2,1,0:T(8,128)} %get-tuple-element.20), calls=%async_computation | async-start | bytes 131072 | tf_op jit(solution)/shard_map/all_to_all | solution.py:632

commit v10 on v9

--- a/solution.py
+++ b/solution.py
@@ -323,11 +323,10 @@
     tile[6:8, :] = jnp.zeros((2, LANES), jnp.float32)
     member = position() % LAYER
     tile[8:10, :] = tile[pl.ds(2 * member, 2), :]
-    tile[10:12, :] = jnp.zeros((2, LANES), jnp.float32)
-    tile[12:16, :] = current[6 + member, 6:10, :]
-    whole = tile[8:16, :]
-    for slot in range(16):
-        pay_out[slot] = whole
+    tile[10:14, :] = current[6 + member, 6:10, :]
+    for at in range(6):
+        row = jnp.broadcast_to(tile[8 + at : 9 + at, :], (16, LANES))
+        pay_out[:, at * LANES : (at + 1) * LANES] = row
 
 
 DEPTH2 = 32
@@ -560,7 +559,7 @@
 def pre1(*pieces):
     plane, work = f32(DEPTH1, ROWS1, LANES), buffer(DEPTH1, ROWS1, LANES)
     scratch = [work, work, buffer(6, ROWS1, LANES), buffer(16, LANES)]
-    out = (f32(16, 8, LANES), f32(3, DEPTH1, ROWS1, LANES)) + (plane,) * 4
+    out = (f32(16, 6 * LANES), f32(3, DEPTH1, ROWS1, LANES)) + (plane,) * 4
     return call(pre1_kernel, out, scratch, "pre1", *pieces)
 
 
@@ -629,12 +628,14 @@
     outer = both(layers_apart(jnp.where(first_core, upwards, downwards), 1))
     pay, *kept1 = pre1(rest1, beta1, diag1, outer, absorb1)
 
+    place = lax.axis_index("gx")
+    start = (place >> 2) + (((place & 3) ^ 3) >> 1)
+    pay, start = lax.optimization_barrier((pay, start))
     rows = lax.all_to_all(pay, "gx", 0, 0, axis_index_groups=column)
-    place = lax.axis_index("gx")
-    start = place // LAYER + jnp.where(place % LAYER < 2, 1, 0)
-    fields = jnp.pad(rows[:, 4:8], ((2, 2), (0, 0), (0, 0)))
+    rows, start = lax.optimization_barrier((rows, start))
+    fields = jnp.pad(rows[:, 2 * LANES :], ((2, 2), (0, 0)))
     fields = lax.dynamic_slice_in_dim(fields, start, 4)
-    rows = jnp.concatenate([rows[:, 0:2].reshape(-1, LANES), fields.reshape(-1, LANES)])
+    rows = jnp.concatenate([x.reshape(-1, LANES) for x in (rows[:, : 2 * LANES], fields)])
     rows = jnp.broadcast_to(rows, (2 * wide,) + rows.shape)
     rows = lax.all_to_all(rows, ("gx", "gy"), 0, 0, axis_index_groups=cores)
     packed = both(rows).reshape(-1, SLOT, LANES)

time: 97.3 us -> 96.1 us (0.988)
  blocking collectives: 40.7 us -> 66.1 us
  starting transfers between devices: 19.5 us -> 5.16 us
  waiting for transfers between devices: 26.1 us -> 14.5 us
    all_to_all x0 -> x1, blocking collectives: none -> 25.7 us  [body(): rows = lax.all_to_all(pay, 'gx', 0, 0, axis_index_groups=column)]
    all_to_all x1 -> x0, starting transfers between devices: 14.3 us -> none  [body(): rows = lax.all_to_all(pay, 'gx', 0, 0, axis_index_groups=column)]
    all_to_all x1 -> x0, waiting for transfers between devices: 11.7 us -> none  [body(): rows = lax.all_to_all(pay, 'gx', 0, 0, axis_index_groups=column)]
  transfers between devices with their start and end apart: 5 -> 4, of which waited for: 4 -> 3; matrix products, arithmetic and copies ran while one was open for 0% -> 0% of each run, Pallas kernels for 0% -> 0%
where the time goes in v10:
time: 96.1 us; the launch traced here: 95.6 us
  blocking collectives  66.1 us (69%)
  waiting for transfers between devices  14.5 us (15%)
  Pallas kernels  8.57 us (9%)
  starting transfers between devices  5.16 us (5%)
    all_to_all x1, blocking collectives, body(): rows = lax.all_to_all(pay, 'gx', 0, 0, axis_index_groups=column)  25.7 us
    all_to_all x1, blocking collectives, body(): rows = lax.all_to_all(rows, ('gx', 'gy'), 0, 0, axis_index_groups=cores)  16.7 us
    all_gather x1, blocking collectives, body(): own = lax.all_gather(local, 'gx', axis_index_groups=near)  12.3 us
    all_gather x4, blocking collectives, both(): return lax.all_gather(value, 'gx', axis_index_groups=chips)  11.5 us
    ppermute x3, waiting for transfers between devices, layers_apart(): lax.ppermute(value, 'gx', [(i, j) for i, j in ways if 0 <= j < count])  10.7 us
    pallas_call x3, Pallas kernels, call(): pl.pallas_call(kernel, out_shape=out, scratch_shapes=scratch, name=name,...  8.57 us
    ppermute x3, starting transfers between devices, layers_apart(): lax.ppermute(value, 'gx', [(i, j) for i, j in ways if 0 <= j < count])  3.88 us
    ppermute x1, waiting for transfers between devices, columns_apart(): return lax.ppermute(value, ('gx', 'gy'), ways)  3.8 us
  transfers between devices with their start and end apart: 4, of which 3 were waited for; matrix products, arithmetic and copies ran while one was open for 0% of the time, Pallas kernels for 0%

profile of v10, /device:TPU:1, one launch (start us, length us, event | category | flops | bytes accessed | tf_op | source)
XLA Modules:
  0.0 95.6 jit_solution(5053158657073076927)
XLA Ops:
  0.0 0.8 pad_maximum_fusion.5
  0.8 12.3 %all-gather = f32[12,2,16,128]{3,2,1,0:T(8,128)S(1)} all-gather(f32[3,2,16,128]{3,2,1,0:T(8,128)S(1)} %pad_maximum_fusion.5), channel_id=2, replica_groups={{0,8,16,24},{32,40,48,56},{64,72,80,88},{96,104,112,120},{128,136,144,1..., dimensions={0}, use_global_device_ids=true | all-gather | bytes 245760 | tf_op jit(solution)/shard_map/all_gather | solution.py:611
  13.1 1.3 %collective-permute-start = (f32[4,3,2,16,128]{4,3,2,1,0:T(8,128)S(1)}, f32[4,3,2,16,128]{4,3,2,1,0:T(8,128)S(1)}, u32[]{:S(2)}, u32[]{:S(2)}) collective-permute-start(f32[4,3,2,16,128]{4,3,2,1,0:T(8,128)S(1)} %bitcast.31), channel_id=1, source_target_pairs={{0,1},{1,2},{2,3},{3,4},{4,5},{5,6},{6,7},{9,8},{10,9},{11,10},{12... | collective-permute-start | bytes 589832 | tf_op jit(solution)/shard_map/ppermute | solution.py:590
  14.3 1.3 %collective-permute-start.1 = (f32[4,3,2,16,128]{4,3,2,1,0:T(8,128)S(1)}, f32[4,3,2,16,128]{4,3,2,1,0:T(8,128)S(1)}, u32[]{:S(2)}, u32[]{:S(2)}) collective-permute-start(f32[4,3,2,16,128]{4,3,2,1,0:T(8,128)S(1)} %bitcast.32), channel_id=1, source_target_pairs={{0,32},{16,48},{32,64},{40,8},{48,80},{56,24},{64,96},{72,40},{80,... | collective-permute-start | bytes 589832 | tf_op jit(solution)/shard_map/ppermute | solution.py:579
  15.7 3.8 %collective-permute-done = f32[4,3,2,16,128]{4,3,2,1,0:T(8,128)S(1)} collective-permute-done((f32[4,3,2,16,128]{4,3,2,1,0:T(8,128)S(1)}, f32[4,3,2,16,128]{4,3,2,1,0:T(8,128)S(1)}, u32[]{:S(2)}, u32[]{:S(2)}) %collective-permute-start) | collective-permute-done | bytes 196640 | tf_op jit(solution)/shard_map/ppermute | solution.py:590
  19.5 2.1 %all-gather.1 = f32[8,3,2,16,128]{4,3,2,1,0:T(8,128)S(1)} all-gather(f32[4,3,2,16,128]{4,3,2,1,0:T(8,128)S(1)} %collective-permute-done), channel_id=3, replica_groups={{0,8},{16,24},{32,40},{48,56},{64,72},{80,88},{96,104},{112,120},{128,1..., dimensions={0}, use_global_device_ids=true | all-gather | bytes 589824 | tf_op jit(solution)/shard_map/all_gather | solution.py:608
  21.7 1.3 %collective-permute-start.2 = (f32[76,8,128]{2,1,0:T(8,128)S(1)}, f32[76,8,128]{2,1,0:T(8,128)S(1)}, u32[]{:S(2)}, u32[]{:S(2)}) collective-permute-start(f32[76,8,128]{2,1,0:T(8,128)S(1)} %pad_maximum_fusion.2), channel_id=1, source_target_pairs={{0,32},{16,48},{32,64},{40,8},{48,80},{56,24},{64,96},{72,40},{80,... | collective-permute-start | bytes 933896 | tf_op jit(solution)/shard_map/ppermute | solution.py:579
  23.1 0.0 collective-permute-done.1
  23.1 6.2 %collective-permute-done.2 = f32[76,8,128]{2,1,0:T(8,128)S(1)} collective-permute-done((f32[76,8,128]{2,1,0:T(8,128)S(1)}, f32[76,8,128]{2,1,0:T(8,128)S(1)}, u32[]{:S(2)}, u32[]{:S(2)}) %collective-permute-start.2) | collective-permute-done | bytes 311328 | tf_op jit(solution)/shard_map/ppermute | solution.py:579
  29.4 2.5 %all-gather.2 = f32[248,8,128]{2,1,0:T(8,128)S(1)} all-gather(f32[124,8,128]{2,1,0:T(8,128)S(1)} %pad_maximum_fusion.1), channel_id=4, replica_groups={{0,8},{16,24},{32,40},{48,56},{64,72},{80,88},{96,104},{112,120},{128,1..., dimensions={0}, use_global_device_ids=true | all-gather | bytes 1523712 | tf_op jit(solution)/shard_map/all_gather | solution.py:608
  31.9 2.3 %pre0.1 = (f32[7,10,32,128]{3,2,1,0:T(8,128)S(1)}, f32[6,16,128]{2,1,0:T(8,128)S(1)}, f32[8,16,128]{2,1,0:T(8,128)S(1)}, f32[6,16,128]{2,1,0:T(8,128)S(1)}, f32[4,16,128]{2,1,0:T(8,128)S(1)}) custom-call(f32[4,3,2,48,128]{4,3,2,1,0:T(8,128)S(1)} %pad_maximum_fusion.own, f32[2,124,8,128]{3,2,1,0:T(8,128)S(1)} %bitcast.26), custom_call_target="tpu_custom_call" | custom-call | tf_op jit(solution)/shard_map/pre0/pallas_call | solution.py:542
  34.2 1.3 %collective-permute-start.3 = (f32[16,16,128]{2,1,0:T(8,128)S(1)}, f32[16,16,128]{2,1,0:T(8,128)S(1)}, u32[]{:S(2)}, u32[]{:S(2)}) collective-permute-start(f32[16,16,128]{2,1,0:T(8,128)S(1)} %maximum_select_fusion), channel_id=1, source_target_pairs={{0,32},{16,48},{32,64},{40,8},{48,80},{56,24},{64,96},{72,40},{80,... | collective-permute-start | bytes 393224 | tf_op jit(solution)/shard_map/ppermute | solution.py:579
  35.5 4.4 %collective-permute-done.3 = f32[16,16,128]{2,1,0:T(8,128)S(1)} collective-permute-done((f32[16,16,128]{2,1,0:T(8,128)S(1)}, f32[16,16,128]{2,1,0:T(8,128)S(1)}, u32[]{:S(2)}, u32[]{:S(2)}) %collective-permute-start.3) | collective-permute-done | bytes 131104 | tf_op jit(solution)/shard_map/ppermute | solution.py:579
  39.9 2.0 %all-gather.3 = f32[32,16,128]{2,1,0:T(8,128)S(1)} all-gather(f32[16,16,128]{2,1,0:T(8,128)S(1)} %collective-permute-done.3), channel_id=5, replica_groups={{0,8},{16,24},{32,40},{48,56},{64,72},{80,88},{96,104},{112,120},{128,1..., dimensions={0}, use_global_device_ids=true | all-gather | bytes 393216 | tf_op jit(solution)/shard_map/all_gather | solution.py:608
  41.9 0.8 pre1.1
  42.8 0.1 copy.4
  42.8 25.7 %all_to_all.17 = f32[16,1,768]{2,1,0:T(1,128)S(1)} all-to-all(f32[16,1,768]{2,1,0:T(1,128)S(1)} %copy.4), channel_id=1, replica_groups={{0,32,64,96,128,160,192,224,256,288,320,352,384,416,448,480},{8,40,72,1..., dimensions={0} | all-to-all | bytes 98304 | tf_op jit(solution)/shard_map/all_to_all | solution.py:634
  68.6 16.7 %all_to_all.18 = f32[16,48,128]{2,1,0:T(8,128)S(1)} all-to-all(f32[16,48,128]{2,1,0:T(8,128)S(1)} %broadcast_in_dim.3), channel_id=1, replica_groups={{0,1,2,3,4,5,6,7,16,17,18,19,20,21,22,23},{8,9,10,11,12,13,14,15,24,25,..., dimensions={0} | all-to-all | bytes 786432 | tf_op jit(solution)/shard_map/all_to_all | solution.py:640
  85.3 4.9 %all-gather.4.packed = f32[32,48,128]{2,1,0:T(8,128)S(1)} all-gather(f32[16,48,128]{2,1,0:T(8,128)S(1)} %all_to_all.18), channel_id=6, replica_groups={{0,8},{16,24},{32,40},{48,56},{64,72},{80,88},{96,104},{112,120},{128,1..., dimensions={0}, use_global_device_ids=true | all-gather | bytes 1179648 | tf_op jit(solution)/shard_map/all_gather | solution.py:608
  90.2 5.5 %finish.1 = f32[2,16,128]{2,1,0:T(8,128)} custom-call(f32[1536,128]{1,0:T(8,128)S(1)} %bitcast.25, f32[32,48,128]{2,1,0:T(8,128)S(1)} %all-gather.4.packed, f32[3,16,16,128]{3,2,1,0:T(8,128)S(1)} %get-tuple-element.29.region1, f32[16,16,128]{2,1,0:T(8,128)S(1)} %get-tuple-element.30.inverse1, f32[16,16,128]{2,1,0:T(8,128)S(1)} %get-tuple-element.31.first1, ...), custom_call_target="tpu_custom_call" | custom-call | tf_op jit(solution)/shard_map/finish/pallas_call | solution.py:542
  (20 shorter events, 0.3 us)
Async XLA Ops:
  13.1 6.4 %collective-permute-start = (f32[4,3,2,16,128]{4,3,2,1,0:T(8,128)S(1)}, f32[4,3,2,16,128]{4,3,2,1,0:T(8,128)S(1)}, u32[]{:S(2)}, u32[]{:S(2)}) collective-permute-start(f32[4,3,2,16,128]{4,3,2,1,0:T(8,128)S(1)} %bitcast.31), channel_id=1, source_target_pairs={{0,1},{1,2},{2,3},{3,4},{4,5},{5,6},{6,7},{9,8},{10,9},{11,10},{12... | collective-permute-start | bytes 589832 | tf_op jit(solution)/shard_map/ppermute | solution.py:590
  14.3 8.7 %collective-permute-start.1 = (f32[4,3,2,16,128]{4,3,2,1,0:T(8,128)S(1)}, f32[4,3,2,16,128]{4,3,2,1,0:T(8,128)S(1)}, u32[]{:S(2)}, u32[]{:S(2)}) collective-permute-start(f32[4,3,2,16,128]{4,3,2,1,0:T(8,128)S(1)} %bitcast.32), channel_id=1, source_target_pairs={{0,32},{16,48},{32,64},{40,8},{48,80},{56,24},{64,96},{72,40},{80,... | collective-permute-start | bytes 589832 | tf_op jit(solution)/shard_map/ppermute | solution.py:579
  21.7 7.6 %collective-permute-start.2 = (f32[76,8,128]{2,1,0:T(8,128)S(1)}, f32[76,8,128]{2,1,0:T(8,128)S(1)}, u32[]{:S(2)}, u32[]{:S(2)}) collective-permute-start(f32[76,8,128]{2,1,0:T(8,128)S(1)} %pad_maximum_fusion.2), channel_id=1, source_target_pairs={{0,32},{16,48},{32,64},{40,8},{48,80},{56,24},{64,96},{72,40},{80,... | collective-permute-start | bytes 933896 | tf_op jit(solution)/shard_map/ppermute | solution.py:579
  34.2 5.7 %collective-permute-start.3 = (f32[16,16,128]{2,1,0:T(8,128)S(1)}, f32[16,16,128]{2,1,0:T(8,128)S(1)}, u32[]{:S(2)}, u32[]{:S(2)}) collective-permute-start(f32[16,16,128]{2,1,0:T(8,128)S(1)} %maximum_select_fusion), channel_id=1, source_target_pairs={{0,32},{16,48},{32,64},{40,8},{48,80},{56,24},{64,96},{72,40},{80,... | collective-permute-start | bytes 393224 | tf_op jit(solution)/shard_map/ppermute | solution.py:579

commit v11 on v10

--- a/solution.py
+++ b/solution.py
@@ -261,16 +261,16 @@
 ROWS1 = 16
 
 
-def gather_level1(region, rest, beta, diag, outer):
-    region[0, 1:6] = outer[0, 0:5]
+def gather_level1(region, rest, beta, diag, below, above):
+    region[0, 1:6] = below[0:5]
     region[0, 6:10] = rest[1:5]
-    region[0, 10:15] = outer[1, 0:5]
-    region[1, 0:6] = outer[0, 5:11]
+    region[0, 10:15] = above[0:5]
+    region[1, 0:6] = below[5:11]
     region[1, 6:10] = beta[2:6]
-    region[1, 10:16] = outer[1, 5:11]
-    region[2, 1:6] = outer[0, 11:16]
+    region[1, 10:16] = above[5:11]
+    region[2, 1:6] = below[11:16]
     region[2, 6:10] = diag[1:5]
-    region[2, 10:15] = outer[1, 11:16]
+    region[2, 10:15] = above[11:16]
 
 
 CHUNK1 = 4
@@ -301,10 +301,10 @@
 
 
 def pre1_kernel(
-    rest1, beta1, diag1, outer, absorb, pay_out, region, inverse, first, second, third,
+    rest1, beta1, diag1, below, above, absorb, pay_out, region, inverse, first, second, third,
     one, two, tmp, tile,
 ):
-    gather_level1(region, rest1, beta1, diag1, outer)
+    gather_level1(region, rest1, beta1, diag1, below, above)
     shape = Packed(2, ROWS1, False)
     level1_parts(shape, region, inverse, first, second, third)
     source = lambda start, stop: region[0, start:stop]
@@ -579,6 +579,12 @@
     return lax.ppermute(value, "gx", [(i, j) for i, j in ways if 0 <= j < count])
 
 
+def shifted(value, steps):
+    count = lax.axis_size("gx")
+    pairs = [(i, i + steps) for i in range(count) if 0 <= i + steps < count]
+    return lax.ppermute(value, "gx", pairs)
+
+
 def columns_apart(value):
     count, wide = lax.axis_size("gx"), lax.axis_size("gy")
     ways = [
@@ -625,8 +631,8 @@
 
     upwards = jnp.concatenate([rest1[0:5], beta1[0:6], diag1[0:5]])
     downwards = jnp.concatenate([rest1[1:6], beta1[2:8], diag1[1:6]])
-    outer = both(layers_apart(jnp.where(first_core, upwards, downwards), 1))
-    pay, *kept1 = pre1(rest1, beta1, diag1, outer, absorb1)
+    below, above = shifted(upwards, LAYER), shifted(downwards, -LAYER)
+    pay, *kept1 = pre1(rest1, beta1, diag1, below, above, absorb1)
 
     place = lax.axis_index("gx")
     start = (place >> 2) + (((place & 3) ^ 3) >> 1)

time: 96.1 us -> 96.8 us (level)
  starting transfers between devices: 5.16 us -> 7.09 us
  blocking collectives: 66.1 us -> 64.3 us
    ppermute x0 -> x2, waiting for transfers between devices: none -> 4.97 us  [shifted(): return lax.ppermute(value, 'gx', pairs)]
    ppermute x3 -> x2, waiting for transfers between devices: 10.7 us -> 6.25 us  [layers_apart(): lax.ppermute(value, 'gx', [(i, j) for i, j in ways if 0 <= j < count])]
    ppermute x0 -> x2, starting transfers between devices: none -> 3.22 us  [shifted(): return lax.ppermute(value, 'gx', pairs)]
    ppermute x3 -> x2, starting transfers between devices: 3.88 us -> 2.58 us  [layers_apart(): lax.ppermute(value, 'gx', [(i, j) for i, j in ways if 0 <= j < count])]
    all_gather x4 -> x3, blocking collectives: 11.5 us -> 10.5 us  [both(): return lax.all_gather(value, 'gx', axis_index_groups=chips)]
  transfers between devices with their start and end apart: 4 -> 5, of which waited for: 3 -> 4; matrix products, arithmetic and copies ran while one was open for 0% -> 0% of each run, Pallas kernels for 0% -> 0%
where the time goes in v11:
time: 96.8 us; the launch traced here: 96.3 us
  blocking collectives  64.3 us (66%)
  waiting for transfers between devices  15 us (15%)
  Pallas kernels  8.57 us (9%)
  starting transfers between devices  7.09 us (7%)
    all_to_all x1, blocking collectives, body(): rows = lax.all_to_all(pay, 'gx', 0, 0, axis_index_groups=column)  24.8 us
    all_to_all x1, blocking collectives, body(): rows = lax.all_to_all(rows, ('gx', 'gy'), 0, 0, axis_index_groups=cores)  16.6 us
    all_gather x1, blocking collectives, body(): own = lax.all_gather(local, 'gx', axis_index_groups=near)  12.3 us
    all_gather x3, blocking collectives, both(): return lax.all_gather(value, 'gx', axis_index_groups=chips)  10.5 us
    pallas_call x3, Pallas kernels, call(): pl.pallas_call(kernel, out_shape=out, scratch_shapes=scratch, name=name,...  8.57 us
    ppermute x2, waiting for transfers between devices, layers_apart(): lax.ppermute(value, 'gx', [(i, j) for i, j in ways if 0 <= j < count])  6.25 us
    ppermute x2, waiting for transfers between devices, shifted(): return lax.ppermute(value, 'gx', pairs)  4.97 us
    ppermute x1, waiting for transfers between devices, columns_apart(): return lax.ppermute(value, ('gx', 'gy'), ways)  3.8 us
  transfers between devices with their start and end apart: 5, of which 4 were waited for; matrix products, arithmetic and copies ran while one was open for 0% of the time, Pallas kernels for 0%

profile of v11, /device:TPU:1, one launch (start us, length us, event | category | flops | bytes accessed | tf_op | source)
XLA Modules:
  0.0 96.3 jit_solution(3170251365116435343)
XLA Ops:
  0.0 0.8 pad_maximum_fusion.7
  0.8 12.3 %all-gather = f32[12,2,16,128]{3,2,1,0:T(8,128)S(1)} all-gather(f32[3,2,16,128]{3,2,1,0:T(8,128)S(1)} %pad_maximum_fusion.7), channel_id=2, replica_groups={{0,8,16,24},{32,40,48,56},{64,72,80,88},{96,104,112,120},{128,136,144,1..., dimensions={0}, use_global_device_ids=true | all-gather | bytes 245760 | tf_op jit(solution)/shard_map/all_gather | solution.py:617
  13.1 1.3 %collective-permute-start = (f32[4,3,2,16,128]{4,3,2,1,0:T(8,128)S(1)}, f32[4,3,2,16,128]{4,3,2,1,0:T(8,128)S(1)}, u32[]{:S(2)}, u32[]{:S(2)}) collective-permute-start(f32[4,3,2,16,128]{4,3,2,1,0:T(8,128)S(1)} %bitcast.29), channel_id=1, source_target_pairs={{0,1},{1,2},{2,3},{3,4},{4,5},{5,6},{6,7},{9,8},{10,9},{11,10},{12... | collective-permute-start | bytes 589832 | tf_op jit(solution)/shard_map/ppermute | solution.py:596
  14.3 1.3 %collective-permute-start.1 = (f32[4,3,2,16,128]{4,3,2,1,0:T(8,128)S(1)}, f32[4,3,2,16,128]{4,3,2,1,0:T(8,128)S(1)}, u32[]{:S(2)}, u32[]{:S(2)}) collective-permute-start(f32[4,3,2,16,128]{4,3,2,1,0:T(8,128)S(1)} %bitcast.30), channel_id=1, source_target_pairs={{0,32},{16,48},{32,64},{40,8},{48,80},{56,24},{64,96},{72,40},{80,... | collective-permute-start | bytes 589832 | tf_op jit(solution)/shard_map/ppermute | solution.py:579
  15.7 3.8 %collective-permute-done = f32[4,3,2,16,128]{4,3,2,1,0:T(8,128)S(1)} collective-permute-done((f32[4,3,2,16,128]{4,3,2,1,0:T(8,128)S(1)}, f32[4,3,2,16,128]{4,3,2,1,0:T(8,128)S(1)}, u32[]{:S(2)}, u32[]{:S(2)}) %collective-permute-start) | collective-permute-done | bytes 196640 | tf_op jit(solution)/shard_map/ppermute | solution.py:596
  19.5 2.1 %all-gather.1 = f32[8,3,2,16,128]{4,3,2,1,0:T(8,128)S(1)} all-gather(f32[4,3,2,16,128]{4,3,2,1,0:T(8,128)S(1)} %collective-permute-done), channel_id=3, replica_groups={{0,8},{16,24},{32,40},{48,56},{64,72},{80,88},{96,104},{112,120},{128,1..., dimensions={0}, use_global_device_ids=true | all-gather | bytes 589824 | tf_op jit(solution)/shard_map/all_gather | solution.py:614
  21.7 1.3 %collective-permute-start.2 = (f32[76,8,128]{2,1,0:T(8,128)S(1)}, f32[76,8,128]{2,1,0:T(8,128)S(1)}, u32[]{:S(2)}, u32[]{:S(2)}) collective-permute-start(f32[76,8,128]{2,1,0:T(8,128)S(1)} %pad_maximum_fusion.2), channel_id=1, source_target_pairs={{0,32},{16,48},{32,64},{40,8},{48,80},{56,24},{64,96},{72,40},{80,... | collective-permute-start | bytes 933896 | tf_op jit(solution)/shard_map/ppermute | solution.py:579
  23.1 0.0 collective-permute-done.1
  23.1 6.2 %collective-permute-done.2 = f32[76,8,128]{2,1,0:T(8,128)S(1)} collective-permute-done((f32[76,8,128]{2,1,0:T(8,128)S(1)}, f32[76,8,128]{2,1,0:T(8,128)S(1)}, u32[]{:S(2)}, u32[]{:S(2)}) %collective-permute-start.2) | collective-permute-done | bytes 311328 | tf_op jit(solution)/shard_map/ppermute | solution.py:579
  29.4 2.5 %all-gather.2 = f32[248,8,128]{2,1,0:T(8,128)S(1)} all-gather(f32[124,8,128]{2,1,0:T(8,128)S(1)} %pad_maximum_fusion.1), channel_id=4, replica_groups={{0,8},{16,24},{32,40},{48,56},{64,72},{80,88},{96,104},{112,120},{128,1..., dimensions={0}, use_global_device_ids=true | all-gather | bytes 1523712 | tf_op jit(solution)/shard_map/all_gather | solution.py:614
  31.9 2.3 %pre0.1 = (f32[7,10,32,128]{3,2,1,0:T(8,128)S(1)}, f32[6,16,128]{2,1,0:T(8,128)S(1)}, f32[8,16,128]{2,1,0:T(8,128)S(1)}, f32[6,16,128]{2,1,0:T(8,128)S(1)}, f32[4,16,128]{2,1,0:T(8,128)S(1)}) custom-call(f32[4,3,2,48,128]{4,3,2,1,0:T(8,128)S(1)} %pad_maximum_fusion.own, f32[2,124,8,128]{3,2,1,0:T(8,128)S(1)} %bitcast.25), custom_call_target="tpu_custom_call" | custom-call | tf_op jit(solution)/shard_map/pre0/pallas_call | solution.py:542
  34.2 1.9 %collective-permute-start.3 = (f32[16,16,128]{2,1,0:T(8,128)S(1)}, f32[16,16,128]{2,1,0:T(8,128)S(1)}, u32[]{:S(2)}, u32[]{:S(2)}) collective-permute-start(f32[16,16,128]{2,1,0:T(8,128)S(1)} %pad_maximum_fusion.4), channel_id=1, source_target_pairs={{0,32},{8,40},{16,48},{24,56},{32,64},{40,72},{48,80},{56,88},{64,... | collective-permute-start | bytes 393224 | tf_op jit(solution)/shard_map/ppermute | solution.py:585
  36.2 1.3 %collective-permute-start.4 = (f32[16,16,128]{2,1,0:T(8,128)S(1)}, f32[16,16,128]{2,1,0:T(8,128)S(1)}, u32[]{:S(2)}, u32[]{:S(2)}) collective-permute-start(f32[16,16,128]{2,1,0:T(8,128)S(1)} %pad_maximum_fusion.5), channel_id=1, source_target_pairs={{32,0},{40,8},{48,16},{56,24},{64,32},{72,40},{80,48},{88,56},{96,... | collective-permute-start | bytes 393224 | tf_op jit(solution)/shard_map/ppermute | solution.py:585
  37.5 1.2 %collective-permute-done.3.below = f32[16,16,128]{2,1,0:T(8,128)S(1)} collective-permute-done((f32[16,16,128]{2,1,0:T(8,128)S(1)}, f32[16,16,128]{2,1,0:T(8,128)S(1)}, u32[]{:S(2)}, u32[]{:S(2)}) %collective-permute-start.3) | collective-permute-done | bytes 131104 | tf_op jit(solution)/shard_map/ppermute | solution.py:585
  38.6 3.8 %collective-permute-done.4.above = f32[16,16,128]{2,1,0:T(8,128)S(1)} collective-permute-done((f32[16,16,128]{2,1,0:T(8,128)S(1)}, f32[16,16,128]{2,1,0:T(8,128)S(1)}, u32[]{:S(2)}, u32[]{:S(2)}) %collective-permute-start.4) | collective-permute-done | bytes 131104 | tf_op jit(solution)/shard_map/ppermute | solution.py:585
  42.5 0.8 pre1.1
  43.3 0.1 copy.4
  43.4 24.8 %all_to_all.17 = f32[16,1,768]{2,1,0:T(1,128)S(1)} all-to-all(f32[16,1,768]{2,1,0:T(1,128)S(1)} %copy.4), channel_id=1, replica_groups={{0,32,64,96,128,160,192,224,256,288,320,352,384,416,448,480},{8,40,72,1..., dimensions={0} | all-to-all | bytes 98304 | tf_op jit(solution)/shard_map/all_to_all | solution.py:640
  68.2 16.6 %all_to_all.18 = f32[16,48,128]{2,1,0:T(8,128)S(1)} all-to-all(f32[16,48,128]{2,1,0:T(8,128)S(1)} %broadcast_in_dim.3), channel_id=1, replica_groups={{0,1,2,3,4,5,6,7,16,17,18,19,20,21,22,23},{8,9,10,11,12,13,14,15,24,25,..., dimensions={0} | all-to-all | bytes 786432 | tf_op jit(solution)/shard_map/all_to_all | solution.py:646
  84.9 5.9 %all-gather.3.packed = f32[32,48,128]{2,1,0:T(8,128)S(1)} all-gather(f32[16,48,128]{2,1,0:T(8,128)S(1)} %all_to_all.18), channel_id=5, replica_groups={{0,8},{16,24},{32,40},{48,56},{64,72},{80,88},{96,104},{112,120},{128,1..., dimensions={0}, use_global_device_ids=true | all-gather | bytes 1179648 | tf_op jit(solution)/shard_map/all_gather | solution.py:614
  90.8 5.5 %finish.1 = f32[2,16,128]{2,1,0:T(8,128)} custom-call(f32[1536,128]{1,0:T(8,128)S(1)} %bitcast.24, f32[32,48,128]{2,1,0:T(8,128)S(1)} %all-gather.3.packed, f32[3,16,16,128]{3,2,1,0:T(8,128)S(1)} %get-tuple-element.29.region1, f32[16,16,128]{2,1,0:T(8,128)S(1)} %get-tuple-element.30.inverse1, f32[16,16,128]{2,1,0:T(8,128)S(1)} %get-tuple-element.31.first1, ...), custom_call_target="tpu_custom_call" | custom-call | tf_op jit(solution)/shard_map/finish/pallas_call | solution.py:542
  (21 shorter events, 0.3 us)
Async XLA Ops:
  13.1 6.4 %collective-permute-start = (f32[4,3,2,16,128]{4,3,2,1,0:T(8,128)S(1)}, f32[4,3,2,16,128]{4,3,2,1,0:T(8,128)S(1)}, u32[]{:S(2)}, u32[]{:S(2)}) collective-permute-start(f32[4,3,2,16,128]{4,3,2,1,0:T(8,128)S(1)} %bitcast.29), channel_id=1, source_target_pairs={{0,1},{1,2},{2,3},{3,4},{4,5},{5,6},{6,7},{9,8},{10,9},{11,10},{12... | collective-permute-start | bytes 589832 | tf_op jit(solution)/shard_map/ppermute | solution.py:596
  14.3 8.7 %collective-permute-start.1 = (f32[4,3,2,16,128]{4,3,2,1,0:T(8,128)S(1)}, f32[4,3,2,16,128]{4,3,2,1,0:T(8,128)S(1)}, u32[]{:S(2)}, u32[]{:S(2)}) collective-permute-start(f32[4,3,2,16,128]{4,3,2,1,0:T(8,128)S(1)} %bitcast.30), channel_id=1, source_target_pairs={{0,32},{16,48},{32,64},{40,8},{48,80},{56,24},{64,96},{72,40},{80,... | collective-permute-start | bytes 589832 | tf_op jit(solution)/shard_map/ppermute | solution.py:579
  21.7 7.6 %collective-permute-start.2 = (f32[76,8,128]{2,1,0:T(8,128)S(1)}, f32[76,8,128]{2,1,0:T(8,128)S(1)}, u32[]{:S(2)}, u32[]{:S(2)}) collective-permute-start(f32[76,8,128]{2,1,0:T(8,128)S(1)} %pad_maximum_fusion.2), channel_id=1, source_target_pairs={{0,32},{16,48},{32,64},{40,8},{48,80},{56,24},{64,96},{72,40},{80,... | collective-permute-start | bytes 933896 | tf_op jit(solution)/shard_map/ppermute | solution.py:579
  34.2 4.4 %collective-permute-start.3 = (f32[16,16,128]{2,1,0:T(8,128)S(1)}, f32[16,16,128]{2,1,0:T(8,128)S(1)}, u32[]{:S(2)}, u32[]{:S(2)}) collective-permute-start(f32[16,16,128]{2,1,0:T(8,128)S(1)} %pad_maximum_fusion.4), channel_id=1, source_target_pairs={{0,32},{8,40},{16,48},{24,56},{32,64},{40,72},{48,80},{56,88},{64,... | collective-permute-start | bytes 393224 | tf_op jit(solution)/shard_map/ppermute | solution.py:585
  36.2 6.3 %collective-permute-start.4 = (f32[16,16,128]{2,1,0:T(8,128)S(1)}, f32[16,16,128]{2,1,0:T(8,128)S(1)}, u32[]{:S(2)}, u32[]{:S(2)}) collective-permute-start(f32[16,16,128]{2,1,0:T(8,128)S(1)} %pad_maximum_fusion.5), channel_id=1, source_target_pairs={{32,0},{40,8},{48,16},{56,24},{64,32},{72,40},{80,48},{88,56},{96,... | collective-permute-start | bytes 393224 | tf_op jit(solution)/shard_map/ppermute | solution.py:585

commit v12 on v10

--- a/solution.py
+++ b/solution.py
@@ -196,12 +196,16 @@
     return 0.125 * jnp.where(even, take(0) + take(1), take(2) + take(3))
 
 
+RIM_REACH = (3, 3, 4)
+END_REACH = (2, 2, 3)
+RIMS = (0, 12, 24)
+ENDS = (40, 48, 56)
 KEPT0 = 10
 KEPT_ROWS0 = 32
 
 
 def pre0_kernel(
-    own, outer, kept_out, rest_out, beta_out, diag_out, absorb_out,
+    own, outer, rims, kept_out, rest_out, beta_out, diag_out, absorb_out,
     diag, inverse, first, second, third, one, two, tmp,
 ):
     zero = jnp.zeros((8, LANES), jnp.float32)
@@ -216,14 +220,18 @@
                     continue
                 side = part // 2
                 at = 2 * (6 * member + 2 * kind + plane % 2)
-                rows = [outer[side, at + tile] for tile in (48, 0, 1, 49)]
-                reach = 3 if kind == 2 else 2
-                near = member - (LAYER - reach) if side == 0 else member
-                if 0 <= near < reach:
-                    at = 96 + 2 * (2 * (2 * kind + near) + plane % 2)
-                    ends = outer[side, at], outer[side, at + 1]
-                else:
-                    ends = zero, zero
+                own_rows = [outer[side, at], outer[side, at + 1]]
+                outward = LAYER - 1 - member if side == 0 else member
+                found_tiles = []
+                for first_tile, reach in ((RIMS[kind], RIM_REACH[kind]), (ENDS[kind], END_REACH[kind])):
+                    if outward < reach:
+                        index = reach - 1 - outward if side == 0 else outward
+                        at = first_tile + 2 * (2 * index + plane % 2)
+                        found_tiles.append((rims[side, at], rims[side, at + 1]))
+                    else:
+                        found_tiles.append((zero, zero))
+                rim, ends = found_tiles
+                rows = [rim[0], *own_rows, rim[1]]
                 found.append(jnp.concatenate([ends[0], *rows, ends[1]]))
             return jnp.stack(found)
 
@@ -618,10 +626,13 @@
     layer = jnp.concatenate([sides[0], own, sides[1]], axis=-2)
     rims = jnp.concatenate([sides[0, ..., 8:, :], sides[1, ..., :8, :]], axis=-2)
     ends = jnp.concatenate([sides[0, ..., :8, :], sides[1, ..., 8:, :]], axis=-2)
-    near2 = jnp.where(first_core, ends[2:, :2], ends[:2, :2])
-    near3 = jnp.where(first_core, ends[1:, 2], ends[:3, 2])
-    rest = layers_apart(tiles_of([rims, near2[:, 0], near2[:, 1], near3]), 1)
-    kept0, rest1, beta1, diag1, absorb1 = pre0(layer, both(tiles_of([outer, rest])))
+    sent = []
+    for rows, reaches in ((rims, RIM_REACH), (ends, END_REACH)):
+        for kind, reach in enumerate(reaches):
+            sent.append(jnp.where(first_core, rows[LAYER - reach :, kind], rows[:reach, kind]))
+    rest = layers_apart(tiles_of(sent), 1)
+    outer = both(tiles_of([outer]))
+    kept0, rest1, beta1, diag1, absorb1 = pre0(layer, outer, both(rest))
 
     upwards = jnp.concatenate([rest1[0:5], beta1[0:6], diag1[0:5]])
     downwards = jnp.concatenate([rest1[1:6], beta1[2:8], diag1[1:6]])

time: 96.1 us -> 95.4 us (level)
  waiting for transfers between devices: 14.5 us -> 12 us
  blocking collectives: 66.1 us -> 67.9 us
    ppermute x3, waiting for transfers between devices: 10.7 us -> 8.22 us  [layers_apart(): lax.ppermute(value, 'gx', [(i, j) for i, j in ways if 0 <= j < count])]
    all_gather x4 -> x5, blocking collectives: 11.5 us -> 13.2 us  [both(): return lax.all_gather(value, 'gx', axis_index_groups=chips)]
where the time goes in v12:
time: 95.4 us; the launch traced here: 95 us
  blocking collectives  67.9 us (71%)
  waiting for transfers between devices  12 us (13%)
  Pallas kernels  8.57 us (9%)
  starting transfers between devices  5.16 us (5%)
    all_to_all x1, blocking collectives, body(): rows = lax.all_to_all(pay, 'gx', 0, 0, axis_index_groups=column)  25.7 us
    all_to_all x1, blocking collectives, body(): rows = lax.all_to_all(rows, ('gx', 'gy'), 0, 0, axis_index_groups=cores)  16.7 us
    all_gather x5, blocking collectives, both(): return lax.all_gather(value, 'gx', axis_index_groups=chips)  13.2 us
    all_gather x1, blocking collectives, body(): own = lax.all_gather(local, 'gx', axis_index_groups=near)  12.3 us
    pallas_call x3, Pallas kernels, call(): pl.pallas_call(kernel, out_shape=out, scratch_shapes=scratch, name=name,...  8.57 us
    ppermute x3, waiting for transfers between devices, layers_apart(): lax.ppermute(value, 'gx', [(i, j) for i, j in ways if 0 <= j < count])  8.22 us
    ppermute x3, starting transfers between devices, layers_apart(): lax.ppermute(value, 'gx', [(i, j) for i, j in ways if 0 <= j < count])  3.88 us
    ppermute x1, waiting for transfers between devices, columns_apart(): return lax.ppermute(value, ('gx', 'gy'), ways)  3.8 us
  transfers between devices with their start and end apart: 4, of which 3 were waited for; matrix products, arithmetic and copies ran while one was open for 0% of the time, Pallas kernels for 0%

profile of v12, /device:TPU:1, one launch (start us, length us, event | category | flops | bytes accessed | tf_op | source)
XLA Modules:
  0.0 95.0 jit_solution(15462853472846063234)
XLA Ops:
  0.0 0.8 pad_maximum_fusion.3
  0.8 12.3 %all-gather = f32[12,2,16,128]{3,2,1,0:T(8,128)S(1)} all-gather(f32[3,2,16,128]{3,2,1,0:T(8,128)S(1)} %pad_maximum_fusion.3), channel_id=2, replica_groups={{0,8,16,24},{32,40,48,56},{64,72,80,88},{96,104,112,120},{128,136,144,1..., dimensions={0}, use_global_device_ids=true | all-gather | bytes 245760 | tf_op jit(solution)/shard_map/all_gather | solution.py:619
  13.1 1.3 %collective-permute-start = (f32[4,3,2,16,128]{4,3,2,1,0:T(8,128)S(1)}, f32[4,3,2,16,128]{4,3,2,1,0:T(8,128)S(1)}, u32[]{:S(2)}, u32[]{:S(2)}) collective-permute-start(f32[4,3,2,16,128]{4,3,2,1,0:T(8,128)S(1)} %bitcast.32), channel_id=1, source_target_pairs={{0,1},{1,2},{2,3},{3,4},{4,5},{5,6},{6,7},{9,8},{10,9},{11,10},{12... | collective-permute-start | bytes 589832 | tf_op jit(solution)/shard_map/ppermute | solution.py:598
  14.3 1.3 %collective-permute-start.1 = (f32[4,3,2,16,128]{4,3,2,1,0:T(8,128)S(1)}, f32[4,3,2,16,128]{4,3,2,1,0:T(8,128)S(1)}, u32[]{:S(2)}, u32[]{:S(2)}) collective-permute-start(f32[4,3,2,16,128]{4,3,2,1,0:T(8,128)S(1)} %bitcast.33), channel_id=1, source_target_pairs={{0,32},{16,48},{32,64},{40,8},{48,80},{56,24},{64,96},{72,40},{80,... | collective-permute-start | bytes 589832 | tf_op jit(solution)/shard_map/ppermute | solution.py:587
  15.7 3.8 %collective-permute-done = f32[4,3,2,16,128]{4,3,2,1,0:T(8,128)S(1)} collective-permute-done((f32[4,3,2,16,128]{4,3,2,1,0:T(8,128)S(1)}, f32[4,3,2,16,128]{4,3,2,1,0:T(8,128)S(1)}, u32[]{:S(2)}, u32[]{:S(2)}) %collective-permute-start) | collective-permute-done | bytes 196640 | tf_op jit(solution)/shard_map/ppermute | solution.py:598
  19.5 2.1 %all-gather.1 = f32[8,3,2,16,128]{4,3,2,1,0:T(8,128)S(1)} all-gather(f32[4,3,2,16,128]{4,3,2,1,0:T(8,128)S(1)} %collective-permute-done), channel_id=3, replica_groups={{0,8},{16,24},{32,40},{48,56},{64,72},{80,88},{96,104},{112,120},{128,1..., dimensions={0}, use_global_device_ids=true | all-gather | bytes 589824 | tf_op jit(solution)/shard_map/all_gather | solution.py:616
  21.7 1.3 %collective-permute-start.2 = (f32[68,8,128]{2,1,0:T(8,128)S(1)}, f32[68,8,128]{2,1,0:T(8,128)S(1)}, u32[]{:S(2)}, u32[]{:S(2)}) collective-permute-start(f32[68,8,128]{2,1,0:T(8,128)S(1)} %constant_dynamic-update-slice_fusion), channel_id=1, source_target_pairs={{0,32},{16,48},{32,64},{40,8},{48,80},{56,24},{64,96},{72,40},{80,... | collective-permute-start | bytes 835592 | tf_op jit(solution)/shard_map/ppermute | solution.py:587
  23.0 0.0 collective-permute-done.1
  23.1 2.1 %all_gather.37.outer = f32[2,48,8,128]{3,2,1,0:T(8,128)S(1)} all-gather(f32[1,48,8,128]{3,2,1,0:T(8,128)S(1)} %bitcast.41), channel_id=1, replica_groups={{0,8},{16,24},{32,40},{48,56},{64,72},{80,88},{96,104},{112,120},{128,1..., dimensions={0}, use_global_device_ids=true | all-gather | bytes 589824 | tf_op jit(solution)/shard_map/all_gather | solution.py:616
  25.2 3.8 %collective-permute-done.2 = f32[68,8,128]{2,1,0:T(8,128)S(1)} collective-permute-done((f32[68,8,128]{2,1,0:T(8,128)S(1)}, f32[68,8,128]{2,1,0:T(8,128)S(1)}, u32[]{:S(2)}, u32[]{:S(2)}) %collective-permute-start.2) | collective-permute-done | bytes 278560 | tf_op jit(solution)/shard_map/ppermute | solution.py:587
  29.0 2.2 %all-gather.2 = f32[136,8,128]{2,1,0:T(8,128)S(1)} all-gather(f32[68,8,128]{2,1,0:T(8,128)S(1)} %collective-permute-done.2), channel_id=4, replica_groups={{0,8},{16,24},{32,40},{48,56},{64,72},{80,88},{96,104},{112,120},{128,1..., dimensions={0}, use_global_device_ids=true | all-gather | bytes 835584 | tf_op jit(solution)/shard_map/all_gather | solution.py:616
  31.2 2.3 %pre0.1 = (f32[7,10,32,128]{3,2,1,0:T(8,128)S(1)}, f32[6,16,128]{2,1,0:T(8,128)S(1)}, f32[8,16,128]{2,1,0:T(8,128)S(1)}, f32[6,16,128]{2,1,0:T(8,128)S(1)}, f32[4,16,128]{2,1,0:T(8,128)S(1)}) custom-call(f32[4,3,2,48,128]{4,3,2,1,0:T(8,128)S(1)} %pad_maximum_fusion.own, f32[2,48,8,128]{3,2,1,0:T(8,128)S(1)} %all_gather.37.outer, f32[2,68,8,128]{3,2,1,0:T(8,128)S(1)} %bitcast.28), custom_call_target="tpu_custom_call" | custom-call | tf_op jit(solution)/shard_map/pre0/pallas_call | solution.py:550
  33.5 1.3 %collective-permute-start.3 = (f32[16,16,128]{2,1,0:T(8,128)S(1)}, f32[16,16,128]{2,1,0:T(8,128)S(1)}, u32[]{:S(2)}, u32[]{:S(2)}) collective-permute-start(f32[16,16,128]{2,1,0:T(8,128)S(1)} %maximum_select_fusion), channel_id=1, source_target_pairs={{0,32},{16,48},{32,64},{40,8},{48,80},{56,24},{64,96},{72,40},{80,... | collective-permute-start | bytes 393224 | tf_op jit(solution)/shard_map/ppermute | solution.py:587
  34.9 4.4 %collective-permute-done.3 = f32[16,16,128]{2,1,0:T(8,128)S(1)} collective-permute-done((f32[16,16,128]{2,1,0:T(8,128)S(1)}, f32[16,16,128]{2,1,0:T(8,128)S(1)}, u32[]{:S(2)}, u32[]{:S(2)}) %collective-permute-start.3) | collective-permute-done | bytes 131104 | tf_op jit(solution)/shard_map/ppermute | solution.py:587
  39.3 2.0 %all-gather.3 = f32[32,16,128]{2,1,0:T(8,128)S(1)} all-gather(f32[16,16,128]{2,1,0:T(8,128)S(1)} %collective-permute-done.3), channel_id=5, replica_groups={{0,8},{16,24},{32,40},{48,56},{64,72},{80,88},{96,104},{112,120},{128,1..., dimensions={0}, use_global_device_ids=true | all-gather | bytes 393216 | tf_op jit(solution)/shard_map/all_gather | solution.py:616
  41.2 0.8 pre1.1
  42.1 0.1 copy.4
  42.1 25.7 %all_to_all.17 = f32[16,1,768]{2,1,0:T(1,128)S(1)} all-to-all(f32[16,1,768]{2,1,0:T(1,128)S(1)} %copy.4), channel_id=1, replica_groups={{0,32,64,96,128,160,192,224,256,288,320,352,384,416,448,480},{8,40,72,1..., dimensions={0} | all-to-all | bytes 98304 | tf_op jit(solution)/shard_map/all_to_all | solution.py:645
  67.9 16.7 %all_to_all.18 = f32[16,48,128]{2,1,0:T(8,128)S(1)} all-to-all(f32[16,48,128]{2,1,0:T(8,128)S(1)} %broadcast_in_dim.3), channel_id=1, replica_groups={{0,1,2,3,4,5,6,7,16,17,18,19,20,21,22,23},{8,9,10,11,12,13,14,15,24,25,..., dimensions={0} | all-to-all | bytes 786432 | tf_op jit(solution)/shard_map/all_to_all | solution.py:651
  84.6 4.9 %all-gather.4.packed = f32[32,48,128]{2,1,0:T(8,128)S(1)} all-gather(f32[16,48,128]{2,1,0:T(8,128)S(1)} %all_to_all.18), channel_id=6, replica_groups={{0,8},{16,24},{32,40},{48,56},{64,72},{80,88},{96,104},{112,120},{128,1..., dimensions={0}, use_global_device_ids=true | all-gather | bytes 1179648 | tf_op jit(solution)/shard_map/all_gather | solution.py:616
  89.5 5.5 %finish.1 = f32[2,16,128]{2,1,0:T(8,128)} custom-call(f32[1536,128]{1,0:T(8,128)S(1)} %bitcast.27, f32[32,48,128]{2,1,0:T(8,128)S(1)} %all-gather.4.packed, f32[3,16,16,128]{3,2,1,0:T(8,128)S(1)} %get-tuple-element.29.region1, f32[16,16,128]{2,1,0:T(8,128)S(1)} %get-tuple-element.30.inverse1, f32[16,16,128]{2,1,0:T(8,128)S(1)} %get-tuple-element.31.first1, ...), custom_call_target="tpu_custom_call" | custom-call | tf_op jit(solution)/shard_map/finish/pallas_call | solution.py:550
  (24 shorter events, 0.3 us)
Async XLA Ops:
  13.1 6.4 %collective-permute-start = (f32[4,3,2,16,128]{4,3,2,1,0:T(8,128)S(1)}, f32[4,3,2,16,128]{4,3,2,1,0:T(8,128)S(1)}, u32[]{:S(2)}, u32[]{:S(2)}) collective-permute-start(f32[4,3,2,16,128]{4,3,2,1,0:T(8,128)S(1)} %bitcast.32), channel_id=1, source_target_pairs={{0,1},{1,2},{2,3},{3,4},{4,5},{5,6},{6,7},{9,8},{10,9},{11,10},{12... | collective-permute-start | bytes 589832 | tf_op jit(solution)/shard_map/ppermute | solution.py:598
  14.3 8.7 %collective-permute-start.1 = (f32[4,3,2,16,128]{4,3,2,1,0:T(8,128)S(1)}, f32[4,3,2,16,128]{4,3,2,1,0:T(8,128)S(1)}, u32[]{:S(2)}, u32[]{:S(2)}) collective-permute-start(f32[4,3,2,16,128]{4,3,2,1,0:T(8,128)S(1)} %bitcast.33), channel_id=1, source_target_pairs={{0,32},{16,48},{32,64},{40,8},{48,80},{56,24},{64,96},{72,40},{80,... | collective-permute-start | bytes 589832 | tf_op jit(solution)/shard_map/ppermute | solution.py:587
  21.7 7.3 %collective-permute-start.2 = (f32[68,8,128]{2,1,0:T(8,128)S(1)}, f32[68,8,128]{2,1,0:T(8,128)S(1)}, u32[]{:S(2)}, u32[]{:S(2)}) collective-permute-start(f32[68,8,128]{2,1,0:T(8,128)S(1)} %constant_dynamic-update-slice_fusion), channel_id=1, source_target_pairs={{0,32},{16,48},{32,64},{40,8},{48,80},{56,24},{64,96},{72,40},{80,... | collective-permute-start | bytes 835592 | tf_op jit(solution)/shard_map/ppermute | solution.py:587
  33.5 5.7 %collective-permute-start.3 = (f32[16,16,128]{2,1,0:T(8,128)S(1)}, f32[16,16,128]{2,1,0:T(8,128)S(1)}, u32[]{:S(2)}, u32[]{:S(2)}) collective-permute-start(f32[16,16,128]{2,1,0:T(8,128)S(1)} %maximum_select_fusion), channel_id=1, source_target_pairs={{0,32},{16,48},{32,64},{40,8},{48,80},{56,24},{64,96},{72,40},{80,... | collective-permute-start | bytes 393224 | tf_op jit(solution)/shard_map/ppermute | solution.py:587

commit v13 on v12

--- a/solution.py
+++ b/solution.py
@@ -205,7 +205,7 @@
 
 
 def pre0_kernel(
-    own, outer, rims, kept_out, rest_out, beta_out, diag_out, absorb_out,
+    own, outer, rims, kept_out, rest_out, beta_out, diag_out, absorb_out, send_out,
     diag, inverse, first, second, third, one, two, tmp,
 ):
     zero = jnp.zeros((8, LANES), jnp.float32)
@@ -263,6 +263,12 @@
     beta_out[...] = betas
     diag_out[...] = wide + half * (here + betas[0:6]) + half * (here + betas[2:8]) + share
     absorb_out[...] = wide[1:5]
+    core = position() & 1
+    at = 0
+    for ref, count, first_plane in ((rest_out, 5, core), (beta_out, 6, 2 * core), (diag_out, 5, core)):
+        for plane in range(count):
+            send_out[at : at + 12, :] = ref[first_plane + plane, 2:14, :]
+            at += 12
 
 
 DEPTH1 = 16
@@ -270,15 +276,18 @@
 
 
 def gather_level1(region, rest, beta, diag, outer):
-    region[0, 1:6] = outer[0, 0:5]
+    blank = jnp.zeros((2, LANES), jnp.float32)
+    for side, start in ((0, 0), (1, 10)):
+        at = 0
+        for kind, first_plane, count in ((0, 1 - side, 5), (1, 0, 6), (2, 1 - side, 5)):
+            for plane in range(start + first_plane, start + first_plane + count):
+                region[kind, plane, 0:2, :] = blank
+                region[kind, plane, 2:14, :] = outer[side, at : at + 12, :]
+                region[kind, plane, 14:16, :] = blank
+                at += 12
     region[0, 6:10] = rest[1:5]
-    region[0, 10:15] = outer[1, 0:5]
-    region[1, 0:6] = outer[0, 5:11]
     region[1, 6:10] = beta[2:6]
-    region[1, 10:16] = outer[1, 5:11]
-    region[2, 1:6] = outer[0, 11:16]
     region[2, 6:10] = diag[1:5]
-    region[2, 10:15] = outer[1, 11:16]
 
 
 CHUNK1 = 4
@@ -560,7 +569,7 @@
     plane = buffer(24, ROWS0, LANES)
     scratch = [plane] * 7 + [buffer(20, 64, LANES)]
     coarse = lambda count: f32(count, ROWS1, LANES)
-    out = (f32(7, KEPT0, KEPT_ROWS0, LANES), coarse(6), coarse(8), coarse(6), coarse(4))
+    out = (f32(7, KEPT0, KEPT_ROWS0, LANES), coarse(6), coarse(8), coarse(6), coarse(4), f32(192, LANES))
     return call(pre0_kernel, out, scratch, "pre0", *pieces)
 
 
@@ -632,11 +641,9 @@
             sent.append(jnp.where(first_core, rows[LAYER - reach :, kind], rows[:reach, kind]))
     rest = layers_apart(tiles_of(sent), 1)
     outer = both(tiles_of([outer]))
-    kept0, rest1, beta1, diag1, absorb1 = pre0(layer, outer, both(rest))
-
-    upwards = jnp.concatenate([rest1[0:5], beta1[0:6], diag1[0:5]])
-    downwards = jnp.concatenate([rest1[1:6], beta1[2:8], diag1[1:6]])
-    outer = both(layers_apart(jnp.where(first_core, upwards, downwards), 1))
+    kept0, rest1, beta1, diag1, absorb1, sent1 = pre0(layer, outer, both(rest))
+
+    outer = both(layers_apart(sent1, 1))
     pay, *kept1 = pre1(rest1, beta1, diag1, outer, absorb1)
 
     place = lax.axis_index("gx")

time: 95.4 us -> 95 us (level)
  no operation moved by 1% of the time
where the time goes in v13:
time: 95 us; the launch traced here: 94.5 us
  blocking collectives  67.8 us (71%)
  waiting for transfers between devices  11.7 us (12%)
  Pallas kernels  8.62 us (9%)
  starting transfers between devices  5.16 us (5%)
    all_to_all x1, blocking collectives, body(): rows = lax.all_to_all(pay, 'gx', 0, 0, axis_index_groups=column)  25.7 us
    all_to_all x1, blocking collectives, body(): rows = lax.all_to_all(rows, ('gx', 'gy'), 0, 0, axis_index_groups=cores)  16.7 us
    all_gather x5, blocking collectives, both(): return lax.all_gather(value, 'gx', axis_index_groups=chips)  13.2 us
    all_gather x1, blocking collectives, body(): own = lax.all_gather(local, 'gx', axis_index_groups=near)  12.3 us
    pallas_call x3, Pallas kernels, call(): pl.pallas_call(kernel, out_shape=out, scratch_shapes=scratch, name=name,...  8.62 us
    ppermute x3, waiting for transfers between devices, layers_apart(): lax.ppermute(value, 'gx', [(i, j) for i, j in ways if 0 <= j < count])  7.87 us
    ppermute x3, starting transfers between devices, layers_apart(): lax.ppermute(value, 'gx', [(i, j) for i, j in ways if 0 <= j < count])  3.88 us
    ppermute x1, waiting for transfers between devices, columns_apart(): return lax.ppermute(value, ('gx', 'gy'), ways)  3.8 us
  transfers between devices with their start and end apart: 4, of which 3 were waited for; matrix products, arithmetic and copies ran while one was open for 0% of the time, Pallas kernels for 0%

profile of v13, /device:TPU:1, one launch (start us, length us, event | category | flops | bytes accessed | tf_op | source)
XLA Modules:
  0.0 94.5 jit_solution(11341631307513454983)
XLA Ops:
  0.0 0.8 pad_maximum_fusion.3
  0.8 12.3 %all-gather = f32[12,2,16,128]{3,2,1,0:T(8,128)S(1)} all-gather(f32[3,2,16,128]{3,2,1,0:T(8,128)S(1)} %pad_maximum_fusion.3), channel_id=2, replica_groups={{0,8,16,24},{32,40,48,56},{64,72,80,88},{96,104,112,120},{128,136,144,1..., dimensions={0}, use_global_device_ids=true | all-gather | bytes 245760 | tf_op jit(solution)/shard_map/all_gather | solution.py:628
  13.1 1.3 %collective-permute-start = (f32[4,3,2,16,128]{4,3,2,1,0:T(8,128)S(1)}, f32[4,3,2,16,128]{4,3,2,1,0:T(8,128)S(1)}, u32[]{:S(2)}, u32[]{:S(2)}) collective-permute-start(f32[4,3,2,16,128]{4,3,2,1,0:T(8,128)S(1)} %bitcast.32), channel_id=1, source_target_pairs={{0,1},{1,2},{2,3},{3,4},{4,5},{5,6},{6,7},{9,8},{10,9},{11,10},{12... | collective-permute-start | bytes 589832 | tf_op jit(solution)/shard_map/ppermute | solution.py:607
  14.3 1.3 %collective-permute-start.1 = (f32[4,3,2,16,128]{4,3,2,1,0:T(8,128)S(1)}, f32[4,3,2,16,128]{4,3,2,1,0:T(8,128)S(1)}, u32[]{:S(2)}, u32[]{:S(2)}) collective-permute-start(f32[4,3,2,16,128]{4,3,2,1,0:T(8,128)S(1)} %bitcast.33), channel_id=1, source_target_pairs={{0,32},{16,48},{32,64},{40,8},{48,80},{56,24},{64,96},{72,40},{80,... | collective-permute-start | bytes 589832 | tf_op jit(solution)/shard_map/ppermute | solution.py:596
  15.7 3.8 %collective-permute-done = f32[4,3,2,16,128]{4,3,2,1,0:T(8,128)S(1)} collective-permute-done((f32[4,3,2,16,128]{4,3,2,1,0:T(8,128)S(1)}, f32[4,3,2,16,128]{4,3,2,1,0:T(8,128)S(1)}, u32[]{:S(2)}, u32[]{:S(2)}) %collective-permute-start) | collective-permute-done | bytes 196640 | tf_op jit(solution)/shard_map/ppermute | solution.py:607
  19.5 2.1 %all-gather.1 = f32[8,3,2,16,128]{4,3,2,1,0:T(8,128)S(1)} all-gather(f32[4,3,2,16,128]{4,3,2,1,0:T(8,128)S(1)} %collective-permute-done), channel_id=3, replica_groups={{0,8},{16,24},{32,40},{48,56},{64,72},{80,88},{96,104},{112,120},{128,1..., dimensions={0}, use_global_device_ids=true | all-gather | bytes 589824 | tf_op jit(solution)/shard_map/all_gather | solution.py:625
  21.7 1.3 %collective-permute-start.2 = (f32[68,8,128]{2,1,0:T(8,128)S(1)}, f32[68,8,128]{2,1,0:T(8,128)S(1)}, u32[]{:S(2)}, u32[]{:S(2)}) collective-permute-start(f32[68,8,128]{2,1,0:T(8,128)S(1)} %constant_dynamic-update-slice_fusion), channel_id=1, source_target_pairs={{0,32},{16,48},{32,64},{40,8},{48,80},{56,24},{64,96},{72,40},{80,... | collective-permute-start | bytes 835592 | tf_op jit(solution)/shard_map/ppermute | solution.py:596
  23.0 0.0 collective-permute-done.1
  23.1 2.1 %all_gather.37.outer = f32[2,48,8,128]{3,2,1,0:T(8,128)S(1)} all-gather(f32[1,48,8,128]{3,2,1,0:T(8,128)S(1)} %bitcast.41), channel_id=1, replica_groups={{0,8},{16,24},{32,40},{48,56},{64,72},{80,88},{96,104},{112,120},{128,1..., dimensions={0}, use_global_device_ids=true | all-gather | bytes 589824 | tf_op jit(solution)/shard_map/all_gather | solution.py:625
  25.2 3.8 %collective-permute-done.2 = f32[68,8,128]{2,1,0:T(8,128)S(1)} collective-permute-done((f32[68,8,128]{2,1,0:T(8,128)S(1)}, f32[68,8,128]{2,1,0:T(8,128)S(1)}, u32[]{:S(2)}, u32[]{:S(2)}) %collective-permute-start.2) | collective-permute-done | bytes 278560 | tf_op jit(solution)/shard_map/ppermute | solution.py:596
  29.0 2.2 %all-gather.2 = f32[136,8,128]{2,1,0:T(8,128)S(1)} all-gather(f32[68,8,128]{2,1,0:T(8,128)S(1)} %collective-permute-done.2), channel_id=4, replica_groups={{0,8},{16,24},{32,40},{48,56},{64,72},{80,88},{96,104},{112,120},{128,1..., dimensions={0}, use_global_device_ids=true | all-gather | bytes 835584 | tf_op jit(solution)/shard_map/all_gather | solution.py:625
  31.2 2.3 %pre0.1 = (f32[7,10,32,128]{3,2,1,0:T(8,128)S(1)}, f32[6,16,128]{2,1,0:T(8,128)S(1)}, f32[8,16,128]{2,1,0:T(8,128)S(1)}, f32[6,16,128]{2,1,0:T(8,128)S(1)}, f32[...) custom-call(f32[4,3,2,48,128]{4,3,2,1,0:T(8,128)S(1)} %pad_maximum_fusion.own, f32[2,48,8,128]{3,2,1,0:T(8,128)S(1)} %all_gather.37.outer, ...), custom_call_target="tpu_custom_call" | custom-call | tf_op jit(solution)/shard_map/pre0/pallas_call | solution.py:559
  33.5 1.3 %collective-permute-start.3 = (f32[192,128]{1,0:T(8,128)S(1)}, f32[192,128]{1,0:T(8,128)S(1)}, u32[]{:S(2)}, u32[]{:S(2)}) collective-permute-start(f32[192,128]{1,0:T(8,128)S(1)} %get-tuple-element.24), channel_id=1, source_target_pairs={{0,32},{16,48},{32,64},{40,8},{48,80},{56,24},{64,96},{72,40},{80,... | collective-permute-start | bytes 294920 | tf_op jit(solution)/shard_map/ppermute | solution.py:596
  34.8 4.1 %collective-permute-done.3 = f32[192,128]{1,0:T(8,128)S(1)} collective-permute-done((f32[192,128]{1,0:T(8,128)S(1)}, f32[192,128]{1,0:T(8,128)S(1)}, u32[]{:S(2)}, u32[]{:S(2)}) %collective-permute-start.3) | collective-permute-done | bytes 98336 | tf_op jit(solution)/shard_map/ppermute | solution.py:596
  38.8 1.9 %all-gather.3 = f32[384,128]{1,0:T(8,128)S(1)} all-gather(f32[192,128]{1,0:T(8,128)S(1)} %collective-permute-done.3), channel_id=5, replica_groups={{0,8},{16,24},{32,40},{48,56},{64,72},{80,88},{96,104},{112,120},{128,1..., dimensions={0}, use_global_device_ids=true | all-gather | bytes 294912 | tf_op jit(solution)/shard_map/all_gather | solution.py:625
  40.8 0.9 pre1.1
  41.6 0.1 copy.4
  41.7 25.7 %all_to_all.17 = f32[16,1,768]{2,1,0:T(1,128)S(1)} all-to-all(f32[16,1,768]{2,1,0:T(1,128)S(1)} %copy.4), channel_id=1, replica_groups={{0,32,64,96,128,160,192,224,256,288,320,352,384,416,448,480},{8,40,72,1..., dimensions={0} | all-to-all | bytes 98304 | tf_op jit(solution)/shard_map/all_to_all | solution.py:652
  67.5 16.7 %all_to_all.18 = f32[16,48,128]{2,1,0:T(8,128)S(1)} all-to-all(f32[16,48,128]{2,1,0:T(8,128)S(1)} %broadcast_in_dim.3), channel_id=1, replica_groups={{0,1,2,3,4,5,6,7,16,17,18,19,20,21,22,23},{8,9,10,11,12,13,14,15,24,25,..., dimensions={0} | all-to-all | bytes 786432 | tf_op jit(solution)/shard_map/all_to_all | solution.py:658
  84.2 4.9 %all-gather.4.packed = f32[32,48,128]{2,1,0:T(8,128)S(1)} all-gather(f32[16,48,128]{2,1,0:T(8,128)S(1)} %all_to_all.18), channel_id=6, replica_groups={{0,8},{16,24},{32,40},{48,56},{64,72},{80,88},{96,104},{112,120},{128,1..., dimensions={0}, use_global_device_ids=true | all-gather | bytes 1179648 | tf_op jit(solution)/shard_map/all_gather | solution.py:625
  89.0 5.5 %finish.1 = f32[2,16,128]{2,1,0:T(8,128)} custom-call(f32[1536,128]{1,0:T(8,128)S(1)} %bitcast.27, f32[32,48,128]{2,1,0:T(8,128)S(1)} %all-gather.4.packed, f32[3,16,16,128]{3,2,1,0:T(8,128)S(1)} %get-tuple-element.31.region1, f32[16,16,128]{2,1,0:T(8,128)S(1)} %get-tuple-element.32.inverse1, f32[16,16,128]{2,1,0:T(8,128)S(1)} %get-tuple-element.33.first1, ...), custom_call_target="tpu_custom_call" | custom-call | tf_op jit(solution)/shard_map/finish/pallas_call | solution.py:559
  (20 shorter events, 0.2 us)
Async XLA Ops:
  13.1 6.4 %collective-permute-start = (f32[4,3,2,16,128]{4,3,2,1,0:T(8,128)S(1)}, f32[4,3,2,16,128]{4,3,2,1,0:T(8,128)S(1)}, u32[]{:S(2)}, u32[]{:S(2)}) collective-permute-start(f32[4,3,2,16,128]{4,3,2,1,0:T(8,128)S(1)} %bitcast.32), channel_id=1, source_target_pairs={{0,1},{1,2},{2,3},{3,4},{4,5},{5,6},{6,7},{9,8},{10,9},{11,10},{12... | collective-permute-start | bytes 589832 | tf_op jit(solution)/shard_map/ppermute | solution.py:607
  14.3 8.7 %collective-permute-start.1 = (f32[4,3,2,16,128]{4,3,2,1,0:T(8,128)S(1)}, f32[4,3,2,16,128]{4,3,2,1,0:T(8,128)S(1)}, u32[]{:S(2)}, u32[]{:S(2)}) collective-permute-start(f32[4,3,2,16,128]{4,3,2,1,0:T(8,128)S(1)} %bitcast.33), channel_id=1, source_target_pairs={{0,32},{16,48},{32,64},{40,8},{48,80},{56,24},{64,96},{72,40},{80,... | collective-permute-start | bytes 589832 | tf_op jit(solution)/shard_map/ppermute | solution.py:596
  21.7 7.3 %collective-permute-start.2 = (f32[68,8,128]{2,1,0:T(8,128)S(1)}, f32[68,8,128]{2,1,0:T(8,128)S(1)}, u32[]{:S(2)}, u32[]{:S(2)}) collective-permute-start(f32[68,8,128]{2,1,0:T(8,128)S(1)} %constant_dynamic-update-slice_fusion), channel_id=1, source_target_pairs={{0,32},{16,48},{32,64},{40,8},{48,80},{56,24},{64,96},{72,40},{80,... | collective-permute-start | bytes 835592 | tf_op jit(solution)/shard_map/ppermute | solution.py:596
  33.5 5.4 %collective-permute-start.3 = (f32[192,128]{1,0:T(8,128)S(1)}, f32[192,128]{1,0:T(8,128)S(1)}, u32[]{:S(2)}, u32[]{:S(2)}) collective-permute-start(f32[192,128]{1,0:T(8,128)S(1)} %get-tuple-element.24), channel_id=1, source_target_pairs={{0,32},{16,48},{32,64},{40,8},{48,80},{56,24},{64,96},{72,40},{80,... | collective-permute-start | bytes 294920 | tf_op jit(solution)/shard_map/ppermute | solution.py:596

commit v14 on v13

--- a/solution.py
+++ b/solution.py
@@ -202,6 +202,13 @@
 ENDS = (40, 48, 56)
 KEPT0 = 10
 KEPT_ROWS0 = 32
+
+
+MESSAGE1 = [(kind, away) for kind in range(3) for away in range(1, 7 if kind == 1 else 6)]
+
+
+def message_rows(kind, away):
+    return (2, 14) if away < (3 if kind == 1 else 2) else (4, 12)
 
 
 def pre0_kernel(
@@ -265,10 +272,12 @@
     absorb_out[...] = wide[1:5]
     core = position() & 1
     at = 0
-    for ref, count, first_plane in ((rest_out, 5, core), (beta_out, 6, 2 * core), (diag_out, 5, core)):
-        for plane in range(count):
-            send_out[at : at + 12, :] = ref[first_plane + plane, 2:14, :]
-            at += 12
+    for kind, away in MESSAGE1:
+        ref, near = ((rest_out, 5), (beta_out, 6), (diag_out, 5))[kind]
+        low, high = message_rows(kind, away)
+        plane = near - away + core * (2 * away - 5)
+        send_out[at : at + high - low, :] = ref[plane, low:high, :]
+        at += high - low
 
 
 DEPTH1 = 16
@@ -276,15 +285,15 @@
 
 
 def gather_level1(region, rest, beta, diag, outer):
-    blank = jnp.zeros((2, LANES), jnp.float32)
-    for side, start in ((0, 0), (1, 10)):
+    for side in range(2):
         at = 0
-        for kind, first_plane, count in ((0, 1 - side, 5), (1, 0, 6), (2, 1 - side, 5)):
-            for plane in range(start + first_plane, start + first_plane + count):
-                region[kind, plane, 0:2, :] = blank
-                region[kind, plane, 2:14, :] = outer[side, at : at + 12, :]
-                region[kind, plane, 14:16, :] = blank
-                at += 12
+        for kind, away in MESSAGE1:
+            plane = 6 - away if side == 0 else 9 + away
+            low, high = message_rows(kind, away)
+            region[kind, plane, 0:low, :] = jnp.zeros((low, LANES), jnp.float32)
+            region[kind, plane, low:high, :] = outer[side, at : at + high - low, :]
+            region[kind, plane, high:16, :] = jnp.zeros((16 - high, LANES), jnp.float32)
+            at += high - low
     region[0, 6:10] = rest[1:5]
     region[1, 6:10] = beta[2:6]
     region[2, 6:10] = diag[1:5]
@@ -569,7 +578,7 @@
     plane = buffer(24, ROWS0, LANES)
     scratch = [plane] * 7 + [buffer(20, 64, LANES)]
     coarse = lambda count: f32(count, ROWS1, LANES)
-    out = (f32(7, KEPT0, KEPT_ROWS0, LANES), coarse(6), coarse(8), coarse(6), coarse(4), f32(192, LANES))
+    out = (f32(7, KEPT0, KEPT_ROWS0, LANES), coarse(6), coarse(8), coarse(6), coarse(4), f32(144, LANES))
     return call(pre0_kernel, out, scratch, "pre0", *pieces)
 
 

time: 95 us -> 94.7 us (level)
  no operation moved by 1% of the time
where the time goes in v14:
time: 94.7 us; the launch traced here: 94.2 us
  blocking collectives  67.8 us (72%)
  waiting for transfers between devices  11.4 us (12%)
  Pallas kernels  8.61 us (9%)
  starting transfers between devices  5.16 us (5%)
    all_to_all x1, blocking collectives, body(): rows = lax.all_to_all(pay, 'gx', 0, 0, axis_index_groups=column)  25.7 us
    all_to_all x1, blocking collectives, body(): rows = lax.all_to_all(rows, ('gx', 'gy'), 0, 0, axis_index_groups=cores)  16.7 us
    all_gather x5, blocking collectives, both(): return lax.all_gather(value, 'gx', axis_index_groups=chips)  13.1 us
    all_gather x1, blocking collectives, body(): own = lax.all_gather(local, 'gx', axis_index_groups=near)  12.3 us
    pallas_call x3, Pallas kernels, call(): pl.pallas_call(kernel, out_shape=out, scratch_shapes=scratch, name=name,...  8.61 us
    ppermute x3, waiting for transfers between devices, layers_apart(): lax.ppermute(value, 'gx', [(i, j) for i, j in ways if 0 <= j < count])  7.61 us
    ppermute x3, starting transfers between devices, layers_apart(): lax.ppermute(value, 'gx', [(i, j) for i, j in ways if 0 <= j < count])  3.88 us
    ppermute x1, waiting for transfers between devices, columns_apart(): return lax.ppermute(value, ('gx', 'gy'), ways)  3.8 us
  transfers between devices with their start and end apart: 4, of which 3 were waited for; matrix products, arithmetic and copies ran while one was open for 0% of the time, Pallas kernels for 0%

profile of v14, /device:TPU:1, one launch (start us, length us, event | category | flops | bytes accessed | tf_op | source)
XLA Modules:
  0.0 94.2 jit_solution(6735353373091720724)
XLA Ops:
  0.0 0.8 pad_maximum_fusion.3
  0.8 12.3 %all-gather = f32[12,2,16,128]{3,2,1,0:T(8,128)S(1)} all-gather(f32[3,2,16,128]{3,2,1,0:T(8,128)S(1)} %pad_maximum_fusion.3), channel_id=2, replica_groups={{0,8,16,24},{32,40,48,56},{64,72,80,88},{96,104,112,120},{128,136,144,1..., dimensions={0}, use_global_device_ids=true | all-gather | bytes 245760 | tf_op jit(solution)/shard_map/all_gather | solution.py:637
  13.1 1.3 %collective-permute-start = (f32[4,3,2,16,128]{4,3,2,1,0:T(8,128)S(1)}, f32[4,3,2,16,128]{4,3,2,1,0:T(8,128)S(1)}, u32[]{:S(2)}, u32[]{:S(2)}) collective-permute-start(f32[4,3,2,16,128]{4,3,2,1,0:T(8,128)S(1)} %bitcast.32), channel_id=1, source_target_pairs={{0,1},{1,2},{2,3},{3,4},{4,5},{5,6},{6,7},{9,8},{10,9},{11,10},{12... | collective-permute-start | bytes 589832 | tf_op jit(solution)/shard_map/ppermute | solution.py:616
  14.3 1.3 %collective-permute-start.1 = (f32[4,3,2,16,128]{4,3,2,1,0:T(8,128)S(1)}, f32[4,3,2,16,128]{4,3,2,1,0:T(8,128)S(1)}, u32[]{:S(2)}, u32[]{:S(2)}) collective-permute-start(f32[4,3,2,16,128]{4,3,2,1,0:T(8,128)S(1)} %bitcast.33), channel_id=1, source_target_pairs={{0,32},{16,48},{32,64},{40,8},{48,80},{56,24},{64,96},{72,40},{80,... | collective-permute-start | bytes 589832 | tf_op jit(solution)/shard_map/ppermute | solution.py:605
  15.7 3.8 %collective-permute-done = f32[4,3,2,16,128]{4,3,2,1,0:T(8,128)S(1)} collective-permute-done((f32[4,3,2,16,128]{4,3,2,1,0:T(8,128)S(1)}, f32[4,3,2,16,128]{4,3,2,1,0:T(8,128)S(1)}, u32[]{:S(2)}, u32[]{:S(2)}) %collective-permute-start) | collective-permute-done | bytes 196640 | tf_op jit(solution)/shard_map/ppermute | solution.py:616
  19.5 2.1 %all-gather.1 = f32[8,3,2,16,128]{4,3,2,1,0:T(8,128)S(1)} all-gather(f32[4,3,2,16,128]{4,3,2,1,0:T(8,128)S(1)} %collective-permute-done), channel_id=3, replica_groups={{0,8},{16,24},{32,40},{48,56},{64,72},{80,88},{96,104},{112,120},{128,1..., dimensions={0}, use_global_device_ids=true | all-gather | bytes 589824 | tf_op jit(solution)/shard_map/all_gather | solution.py:634
  21.7 1.3 %collective-permute-start.2 = (f32[68,8,128]{2,1,0:T(8,128)S(1)}, f32[68,8,128]{2,1,0:T(8,128)S(1)}, u32[]{:S(2)}, u32[]{:S(2)}) collective-permute-start(f32[68,8,128]{2,1,0:T(8,128)S(1)} %constant_dynamic-update-slice_fusion), channel_id=1, source_target_pairs={{0,32},{16,48},{32,64},{40,8},{48,80},{56,24},{64,96},{72,40},{80,... | collective-permute-start | bytes 835592 | tf_op jit(solution)/shard_map/ppermute | solution.py:605
  23.0 0.0 collective-permute-done.1
  23.1 2.1 %all_gather.37.outer = f32[2,48,8,128]{3,2,1,0:T(8,128)S(1)} all-gather(f32[1,48,8,128]{3,2,1,0:T(8,128)S(1)} %bitcast.41), channel_id=1, replica_groups={{0,8},{16,24},{32,40},{48,56},{64,72},{80,88},{96,104},{112,120},{128,1..., dimensions={0}, use_global_device_ids=true | all-gather | bytes 589824 | tf_op jit(solution)/shard_map/all_gather | solution.py:634
  25.2 3.8 %collective-permute-done.2 = f32[68,8,128]{2,1,0:T(8,128)S(1)} collective-permute-done((f32[68,8,128]{2,1,0:T(8,128)S(1)}, f32[68,8,128]{2,1,0:T(8,128)S(1)}, u32[]{:S(2)}, u32[]{:S(2)}) %collective-permute-start.2) | collective-permute-done | bytes 278560 | tf_op jit(solution)/shard_map/ppermute | solution.py:605
  29.0 2.2 %all-gather.2 = f32[136,8,128]{2,1,0:T(8,128)S(1)} all-gather(f32[68,8,128]{2,1,0:T(8,128)S(1)} %collective-permute-done.2), channel_id=4, replica_groups={{0,8},{16,24},{32,40},{48,56},{64,72},{80,88},{96,104},{112,120},{128,1..., dimensions={0}, use_global_device_ids=true | all-gather | bytes 835584 | tf_op jit(solution)/shard_map/all_gather | solution.py:634
  31.2 2.3 %pre0.1 = (f32[7,10,32,128]{3,2,1,0:T(8,128)S(1)}, f32[6,16,128]{2,1,0:T(8,128)S(1)}, f32[8,16,128]{2,1,0:T(8,128)S(1)}, f32[6,16,128]{2,1,0:T(8,128)S(1)}, f32[...) custom-call(f32[4,3,2,48,128]{4,3,2,1,0:T(8,128)S(1)} %pad_maximum_fusion.own, f32[2,48,8,128]{3,2,1,0:T(8,128)S(1)} %all_gather.37.outer, ...), custom_call_target="tpu_custom_call" | custom-call | tf_op jit(solution)/shard_map/pre0/pallas_call | solution.py:568
  33.5 1.3 %collective-permute-start.3 = (f32[144,128]{1,0:T(8,128)S(1)}, f32[144,128]{1,0:T(8,128)S(1)}, u32[]{:S(2)}, u32[]{:S(2)}) collective-permute-start(f32[144,128]{1,0:T(8,128)S(1)} %get-tuple-element.24), channel_id=1, source_target_pairs={{0,32},{16,48},{32,64},{40,8},{48,80},{56,24},{64,96},{72,40},{80,... | collective-permute-start | bytes 221192 | tf_op jit(solution)/shard_map/ppermute | solution.py:605
  34.8 3.8 %collective-permute-done.3 = f32[144,128]{1,0:T(8,128)S(1)} collective-permute-done((f32[144,128]{1,0:T(8,128)S(1)}, f32[144,128]{1,0:T(8,128)S(1)}, u32[]{:S(2)}, u32[]{:S(2)}) %collective-permute-start.3) | collective-permute-done | bytes 73760 | tf_op jit(solution)/shard_map/ppermute | solution.py:605
  38.6 1.9 %all-gather.3 = f32[288,128]{1,0:T(8,128)S(1)} all-gather(f32[144,128]{1,0:T(8,128)S(1)} %collective-permute-done.3), channel_id=5, replica_groups={{0,8},{16,24},{32,40},{48,56},{64,72},{80,88},{96,104},{112,120},{128,1..., dimensions={0}, use_global_device_ids=true | all-gather | bytes 221184 | tf_op jit(solution)/shard_map/all_gather | solution.py:634
  40.5 0.8 pre1.1
  41.3 0.1 copy.4
  41.4 25.7 %all_to_all.17 = f32[16,1,768]{2,1,0:T(1,128)S(1)} all-to-all(f32[16,1,768]{2,1,0:T(1,128)S(1)} %copy.4), channel_id=1, replica_groups={{0,32,64,96,128,160,192,224,256,288,320,352,384,416,448,480},{8,40,72,1..., dimensions={0} | all-to-all | bytes 98304 | tf_op jit(solution)/shard_map/all_to_all | solution.py:661
  67.2 16.7 %all_to_all.18 = f32[16,48,128]{2,1,0:T(8,128)S(1)} all-to-all(f32[16,48,128]{2,1,0:T(8,128)S(1)} %broadcast_in_dim.3), channel_id=1, replica_groups={{0,1,2,3,4,5,6,7,16,17,18,19,20,21,22,23},{8,9,10,11,12,13,14,15,24,25,..., dimensions={0} | all-to-all | bytes 786432 | tf_op jit(solution)/shard_map/all_to_all | solution.py:667
  83.9 4.9 %all-gather.4.packed = f32[32,48,128]{2,1,0:T(8,128)S(1)} all-gather(f32[16,48,128]{2,1,0:T(8,128)S(1)} %all_to_all.18), channel_id=6, replica_groups={{0,8},{16,24},{32,40},{48,56},{64,72},{80,88},{96,104},{112,120},{128,1..., dimensions={0}, use_global_device_ids=true | all-gather | bytes 1179648 | tf_op jit(solution)/shard_map/all_gather | solution.py:634
  88.7 5.5 %finish.1 = f32[2,16,128]{2,1,0:T(8,128)} custom-call(f32[1536,128]{1,0:T(8,128)S(1)} %bitcast.27, f32[32,48,128]{2,1,0:T(8,128)S(1)} %all-gather.4.packed, f32[3,16,16,128]{3,2,1,0:T(8,128)S(1)} %get-tuple-element.31.region1, f32[16,16,128]{2,1,0:T(8,128)S(1)} %get-tuple-element.32.inverse1, f32[16,16,128]{2,1,0:T(8,128)S(1)} %get-tuple-element.33.first1, ...), custom_call_target="tpu_custom_call" | custom-call | tf_op jit(solution)/shard_map/finish/pallas_call | solution.py:568
  (20 shorter events, 0.2 us)
Async XLA Ops:
  13.1 6.4 %collective-permute-start = (f32[4,3,2,16,128]{4,3,2,1,0:T(8,128)S(1)}, f32[4,3,2,16,128]{4,3,2,1,0:T(8,128)S(1)}, u32[]{:S(2)}, u32[]{:S(2)}) collective-permute-start(f32[4,3,2,16,128]{4,3,2,1,0:T(8,128)S(1)} %bitcast.32), channel_id=1, source_target_pairs={{0,1},{1,2},{2,3},{3,4},{4,5},{5,6},{6,7},{9,8},{10,9},{11,10},{12... | collective-permute-start | bytes 589832 | tf_op jit(solution)/shard_map/ppermute | solution.py:616
  14.3 8.7 %collective-permute-start.1 = (f32[4,3,2,16,128]{4,3,2,1,0:T(8,128)S(1)}, f32[4,3,2,16,128]{4,3,2,1,0:T(8,128)S(1)}, u32[]{:S(2)}, u32[]{:S(2)}) collective-permute-start(f32[4,3,2,16,128]{4,3,2,1,0:T(8,128)S(1)} %bitcast.33), channel_id=1, source_target_pairs={{0,32},{16,48},{32,64},{40,8},{48,80},{56,24},{64,96},{72,40},{80,... | collective-permute-start | bytes 589832 | tf_op jit(solution)/shard_map/ppermute | solution.py:605
  21.7 7.3 %collective-permute-start.2 = (f32[68,8,128]{2,1,0:T(8,128)S(1)}, f32[68,8,128]{2,1,0:T(8,128)S(1)}, u32[]{:S(2)}, u32[]{:S(2)}) collective-permute-start(f32[68,8,128]{2,1,0:T(8,128)S(1)} %constant_dynamic-update-slice_fusion), channel_id=1, source_target_pairs={{0,32},{16,48},{32,64},{40,8},{48,80},{56,24},{64,96},{72,40},{80,... | collective-permute-start | bytes 835592 | tf_op jit(solution)/shard_map/ppermute | solution.py:605
  33.5 5.1 %collective-permute-start.3 = (f32[144,128]{1,0:T(8,128)S(1)}, f32[144,128]{1,0:T(8,128)S(1)}, u32[]{:S(2)}, u32[]{:S(2)}) collective-permute-start(f32[144,128]{1,0:T(8,128)S(1)} %get-tuple-element.24), channel_id=1, source_target_pairs={{0,32},{16,48},{32,64},{40,8},{48,80},{56,24},{64,96},{72,40},{80,... | collective-permute-start | bytes 221192 | tf_op jit(solution)/shard_map/ppermute | solution.py:605
